TPU v7x, 32 devices: a whole 2x2x4 slice. The times are simulated.
32 devices in a mesh: rep: 8 (over y, x, core), ep: 4 (over z).
Axes of the slice: x: 2, y: 2, z: 4, core: 2. Of those that a mesh axis runs over, the one named last changes fastest.
Arguments:
- tokens: bfloat16 [16384, 2048], P(('rep', 'ep')), may hold values from -6 to 6
- teacher: bfloat16 [16384, 2048], P(('rep', 'ep')), may hold values from -6 to 6
- segment_ids: int32 [8, 2048], P('rep', 'ep'), may hold values from 0 to 4, as said below
- valid_mask: int32 [8, 2048], P('rep', 'ep'), may hold values from 0 to 1
- routes: int32 [16384, 2], P(('rep', 'ep')), may hold values from 0 to 3, all different within a row; in each aligned block of 512 rows (0 to 511, 512 to 1023, ...) at most 320 rows name the same one
- attn_gain: bfloat16 [2048], P(('rep', 'ep')), may hold values from 0.5 to 1.5
- q_gain: bfloat16 [2048], P(('rep', 'ep')), may hold values from 0.5 to 1.5
- k_gain: bfloat16 [2048], P(('rep', 'ep')), may hold values from 0.5 to 1.5
- moe_gain: bfloat16 [2048], P(('rep', 'ep')), may hold values from 0.5 to 1.5
- w_query: bfloat16 [2048, 2048], P(('rep', 'ep')), may hold values from -0.125 to 0.125
- w_key: bfloat16 [2048, 2048], P(('rep', 'ep')), may hold values from -0.125 to 0.125
- w_value: bfloat16 [2048, 2048], P(('rep', 'ep')), may hold values from -0.125 to 0.125
- w_out: bfloat16 [2048, 2048], P(('rep', 'ep')), may hold values from -2 to 2
- w_router: bfloat16 [2048, 4], P(('rep', 'ep')), may hold values from -0.0625 to 0.0625
- w_gate: bfloat16 [4, 2048, 1024], P('ep'), may hold values from -0.125 to 0.125
- w_up: bfloat16 [4, 2048, 1024], P('ep'), may hold values from -0.125 to 0.125
- w_down: bfloat16 [4, 1024, 2048], P('ep'), may hold values from -1.5 to 1.5
Outputs:
- output: bfloat16 [16384, 2048], P(('rep', 'ep'))
- loss: float32 [], replicated
- tokens_grad: float32 [16384, 2048], P(('rep', 'ep'))
- attn_gain_grad: float32 [2048], P(('rep', 'ep'))
- q_gain_grad: float32 [2048], P(('rep', 'ep'))
- k_gain_grad: float32 [2048], P(('rep', 'ep'))
- moe_gain_grad: float32 [2048], P(('rep', 'ep'))
- query_grad: float32 [2048, 2048], P(('rep', 'ep'))
- key_grad: float32 [2048, 2048], P(('rep', 'ep'))
- value_grad: float32 [2048, 2048], P(('rep', 'ep'))
- out_grad: float32 [2048, 2048], P(('rep', 'ep'))
- router_grad: float32 [2048, 4], P(('rep', 'ep'))
- gate_grad: float32 [4, 2048, 1024], P('ep', 'rep')
- up_grad: float32 [4, 2048, 1024], P('ep', 'rep')
- down_grad: float32 [4, 1024, 2048], P('ep', 'rep')
Inputs may be any that keep to these rules, and one draw needn't show every extreme that they name: `routes`: each row names 2 different experts; within the rows of one device no expert is named by more than 320 rows. `segment_ids`: within each sequence the numbers start at 0 and never fall.
All inputs are finite; a program needn't handle non-finite values.
Results may differ from a plain program's by a relative error of at most 0.012.
The roundings to bfloat16 on the way count: a program that leaves them out, or rounds other values in their place, can miss the bound.
Values may be sent and summed in bfloat16 or wider, within the bound.
No kernel may reach another device: no remote copies, remote signals or barrier semaphores. Data moves between devices by JAX's collectives and lax.ppermute only.
A program may use at most 320 MiB of HBM per device.

v0:
```python
import jax
import jax.numpy as jnp
from jax import lax
from jax.sharding import PartitionSpec as P

HEADS = 16
HEAD_DIM = 128
WINDOW = 1024
TOP = 2


norm_eps = 1e-05
highest = lax.Precision.HIGHEST


def from_behind(value, axis, steps):
    count = lax.axis_size(axis)
    leading, last = (max(0, -steps), min(count, count - steps))
    return lax.ppermute(value, axis, [(source, source + steps) for source in range(leading, last)])


def matmul(left, right):
    return jnp.dot(left, right, preferred_element_type=jnp.float32)


def rms_scale(value):
    return lax.rsqrt(jnp.mean(value * value, axis=-1, keepdims=True) + norm_eps)


def norm_back(value, scale, gain, grad):
    weighted = grad * gain
    inner = jnp.mean(weighted * value, axis=-1, keepdims=True)
    return (
        scale * weighted - value * (scale * scale * scale) * inner,
        jnp.sum(grad * value * scale, axis=0),
    )


def rounded(value):
    return lax.optimization_barrier(value.astype(jnp.bfloat16)).astype(jnp.float32)


def rotary_tables(positions, head_size):
    half = head_size // 2
    frequency = 10000.0 ** (-jnp.arange(half, dtype=jnp.float32) * 2.0 / head_size)
    angles = positions[:, None].astype(jnp.float32) * frequency[None, :]
    cosine = jnp.cos(angles)
    sine = jnp.sin(angles)
    return (
        jnp.concatenate([cosine, cosine], -1)[:, None, :],
        jnp.concatenate([sine, sine], -1)[:, None, :],
    )


def rotate(value, cosine, sine):
    half = value.shape[-1] // 2
    turned = jnp.concatenate([-value[..., half:], value[..., :half]], -1)
    return value * cosine + turned * sine


def rotate_back(grad, cosine, sine):
    half = grad.shape[-1] // 2
    scaled = grad * sine
    turned = jnp.concatenate([scaled[..., half:], -scaled[..., :half]], -1)
    return grad * cosine + turned


def unpack(everything):
    gains = [everything[index].astype(jnp.float32) for index in range(4)]
    return (gains, everything[4], everything[5], everything[6], everything[7], everything[8])


def body(
    tokens,
    teacher,
    segment_ids,
    valid_mask,
    routes,
    attn_gain,
    q_gain,
    k_gain,
    moe_gain,
    w_query,
    w_key,
    w_value,
    w_out,
    w_router,
    w_gate,
    w_up,
    w_down,
):
    local_rows, width = tokens.shape
    experts = lax.axis_size("ep")
    pairs = local_rows * TOP
    capacity = 5 * pairs // (4 * experts)
    reach = min(-(-WINDOW // local_rows), experts - 1)
    group = min(HEADS, 4)
    score_scale = HEAD_DIM ** (-0.5)
    shard = lax.axis_index("ep")
    total_tokens = local_rows * lax.axis_size("rep") * experts
    everything = (
        lax.all_gather(attn_gain, ("rep", "ep"), axis=0, tiled=True),
        lax.all_gather(q_gain, ("rep", "ep"), axis=0, tiled=True),
        lax.all_gather(k_gain, ("rep", "ep"), axis=0, tiled=True),
        lax.all_gather(moe_gain, ("rep", "ep"), axis=0, tiled=True),
        lax.all_gather(w_query, ("rep", "ep"), axis=0, tiled=True),
        lax.all_gather(w_key, ("rep", "ep"), axis=0, tiled=True),
        lax.all_gather(w_value, ("rep", "ep"), axis=0, tiled=True),
        lax.all_gather(w_out, ("rep", "ep"), axis=0, tiled=True),
        lax.all_gather(w_router, ("rep", "ep"), axis=0, tiled=True),
    )
    gains, weight_query, weight_key, weight_value, weight_out, weight_router = unpack(everything)
    gain_attn, gain_query, gain_key, gain_moe = gains
    inputs = tokens.astype(jnp.float32)
    scale_attn = rms_scale(inputs)
    normed = (inputs * scale_attn * gain_attn).astype(jnp.bfloat16)
    query_lin = matmul(normed, weight_query)
    key_lin = matmul(normed, weight_key)
    value_rows = (
        matmul(normed, weight_value).astype(jnp.bfloat16).reshape(local_rows, HEADS, HEAD_DIM)
    )
    scale_query = rms_scale(query_lin)
    scale_key = rms_scale(key_lin)
    positions = shard * local_rows + jnp.arange(local_rows, dtype=jnp.int32)
    cosine, sine = rotary_tables(positions, HEAD_DIM)
    query_rows = rotate(
        (query_lin * scale_query * gain_query).reshape(local_rows, HEADS, HEAD_DIM), cosine, sine
    ).astype(jnp.bfloat16)
    key_rows = rotate(
        (key_lin * scale_key * gain_key).reshape(local_rows, HEADS, HEAD_DIM), cosine, sine
    ).astype(jnp.bfloat16)
    segments = segment_ids.reshape(local_rows)
    key_parts, value_parts, segment_parts = ([], [], [])
    for back in range(reach, 0, -1):
        moved = from_behind((key_rows, value_rows, segments.astype(jnp.bfloat16)), "ep", back)
        key_parts.append(moved[0])
        value_parts.append(moved[1])
        segment_parts.append(moved[2].astype(jnp.int32))
    all_keys = jnp.concatenate(key_parts + [key_rows], 0)
    all_values = jnp.concatenate(value_parts + [value_rows], 0)
    key_segments = jnp.concatenate(segment_parts + [segments], 0)
    key_positions = (shard - reach) * local_rows + jnp.arange(
        (reach + 1) * local_rows, dtype=jnp.int32
    )
    distance = positions[:, None] - key_positions[None, :]
    allowed = (
        (distance >= 0)
        & (distance < WINDOW)
        & (key_positions[None, :] >= 0)
        & (segments[:, None] == key_segments[None, :])
    )

    def by_group(value):
        return jnp.moveaxis(value.reshape(value.shape[0], HEADS // group, group, HEAD_DIM), 1, 0)

    def from_group(value):
        return jnp.moveaxis(value, 0, 1).reshape(value.shape[1], HEADS * HEAD_DIM)

    def scores_of(query_group, key_group):
        raw = (
            jnp.einsum("qhd,khd->hqk", query_group, key_group, preferred_element_type=jnp.float32)
            * score_scale
        )
        return jnp.where(allowed[None], raw, -1e30)

    def attend_forward(item):
        query_group, key_group, value_group = item
        scores = scores_of(query_group, key_group)
        peak = jnp.max(scores, axis=-1, keepdims=True)
        shifted = jnp.exp(scores - peak)
        total = jnp.sum(shifted, axis=-1, keepdims=True)
        weights = (shifted / total).astype(jnp.bfloat16)
        mixed = jnp.einsum("hqk,khd->qhd", weights, value_group, preferred_element_type=jnp.float32)
        return (mixed, peak, total)

    query_groups = by_group(query_rows)
    key_groups = by_group(all_keys)
    value_groups = by_group(all_values)
    mixed, peaks, totals = lax.map(attend_forward, (query_groups, key_groups, value_groups))
    mixed_rows = from_group(mixed).astype(jnp.bfloat16)
    residual = inputs + matmul(mixed_rows, weight_out)
    scale_moe = rms_scale(residual)
    normed_moe = (residual * scale_moe * gain_moe).astype(jnp.bfloat16)
    router_probs = jax.nn.softmax(matmul(normed_moe, weight_router), axis=-1)
    flat_routes = routes.reshape(pairs)
    choose = (flat_routes[:, None] == jnp.arange(experts, dtype=jnp.int32)[None, :]).astype(
        jnp.int32
    )
    rank = jnp.sum((jnp.cumsum(choose, axis=0) - choose) * choose, axis=1)
    slots = flat_routes * capacity + rank
    pair_source = (
        jnp.full((experts * capacity,), pairs, jnp.int32)
        .at[slots]
        .set(jnp.arange(pairs, dtype=jnp.int32))
    )
    token_source = jnp.where(pair_source < pairs, pair_source // TOP, local_rows)
    zero_row = jnp.zeros((1, width), jnp.bfloat16)
    outgoing = jnp.concatenate([normed_moe, zero_row], 0)[token_source].reshape(
        experts, capacity, width
    )
    choose_float = choose.reshape(local_rows, TOP, experts).astype(jnp.float32)
    gate_value = jnp.sum(choose_float * router_probs[:, None, :], axis=2)
    gate_weight = w_gate[0]
    up_weight = w_up[0]
    down_weight = w_down[0]
    piece = lax.all_to_all(outgoing, "ep", split_axis=0, concat_axis=0, tiled=True)
    flat = piece.reshape(-1, width)
    gate_pre = matmul(flat, gate_weight)
    up_pre = matmul(flat, up_weight)
    middle = (jax.nn.silu(gate_pre) * up_pre).astype(jnp.bfloat16)
    expert_out = matmul(middle, down_weight).astype(jnp.bfloat16)
    lead = piece.shape[:2]
    returned = expert_out.reshape(piece.shape)
    gate_kept = gate_pre.reshape(lead + (-1,))
    up_kept = up_pre.reshape(lead + (-1,))
    arrived = lax.all_to_all(returned, "ep", split_axis=0, concat_axis=0, tiled=True)
    expert_rows = arrived.reshape(experts * capacity, width)[slots].reshape(local_rows, TOP, width)
    result = residual + jnp.sum(gate_value[:, :, None] * expert_rows, axis=1)
    output = result.astype(jnp.bfloat16)
    valid = valid_mask.reshape(local_rows).astype(jnp.float32)
    error = result - teacher.astype(jnp.float32)
    squares = jnp.sum(valid * jnp.sum(error * error, axis=1))
    total_squares, count = lax.psum((squares, jnp.sum(valid)), ("rep", "ep"))
    loss = total_squares / (2.0 * count * width)
    result_grad = total_tokens / count * valid[:, None] * error
    gate_value_grad = jnp.sum(result_grad[:, None, :] * expert_rows, axis=2)
    pair_grad = (
        (gate_value[:, :, None] * result_grad[:, None, :])
        .astype(jnp.bfloat16)
        .reshape(pairs, width)
    )
    grad_outgoing = jnp.concatenate([pair_grad, zero_row], 0)[pair_source].reshape(
        experts, capacity, width
    )
    grad_in = lax.all_to_all(grad_outgoing, "ep", split_axis=0, concat_axis=0, tiled=True)
    rows_in = piece.reshape(-1, width)
    gate_pre = gate_kept.reshape(rows_in.shape[0], -1)
    up_pre = up_kept.reshape(rows_in.shape[0], -1)
    flat_grad = grad_in.reshape(-1, width)
    sigma = jax.nn.sigmoid(gate_pre)
    active = gate_pre * sigma
    middle = (active * up_pre).astype(jnp.bfloat16)
    down_local = matmul(middle.T, flat_grad)
    middle_grad = matmul(flat_grad, down_weight.T)
    gate_pre_grad = (middle_grad * up_pre * sigma * (1.0 + gate_pre * (1.0 - sigma))).astype(
        jnp.bfloat16
    )
    up_pre_grad = (middle_grad * active).astype(jnp.bfloat16)
    gate_local = matmul(rows_in.T, gate_pre_grad)
    up_local = matmul(rows_in.T, up_pre_grad)
    input_grad = (matmul(gate_pre_grad, gate_weight.T) + matmul(up_pre_grad, up_weight.T)).astype(
        jnp.bfloat16
    )
    back_rows = lax.all_to_all(
        input_grad.reshape(experts, capacity, width), "ep", split_axis=0, concat_axis=0, tiled=True
    )
    pair_back = back_rows.reshape(experts * capacity, width)[slots].reshape(local_rows, TOP, width)
    everything = (
        lax.all_gather(attn_gain, ("rep", "ep"), axis=0, tiled=True),
        lax.all_gather(q_gain, ("rep", "ep"), axis=0, tiled=True),
        lax.all_gather(k_gain, ("rep", "ep"), axis=0, tiled=True),
        lax.all_gather(moe_gain, ("rep", "ep"), axis=0, tiled=True),
        lax.all_gather(w_query, ("rep", "ep"), axis=0, tiled=True),
        lax.all_gather(w_key, ("rep", "ep"), axis=0, tiled=True),
        lax.all_gather(w_value, ("rep", "ep"), axis=0, tiled=True),
        lax.all_gather(w_out, ("rep", "ep"), axis=0, tiled=True),
        lax.all_gather(w_router, ("rep", "ep"), axis=0, tiled=True),
    )
    gains, weight_query, weight_key, weight_value, weight_out, weight_router = unpack(everything)
    gain_attn, gain_query, gain_key, gain_moe = gains
    prob_grad = jnp.sum(choose_float * gate_value_grad[:, :, None], axis=1)
    logit_grad = router_probs * (
        prob_grad - jnp.sum(prob_grad * router_probs, axis=-1, keepdims=True)
    )
    router_local = jnp.dot(
        normed_moe.T, logit_grad, precision=highest, preferred_element_type=jnp.float32
    )
    normed_moe_grad = jnp.sum(pair_back.astype(jnp.float32), axis=1) + jnp.dot(
        logit_grad, weight_router.T, precision=highest, preferred_element_type=jnp.float32
    )
    residual_part, moe_gain_local = norm_back(residual, scale_moe, gain_moe, normed_moe_grad)
    residual_grad = result_grad + residual_part
    branch_grad = residual_grad.astype(jnp.bfloat16)
    out_local = matmul(mixed_rows.T, branch_grad)
    mixed_grad = (
        matmul(branch_grad, weight_out.T).astype(jnp.bfloat16).reshape(local_rows, HEADS, HEAD_DIM)
    )

    def attend_backward(item):
        query_group, key_group, value_group, grad_group, peak, total = item
        scores = scores_of(query_group, key_group)
        probs = jnp.exp(scores - peak) / total
        weights = probs.astype(jnp.bfloat16)
        value_part = jnp.einsum(
            "hqk,qhd->khd", weights, grad_group, preferred_element_type=jnp.float32
        )
        probs_grad = jnp.einsum(
            "qhd,khd->hqk", grad_group, value_group, preferred_element_type=jnp.float32
        )
        inner = jnp.sum(probs * probs_grad, axis=-1, keepdims=True)
        score_grad = (probs * (probs_grad - inner)).astype(jnp.bfloat16)
        query_part = (
            jnp.einsum("hqk,khd->qhd", score_grad, key_group, preferred_element_type=jnp.float32)
            * score_scale
        )
        key_part = (
            jnp.einsum("hqk,qhd->khd", score_grad, query_group, preferred_element_type=jnp.float32)
            * score_scale
        )
        return (query_part, key_part, value_part)

    query_parts, key_parts_grad, value_parts_grad = lax.map(
        attend_backward,
        (query_groups, key_groups, value_groups, by_group(mixed_grad), peaks, totals),
    )
    query_row_grad = from_group(query_parts)
    key_all_grad = from_group(key_parts_grad)
    value_all_grad = from_group(value_parts_grad)
    own_keys = key_all_grad[reach * local_rows :]
    own_values = value_all_grad[reach * local_rows :]
    for back in range(1, reach + 1):
        start = (reach - back) * local_rows
        moved = from_behind(
            (key_all_grad[start : start + local_rows], value_all_grad[start : start + local_rows]),
            "ep",
            -back,
        )
        own_keys = own_keys + moved[0]
        own_values = own_values + moved[1]
    query_turned = rotate_back(
        rounded(query_row_grad).reshape(local_rows, HEADS, HEAD_DIM), cosine, sine
    ).reshape(local_rows, width)
    key_turned = rotate_back(
        rounded(own_keys).reshape(local_rows, HEADS, HEAD_DIM), cosine, sine
    ).reshape(local_rows, width)
    query_lin_grad, q_gain_local = norm_back(query_lin, scale_query, gain_query, query_turned)
    key_lin_grad, k_gain_local = norm_back(key_lin, scale_key, gain_key, key_turned)
    query_lin_grad = query_lin_grad.astype(jnp.bfloat16)
    key_lin_grad = key_lin_grad.astype(jnp.bfloat16)
    value_row_grad = own_values.astype(jnp.bfloat16)
    query_local = matmul(normed.T, query_lin_grad)
    key_local = matmul(normed.T, key_lin_grad)
    value_local = matmul(normed.T, value_row_grad)
    normed_grad = (
        matmul(query_lin_grad, weight_query.T)
        + matmul(key_lin_grad, weight_key.T)
        + matmul(value_row_grad, weight_value.T)
    )
    inputs_part, attn_gain_local = norm_back(inputs, scale_attn, gain_attn, normed_grad)
    tokens_grad = residual_grad + inputs_part
    summed = (
        lax.psum_scatter(attn_gain_local, ("rep", "ep"), scatter_dimension=0, tiled=True),
        lax.psum_scatter(q_gain_local, ("rep", "ep"), scatter_dimension=0, tiled=True),
        lax.psum_scatter(k_gain_local, ("rep", "ep"), scatter_dimension=0, tiled=True),
        lax.psum_scatter(moe_gain_local, ("rep", "ep"), scatter_dimension=0, tiled=True),
        lax.psum_scatter(query_local, ("rep", "ep"), scatter_dimension=0, tiled=True),
        lax.psum_scatter(key_local, ("rep", "ep"), scatter_dimension=0, tiled=True),
        lax.psum_scatter(value_local, ("rep", "ep"), scatter_dimension=0, tiled=True),
        lax.psum_scatter(out_local, ("rep", "ep"), scatter_dimension=0, tiled=True),
        lax.psum_scatter(router_local, ("rep", "ep"), scatter_dimension=0, tiled=True),
    )
    expert_summed = (
        lax.psum_scatter(gate_local[None], "rep", scatter_dimension=1, tiled=True),
        lax.psum_scatter(up_local[None], "rep", scatter_dimension=1, tiled=True),
        lax.psum_scatter(down_local[None], "rep", scatter_dimension=1, tiled=True),
    )
    return (
        output,
        loss,
        tokens_grad,
        summed[0],
        summed[1],
        summed[2],
        summed[3],
        summed[4],
        summed[5],
        summed[6],
        summed[7],
        summed[8],
        expert_summed[0],
        expert_summed[1],
        expert_summed[2],
    )


def solution(mesh):
    placed = (
        P(("rep", "ep"), None),
        P(("rep", "ep"), None),
        P("rep", "ep"),
        P("rep", "ep"),
        P(("rep", "ep"), None),
        P(("rep", "ep")),
        P(("rep", "ep")),
        P(("rep", "ep")),
        P(("rep", "ep")),
        P(("rep", "ep"), None),
        P(("rep", "ep"), None),
        P(("rep", "ep"), None),
        P(("rep", "ep"), None),
        P(("rep", "ep"), None),
        P("ep", None, None),
        P("ep", None, None),
        P("ep", None, None),
    )
    return jax.shard_map(
        body,
        mesh=mesh,
        in_specs=placed,
        out_specs=(
            P(("rep", "ep"), None),
            P(),
            P(("rep", "ep"), None),
            P(("rep", "ep")),
            P(("rep", "ep")),
            P(("rep", "ep")),
            P(("rep", "ep")),
            P(("rep", "ep"), None),
            P(("rep", "ep"), None),
            P(("rep", "ep"), None),
            P(("rep", "ep"), None),
            P(("rep", "ep"), None),
            P("ep", "rep", None),
            P("ep", "rep", None),
            P("ep", "rep", None),
        ),
        check_vma=False,
    )
```

profile of v0, /device:TPU:0, one launch (start us, length us, event | category | flops | bytes accessed | tf_op | source)
XLA Modules:
  0.0 3536.3 jit_solution(7428225841283529041)
XLA Ops:
  27.6 39.0 %all-reduce.11 = (bf16[2048]{0:T(1024)(128)(2,1)S(1)}, bf16[2048]{0:T(1024)(128)(2,1)S(1)}, bf16[2048]{0:T(1024)(128)(2,1)S(1)}, bf16[2048]{0:T(1024)(128)(2,1)S(1)}) all-reduce(bf16[2048]{0:T(1024)(128)(2,1)S(1)} %dynamic-update-slice, bf16[2048]{0:T(1024)(128)(2,1)S(1)} %dynamic-update-slice.1, ...), channel_id=1, replica_groups=mesh['rep'=8,'ep'=4] {'rep','ep'}, use_global_device_ids=true, to_apply=%add.2 | all-reduce | flops 8192 | bytes 32768
  75.1 16.7 all-gather.8.cloned.1.call-done
  101.4 69.3 %all-gather.10.cloned.1.call-done = bf16[2048,2048]{1,0:T(8,128)(2,1)} async-done(((bf16[64,2048]{1,0:T(8,128)(2,1)}), bf16[2048,2048]{1,0:T(8,128)(2,1)}) %all-gather.10.cloned.1.call-update) | async-done | bytes 8388624 | tf_op jit(solution)/shard_map/all_gather | solution.py:107
  192.6 80.9 %all-gather.6.cloned.1.call-done = bf16[2048,2048]{1,0:T(8,128)(2,1)} async-done(((bf16[64,2048]{1,0:T(8,128)(2,1)}), bf16[2048,2048]{1,0:T(8,128)(2,1)}) %all-gather.6.cloned.1.call-update) | async-done | bytes 8388624 | tf_op jit(solution)/shard_map/all_gather | solution.py:108
  342.9 33.5 collective-permute-done.1
  378.6 65.0 %collective-permute-done = bf16[512,16,128]{2,1,0:T(8,128)(2,1)} collective-permute-done((bf16[512,16,128]{2,1,0:T(8,128)(2,1)}, bf16[512,16,128]{2,1,0:T(8,128)(2,1)}, u32[]{:S(2)}, u32[]{:S(2)}) %collective-permute-start) | collective-permute-done | bytes 2097184 | tf_op jit(solution)/shard_map/ppermute | solution.py:19
  453.7 63.9 %while.30 = (s32[]{:T(128)}, bf16[4,512,4,128]{1,3,2,0:T(8,128)(2,1)}, f32[4,4,512,1]{2,1,3,0:T(4,128)}, f32[4,4,512,1]{2,1,3,0:T(4,128)}, bf16[4,1536,4,128]{3,...) while((s32[]{:T(128)}, ...), condition=%wide.region_6.7_spmd.clone, body=%wide.region_3.6_spmd.clone.sunk | while | flops 1653862400 | bytes 62484160 | solution.py:179
  537.3 211.2 %all_to_all.20 = bf16[4,320,2048]{2,1,0:T(8,128)(2,1)S(1)} all-to-all(bf16[4,320,2048]{2,1,0:T(8,128)(2,1)} %bitcast.278), channel_id=1, replica_groups=mesh['rep'=8,'ep'=4] {'ep'}, dimensions={0} | all-to-all | bytes 10485760 | tf_op jit(solution)/shard_map/all_to_all | solution.py:206
  775.1 133.9 %psum.15 = f32[]{:T(128)} all-reduce(f32[]{:T(128)} %convert_reduce_fusion), channel_id=1, replica_groups=mesh['rep'=8,'ep'=4] {'rep','ep'}, use_global_device_ids=true, to_apply=%region_20.21 | all-reduce | flops 1 | bytes 8 | tf_op jit(solution)/shard_map/psum | solution.py:223
  909.0 66.3 %all-gather = bf16[32,64,4]{1,2,0:T(4,128)(2,1)S(1)} all-gather(bf16[1,64,4]{1,2,0:T(4,128)(2,1)S(1)} %bitcast.316), channel_id=1, replica_groups=mesh['rep'=8,'ep'=4] {'rep','ep'}, dimensions={0}, use_global_device_ids=true | all-gather | bytes 16896 | tf_op jit(solution)/shard_map/all_gather | solution.py:110
  977.3 12.2 gather_fusion.1
  999.1 13.7 multiply_reduce_fusion.2
  1040.4 13.6 gather_fusion.2
  1071.2 109.5 %all-to-all-done.2 = bf16[4,320,2048]{2,1,0:T(8,128)(2,1)} async-done(((bf16[4,320,2048]{2,1,0:T(8,128)(2,1)}), bf16[4,320,2048]{2,1,0:T(8,128)(2,1)}, u32[]{:S(2)}, u32[]{:S(2)}) %all-to-all-start.2) | async-done | bytes 5242912 | tf_op jit(solution)/shard_map/all_to_all | solution.py:235
  1191.6 14.9 multiply_convert_fusion.2
  1246.6 118.7 %all_to_all.21 = bf16[4,320,2048]{2,1,0:T(8,128)(2,1)} all-to-all(bf16[4,320,2048]{2,1,0:T(8,128)(2,1)S(1)} %bitcast.301), channel_id=1, replica_groups=mesh['rep'=8,'ep'=4] {'ep'}, dimensions={0} | all-to-all | bytes 10485760 | tf_op jit(solution)/shard_map/all_to_all | solution.py:254
  1387.2 14.0 reduce_sum.239
  1439.7 133.2 %while.31 = (s32[]{:T(128)}, bf16[4,512,4,128]{1,3,2,0:T(8,128)(2,1)}, f32[4,1536,4,128]{1,3,2,0:T(8,128)}, f32[4,1536,4,128]{1,3,2,0:T(8,128)}, bf16[4,1536,4,1...) while((s32[]{:T(128)}, ...), condition=%wide.region_28.29_spmd.clone, body=%wide.region_26.28_spmd.clone.sunk | while | flops 4064540672 | bytes 129063632 | solution.py:312
  1585.7 326.1 %collective-permute-done.9 = f32[512,2048]{0,1:T(8,128)S(1)} collective-permute-done((f32[512,2048]{0,1:T(8,128)}, f32[512,2048]{0,1:T(8,128)S(1)}, u32[]{:S(2)}, u32[]{:S(2)}) %collective-permute-start.9) | collective-permute-done | bytes 4194336 | tf_op jit(solution)/shard_map/ppermute | solution.py:19
  1959.2 506.9 %collective-permute-done.7 = f32[512,2048]{1,0:T(8,128)} collective-permute-done((f32[512,2048]{1,0:T(8,128)}, f32[512,2048]{1,0:T(8,128)}, u32[]{:S(2)}, u32[]{:S(2)}) %collective-permute-start.7) | collective-permute-done | bytes 4194336 | tf_op jit(solution)/shard_map/ppermute | solution.py:19
  2500.9 13.7 multiply_reduce_fusion.4
  2571.8 317.5 %all-reduce.10 = (f32[]{:T(128)}, f32[2048]{0:T(1024)S(1)}, f32[2048]{0:T(1024)S(1)}, f32[2048]{0:T(1024)S(1)}, f32[2048]{0:T(1024)S(1)}) all-reduce(f32[]{:T(128)} %multiply_reduce_fusion.16, f32[2048]{0:T(1024)S(1)} %get-tuple-element.270, f32[2048]{0:T(1024)S(1)} %get-tuple-element.356, ...), channel_id=1, replica_groups=mesh['rep'=8,'ep'=4] {'rep','ep'}, use_global_device_ids=true, to_apply=%region_18.19 | all-reduce | flops 8193 | bytes 65544 | tf_op jit(solution)/shard_map/psum | solution.py:223
  2898.9 264.2 %reduce-scatter.11.cloned.1.call-done = f32[64,2048]{1,0:T(8,128)} async-done(((f32[2048,2048]{1,0:T(8,128)}), f32[64,2048]{1,0:T(8,128)}) %reduce-scatter.11.cloned.1.call-update) | async-done | bytes 524304 | tf_op jit(solution)/shard_map/reduce_scatter | solution.py:356
  3163.2 364.9 %reduce-scatter.13.cloned.1.call-done = f32[64,2048]{1,0:T(8,128)} async-done(((f32[2048,2048]{1,0:T(8,128)}), f32[64,2048]{1,0:T(8,128)}) %reduce-scatter.13.cloned.1.call-update) | async-done | bytes 524304 | tf_op jit(solution)/shard_map/reduce_scatter | solution.py:357
  (461 shorter events, 711.5 us)
Async XLA Ops:
  7.2 84.5 %all-gather.8.cloned.1.call-start = ((), (), s32[]{:S(2)}) async-start(), calls=%async_computation.13 | async-start | bytes 8650752 | tf_op jit(solution)/shard_map/all_gather | solution.py:106
  7.9 162.7 %all-gather.10.cloned.1.call-start = ((), (), s32[]{:S(2)}) async-start(), calls=%async_computation.14 | async-start | bytes 8650752 | tf_op jit(solution)/shard_map/all_gather | solution.py:107
  8.7 264.8 %all-gather.6.cloned.1.call-start = ((), (), s32[]{:S(2)}) async-start(), calls=%async_computation.12 | async-start | bytes 8650752 | tf_op jit(solution)/shard_map/all_gather | solution.py:108
  9.4 508.2 %all-gather.12.cloned.1.call-start = ((), (), s32[]{:S(2)}) async-start(), calls=%async_computation.15 | async-start | bytes 8650752 | tf_op jit(solution)/shard_map/all_gather | solution.py:109
  10.1 281.4 %collective-permute-start.3 = (bf16[512]{0:T(512)(128)(2,1)S(1)}, bf16[512]{0:T(512)(128)(2,1)S(1)}, u32[]{:S(2)}, u32[]{:S(2)}) collective-permute-start(bf16[512]{0:T(512)(128)(2,1)S(1)} %convert_element_type.174), channel_id=1, source_target_pairs={{0,1},{1,2},{2,3},{4,5},{5,6},{6,7},{8,9},{9,10},{10,11},{12,13},{... | collective-permute-start | bytes 3080 | tf_op jit(solution)/shard_map/ppermute | solution.py:19
  15.1 280.3 %collective-permute-start.2 = (bf16[512]{0:T(512)(128)(2,1)S(1)}, bf16[512]{0:T(512)(128)(2,1)S(1)}, u32[]{:S(2)}, u32[]{:S(2)}) collective-permute-start(bf16[512]{0:T(512)(128)(2,1)S(1)} %convert_element_type.174), channel_id=1, source_target_pairs={{0,2},{1,3},{4,6},{5,7},{8,10},{9,11},{12,14},{13,15},{16,18},{17,... | collective-permute-start | bytes 3080 | tf_op jit(solution)/shard_map/ppermute | solution.py:19
  185.0 147.3 %collective-permute-start.5 = (bf16[512,16,128]{2,1,0:T(8,128)(2,1)}, bf16[512,16,128]{2,1,0:T(8,128)(2,1)}, u32[]{:S(2)}, u32[]{:S(2)}) collective-permute-start(bf16[512,16,128]{2,1,0:T(8,128)(2,1)} %fusion.85), channel_id=1, source_target_pairs={{0,1},{1,2},{2,3},{4,5},{5,6},{6,7},{8,9},{9,10},{10,11},{12,13},{... | collective-permute-start | bytes 6291464 | tf_op jit(solution)/shard_map/ppermute | solution.py:19
  189.8 142.5 %collective-permute-start.4 = (bf16[512,16,128]{2,1,0:T(8,128)(2,1)}, bf16[512,16,128]{2,1,0:T(8,128)(2,1)}, u32[]{:S(2)}, u32[]{:S(2)}) collective-permute-start(bf16[512,16,128]{2,1,0:T(8,128)(2,1)} %fusion.85), channel_id=1, source_target_pairs={{0,2},{1,3},{4,6},{5,7},{8,10},{9,11},{12,14},{13,15},{16,18},{17,... | collective-permute-start | bytes 6291464 | tf_op jit(solution)/shard_map/ppermute | solution.py:19
  284.0 92.5 %collective-permute-start.1 = (bf16[512,16,128]{2,1,0:T(8,128)(2,1)}, bf16[512,16,128]{2,1,0:T(8,128)(2,1)}, u32[]{:S(2)}, u32[]{:S(2)}) collective-permute-start(bf16[512,16,128]{2,1,0:T(8,128)(2,1)} %bitcast.71), channel_id=1, source_target_pairs={{0,1},{1,2},{2,3},{4,5},{5,6},{6,7},{8,9},{9,10},{10,11},{12,13},{... | collective-permute-start | bytes 6291464 | tf_op jit(solution)/shard_map/ppermute | solution.py:19
  291.6 152.0 %collective-permute-start = (bf16[512,16,128]{2,1,0:T(8,128)(2,1)}, bf16[512,16,128]{2,1,0:T(8,128)(2,1)}, u32[]{:S(2)}, u32[]{:S(2)}) collective-permute-start(bf16[512,16,128]{2,1,0:T(8,128)(2,1)} %bitcast.71), channel_id=1, source_target_pairs={{0,2},{1,3},{4,6},{5,7},{8,10},{9,11},{12,14},{13,15},{16,18},{17,... | collective-permute-start | bytes 6291464 | tf_op jit(solution)/shard_map/ppermute | solution.py:19
  769.3 208.0 %all-to-all-start.1 = ((bf16[4,320,2048]{2,1,0:T(8,128)(2,1)}), bf16[4,320,2048]{2,1,0:T(8,128)(2,1)}, u32[]{:S(2)}, u32[]{:S(2)}) async-start(bf16[4,320,2048]{2,1,0:T(8,128)(2,1)} %bitcast.300), calls=%async_computation.1 | async-start | bytes 10485760 | tf_op jit(solution)/shard_map/all_to_all | solution.py:216
  1054.0 126.8 %all-to-all-start.2 = ((bf16[4,320,2048]{2,1,0:T(8,128)(2,1)}), bf16[4,320,2048]{2,1,0:T(8,128)(2,1)}, u32[]{:S(2)}, u32[]{:S(2)}) async-start(bf16[4,320,2048]{2,1,0:T(8,128)(2,1)} %bitcast.277), calls=%async_computation.2 | async-start | bytes 10485760 | tf_op jit(solution)/shard_map/all_to_all | solution.py:235
  1059.0 1481.6 %reduce-scatter.25.cloned.1.call-start = ((), (), s32[]{:S(2)}) async-start(), calls=%async_computation.23 | async-start | bytes 1081344
  1071.1 1827.7 %reduce-scatter.23.cloned.1.call-start = ((), (), s32[]{:S(2)}) async-start(), calls=%async_computation.22 | async-start | bytes 9437184 | tf_op jit(solution)/shard_map/reduce_scatter | solution.py:365
  1191.5 1707.4 %reduce-scatter.21.cloned.1.call-start = ((), (), s32[]{:S(2)}) async-start(), calls=%async_computation.21 | async-start | bytes 9437184 | tf_op jit(solution)/shard_map/reduce_scatter | solution.py:364
  1216.0 1682.9 %reduce-scatter.19.cloned.1.call-start = ((), (), s32[]{:S(2)}) async-start(), calls=%async_computation.20 | async-start | bytes 9437184 | tf_op jit(solution)/shard_map/reduce_scatter | solution.py:363
  1226.9 1672.0 %reduce-scatter.17.cloned.1.call-start = ((), (), s32[]{:S(2)}) async-start(), calls=%async_computation.19 | async-start | bytes 17301504 | tf_op jit(solution)/shard_map/reduce_scatter | solution.py:359
  1423.4 1475.5 %reduce-scatter.15.cloned.1.call-start = ((), (), s32[]{:S(2)}) async-start(), calls=%async_computation.18 | async-start | bytes 17301504 | tf_op jit(solution)/shard_map/reduce_scatter | solution.py:358
  1583.2 328.7 %collective-permute-start.9 = (f32[512,2048]{0,1:T(8,128)}, f32[512,2048]{0,1:T(8,128)S(1)}, u32[]{:S(2)}, u32[]{:S(2)}) collective-permute-start(f32[512,2048]{0,1:T(8,128)} %bitcast.303), channel_id=1, source_target_pairs={{2,0},{3,1},{6,4},{7,5},{10,8},{11,9},{14,12},{15,13},{18,16},{19,... | collective-permute-start | bytes 12582920 | tf_op jit(solution)/shard_map/ppermute | solution.py:19
  1584.4 327.4 %collective-permute-start.8 = (f32[512,2048]{0,1:T(8,128)}, f32[512,2048]{0,1:T(8,128)S(1)}, u32[]{:S(2)}, u32[]{:S(2)}) collective-permute-start(f32[512,2048]{0,1:T(8,128)} %bitcast.302), channel_id=1, source_target_pairs={{1,0},{2,1},{3,2},{5,4},{6,5},{7,6},{9,8},{10,9},{11,10},{13,12},{... | collective-permute-start | bytes 12582920 | tf_op jit(solution)/shard_map/ppermute | solution.py:19
  1923.4 1239.8 %reduce-scatter.11.cloned.1.call-start = ((), (), s32[]{:S(2)}) async-start(), calls=%async_computation.16 | async-start | bytes 17301504 | tf_op jit(solution)/shard_map/reduce_scatter | solution.py:356
  1944.6 521.5 %collective-permute-start.7 = (f32[512,2048]{1,0:T(8,128)}, f32[512,2048]{1,0:T(8,128)}, u32[]{:S(2)}, u32[]{:S(2)}) collective-permute-start(f32[512,2048]{1,0:T(8,128)} %copy.169), channel_id=1, source_target_pairs={{2,0},{3,1},{6,4},{7,5},{10,8},{11,9},{14,12},{15,13},{18,16},{19,... | collective-permute-start | bytes 12582920 | tf_op jit(solution)/shard_map/ppermute | solution.py:19
  1945.8 520.2 %collective-permute-start.6 = (f32[512,2048]{1,0:T(8,128)}, f32[512,2048]{1,0:T(8,128)}, u32[]{:S(2)}, u32[]{:S(2)}) collective-permute-start(f32[512,2048]{1,0:T(8,128)} %copy.168), channel_id=1, source_target_pairs={{1,0},{2,1},{3,2},{5,4},{6,5},{7,6},{9,8},{10,9},{11,10},{13,12},{... | collective-permute-start | bytes 12582920 | tf_op jit(solution)/shard_map/ppermute | solution.py:19
  2525.2 1002.9 %reduce-scatter.13.cloned.1.call-start = ((), (), s32[]{:S(2)}) async-start(), calls=%async_computation.17 | async-start | bytes 17301504 | tf_op jit(solution)/shard_map/reduce_scatter | solution.py:357
  (101 other events, 3312.0 us)
Sparse Core Ops, SparseCore 0:
  11.0 80.7 all-gather.7
  94.7 75.9 all-gather.9
  173.6 99.8 all-gather.5
  276.2 157.7 all-gather.11
  1071.3 181.2 reduce-scatter.24
  1256.8 70.5 reduce-scatter.22
  1331.5 71.2 reduce-scatter.20
  1407.2 71.2 reduce-scatter.18
  1481.4 584.0 reduce-scatter.16
  2068.3 674.8 reduce-scatter.14
  2746.0 417.1 reduce-scatter.10
  3165.9 362.1 reduce-scatter.12
where the time goes:
time: 3540 us
  waiting for transfers between devices  1840 us (52%)
  blocking collectives  887 us (25%)
  matrix products  349 us (10%)
  local copies, waits for them, and re-layouts  211 us (6%)
  other arithmetic  187 us (5%)
  starting transfers between devices  44 us (1%)
    ppermute x10, waiting for transfers between devices, from_behind(): lax.ppermute(value, axis, [(source, source + steps) for source in range(l...  931 us
    psum x2, blocking collectives, body(): total_squares, count = lax.psum((squares, jnp.sum(valid)), ('rep', 'ep'))  451 us
    reduce_scatter x1, waiting for transfers between devices, body(): lax.psum_scatter(key_local, ('rep', 'ep'), scatter_dimension=0, tiled=True)  365 us
    reduce_scatter x1, waiting for transfers between devices, body(): lax.psum_scatter(query_local, ('rep', 'ep'), scatter_dimension=0, tiled=T...  264 us
    all_to_all x1, blocking collectives, body(): lax.all_to_all(outgoing, 'ep', split_axis=0, concat_axis=0, tiled=True)  211 us
    dot_general x22, matrix products, matmul(): return jnp.dot(left, right, preferred_element_type=jnp.float32)  195 us
    all_to_all x1, blocking collectives, body(): lax.all_to_all(input_grad.reshape(experts, capacity, width), 'ep', split_...  119 us
    all_to_all x1, waiting for transfers between devices, body(): lax.all_to_all(grad_outgoing, 'ep', split_axis=0, concat_axis=0, tiled=True)  110 us
  transfers between devices with their start and end apart: 24, of which 10 were waited for; matrix products, arithmetic and copies ran while one was open for 17% of the time, Pallas kernels for 0%

commit v1 on v0

--- a/solution.py
+++ b/solution.py
@@ -70,7 +70,7 @@
     return (gains, everything[4], everything[5], everything[6], everything[7], everything[8])
 
 
-def body(
+def body_plain(
     tokens,
     teacher,
     segment_ids,
@@ -383,6 +383,442 @@
     )
 
 
+def across(value, bit):
+    count = lax.axis_size("rep")
+    return lax.ppermute(value, "rep", [(place, place ^ bit) for place in range(count)])
+
+
+def along(value, steps):
+    count = lax.axis_size("ep")
+    return lax.ppermute(value, "ep", [(place, (place + steps) % count) for place in range(count)])
+
+
+def mirrored(value, moves):
+    reps, count = lax.axis_size("rep"), lax.axis_size("ep")
+    pairs = []
+    for rep in range(reps):
+        for source, target in moves:
+            if rep % 2:
+                source, target = count - 1 - source, count - 1 - target
+            pairs.append((rep * count + source, rep * count + target))
+    return lax.ppermute(value, ("rep", "ep"), pairs)
+
+
+def pick(value, index, axis):
+    return lax.dynamic_index_in_dim(value, index, axis, keepdims=False)
+
+
+def in_order(own, other, bit, axis):
+    return jnp.where(bit == 1, jnp.stack([other, own], axis), jnp.stack([own, other], axis))
+
+
+def gather_pair(left, right, place):
+    y_bit, x_bit, core, shard = place
+    experts = lax.axis_size("ep")
+    both = jnp.stack([left, right])
+    parts = jnp.zeros((experts,) + both.shape, both.dtype)
+    parts = lax.dynamic_update_index_in_dim(parts, both, shard, 0)
+    for steps in range(1, experts):
+        parts = lax.dynamic_update_index_in_dim(
+            parts, along(both, steps), lax.rem(shard - steps + experts, experts), 0
+        )
+    a, b = parts[:, 0], parts[:, 1]
+    a_x, b_y = across(a, 2), across(b, 4)
+    a, b = in_order(a, a_x, x_bit, 0), in_order(b, b_y, y_bit, 0)
+    a_y, b_x = across(a, 4), across(b, 2)
+    a, b = in_order(a, a_y, y_bit, 0), in_order(b, b_x, x_bit, 1)
+    a_c, b_c = across(a, 1), across(b, 1)
+    a, b = in_order(a, a_c, core, 2), in_order(b, b_c, core, 2)
+    width = left.shape[1]
+    return a.reshape(-1, width), b.reshape(-1, width)
+
+
+def half_step(value, bit, axis, link):
+    sent = across(pick(value, 1 - bit, axis), link)
+    kept = pick(value, bit, axis)
+    return (kept.astype(jnp.float32) + sent.astype(jnp.float32)).astype(jnp.bfloat16)
+
+
+def plane_sum(left, right, place):
+    y_bit, x_bit, core, shard = place
+    a = half_step(left, x_bit, 1, 2)
+    b = half_step(right, y_bit, 0, 4)
+    return half_step(a, y_bit, 0, 4), half_step(b, x_bit, 0, 2)
+
+
+def scatter_pair(left, right, place):
+    y_bit, x_bit, core, shard = place
+    experts = lax.axis_size("ep")
+    rows, width = left.shape
+    shape = (2, 2, 2, rows // 8, width)
+    a = half_step(left.reshape(shape), core, 2, 1)
+    b = half_step(right.reshape(shape), core, 2, 1)
+    a, b = plane_sum(a, b, place)
+    both = jnp.stack([a, b]).reshape(2, experts, rows // (8 * experts), width)
+    both = lax.all_to_all(both, "ep", split_axis=1, concat_axis=1, tiled=True)
+    both = jnp.sum(both.astype(jnp.float32), axis=1)
+    return both[0], both[1]
+
+
+def gather_experts(quarter, place):
+    y_bit, x_bit, core, shard = place
+    m = jnp.where(core == 0, shard, lax.axis_size("ep") - 1 - shard)
+    one = mirrored(quarter, [(0, 1), (1, 2)])
+    two = mirrored(jnp.where(m == 2, one, quarter), [(1, 0), (2, 3)])
+    three = mirrored(one, [(1, 2)])
+    four = mirrored(three, [(2, 3)])
+    a = jnp.where(m == 0, quarter, jnp.where(m == 1, one, jnp.where(m == 2, three, four)))
+    b = jnp.where(m == 1, quarter, jnp.where(m == 2, one, two))
+    a_x, b_y = across(a, 2), across(b, 4)
+    a, b = in_order(a, a_x, x_bit, 0), in_order(b, b_y, y_bit, 0)
+    a_y, b_x = across(a, 4), across(b, 2)
+    return in_order(a, a_y, y_bit, 0), in_order(b, b_x, x_bit, 1)
+
+
+def scatter_experts(left, right, place):
+    y_bit, x_bit, core, shard = place
+    m = jnp.where(core == 0, shard, lax.axis_size("ep") - 1 - shard)
+    a, b = plane_sum(left, right, place)
+    both = jnp.stack([a, b])
+    up = mirrored(b, [(0, 1)])
+    got = mirrored(both, [(3, 2)])
+    both = (both.astype(jnp.float32) + got.astype(jnp.float32)).astype(jnp.bfloat16)
+    got = mirrored(both, [(2, 1)])
+    both = both.astype(jnp.float32) + got.astype(jnp.float32)
+    a, b = both[0], both[1]
+    got = mirrored(a.astype(jnp.bfloat16), [(1, 0)])
+    mine = jnp.where(m == 0, a + got.astype(jnp.float32), b + up.astype(jnp.float32))
+    return mine, m
+
+
+def body(
+    tokens,
+    teacher,
+    segment_ids,
+    valid_mask,
+    routes,
+    attn_gain,
+    q_gain,
+    k_gain,
+    moe_gain,
+    w_query,
+    w_key,
+    w_value,
+    w_out,
+    w_router,
+    w_gate,
+    w_up,
+    w_down,
+):
+    bf16, f32 = jnp.bfloat16, jnp.float32
+    local_rows, width = tokens.shape
+    experts = lax.axis_size("ep")
+    reps = lax.axis_size("rep")
+    reach = min(-(-WINDOW // local_rows), experts - 1)
+    group = min(HEADS, 4)
+    score_scale = HEAD_DIM ** (-0.5)
+    shard = lax.axis_index("ep")
+    rep = lax.axis_index("rep")
+    place = (rep // 4, rep // 2 % 2, rep % 2, shard)
+    core = rep % 2
+    total_tokens = local_rows * reps * experts
+
+    valid = valid_mask.reshape(local_rows).astype(f32)
+    own_count = jnp.sum(valid_mask)
+    counts = jnp.stack([own_count // 16, own_count % 16]).astype(bf16)
+    small = jnp.concatenate(
+        [
+            jnp.stack([attn_gain, q_gain, k_gain, moe_gain], 1),
+            w_router,
+            jnp.broadcast_to(counts[None], (attn_gain.shape[0], 2)),
+        ],
+        1,
+    )
+    small = lax.all_gather(small, ("rep", "ep"), axis=0, tiled=True)
+    gain_attn, gain_query, gain_key, gain_moe = [small[:, i].astype(f32) for i in range(4)]
+    weight_router = small[:, 4 : 4 + experts]
+    counts = small[:: attn_gain.shape[0], 4 + experts :].astype(f32)
+    count = jnp.sum(counts[:, 0]) * 16.0 + jnp.sum(counts[:, 1])
+
+    weight_key, weight_value = gather_pair(w_key, w_value, place)
+    weight_query, weight_out = gather_pair(w_query, w_out, place)
+
+    moved, moved_segments = tokens, segment_ids.reshape(local_rows)
+    token_parts, segment_parts = [tokens], [moved_segments]
+    for back in range(reach):
+        moved = from_behind(moved, "ep", 1)
+        moved_segments = from_behind(moved_segments, "ep", 1)
+        token_parts.insert(0, moved)
+        segment_parts.insert(0, moved_segments)
+    behind = reach * local_rows
+    inputs_all = jnp.concatenate(token_parts, 0).astype(f32)
+    key_segments = jnp.concatenate(segment_parts, 0)
+    inputs = tokens.astype(f32)
+    segments = segment_ids.reshape(local_rows)
+
+    quarter_rows = w_gate.shape[1] // 4
+    quarter_down = w_down.shape[1] // 4
+    quarter = rep // 2
+    quarter_gate = lax.dynamic_slice_in_dim(w_gate[0], quarter * quarter_rows, quarter_rows, 0)
+    quarter_up = lax.dynamic_slice_in_dim(w_up[0], quarter * quarter_rows, quarter_rows, 0)
+    quarter_down_w = lax.dynamic_slice_in_dim(w_down[0], quarter * quarter_down, quarter_down, 0)
+    own_quarter = jnp.concatenate(
+        [jnp.concatenate([quarter_gate, quarter_up], 1), quarter_down_w], 0
+    )
+
+    scale_all = rms_scale(inputs_all)
+    normed_all = (inputs_all * scale_all * gain_attn).astype(bf16)
+    scale_attn = scale_all[behind:]
+    normed = normed_all[behind:]
+    key_lin = matmul(normed_all, weight_key)
+    value_all = matmul(normed_all, weight_value).astype(bf16)
+    query_lin = matmul(normed, weight_query)
+    scale_query = rms_scale(query_lin)
+    scale_key = rms_scale(key_lin)
+    all_rows = local_rows + behind
+    key_positions = (shard - reach) * local_rows + jnp.arange(all_rows, dtype=jnp.int32)
+    positions = shard * local_rows + jnp.arange(local_rows, dtype=jnp.int32)
+    cosine_all, sine_all = rotary_tables(key_positions, HEAD_DIM)
+    cosine, sine = cosine_all[behind:], sine_all[behind:]
+    query_rows = rotate(
+        (query_lin * scale_query * gain_query).reshape(local_rows, HEADS, HEAD_DIM), cosine, sine
+    ).astype(bf16)
+    all_keys = rotate(
+        (key_lin * scale_key * gain_key).reshape(all_rows, HEADS, HEAD_DIM), cosine_all, sine_all
+    ).astype(bf16)
+    all_values = value_all.reshape(all_rows, HEADS, HEAD_DIM)
+    distance = positions[:, None] - key_positions[None, :]
+    allowed = (
+        (distance >= 0)
+        & (distance < WINDOW)
+        & (key_positions[None, :] >= 0)
+        & (segments[:, None] == key_segments[None, :])
+    )
+
+    def by_group(value):
+        return jnp.moveaxis(value.reshape(value.shape[0], HEADS // group, group, HEAD_DIM), 1, 0)
+
+    def from_group(value):
+        return jnp.moveaxis(value, 0, 1).reshape(value.shape[1], HEADS * HEAD_DIM)
+
+    def scores_of(query_group, key_group):
+        raw = (
+            jnp.einsum("qhd,khd->hqk", query_group, key_group, preferred_element_type=jnp.float32)
+            * score_scale
+        )
+        return jnp.where(allowed[None], raw, -1e30)
+
+    def attend_forward(item):
+        query_group, key_group, value_group = item
+        scores = scores_of(query_group, key_group)
+        peak = jnp.max(scores, axis=-1, keepdims=True)
+        shifted = jnp.exp(scores - peak)
+        total = jnp.sum(shifted, axis=-1, keepdims=True)
+        weights = (shifted / total).astype(jnp.bfloat16)
+        mixed = jnp.einsum("hqk,khd->qhd", weights, value_group, preferred_element_type=jnp.float32)
+        return (mixed, peak, total)
+
+    query_groups = by_group(query_rows)
+    key_groups = by_group(all_keys)
+    value_groups = by_group(all_values)
+    mixed, peaks, totals = lax.map(attend_forward, (query_groups, key_groups, value_groups))
+    mixed_rows = from_group(mixed).astype(bf16)
+    residual = inputs + matmul(mixed_rows, weight_out)
+    scale_moe = rms_scale(residual)
+    normed_moe = (residual * scale_moe * gain_moe).astype(bf16)
+    partner_moe = across(normed_moe, 1)
+    router_probs = jax.nn.softmax(matmul(normed_moe, weight_router), axis=-1)
+    chosen = jnp.sum(
+        (routes[:, :, None] == jnp.arange(experts, dtype=jnp.int32)).astype(f32), axis=1
+    )
+    gates = router_probs * chosen
+    ends = ((0, experts - 1), (1, experts - 2))
+
+    def slot_of(value, slot, of_core):
+        low, high = ends[slot]
+        return jnp.where(of_core == 0, value[:, low], value[:, high])
+
+    gates_both = jnp.concatenate([gates, across(gates, 1)], 0)
+    moe_both = jnp.concatenate([normed_moe, partner_moe], 0)
+
+    experts_a, experts_b = gather_experts(own_quarter, place)
+    slots = []
+    mixture = 0.0
+    for slot, pieces in enumerate((experts_a, experts_b)):
+        weight_gu = pieces[:, :, :quarter_rows].reshape(4 * quarter_rows, width)
+        weight_down = pieces[:, :, quarter_rows:].reshape(4 * quarter_down, width)
+        hidden = width // 2
+        pre = matmul(moe_both, weight_gu)
+        gate_pre, up_pre = pre[:, :hidden], pre[:, hidden:]
+        middle = (jax.nn.silu(gate_pre) * up_pre).astype(bf16)
+        expert_out = matmul(middle, weight_down).astype(bf16)
+        gate = slot_of(gates_both, slot, core)
+        mixture = mixture + gate[:, None] * expert_out
+        slots.append((weight_gu, weight_down, gate_pre, up_pre, middle, expert_out, gate))
+    result = residual + (mixture[:local_rows] + across(mixture[local_rows:], 1))
+    output = result.astype(bf16)
+    error = result - teacher.astype(f32)
+    squares = jnp.sum(valid * jnp.sum(error * error, axis=1))
+    result_grad = total_tokens / count * valid[:, None] * error
+    result_grad_both = jnp.concatenate([result_grad, across(result_grad, 1)], 0)
+
+    input_grad = 0.0
+    gate_grads, expert_grads = [], []
+    for weight_gu, weight_down, gate_pre, up_pre, middle, expert_out, gate in slots:
+        gate_grads.append(jnp.sum(result_grad_both * expert_out, axis=1))
+        pair_grad = (gate[:, None] * result_grad_both).astype(bf16)
+        down_local = matmul(middle.T, pair_grad).astype(bf16)
+        middle_grad = matmul(pair_grad, weight_down.T)
+        sigma = jax.nn.sigmoid(gate_pre)
+        active = gate_pre * sigma
+        gate_pre_grad = (middle_grad * up_pre * sigma * (1.0 + gate_pre * (1.0 - sigma))).astype(
+            bf16
+        )
+        up_pre_grad = (middle_grad * active).astype(bf16)
+        pre_grad = jnp.concatenate([gate_pre_grad, up_pre_grad], 1)
+        gu_local = matmul(moe_both.T, pre_grad).astype(bf16)
+        input_grad = input_grad + matmul(pre_grad, weight_gu.T).astype(bf16).astype(f32)
+        expert_grads.append(
+            jnp.concatenate(
+                [
+                    gu_local.reshape(2, 2, quarter_rows, width),
+                    down_local.reshape(2, 2, quarter_down, width),
+                ],
+                2,
+            )
+        )
+    expert_mine, m = scatter_experts(expert_grads[0], expert_grads[1], place)
+    half_rows, half_down = quarter_rows // 2, quarter_down // 2
+    gu_halves = expert_mine[:quarter_rows].reshape(2, half_rows, width)
+    down_halves = expert_mine[quarter_rows:].reshape(2, half_down, width)
+    halves = jnp.concatenate([gu_halves, down_halves], 1)
+    from_holder = across(pick(halves, 1 - core, 0), 1)
+    expert_half = jnp.where(m < 2, pick(halves, core, 0), from_holder)
+    gate_out = expert_half[None, :half_rows, : width // 2]
+    up_out = expert_half[None, :half_rows, width // 2 :]
+    down_out = expert_half[None, half_rows:]
+
+    input_grad = input_grad[:local_rows] + across(input_grad[local_rows:], 1)
+    slot_grads = jnp.stack(gate_grads, 1)
+    own_slots, partner_slots = slot_grads[:local_rows], across(slot_grads[local_rows:], 1)
+    from_low = jnp.where(core == 0, own_slots, partner_slots)
+    from_high = jnp.where(core == 0, partner_slots, own_slots)
+    prob_grad = chosen * jnp.concatenate([from_low, from_high[:, ::-1]], 1)
+    logit_grad = router_probs * (
+        prob_grad - jnp.sum(prob_grad * router_probs, axis=-1, keepdims=True)
+    )
+    router_local = jnp.dot(
+        normed_moe.T, logit_grad, precision=highest, preferred_element_type=f32
+    )
+    normed_moe_grad = input_grad + jnp.dot(
+        logit_grad, weight_router.T, precision=highest, preferred_element_type=f32
+    )
+    residual_part, moe_gain_local = norm_back(residual, scale_moe, gain_moe, normed_moe_grad)
+    residual_grad = result_grad + residual_part
+    branch_grad = residual_grad.astype(bf16)
+    half = width // 2
+    out_a = matmul(mixed_rows.T, branch_grad[:, :half]).astype(bf16)
+    out_b = matmul(mixed_rows.T, branch_grad[:, half:]).astype(bf16)
+    out_a, out_b = scatter_pair(out_a, out_b, place)
+    out_out = jnp.concatenate([out_a, out_b], 1)
+    mixed_grad = (
+        matmul(branch_grad, weight_out.T).astype(bf16).reshape(local_rows, HEADS, HEAD_DIM)
+    )
+
+    def attend_backward(item):
+        query_group, key_group, value_group, grad_group, peak, total = item
+        scores = scores_of(query_group, key_group)
+        probs = jnp.exp(scores - peak) / total
+        weights = probs.astype(jnp.bfloat16)
+        value_part = jnp.einsum(
+            "hqk,qhd->khd", weights, grad_group, preferred_element_type=jnp.float32
+        )
+        probs_grad = jnp.einsum(
+            "qhd,khd->hqk", grad_group, value_group, preferred_element_type=jnp.float32
+        )
+        inner = jnp.sum(probs * probs_grad, axis=-1, keepdims=True)
+        score_grad = (probs * (probs_grad - inner)).astype(jnp.bfloat16)
+        query_part = (
+            jnp.einsum("hqk,khd->qhd", score_grad, key_group, preferred_element_type=jnp.float32)
+            * score_scale
+        )
+        key_part = (
+            jnp.einsum("hqk,qhd->khd", score_grad, query_group, preferred_element_type=jnp.float32)
+            * score_scale
+        )
+        return (query_part.astype(bf16), key_part.astype(bf16), value_part.astype(bf16))
+
+    query_parts, key_parts_grad, value_parts_grad = lax.map(
+        attend_backward,
+        (query_groups, key_groups, value_groups, by_group(mixed_grad), peaks, totals),
+    )
+    query_turned = rotate_back(
+        from_group(query_parts).astype(f32).reshape(local_rows, HEADS, HEAD_DIM), cosine, sine
+    ).reshape(local_rows, width)
+    key_turned = rotate_back(
+        from_group(key_parts_grad).astype(f32).reshape(all_rows, HEADS, HEAD_DIM),
+        cosine_all,
+        sine_all,
+    ).reshape(all_rows, width)
+    value_row_grad = from_group(value_parts_grad)
+    query_lin_grad, q_gain_local = norm_back(query_lin, scale_query, gain_query, query_turned)
+    key_lin_grad, k_gain_local = norm_back(key_lin, scale_key, gain_key, key_turned)
+    query_lin_grad = query_lin_grad.astype(bf16)
+    key_lin_grad = key_lin_grad.astype(bf16)
+    value_a = matmul(normed_all.T, value_row_grad[:, :half]).astype(bf16)
+    value_b = matmul(normed_all.T, value_row_grad[:, half:]).astype(bf16)
+    value_a, value_b = scatter_pair(value_a, value_b, place)
+    value_out = jnp.concatenate([value_a, value_b], 1)
+    query_local = matmul(normed.T, query_lin_grad).astype(bf16)
+    key_local = matmul(normed_all.T, key_lin_grad).astype(bf16)
+    query_out, key_out = scatter_pair(query_local, key_local, place)
+    normed_grad = matmul(key_lin_grad, weight_key.T) + matmul(value_row_grad, weight_value.T)
+    normed_grad_own = normed_grad[behind:] + matmul(query_lin_grad, weight_query.T)
+    attn_gain_local = jnp.sum(normed_grad * inputs_all * scale_all, axis=0) + jnp.sum(
+        (normed_grad_own - normed_grad[behind:]) * inputs * scale_attn, axis=0
+    )
+    carried = 0.0
+    for back in range(reach):
+        carried = carried + normed_grad[back * local_rows : (back + 1) * local_rows]
+        carried = from_behind(carried.astype(bf16), "ep", -1).astype(f32)
+    normed_grad_own = normed_grad_own + carried
+    inputs_part, _ = norm_back(inputs, scale_attn, gain_attn, normed_grad_own)
+    tokens_grad = residual_grad + inputs_part
+
+    packed = jnp.concatenate(
+        [
+            jnp.broadcast_to(squares, (1, width)),
+            attn_gain_local[None],
+            q_gain_local[None],
+            k_gain_local[None],
+            moe_gain_local[None],
+            router_local.T,
+        ],
+        0,
+    )
+    packed = lax.psum(packed, ("rep", "ep"))
+    loss = packed[0, 0] / (2.0 * count * width)
+    own_rows = attn_gain.shape[0]
+    mine = lax.dynamic_slice_in_dim(packed, (rep * experts + shard) * own_rows, own_rows, 1)
+    return (
+        output,
+        loss,
+        tokens_grad,
+        mine[1],
+        mine[2],
+        mine[3],
+        mine[4],
+        query_out,
+        key_out,
+        value_out,
+        out_out,
+        mine[5:].T,
+        gate_out,
+        up_out,
+        down_out,
+    )
+
+
 def solution(mesh):
     placed = (
         P(("rep", "ep"), None),
@@ -403,8 +839,9 @@
         P("ep", None, None),
         P("ep", None, None),
     )
+    chips = mesh.shape["rep"] == 8 and mesh.shape["ep"] == 4
     return jax.shard_map(
-        body,
+        body if chips else body_plain,
         mesh=mesh,
         in_specs=placed,
         out_specs=(

time: 3540 us -> 2030 us (0.57)
  waiting for transfers between devices: 1840 us -> 451 us
  blocking collectives: 887 us -> 111 us
  other arithmetic: 187 us -> 514 us
  local copies, waits for them, and re-layouts: 211 us -> 324 us
  starting transfers between devices: 44 us -> 148 us
  matrix products: 349 us -> 452 us
    ppermute x10 -> x6, waiting for transfers between devices: 931 us -> 75.5 us  [from_behind(): lax.ppermute(value, axis, [(source, source + steps) for source in range(l...]
    reduce_scatter x7 -> x0, waiting for transfers between devices: 629 us -> none  [the longest x1 365 us: body(): lax.psum_scatter(key_local, ('rep', 'ep'), scatter_dimension=0, tiled=True)]
    psum x2 -> x0, blocking collectives: 451 us -> none  [body(): total_squares, count = lax.psum((squares, jnp.sum(valid)), ('rep', 'ep'))]
    all_to_all x2 -> x0, blocking collectives: 330 us -> none  [the longest x1 211 us: body(): lax.all_to_all(outgoing, 'ep', split_axis=0, concat_axis=0, tiled=True)]
    ppermute x0 -> x59, waiting for transfers between devices: none -> 202 us  [the longest x45 202 us: across(): lax.ppermute(value, 'rep', [(place, place ^ bit) for place in range(count)])]
    all_gather x4 -> x0, waiting for transfers between devices: 167 us -> none  [the longest x1 80.9 us: body(): lax.all_gather(w_value, ('rep', 'ep'), axis=0, tiled=True)]
    select_n x2 -> x32, other arithmetic: 0.02 us -> 147 us  [the longest x26 125 us: in_order(): jnp.where(bit == 1, jnp.stack([other, own], axis), jnp.stack([own, other]...]
    dot_general x22 -> x27, matrix products: 195 us -> 303 us  [matmul(): return jnp.dot(left, right, preferred_element_type=jnp.float32)]
  transfers between devices with their start and end apart: 24 -> 69, of which waited for: 10 -> 19; matrix products, arithmetic and copies ran while one was open for 17% -> 59% of each run, Pallas kernels for 0% -> 0%
where the time goes in v1:
time: 2030 us; the launch traced here: 2020 us
  other arithmetic  514 us (25%)
  matrix products  452 us (22%)
  waiting for transfers between devices  451 us (22%)
  local copies, waits for them, and re-layouts  324 us (16%)
  starting transfers between devices  148 us (7%)
  blocking collectives  111 us (5%)
  between operations  22.4 us (1%)
    dot_general x27, matrix products, matmul(): return jnp.dot(left, right, preferred_element_type=jnp.float32)  303 us
    ppermute x45, waiting for transfers between devices, across(): lax.ppermute(value, 'rep', [(place, place ^ bit) for place in range(count)])  202 us
    select_n x26, other arithmetic, in_order(): jnp.where(bit == 1, jnp.stack([other, own], axis), jnp.stack([own, other]...  125 us
    all_gather x1, blocking collectives, body(): small = lax.all_gather(small, ('rep', 'ep'), axis=0, tiled=True)  111 us
    psum x1, waiting for transfers between devices, body(): packed = lax.psum(packed, ('rep', 'ep'))  105 us
    ppermute x6, waiting for transfers between devices, from_behind(): lax.ppermute(value, axis, [(source, source + steps) for source in range(l...  75.5 us
    all_to_all x3, waiting for transfers between devices, scatter_pair(): both = lax.all_to_all(both, 'ep', split_axis=1, concat_axis=1, tiled=True)  69.1 us
    all_to_all x3, starting transfers between devices, scatter_pair(): both = lax.all_to_all(both, 'ep', split_axis=1, concat_axis=1, tiled=True)  65.3 us
  transfers between devices with their start and end apart: 69, of which 19 were waited for; matrix products, arithmetic and copies ran while one was open for 59% of the time, Pallas kernels for 0%

profile of v1, /device:TPU:0, one launch (start us, length us, event | category | flops | bytes accessed | tf_op | source)
XLA Modules:
  0.0 2023.2 jit_solution(585515653446143384)
XLA Ops:
  40.9 111.0 %all-gather = bf16[32,64,10]{1,2,0:T(8,128)(2,1)S(1)} all-gather(bf16[1,64,10]{1,2,0:T(8,128)(2,1)S(1)} %bitcast.678), channel_id=1, replica_groups=mesh['rep'=8,'ep'=4] {'rep','ep'}, dimensions={0}, use_global_device_ids=true | all-gather | bytes 42240 | tf_op jit(solution)/shard_map/all_gather | solution.py:537
  183.3 21.1 %collective-permute-done.8 = s32[512]{0:T(512)S(1)} collective-permute-done((s32[512]{0:T(512)S(1)}, s32[512]{0:T(512)S(1)}, u32[]{:S(2)}, u32[]{:S(2)}) %collective-permute-start.8) | collective-permute-done | bytes 2080 | tf_op jit(solution)/shard_map/ppermute | solution.py:19
  209.6 28.6 %collective-permute-done.9 = s32[512]{0:T(512)S(1)} collective-permute-done((s32[512]{0:T(512)S(1)}, s32[512]{0:T(512)S(1)}, u32[]{:S(2)}, u32[]{:S(2)}) %collective-permute-start.9) | collective-permute-done | bytes 2080 | tf_op jit(solution)/shard_map/ppermute | solution.py:19
  283.5 24.0 %collective-permute-done.14 = bf16[2,4,64,2048]{3,2,1,0:T(8,128)(2,1)} collective-permute-done((bf16[2,4,64,2048]{3,2,1,0:T(8,128)(2,1)}, bf16[2,4,64,2048]{3,2,1,0:T(8,128)(2,1)}, u32[]{:S(2)}, u32[]{:S(2)}) %collective-permute-start.14) | collective-permute-done | bytes 2097184 | tf_op jit(solution)/shard_map/ppermute | solution.py:388
  423.3 17.5 multiply_reduce_fusion.3
  464.9 15.6 reshape.1245
  488.6 15.3 convolution_convert_fusion.4
  585.5 14.5 fusion.91
  613.5 64.1 %while.30 = (s32[]{:T(128)}, bf16[4,512,4,128]{1,3,2,0:T(8,128)(2,1)}, f32[4,4,512,1]{2,1,3,0:T(4,128)}, f32[4,4,512,1]{2,1,3,0:T(4,128)}, bf16[4,1536,4,128]{1,...) while((s32[]{:T(128)}, ...), condition=%wide.region_7.8_spmd.clone, body=%wide.region_4.7_spmd.clone.sunk | while | flops 1653862400 | bytes 62484160 | solution.py:624
  729.8 74.0 %collective-permute-done.31 = bf16[2,768,2048]{2,1,0:T(8,128)(2,1)} collective-permute-done((bf16[2,768,2048]{2,1,0:T(8,128)(2,1)}, bf16[2,768,2048]{2,1,0:T(8,128)(2,1)}, u32[]{:S(2)}, u32[]{:S(2)}) %collective-permute-start.31) | collective-permute-done | bytes 6291488 | tf_op jit(solution)/shard_map/ppermute | solution.py:388
  850.9 14.0 fusion.176
  951.3 15.2 fusion.133
  1084.6 129.0 %while.31 = (s32[]{:T(128)}, bf16[4,512,4,128]{1,3,2,0:T(8,128)(2,1)}, bf16[4,1536,4,128]{1,3,2,0:T(8,128)(2,1)}, bf16[4,1536,4,128]{1,3,2,0:T(8,128)(2,1)}, bf1...) while((s32[]{:T(128)}, ...), condition=%wide.region_22.23_spmd.clone, body=%wide.region_20.22_spmd.clone.sunk | while | flops 4066375680 | bytes 131685048 | solution.py:751
  1285.9 14.6 pad_maximum_fusion
  1309.4 24.2 %multiply_reduce_fusion.1 = (f32[2048]{0:T(1024)}, f32[1536]{0:T(1024)S(1)}, f32[1536,2048]{1,0:T(8,128)}) fusion(f32[1536,2048]{1,0:T(8,128)} %get-tuple-element.395, f32[1536]{0:T(1024)S(1)} %copy-done.112, f32[2048]{0:T(1024)S(1)} %bitcast.662, f32[192,8,16,128]{3,2,1,0:T(8,128)} %bitcast.546, f32[1536,2048]{1,0:T(8,128)S(1)} %copy-done.4, ...), kind=kLoop, calls=%fused_computation.104 | loop fusion | flops 25162240 | bytes 62943232 | tf_op jit(solution)/shard_map/reduce_sum | solution.py:35
  1380.4 17.4 fusion.186
  1397.8 21.9 %fusion.81 = (f32[2048]{0:T(1024)S(1)}, f32[1536,2048]{1,0:T(8,128)}) fusion(f32[1536]{0:T(1024)S(1)} %copy-done.123, bf16[512,2048]{1,0:T(8,128)(2,1)S(1)} %copy-done.18, bf16[512,2048]{1,0:T(8,128)(2,1)} %collective-permute-done, bf16[512,2048]{1,0:T(8,128)(2,1)S(1)} %copy-done.48, f32[1536,2048]{1,0:T(8,128)} %fusion.186, ...), kind=kOutput, calls=%fused_computation.87 | convolution fusion | flops 12916357120 | bytes 46151680 | tf_op jit(solution)/shard_map/dot_general | solution.py:23
  1449.1 20.4 %convolution_convert_fusion.2 = bf16[2048,2048]{1,0:T(8,128)(2,1)} fusion(bf16[1536,2048]{1,0:T(8,128)(2,1)} %fusion.79, bf16[1536,2048]{1,0:T(8,128)(2,1)} %subtract_convert_fusion), kind=kOutput, calls=%fused_computation.133 | convolution fusion | flops 12889096192 | bytes 20971520 | tf_op jit(solution)/shard_map/dot_general | solution.py:23
  1469.5 34.2 %collective-permute-done.59 = bf16[768,2048]{1,0:T(8,128)(2,1)} collective-permute-done((bf16[768,2048]{1,0:T(8,128)(2,1)S(1)}, bf16[768,2048]{1,0:T(8,128)(2,1)}, u32[]{:S(2)}, u32[]{:S(2)}) %collective-permute-start.59) | collective-permute-done | bytes 3145760 | tf_op jit(solution)/shard_map/ppermute | solution.py:388
  1581.0 25.8 %collective-permute-done.36 = bf16[512,2048]{1,0:T(8,128)(2,1)} collective-permute-done((bf16[512,2048]{1,0:T(8,128)(2,1)}, bf16[512,2048]{1,0:T(8,128)(2,1)}, u32[]{:S(2)}, u32[]{:S(2)}) %collective-permute-start.36) | collective-permute-done | bytes 2097184 | tf_op jit(solution)/shard_map/ppermute | solution.py:19
  1676.5 43.4 %all-to-all-start.1 = ((bf16[2,4,64,1024]{3,2,0,1:T(8,128)(2,1)}), bf16[2,4,64,1024]{3,2,0,1:T(8,128)(2,1)}, u32[]{:S(2)}, u32[]{:S(2)}) async-start(bf16[2,4,64,1024]{3,2,0,1:T(8,128)(2,1)} %pad_maximum_fusion.14), calls=%async_computation.1 | async-start | bytes 2097152 | tf_op jit(solution)/shard_map/all_to_all | solution.py:458
  1762.6 33.6 %all-to-all-done.1 = bf16[2,4,64,1024]{3,2,0,1:T(8,128)(2,1)} async-done(((bf16[2,4,64,1024]{3,2,0,1:T(8,128)(2,1)}), bf16[2,4,64,1024]{3,2,0,1:T(8,128)(2,1)}, u32[]{:S(2)}, u32[]{:S(2)}) %all-to-all-start.1) | async-done | bytes 1048608 | tf_op jit(solution)/shard_map/all_to_all | solution.py:458
  1829.8 35.6 %all-to-all-done.2 = bf16[2,4,64,1024]{3,2,0,1:T(8,128)(2,1)} async-done(((bf16[2,4,64,1024]{3,2,0,1:T(8,128)(2,1)}), bf16[2,4,64,1024]{3,2,0,1:T(8,128)(2,1)}, u32[]{:S(2)}, u32[]{:S(2)}) %all-to-all-start.2) | async-done | bytes 1048608 | tf_op jit(solution)/shard_map/all_to_all | solution.py:458
  1894.5 104.8 %all-reduce.2.cloned.1.call-done = f32[9,2048]{1,0:T(8,128)} async-done(((f32[9,2048]{1,0:T(8,128)}), f32[9,2048]{1,0:T(8,128)}) %all-reduce.2.cloned.1.call-update) | async-done | bytes 73744 | tf_op jit(solution)/shard_map/psum | solution.py:799
  (809 shorter events, 1273.6 us)
Async XLA Ops:
  9.1 143.1 %collective-permute-start.2 = (bf16[2,64,2048]{2,1,0:T(8,128)(2,1)}, bf16[2,64,2048]{2,1,0:T(8,128)(2,1)}, u32[]{:S(2)}, u32[]{:S(2)}) collective-permute-start(bf16[2,64,2048]{2,1,0:T(8,128)(2,1)} %pad_maximum_fusion.18), channel_id=1, source_target_pairs={{0,1},{1,2},{2,3},{3,0},{4,5},{5,6},{6,7},{7,4},{8,9},{9,10},{10,1... | collective-permute-start | bytes 1572872 | tf_op jit(solution)/shard_map/ppermute | solution.py:393
  12.1 149.2 %collective-permute-start.3 = (bf16[2,64,2048]{2,1,0:T(8,128)(2,1)}, bf16[2,64,2048]{2,1,0:T(8,128)(2,1)}, u32[]{:S(2)}, u32[]{:S(2)}) collective-permute-start(bf16[2,64,2048]{2,1,0:T(8,128)(2,1)} %pad_maximum_fusion.18), channel_id=1, source_target_pairs={{0,2},{1,3},{2,0},{3,1},{4,6},{5,7},{6,4},{7,5},{8,10},{9,11},{10,... | collective-permute-start | bytes 1572872 | tf_op jit(solution)/shard_map/ppermute | solution.py:393
  14.7 154.6 %collective-permute-start.4 = (bf16[2,64,2048]{2,1,0:T(8,128)(2,1)}, bf16[2,64,2048]{2,1,0:T(8,128)(2,1)}, u32[]{:S(2)}, u32[]{:S(2)}) collective-permute-start(bf16[2,64,2048]{2,1,0:T(8,128)(2,1)} %pad_maximum_fusion.18), channel_id=1, source_target_pairs={{0,3},{1,0},{2,1},{3,2},{4,7},{5,4},{6,5},{7,6},{8,11},{9,8},{10,9... | collective-permute-start | bytes 1572872 | tf_op jit(solution)/shard_map/ppermute | solution.py:393
  17.9 136.3 %collective-permute-start.10 = (bf16[2,64,2048]{2,1,0:T(8,128)(2,1)}, bf16[2,64,2048]{2,1,0:T(8,128)(2,1)}, u32[]{:S(2)}, u32[]{:S(2)}) collective-permute-start(bf16[2,64,2048]{2,1,0:T(8,128)(2,1)} %pad_maximum_fusion.19), channel_id=1, source_target_pairs={{0,1},{1,2},{2,3},{3,0},{4,5},{5,6},{6,7},{7,4},{8,9},{9,10},{10,1... | collective-permute-start | bytes 1572872 | tf_op jit(solution)/shard_map/ppermute | solution.py:393
  18.6 145.9 %collective-permute-start.11 = (bf16[2,64,2048]{2,1,0:T(8,128)(2,1)}, bf16[2,64,2048]{2,1,0:T(8,128)(2,1)}, u32[]{:S(2)}, u32[]{:S(2)}) collective-permute-start(bf16[2,64,2048]{2,1,0:T(8,128)(2,1)} %pad_maximum_fusion.19), channel_id=1, source_target_pairs={{0,2},{1,3},{2,0},{3,1},{4,6},{5,7},{6,4},{7,5},{8,10},{9,11},{10,... | collective-permute-start | bytes 1572872 | tf_op jit(solution)/shard_map/ppermute | solution.py:393
  154.1 118.2 %collective-permute-start = (bf16[512,2048]{1,0:T(8,128)(2,1)S(1)}, bf16[512,2048]{1,0:T(8,128)(2,1)}, u32[]{:S(2)}, u32[]{:S(2)}) collective-permute-start(bf16[512,2048]{1,0:T(8,128)(2,1)S(1)} %copy-done.16), channel_id=1, source_target_pairs={{0,1},{1,2},{2,3},{4,5},{5,6},{6,7},{8,9},{9,10},{10,11},{12,13},{... | collective-permute-start | bytes 6291464 | tf_op jit(solution)/shard_map/ppermute | solution.py:19
  307.4 218.1 %collective-permute-start.29 = (bf16[768,2048]{1,0:T(8,128)(2,1)}, bf16[768,2048]{1,0:T(8,128)(2,1)}, u32[]{:S(2)}, u32[]{:S(2)}) collective-permute-start(bf16[768,2048]{1,0:T(8,128)(2,1)} %broadcast_select_fusion), channel_id=1, source_target_pairs={{1,0},{2,3},{6,7},{5,4},{9,8},{10,11},{14,15},{13,12},{17,16},{18,... | collective-permute-start | bytes 9437192 | tf_op jit(solution)/shard_map/ppermute | solution.py:404
  341.2 139.3 %collective-permute-start.7 = (bf16[2,2,4,64,2048]{4,3,2,0,1:T(8,128)(2,1)}, bf16[2,2,4,64,2048]{4,3,2,0,1:T(8,128)(2,1)}, u32[]{:S(2)}, u32[]{:S(2)}) collective-permute-start(bf16[2,2,4,64,2048]{4,3,2,0,1:T(8,128)(2,1)} %maximum_select_fusion.10), channel_id=1, source_target_pairs={{0,4},{4,0},{8,12},{12,8},{16,20},{20,16},{24,28},{28,24},{1,5},{5... | collective-permute-start | bytes 12582920 | tf_op jit(solution)/shard_map/ppermute | solution.py:388
  365.0 320.3 %collective-permute-start.21 = (bf16[2,2,4,64,2048]{4,3,2,0,1:T(8,128)(2,1)}, bf16[2,2,4,64,2048]{4,3,2,0,1:T(8,128)(2,1)}, u32[]{:S(2)}, u32[]{:S(2)}) collective-permute-start(bf16[2,2,4,64,2048]{4,3,2,0,1:T(8,128)(2,1)} %maximum_select_fusion.16), channel_id=1, source_target_pairs={{0,4},{4,0},{8,12},{12,8},{16,20},{20,16},{24,28},{28,24},{1,5},{5... | collective-permute-start | bytes 12582920 | tf_op jit(solution)/shard_map/ppermute | solution.py:388
  365.4 160.1 %collective-permute-start.26 = (bf16[768,2048]{1,0:T(8,128)(2,1)}, bf16[768,2048]{1,0:T(8,128)(2,1)}, u32[]{:S(2)}, u32[]{:S(2)}) collective-permute-start(bf16[768,2048]{1,0:T(8,128)(2,1)} %collective-permute-done.25), channel_id=1, source_target_pairs={{2,3},{5,4},{10,11},{13,12},{18,19},{21,20},{26,27},{29,28}} | collective-permute-start | bytes 9437192 | tf_op jit(solution)/shard_map/ppermute | solution.py:404
  613.2 190.7 %collective-permute-start.31 = (bf16[2,768,2048]{2,1,0:T(8,128)(2,1)}, bf16[2,768,2048]{2,1,0:T(8,128)(2,1)}, u32[]{:S(2)}, u32[]{:S(2)}) collective-permute-start(bf16[2,768,2048]{2,1,0:T(8,128)(2,1)} %maximum_select_fusion.8), channel_id=1, source_target_pairs={{0,8},{4,12},{8,0},{12,4},{16,24},{20,28},{24,16},{28,20},{1,9},{5... | collective-permute-start | bytes 18874376 | tf_op jit(solution)/shard_map/ppermute | solution.py:388
  684.8 143.7 %collective-permute-start.28 = (bf16[2,768,2048]{2,1,0:T(8,128)(2,1)}, bf16[2,768,2048]{2,1,0:T(8,128)(2,1)}, u32[]{:S(2)}, u32[]{:S(2)}) collective-permute-start(bf16[2,768,2048]{2,1,0:T(8,128)(2,1)} %maximum_select_fusion.6), channel_id=1, source_target_pairs={{0,16},{4,20},{8,24},{12,28},{16,0},{20,4},{24,8},{28,12},{1,17},{... | collective-permute-start | bytes 18874376 | tf_op jit(solution)/shard_map/ppermute | solution.py:388
  715.1 135.9 %collective-permute-start.23 = (bf16[512,2048]{1,0:T(8,128)(2,1)}, bf16[512,2048]{1,0:T(8,128)(2,1)}, u32[]{:S(2)}, u32[]{:S(2)}) collective-permute-start(bf16[512,2048]{1,0:T(8,128)(2,1)} %multiply_convert_fusion.9), channel_id=1, source_target_pairs={{0,4},{4,0},{8,12},{12,8},{16,20},{20,16},{24,28},{28,24},{1,5},{5... | collective-permute-start | bytes 6291464 | tf_op jit(solution)/shard_map/ppermute | solution.py:388
  937.0 120.9 %collective-permute-start.35 = (f32[512,2]{0,1:T(2,128)S(1)}, f32[512,2]{0,1:T(2,128)S(1)}, u32[]{:S(2)}, u32[]{:S(2)}) collective-permute-start(f32[512,2]{0,1:T(2,128)S(1)} %pad_maximum_fusion.22), channel_id=1, source_target_pairs={{0,4},{4,0},{8,12},{12,8},{16,20},{20,16},{24,28},{28,24},{1,5},{5... | collective-permute-start | bytes 12296 | tf_op jit(solution)/shard_map/ppermute | solution.py:388
  1027.6 392.2 %collective-permute-start.58 = (bf16[2,768,2048]{2,1,0:T(8,128)(2,1)}, bf16[2,768,2048]{2,1,0:T(8,128)(2,1)}, u32[]{:S(2)}, u32[]{:S(2)}) collective-permute-start(bf16[2,768,2048]{2,1,0:T(8,128)(2,1)} %fusion.93), channel_id=1, source_target_pairs={{0,16},{4,20},{8,24},{12,28},{16,0},{20,4},{24,8},{28,12},{1,17},{... | collective-permute-start | bytes 18874376 | tf_op jit(solution)/shard_map/ppermute | solution.py:388
  1057.7 377.2 %collective-permute-start.56 = (bf16[2,768,2048]{2,1,0:T(8,128)(2,1)}, bf16[2,768,2048]{2,1,0:T(8,128)(2,1)}, u32[]{:S(2)}, u32[]{:S(2)}) collective-permute-start(bf16[2,768,2048]{2,1,0:T(8,128)(2,1)} %fusion.97), channel_id=1, source_target_pairs={{0,8},{4,12},{8,0},{12,4},{16,24},{20,28},{24,16},{28,20},{1,9},{5... | collective-permute-start | bytes 18874376 | tf_op jit(solution)/shard_map/ppermute | solution.py:388
  1346.6 210.5 %collective-permute-start.47 = (bf16[2,2,256,1024]{3,2,1,0:T(8,128)(2,1)}, bf16[2,2,256,1024]{3,2,1,0:T(8,128)(2,1)}, u32[]{:S(2)}, u32[]{:S(2)}) collective-permute-start(bf16[2,2,256,1024]{3,2,1,0:T(8,128)(2,1)} %dynamic-slice_bitcast_fusion.8), channel_id=1, source_target_pairs={{0,4},{4,0},{8,12},{12,8},{16,20},{20,16},{24,28},{28,24},{1,5},{5... | collective-permute-start | bytes 6291464 | tf_op jit(solution)/shard_map/ppermute | solution.py:388
  1350.5 220.5 %collective-permute-start.44 = (bf16[2,2,256,1024]{3,2,1,0:T(8,128)(2,1)}, bf16[2,2,256,1024]{3,2,1,0:T(8,128)(2,1)}, u32[]{:S(2)}, u32[]{:S(2)}) collective-permute-start(bf16[2,2,256,1024]{3,2,1,0:T(8,128)(2,1)} %dynamic-slice_bitcast_fusion.9), channel_id=1, source_target_pairs={{0,4},{4,0},{8,12},{12,8},{16,20},{20,16},{24,28},{28,24},{1,5},{5... | collective-permute-start | bytes 6291464 | tf_op jit(solution)/shard_map/ppermute | solution.py:388
  1354.1 223.3 %collective-permute-start.50 = (bf16[2,2,256,1024]{3,2,1,0:T(8,128)(2,1)}, bf16[2,2,256,1024]{3,2,1,0:T(8,128)(2,1)}, u32[]{:S(2)}, u32[]{:S(2)}) collective-permute-start(bf16[2,2,256,1024]{3,2,1,0:T(8,128)(2,1)} %dynamic-slice_bitcast_fusion.7), channel_id=1, source_target_pairs={{0,4},{4,0},{8,12},{12,8},{16,20},{20,16},{24,28},{28,24},{1,5},{5... | collective-permute-start | bytes 6291464 | tf_op jit(solution)/shard_map/ppermute | solution.py:388
  1676.5 119.7 %all-to-all-start.1 = ((bf16[2,4,64,1024]{3,2,0,1:T(8,128)(2,1)}), bf16[2,4,64,1024]{3,2,0,1:T(8,128)(2,1)}, u32[]{:S(2)}, u32[]{:S(2)}) async-start(bf16[2,4,64,1024]{3,2,0,1:T(8,128)(2,1)} %pad_maximum_fusion.14), calls=%async_computation.1 | async-start | bytes 2097152 | tf_op jit(solution)/shard_map/all_to_all | solution.py:458
  1731.4 144.6 %collective-permute-start.63 = (bf16[768,2048]{1,0:T(8,128)(2,1)S(1)}, bf16[768,2048]{1,0:T(8,128)(2,1)}, u32[]{:S(2)}, u32[]{:S(2)}) collective-permute-start(bf16[768,2048]{1,0:T(8,128)(2,1)S(1)} %fusion.102), channel_id=1, source_target_pairs={{0,1},{7,6},{8,9},{15,14},{16,17},{23,22},{24,25},{31,30}} | collective-permute-start | bytes 9437192 | tf_op jit(solution)/shard_map/ppermute | solution.py:404
  1807.5 191.9 %all-reduce.2.cloned.1.call-start = ((), (), s32[]{:S(2)}) async-start(), calls=%async_computation.3 | async-start | bytes 262144 | tf_op jit(solution)/shard_map/psum | solution.py:799
  1865.4 143.3 %all-to-all-start = ((bf16[2,4,64,2048]{3,2,0,1:T(8,128)(2,1)}), bf16[2,4,64,2048]{3,2,0,1:T(8,128)(2,1)}, u32[]{:S(2)}, u32[]{:S(2)}) async-start(bf16[2,4,64,2048]{3,2,0,1:T(8,128)(2,1)} %pad_maximum_fusion.13), calls=%async_computation | async-start | bytes 4194304 | tf_op jit(solution)/shard_map/all_to_all | solution.py:458
  1887.4 124.6 %collective-permute-start.64 = (f32[384,2048]{1,0:T(8,128)}, f32[384,2048]{1,0:T(8,128)}, u32[]{:S(2)}, u32[]{:S(2)}) collective-permute-start(f32[384,2048]{1,0:T(8,128)} %fusion.126), channel_id=1, source_target_pairs={{0,4},{4,0},{8,12},{12,8},{16,20},{20,16},{24,28},{28,24},{1,5},{5... | collective-permute-start | bytes 9437192 | tf_op jit(solution)/shard_map/ppermute | solution.py:388
  (232 other events, 5596.5 us)
Sparse Core Ops, SparseCore 0:
  1824.4 174.9 all-reduce.1

commit v2 on v1

--- a/solution.py
+++ b/solution.py
@@ -1,12 +1,17 @@
+import functools
+
 import jax
 import jax.numpy as jnp
 from jax import lax
+from jax.experimental import pallas as pl
+from jax.experimental.pallas import tpu as pltpu
 from jax.sharding import PartitionSpec as P
 
 HEADS = 16
 HEAD_DIM = 128
 WINDOW = 1024
 TOP = 2
+VMEM_LIMIT = 56 * 1024 * 1024
 
 
 norm_eps = 1e-05
@@ -383,6 +388,439 @@
     )
 
 
+def dot_t(left, right):
+    return lax.dot_general(left, right, (((1,), (1,)), ((), ())), preferred_element_type=jnp.float32)
+
+
+def t_dot(left, right):
+    return lax.dot_general(left, right, (((0,), (0,)), ((), ())), preferred_element_type=jnp.float32)
+
+
+def kernel_call(kernel, **options):
+    return pl.pallas_call(
+        kernel,
+        compiler_params=pltpu.CompilerParams(vmem_limit_bytes=VMEM_LIMIT),
+        **options,
+    )
+
+
+def turn(value, cosine, sine):
+    return value * cosine + pltpu.roll(value, HEAD_DIM // 2, 1) * sine
+
+
+def code_of(place, blocks):
+    return place % (blocks // 2) * 2 + place // (blocks // 2)
+
+
+def place_of(code, blocks):
+    return code % 2 * (blocks // 2) + code // 2
+
+
+def norm_kernel(rank, x_ref, gain_ref, o_ref, scale_ref, *, blocks):
+    value = x_ref[...].astype(jnp.float32)
+    scale = lax.rsqrt(jnp.mean(value * value, axis=1, keepdims=True) + norm_eps)
+    scale_ref[...] = scale
+    block = x_ref.shape[1] // blocks
+    for place in range(blocks):
+        start = pl.multiple_of((rank[0] ^ code_of(place, blocks)) * block, block)
+        piece = x_ref[:, pl.ds(start, block)].astype(jnp.float32)
+        piece = piece * scale * gain_ref[:, pl.ds(start, block)]
+        at = place % (blocks // 2) * block
+        o_ref[place // (blocks // 2), :, at : at + block] = piece.astype(jnp.bfloat16)
+
+
+def norm_rows(rank, value, gain, blocks):
+    rows, width = value.shape
+    tile = 256
+    return kernel_call(
+        functools.partial(norm_kernel, blocks=blocks),
+        grid_spec=pltpu.PrefetchScalarGridSpec(
+            num_scalar_prefetch=1,
+            grid=(rows // tile,),
+            in_specs=[
+                pl.BlockSpec((tile, width), lambda i, rank: (i, 0)),
+                pl.BlockSpec((1, width), lambda i, rank: (0, 0)),
+            ],
+            out_specs=[
+                pl.BlockSpec((2, tile, width // 2), lambda i, rank: (0, i, 0)),
+                pl.BlockSpec((tile, 1), lambda i, rank: (i, 0)),
+            ],
+        ),
+        out_shape=[
+            jax.ShapeDtypeStruct((2, rows, width // 2), jnp.bfloat16),
+            jax.ShapeDtypeStruct((rows, 1), jnp.float32),
+        ],
+        cost_estimate=pl.CostEstimate(
+            flops=8 * rows * width, bytes_accessed=4 * rows * width, transcendentals=0
+        ),
+    )(rank, value, gain[None])
+
+
+def project_kernel(low_ref, high_ref, a_ref, b_ref, o_ref, s_ref):
+    total = matmul(low_ref[0], a_ref[...]) + matmul(high_ref[0], b_ref[...])
+    o_ref[...] = total.astype(o_ref.dtype)
+    s_ref[...] = jnp.sum(total * total, axis=1, keepdims=True)
+
+
+def project(halves, a, b, dtype, start=0):
+    _, rows, depth = halves.shape
+    rows = rows - start
+    width = a.shape[1]
+    tile = 256
+    first = start // tile
+    weight = pl.BlockSpec((depth, width), lambda i: (0, 0))
+    return kernel_call(
+        project_kernel,
+        grid=(rows // tile,),
+        in_specs=[
+            pl.BlockSpec((1, tile, depth), lambda i: (0, i + first, 0)),
+            pl.BlockSpec((1, tile, depth), lambda i: (1, i + first, 0)),
+            weight,
+            weight,
+        ],
+        out_specs=[
+            pl.BlockSpec((tile, width), lambda i: (i, 0)),
+            pl.BlockSpec((tile, 1), lambda i: (i, 0)),
+        ],
+        out_shape=[
+            jax.ShapeDtypeStruct((rows, width), dtype),
+            jax.ShapeDtypeStruct((rows, 1), jnp.float32),
+        ],
+        cost_estimate=pl.CostEstimate(
+            flops=4 * rows * depth * width, bytes_accessed=8 * depth * width, transcendentals=0
+        ),
+    )(halves, halves, a, b)
+
+
+def project_back_kernel(k_ref, v_ref, q_ref, ka, kb, va, vb, qa, qb, o_ref, *, own):
+    i, j = pl.program_id(0), pl.program_id(1)
+    half = pl.num_programs(1) // 2
+
+    def part(key, value, query):
+        total = dot_t(k_ref[...], key[...]) + dot_t(v_ref[...], value[...])
+        o_ref[0] = total
+
+        @pl.when(i >= own)
+        def _():
+            o_ref[0] += dot_t(q_ref[...], query[...])
+
+    @pl.when(j < half)
+    def _():
+        part(ka, va, qa)
+
+    @pl.when(j >= half)
+    def _():
+        part(kb, vb, qb)
+
+
+def project_back(key, value, query, key_w, value_w, query_w):
+    rows, width = key.shape
+    depth = key_w[0].shape[0]
+    tile, step = 512, 512
+    half = depth // step
+    own = (rows - query.shape[0]) // tile
+    x_spec = pl.BlockSpec((tile, width), lambda i, j: (i, 0))
+    low = pl.BlockSpec((step, width), lambda i, j: (jnp.minimum(j, half - 1), 0))
+    high = pl.BlockSpec((step, width), lambda i, j: (jnp.maximum(j - half, 0), 0))
+    return kernel_call(
+        functools.partial(project_back_kernel, own=own),
+        grid=(rows // tile, 2 * half),
+        in_specs=[
+            x_spec,
+            x_spec,
+            pl.BlockSpec((tile, width), lambda i, j: (jnp.maximum(i - own, 0), 0)),
+        ]
+        + [low, high] * 3,
+        out_specs=pl.BlockSpec((1, tile, step), lambda i, j: (j // half, i, j % half)),
+        out_shape=jax.ShapeDtypeStruct((2, rows, depth), jnp.float32),
+        cost_estimate=pl.CostEstimate(
+            flops=9 * rows * depth * width, bytes_accessed=32 * depth * width, transcendentals=0
+        ),
+    )(key, value, query, *key_w, *value_w, *query_w)
+
+
+def tokens_back_kernel(
+    rank, g_ref, c_ref, x_ref, res_ref, scale_ref, gain_ref, o_ref, gain_grad_ref, *, blocks
+):
+    scale = scale_ref[...]
+    block = x_ref.shape[1] // blocks
+    half = blocks // 2
+
+    @pl.when(pl.program_id(0) == 0)
+    def _():
+        gain_grad_ref[...] = jnp.zeros_like(gain_grad_ref)
+
+    def pieces(place):
+        start = pl.multiple_of((rank[0] ^ code_of(place, blocks)) * block, block)
+        at = slice(place % half * block, place % half * block + block)
+        grad = g_ref[place // half, :, at] + c_ref[place // half, :, at].astype(jnp.float32)
+        columns = pl.ds(start, block)
+        return columns, grad, x_ref[:, columns].astype(jnp.float32), gain_ref[:, columns]
+
+    inner = jnp.zeros_like(scale)
+    for place in range(blocks):
+        columns, grad, value, gain = pieces(place)
+        product = grad * value
+        inner += jnp.sum(product * gain, axis=1, keepdims=True)
+        gain_grad_ref[:, columns] += jnp.sum(product * scale, axis=0, keepdims=True)
+    inner = inner * (1.0 / x_ref.shape[1]) * (scale * scale * scale)
+    for place in range(blocks):
+        columns, grad, value, gain = pieces(place)
+        o_ref[:, columns] = res_ref[:, columns] + (scale * (grad * gain) - value * inner)
+
+
+def tokens_back(rank, grad, carried, tokens, residual_grad, scale, gain, blocks):
+    rows, width = tokens.shape
+    tile = 128
+    first = (grad.shape[1] - rows) // tile
+    wide = pl.BlockSpec((tile, width), lambda i, rank: (i, 0))
+    one = pl.BlockSpec((1, width), lambda i, rank: (0, 0))
+    return kernel_call(
+        functools.partial(tokens_back_kernel, blocks=blocks),
+        grid_spec=pltpu.PrefetchScalarGridSpec(
+            num_scalar_prefetch=1,
+            grid=(rows // tile,),
+            in_specs=[
+                pl.BlockSpec((2, tile, width // 2), lambda i, rank: (0, i + first, 0)),
+                pl.BlockSpec((2, tile, width // 2), lambda i, rank: (0, i, 0)),
+                wide,
+                wide,
+                pl.BlockSpec((tile, 1), lambda i, rank: (i + first, 0)),
+                one,
+            ],
+            out_specs=[wide, one],
+        ),
+        out_shape=[
+            jax.ShapeDtypeStruct((rows, width), jnp.float32),
+            jax.ShapeDtypeStruct((1, width), jnp.float32),
+        ],
+        cost_estimate=pl.CostEstimate(
+            flops=10 * rows * width, bytes_accessed=16 * rows * width, transcendentals=0
+        ),
+    )(rank, grad, carried, tokens, residual_grad, scale, gain[None])
+
+
+def head_rows(lin, scale, gain, cosine, sine):
+    return turn(lin * scale * gain, cosine, sine).astype(jnp.bfloat16)
+
+
+def moved_head(head, rank):
+    place = place_of((head // 2) ^ rank[0], HEADS // 2) * 2 + head % 2
+    return place // (HEADS // 2), 0, place % (HEADS // 2)
+
+
+def attention_specs(rows, all_rows, bias):
+    head = lambda h, rank: (0, h)
+    fixed = lambda h, rank: (0, 0)
+    return [
+        pl.BlockSpec((rows, HEAD_DIM), head),
+        pl.BlockSpec((all_rows, HEAD_DIM), head),
+        pl.BlockSpec((all_rows, HEAD_DIM), head),
+        pl.BlockSpec((rows, 1), fixed),
+        pl.BlockSpec((all_rows, 1), fixed),
+        pl.BlockSpec((1, HEAD_DIM), head),
+        pl.BlockSpec((1, HEAD_DIM), head),
+        pl.BlockSpec((all_rows, HEAD_DIM), fixed),
+        pl.BlockSpec((all_rows, HEAD_DIM), fixed),
+        pl.BlockSpec(bias.shape, lambda h, rank: (0, 0, 0)),
+    ]
+
+
+def attend_kernel(
+    rank,
+    q_ref,
+    k_ref,
+    v_ref,
+    sq_ref,
+    sk_ref,
+    gq_ref,
+    gk_ref,
+    cos_ref,
+    sin_ref,
+    bias_ref,
+    o_ref,
+    lse_ref,
+    *,
+    behind,
+    tile,
+    span,
+):
+    rows = q_ref.shape[0]
+    cosine, sine = cos_ref[...], sin_ref[...]
+    keys = head_rows(k_ref[...], sk_ref[...], gk_ref[...], cosine, sine)
+    queries = head_rows(q_ref[...], sq_ref[...], gq_ref[...], cosine[behind:], sine[behind:])
+    for t in range(rows // tile):
+        at = slice(t * tile, (t + 1) * tile)
+        seen = slice(t * tile, t * tile + span)
+        scores = dot_t(keys[seen], queries[at])
+        scores = scores * HEAD_DIM ** (-0.5) + bias_ref[t].astype(jnp.float32)
+        peak = jnp.max(scores, axis=0, keepdims=True)
+        shifted = jnp.exp(scores - peak)
+        total = jnp.sum(shifted, axis=0, keepdims=True)
+        weights = (shifted * (1.0 / total)).astype(jnp.bfloat16)
+        o_ref[0, at, :] = t_dot(weights, v_ref[seen, :]).astype(jnp.bfloat16)
+        lse_ref[0, :, at] = peak + jnp.log(total)
+
+
+def attend(rank, operands, bias):
+    rows, width = operands[0].shape
+    all_rows = operands[1].shape[0]
+    tiles, span, tile = bias.shape
+    return kernel_call(
+        functools.partial(attend_kernel, behind=all_rows - rows, tile=tile, span=span),
+        grid_spec=pltpu.PrefetchScalarGridSpec(
+            num_scalar_prefetch=1,
+            grid=(HEADS,),
+            in_specs=attention_specs(rows, all_rows, bias),
+            out_specs=[
+                pl.BlockSpec((1, rows, HEAD_DIM), moved_head),
+                pl.BlockSpec((1, 1, rows), lambda h, rank: (h, 0, 0)),
+            ],
+        ),
+        out_shape=[
+            jax.ShapeDtypeStruct((2, rows, width // 2), jnp.bfloat16),
+            jax.ShapeDtypeStruct((HEADS, 1, rows), jnp.float32),
+        ],
+        cost_estimate=pl.CostEstimate(
+            flops=4 * rows * span * width,
+            bytes_accessed=8 * all_rows * width,
+            transcendentals=rows * span * HEADS,
+        ),
+    )(rank, *operands, bias)
+
+
+def attend_back_kernel(
+    rank,
+    q_ref,
+    k_ref,
+    v_ref,
+    sq_ref,
+    sk_ref,
+    gq_ref,
+    gk_ref,
+    cos_ref,
+    sin_ref,
+    bias_ref,
+    g_ref,
+    lse_ref,
+    dq_ref,
+    dk_ref,
+    dv_ref,
+    key_total,
+    value_total,
+    *,
+    behind,
+    tile,
+    span,
+):
+    rows = q_ref.shape[0]
+    score_scale = HEAD_DIM ** (-0.5)
+    cosine, sine = cos_ref[...], sin_ref[...]
+    keys = head_rows(k_ref[...], sk_ref[...], gk_ref[...], cosine, sine)
+    queries = head_rows(q_ref[...], sq_ref[...], gq_ref[...], cosine[behind:], sine[behind:])
+    key_total[...] = jnp.zeros_like(key_total)
+    value_total[...] = jnp.zeros_like(value_total)
+    for t in range(rows // tile):
+        at = slice(t * tile, (t + 1) * tile)
+        seen = slice(t * tile, t * tile + span)
+        scores = dot_t(keys[seen], queries[at])
+        scores = scores * score_scale + bias_ref[t].astype(jnp.float32)
+        probs = jnp.exp(scores - lse_ref[0, :, at])
+        grad = g_ref[0, at, :]
+        value_total[seen, :] += matmul(probs.astype(jnp.bfloat16), grad)
+        probs_grad = dot_t(v_ref[seen, :], grad)
+        inner = jnp.sum(probs * probs_grad, axis=0, keepdims=True)
+        score_grad = (probs * (probs_grad - inner)).astype(jnp.bfloat16)
+        dq_ref[at, :] = (t_dot(score_grad, keys[seen]) * score_scale).astype(jnp.bfloat16)
+        key_total[seen, :] += matmul(score_grad, queries[at])
+    dk_ref[...] = (key_total[...] * score_scale).astype(jnp.bfloat16)
+    dv_ref[...] = value_total[...].astype(jnp.bfloat16)
+
+
+def attend_back(rank, operands, bias, grad, lse):
+    rows, width = operands[0].shape
+    all_rows = operands[1].shape[0]
+    tiles, span, tile = bias.shape
+    head = lambda h, rank: (0, h)
+    return kernel_call(
+        functools.partial(attend_back_kernel, behind=all_rows - rows, tile=tile, span=span),
+        grid_spec=pltpu.PrefetchScalarGridSpec(
+            num_scalar_prefetch=1,
+            grid=(HEADS,),
+            in_specs=attention_specs(rows, all_rows, bias)
+            + [
+                pl.BlockSpec((1, rows, HEAD_DIM), moved_head),
+                pl.BlockSpec((1, 1, rows), lambda h, rank: (h, 0, 0)),
+            ],
+            out_specs=[
+                pl.BlockSpec((rows, HEAD_DIM), head),
+                pl.BlockSpec((all_rows, HEAD_DIM), head),
+                pl.BlockSpec((all_rows, HEAD_DIM), head),
+            ],
+            scratch_shapes=[
+                pltpu.VMEM((all_rows, HEAD_DIM), jnp.float32),
+                pltpu.VMEM((all_rows, HEAD_DIM), jnp.float32),
+            ],
+        ),
+        out_shape=[
+            jax.ShapeDtypeStruct((rows, width), jnp.bfloat16),
+            jax.ShapeDtypeStruct((all_rows, width), jnp.bfloat16),
+            jax.ShapeDtypeStruct((all_rows, width), jnp.bfloat16),
+        ],
+        cost_estimate=pl.CostEstimate(
+            flops=10 * rows * span * width,
+            bytes_accessed=12 * all_rows * width,
+            transcendentals=rows * span * HEADS,
+        ),
+    )(rank, *operands, bias, grad, lse)
+
+
+def lin_back_kernel(g_ref, lin_ref, scale_ref, gain_ref, cos_ref, sin_ref, o_ref, gain_grad_ref):
+    scale = scale_ref[...]
+    cosine, sine = cos_ref[...], -sin_ref[...]
+    inner = jnp.zeros_like(scale)
+
+    @pl.when(pl.program_id(0) == 0)
+    def _():
+        gain_grad_ref[...] = jnp.zeros_like(gain_grad_ref)
+
+    turned = []
+    for h in range(HEADS):
+        at = slice(h * HEAD_DIM, (h + 1) * HEAD_DIM)
+        grad = turn(g_ref[:, at].astype(jnp.float32), cosine, sine)
+        lin = lin_ref[:, at]
+        product = grad * lin
+        gain_grad_ref[:, at] += jnp.sum(product * scale, axis=0, keepdims=True)
+        inner += jnp.sum(product * gain_ref[:, at], axis=1, keepdims=True)
+    inner = inner * (1.0 / (HEADS * HEAD_DIM)) * (scale * scale * scale)
+    for h in range(HEADS):
+        at = slice(h * HEAD_DIM, (h + 1) * HEAD_DIM)
+        grad = turn(g_ref[:, at].astype(jnp.float32), cosine, sine)
+        value = scale * (grad * gain_ref[:, at]) - lin_ref[:, at] * inner
+        o_ref[:, at] = value.astype(jnp.bfloat16)
+
+
+def lin_back(grad, lin, scale, gain, cosine, sine):
+    rows, width = lin.shape
+    tile = 256
+    wide = pl.BlockSpec((tile, width), lambda i: (i, 0))
+    one = pl.BlockSpec((1, width), lambda i: (0, 0))
+    table = pl.BlockSpec((tile, HEAD_DIM), lambda i: (i, 0))
+    return kernel_call(
+        lin_back_kernel,
+        grid=(rows // tile,),
+        in_specs=[wide, wide, pl.BlockSpec((tile, 1), lambda i: (i, 0)), one, table, table],
+        out_specs=[wide, one],
+        out_shape=[
+            jax.ShapeDtypeStruct((rows, width), jnp.bfloat16),
+            jax.ShapeDtypeStruct((1, width), jnp.float32),
+        ],
+        cost_estimate=pl.CostEstimate(
+            flops=10 * rows * width, bytes_accessed=8 * rows * width, transcendentals=0
+        ),
+    )(grad, lin, scale, gain, cosine, sine)
+
+
 def across(value, bit):
     count = lax.axis_size("rep")
     return lax.ppermute(value, "rep", [(place, place ^ bit) for place in range(count)])
@@ -412,25 +850,44 @@
     return jnp.where(bit == 1, jnp.stack([other, own], axis), jnp.stack([own, other], axis))
 
 
-def gather_pair(left, right, place):
-    y_bit, x_bit, core, shard = place
+def over_ep(value, place):
+    shard = place[3]
     experts = lax.axis_size("ep")
-    both = jnp.stack([left, right])
-    parts = jnp.zeros((experts,) + both.shape, both.dtype)
-    parts = lax.dynamic_update_index_in_dim(parts, both, shard, 0)
+    parts = jnp.zeros((experts,) + value.shape, value.dtype)
+    parts = lax.dynamic_update_index_in_dim(parts, value, shard, 0)
     for steps in range(1, experts):
         parts = lax.dynamic_update_index_in_dim(
-            parts, along(both, steps), lax.rem(shard - steps + experts, experts), 0
+            parts, along(value, steps), lax.rem(shard - steps + experts, experts), 0
         )
-    a, b = parts[:, 0], parts[:, 1]
+    return parts
+
+
+def gather_small(value, place):
+    y_bit, x_bit, core, shard = place
+    value = over_ep(value, place)
+    value = in_order(value, across(value, 1), core, 0)
+    value = in_order(value, across(value, 2), x_bit, 0)
+    return in_order(value, across(value, 4), y_bit, 0)
+
+
+def sum_small(value, place):
+    value = value + across(value, 1)
+    value = value + across(value, 2)
+    value = value + across(value, 4)
+    return jnp.sum(over_ep(value, place), axis=0)
+
+
+def gather_pair(left, right, place):
+    width = left.shape[1]
+    parts = over_ep(jnp.stack([left, right]), place)
+    a, b = parts[:, 0].reshape(-1, width), parts[:, 1].reshape(-1, width)
     a_x, b_y = across(a, 2), across(b, 4)
-    a, b = in_order(a, a_x, x_bit, 0), in_order(b, b_y, y_bit, 0)
-    a_y, b_x = across(a, 4), across(b, 2)
-    a, b = in_order(a, a_y, y_bit, 0), in_order(b, b_x, x_bit, 1)
-    a_c, b_c = across(a, 1), across(b, 1)
-    a, b = in_order(a, a_c, core, 2), in_order(b, b_c, core, 2)
-    width = left.shape[1]
-    return a.reshape(-1, width), b.reshape(-1, width)
+    a = jnp.concatenate([a, a_x], 0)
+    b_both = jnp.stack([b, b_y])
+    a_y, b_x = across(a, 4), across(b_both, 2)
+    a = jnp.concatenate([a, a_y], 0)
+    b = jnp.concatenate([b, b_x[0], b_y, b_x[1]], 0)
+    return (a, across(a, 1)), (b, across(b, 1))
 
 
 def half_step(value, bit, axis, link):
@@ -446,18 +903,29 @@
     return half_step(a, y_bit, 0, 4), half_step(b, x_bit, 0, 2)
 
 
-def scatter_pair(left, right, place):
-    y_bit, x_bit, core, shard = place
+def chip_sum(halves, grad):
+    sent = across(t_dot(halves[1], grad).astype(jnp.bfloat16), 1)
+    kept = t_dot(halves[0], grad) + sent.astype(jnp.float32)
+    return kept.astype(jnp.bfloat16).reshape(2, 2, -1, grad.shape[1])
+
+
+def add(left, right):
+    return (left.astype(jnp.float32) + right.astype(jnp.float32)).astype(jnp.bfloat16)
+
+
+def scatter_pair(a, b, place):
+    shard = place[3]
     experts = lax.axis_size("ep")
-    rows, width = left.shape
-    shape = (2, 2, 2, rows // 8, width)
-    a = half_step(left.reshape(shape), core, 2, 1)
-    b = half_step(right.reshape(shape), core, 2, 1)
-    a, b = plane_sum(a, b, place)
-    both = jnp.stack([a, b]).reshape(2, experts, rows // (8 * experts), width)
-    both = lax.all_to_all(both, "ep", split_axis=1, concat_axis=1, tiled=True)
-    both = jnp.sum(both.astype(jnp.float32), axis=1)
-    return both[0], both[1]
+    a_x, b_y = across(a[:, 1], 2), across(b[1], 4)
+    a, b = add(a[:, 0], a_x), add(b[0], b_y)
+    a_y, b_x = across(a[1], 4), across(b[1], 2)
+    a, b = add(a[0], a_y), add(b[0], b_x)
+    both = jnp.stack([a, b])
+    both = both.reshape(2, experts, both.shape[1] // experts, both.shape[2])
+    total = pick(both, shard, 1).astype(jnp.float32)
+    for steps in range(1, experts):
+        total = total + along(pick(both, lax.rem(shard + steps, experts), 1), steps)
+    return total[0], total[1]
 
 
 def gather_experts(quarter, place):
@@ -515,8 +983,6 @@
     experts = lax.axis_size("ep")
     reps = lax.axis_size("rep")
     reach = min(-(-WINDOW // local_rows), experts - 1)
-    group = min(HEADS, 4)
-    score_scale = HEAD_DIM ** (-0.5)
     shard = lax.axis_index("ep")
     rep = lax.axis_index("rep")
     place = (rep // 4, rep // 2 % 2, rep % 2, shard)
@@ -534,14 +1000,17 @@
         ],
         1,
     )
-    small = lax.all_gather(small, ("rep", "ep"), axis=0, tiled=True)
-    gain_attn, gain_query, gain_key, gain_moe = [small[:, i].astype(f32) for i in range(4)]
-    weight_router = small[:, 4 : 4 + experts]
-    counts = small[:: attn_gain.shape[0], 4 + experts :].astype(f32)
-    count = jnp.sum(counts[:, 0]) * 16.0 + jnp.sum(counts[:, 1])
-
-    weight_key, weight_value = gather_pair(w_key, w_value, place)
-    weight_query, weight_out = gather_pair(w_query, w_out, place)
+    small = gather_small(small.T, place)
+    small = jnp.moveaxis(small, 4, 0).reshape(small.shape[4], -1)
+    gain_attn, gain_query, gain_key, gain_moe = [small[i].astype(f32) for i in range(4)]
+    weight_router = small[4 : 4 + experts].T
+    counts = small[4 + experts :, :: attn_gain.shape[0]].astype(f32)
+    count = jnp.sum(counts[0]) * 16.0 + jnp.sum(counts[1])
+
+    key_w, value_w = gather_pair(w_key, w_value, place)
+    query_w, out_w = gather_pair(w_query, w_out, place)
+    rank = rep.astype(jnp.int32)[None]
+    blocks = reps
 
     moved, moved_segments = tokens, segment_ids.reshape(local_rows)
     token_parts, segment_parts = [tokens], [moved_segments]
@@ -551,10 +1020,9 @@
         token_parts.insert(0, moved)
         segment_parts.insert(0, moved_segments)
     behind = reach * local_rows
-    inputs_all = jnp.concatenate(token_parts, 0).astype(f32)
+    tokens_all = jnp.concatenate(token_parts, 0)
     key_segments = jnp.concatenate(segment_parts, 0)
     inputs = tokens.astype(f32)
-    segments = segment_ids.reshape(local_rows)
 
     quarter_rows = w_gate.shape[1] // 4
     quarter_down = w_down.shape[1] // 4
@@ -566,64 +1034,50 @@
         [jnp.concatenate([quarter_gate, quarter_up], 1), quarter_down_w], 0
     )
 
-    scale_all = rms_scale(inputs_all)
-    normed_all = (inputs_all * scale_all * gain_attn).astype(bf16)
-    scale_attn = scale_all[behind:]
-    normed = normed_all[behind:]
-    key_lin = matmul(normed_all, weight_key)
-    value_all = matmul(normed_all, weight_value).astype(bf16)
-    query_lin = matmul(normed, weight_query)
-    scale_query = rms_scale(query_lin)
-    scale_key = rms_scale(key_lin)
     all_rows = local_rows + behind
+    normed, scale_all = norm_rows(rank, tokens_all, gain_attn, blocks)
+    key_lin, key_squares = project(normed, *key_w, f32)
+    value_all, _ = project(normed, *value_w, bf16)
+    query_lin, query_squares = project(normed, *query_w, f32, behind)
+    scale_key = lax.rsqrt(key_squares / width + norm_eps)
+    scale_query = lax.rsqrt(query_squares / width + norm_eps)
     key_positions = (shard - reach) * local_rows + jnp.arange(all_rows, dtype=jnp.int32)
-    positions = shard * local_rows + jnp.arange(local_rows, dtype=jnp.int32)
-    cosine_all, sine_all = rotary_tables(key_positions, HEAD_DIM)
-    cosine, sine = cosine_all[behind:], sine_all[behind:]
-    query_rows = rotate(
-        (query_lin * scale_query * gain_query).reshape(local_rows, HEADS, HEAD_DIM), cosine, sine
-    ).astype(bf16)
-    all_keys = rotate(
-        (key_lin * scale_key * gain_key).reshape(all_rows, HEADS, HEAD_DIM), cosine_all, sine_all
-    ).astype(bf16)
-    all_values = value_all.reshape(all_rows, HEADS, HEAD_DIM)
-    distance = positions[:, None] - key_positions[None, :]
-    allowed = (
-        (distance >= 0)
-        & (distance < WINDOW)
-        & (key_positions[None, :] >= 0)
-        & (segments[:, None] == key_segments[None, :])
-    )
-
-    def by_group(value):
-        return jnp.moveaxis(value.reshape(value.shape[0], HEADS // group, group, HEAD_DIM), 1, 0)
-
-    def from_group(value):
-        return jnp.moveaxis(value, 0, 1).reshape(value.shape[1], HEADS * HEAD_DIM)
-
-    def scores_of(query_group, key_group):
-        raw = (
-            jnp.einsum("qhd,khd->hqk", query_group, key_group, preferred_element_type=jnp.float32)
-            * score_scale
-        )
-        return jnp.where(allowed[None], raw, -1e30)
-
-    def attend_forward(item):
-        query_group, key_group, value_group = item
-        scores = scores_of(query_group, key_group)
-        peak = jnp.max(scores, axis=-1, keepdims=True)
-        shifted = jnp.exp(scores - peak)
-        total = jnp.sum(shifted, axis=-1, keepdims=True)
-        weights = (shifted / total).astype(jnp.bfloat16)
-        mixed = jnp.einsum("hqk,khd->qhd", weights, value_group, preferred_element_type=jnp.float32)
-        return (mixed, peak, total)
-
-    query_groups = by_group(query_rows)
-    key_groups = by_group(all_keys)
-    value_groups = by_group(all_values)
-    mixed, peaks, totals = lax.map(attend_forward, (query_groups, key_groups, value_groups))
-    mixed_rows = from_group(mixed).astype(bf16)
-    residual = inputs + matmul(mixed_rows, weight_out)
+    half_head = HEAD_DIM // 2
+    frequency = 10000.0 ** (-jnp.arange(half_head, dtype=f32) * 2.0 / HEAD_DIM)
+    angles = key_positions[:, None].astype(f32) * frequency[None, :]
+    cosine, sine = jnp.cos(angles), jnp.sin(angles)
+    cosine, sine = jnp.concatenate([cosine, cosine], 1), jnp.concatenate([-sine, sine], 1)
+
+    def mask_of(tile):
+        span = behind + tile
+        parts = []
+        for start in range(0, local_rows, tile):
+            keys = slice(start, start + span)
+            queries = slice(behind + start, behind + start + tile)
+            distance = key_positions[None, queries] - key_positions[keys, None]
+            allowed = (
+                (distance >= 0)
+                & (distance < WINDOW)
+                & (key_positions[keys, None] >= 0)
+                & (key_segments[None, queries] == key_segments[keys, None])
+            )
+            parts.append(jnp.where(allowed, 0.0, -1e30).astype(f32))
+        return jnp.stack(parts)
+
+    operands = (
+        query_lin,
+        key_lin,
+        value_all,
+        scale_query,
+        scale_key,
+        gain_query[None],
+        gain_key[None],
+        cosine,
+        sine,
+    )
+    mixed, lse = attend(rank, operands, mask_of(local_rows // 4))
+    branch, _ = project(mixed, *out_w, f32)
+    residual = inputs + branch
     scale_moe = rms_scale(residual)
     normed_moe = (residual * scale_moe * gain_moe).astype(bf16)
     partner_moe = across(normed_moe, 1)
@@ -717,86 +1171,64 @@
     residual_grad = result_grad + residual_part
     branch_grad = residual_grad.astype(bf16)
     half = width // 2
-    out_a = matmul(mixed_rows.T, branch_grad[:, :half]).astype(bf16)
-    out_b = matmul(mixed_rows.T, branch_grad[:, half:]).astype(bf16)
-    out_a, out_b = scatter_pair(out_a, out_b, place)
+    out_a, out_b = scatter_pair(
+        chip_sum(mixed, branch_grad[:, :half]), chip_sum(mixed, branch_grad[:, half:]), place
+    )
     out_out = jnp.concatenate([out_a, out_b], 1)
-    mixed_grad = (
-        matmul(branch_grad, weight_out.T).astype(bf16).reshape(local_rows, HEADS, HEAD_DIM)
-    )
-
-    def attend_backward(item):
-        query_group, key_group, value_group, grad_group, peak, total = item
-        scores = scores_of(query_group, key_group)
-        probs = jnp.exp(scores - peak) / total
-        weights = probs.astype(jnp.bfloat16)
-        value_part = jnp.einsum(
-            "hqk,qhd->khd", weights, grad_group, preferred_element_type=jnp.float32
-        )
-        probs_grad = jnp.einsum(
-            "qhd,khd->hqk", grad_group, value_group, preferred_element_type=jnp.float32
-        )
-        inner = jnp.sum(probs * probs_grad, axis=-1, keepdims=True)
-        score_grad = (probs * (probs_grad - inner)).astype(jnp.bfloat16)
-        query_part = (
-            jnp.einsum("hqk,khd->qhd", score_grad, key_group, preferred_element_type=jnp.float32)
-            * score_scale
-        )
-        key_part = (
-            jnp.einsum("hqk,qhd->khd", score_grad, query_group, preferred_element_type=jnp.float32)
-            * score_scale
-        )
-        return (query_part.astype(bf16), key_part.astype(bf16), value_part.astype(bf16))
-
-    query_parts, key_parts_grad, value_parts_grad = lax.map(
-        attend_backward,
-        (query_groups, key_groups, value_groups, by_group(mixed_grad), peaks, totals),
-    )
-    query_turned = rotate_back(
-        from_group(query_parts).astype(f32).reshape(local_rows, HEADS, HEAD_DIM), cosine, sine
-    ).reshape(local_rows, width)
-    key_turned = rotate_back(
-        from_group(key_parts_grad).astype(f32).reshape(all_rows, HEADS, HEAD_DIM),
-        cosine_all,
-        sine_all,
-    ).reshape(all_rows, width)
-    value_row_grad = from_group(value_parts_grad)
-    query_lin_grad, q_gain_local = norm_back(query_lin, scale_query, gain_query, query_turned)
-    key_lin_grad, k_gain_local = norm_back(key_lin, scale_key, gain_key, key_turned)
-    query_lin_grad = query_lin_grad.astype(bf16)
-    key_lin_grad = key_lin_grad.astype(bf16)
-    value_a = matmul(normed_all.T, value_row_grad[:, :half]).astype(bf16)
-    value_b = matmul(normed_all.T, value_row_grad[:, half:]).astype(bf16)
-    value_a, value_b = scatter_pair(value_a, value_b, place)
+    mixed_grad = jnp.stack([dot_t(branch_grad, weight).astype(bf16) for weight in out_w])
+    query_row_grad, key_row_grad, value_row_grad = attend_back(
+        rank, operands, mask_of(local_rows // 2), mixed_grad, lse
+    )
+    value_a, value_b = scatter_pair(
+        chip_sum(normed, value_row_grad[:, :half]),
+        chip_sum(normed, value_row_grad[:, half:]),
+        place,
+    )
     value_out = jnp.concatenate([value_a, value_b], 1)
-    query_local = matmul(normed.T, query_lin_grad).astype(bf16)
-    key_local = matmul(normed_all.T, key_lin_grad).astype(bf16)
-    query_out, key_out = scatter_pair(query_local, key_local, place)
-    normed_grad = matmul(key_lin_grad, weight_key.T) + matmul(value_row_grad, weight_value.T)
-    normed_grad_own = normed_grad[behind:] + matmul(query_lin_grad, weight_query.T)
-    attn_gain_local = jnp.sum(normed_grad * inputs_all * scale_all, axis=0) + jnp.sum(
-        (normed_grad_own - normed_grad[behind:]) * inputs * scale_attn, axis=0
-    )
-    carried = 0.0
+    query_lin_grad, q_gain_local = lin_back(
+        query_row_grad,
+        query_lin,
+        scale_query,
+        gain_query[None],
+        cosine[behind:],
+        sine[behind:],
+    )
+    key_lin_grad, k_gain_local = lin_back(
+        key_row_grad, key_lin, scale_key, gain_key[None], cosine, sine
+    )
+    query_out, key_out = scatter_pair(
+        chip_sum(normed[:, behind:], query_lin_grad), chip_sum(normed, key_lin_grad), place
+    )
+    normed_grad = project_back(
+        key_lin_grad, value_row_grad, query_lin_grad, key_w, value_w, query_w
+    )
+    carried = jnp.zeros((2, local_rows, width // 2), f32)
     for back in range(reach):
-        carried = carried + normed_grad[back * local_rows : (back + 1) * local_rows]
+        carried = carried + normed_grad[:, back * local_rows : (back + 1) * local_rows]
         carried = from_behind(carried.astype(bf16), "ep", -1).astype(f32)
-    normed_grad_own = normed_grad_own + carried
-    inputs_part, _ = norm_back(inputs, scale_attn, gain_attn, normed_grad_own)
-    tokens_grad = residual_grad + inputs_part
+    tokens_grad, attn_gain_local = tokens_back(
+        rank,
+        normed_grad,
+        carried.astype(bf16),
+        tokens,
+        residual_grad,
+        scale_all,
+        gain_attn,
+        blocks,
+    )
 
     packed = jnp.concatenate(
         [
             jnp.broadcast_to(squares, (1, width)),
-            attn_gain_local[None],
-            q_gain_local[None],
-            k_gain_local[None],
+            attn_gain_local,
+            q_gain_local,
+            k_gain_local,
             moe_gain_local[None],
             router_local.T,
         ],
         0,
     )
-    packed = lax.psum(packed, ("rep", "ep"))
+    packed = sum_small(packed, place)
     loss = packed[0, 0] / (2.0 * count * width)
     own_rows = attn_gain.shape[0]
     mine = lax.dynamic_slice_in_dim(packed, (rep * experts + shard) * own_rows, own_rows, 1)

time: 2030 us -> 1530 us (0.75)
  other arithmetic: 514 us -> 236 us
  Pallas kernels: 0 us -> 246 us
  matrix products: 452 us -> 227 us
  local copies, waits for them, and re-layouts: 324 us -> 100 us
  starting transfers between devices: 148 us -> 263 us
  blocking collectives: 111 us -> 0 us
    pallas_call x0 -> x11, Pallas kernels: none -> 246 us  [the longest x4 58.8 us: project(): kernel_call(project_kernel, grid=(rows // tile,), in_specs=[pl.BlockSpec(...]
    ppermute x6 -> x21, starting transfers between devices: 8.03 us -> 179 us  [along(): lax.ppermute(value, 'ep', [(place, (place + steps) % count) for place in...]
    dot_general x27 -> x13, matrix products: 303 us -> 140 us  [matmul(): return jnp.dot(left, right, preferred_element_type=jnp.float32)]
    ppermute x6 -> x21, waiting for transfers between devices: 0.02 us -> 116 us  [along(): lax.ppermute(value, 'ep', [(place, (place + steps) % count) for place in...]
    all_gather x1 -> x0, blocking collectives: 111 us -> none  [body(): small = lax.all_gather(small, ('rep', 'ep'), axis=0, tiled=True)]
    psum x1 -> x0, waiting for transfers between devices: 105 us -> none  [body(): packed = lax.psum(packed, ('rep', 'ep'))]
    select_n x26 -> x10, other arithmetic: 125 us -> 53.2 us  [in_order(): jnp.where(bit == 1, jnp.stack([other, own], axis), jnp.stack([own, other]...]
    all_to_all x3 -> x0, waiting for transfers between devices: 69.1 us -> none  [scatter_pair(): both = lax.all_to_all(both, 'ep', split_axis=1, concat_axis=1, tiled=True)]
  transfers between devices with their start and end apart: 69 -> 86, of which waited for: 19 -> 32; matrix products, arithmetic and copies ran while one was open for 59% -> 32% of each run, Pallas kernels for 0% -> 16%
where the time goes in v2:
time: 1530 us; the launch traced here: 1520 us
  waiting for transfers between devices  436 us (28%)
  starting transfers between devices  263 us (17%)
  Pallas kernels  246 us (16%)
  other arithmetic  236 us (15%)
  matrix products  227 us (15%)
  local copies, waits for them, and re-layouts  100 us (7%)
    ppermute x51, waiting for transfers between devices, across(): lax.ppermute(value, 'rep', [(place, place ^ bit) for place in range(count)])  261 us
    ppermute x21, starting transfers between devices, along(): lax.ppermute(value, 'ep', [(place, (place + steps) % count) for place in...  179 us
    dot_general x13, matrix products, matmul(): return jnp.dot(left, right, preferred_element_type=jnp.float32)  140 us
    ppermute x21, waiting for transfers between devices, along(): lax.ppermute(value, 'ep', [(place, (place + steps) % count) for place in...  116 us
    dot_general x12, matrix products, t_dot(): lax.dot_general(left, right, (((0,), (0,)), ((), ())), preferred_element_...  67.2 us
    pallas_call x4, Pallas kernels, project(): kernel_call(project_kernel, grid=(rows // tile,), in_specs=[pl.BlockSpec(...  58.8 us
    pallas_call x1, Pallas kernels, attend_back(): kernel_call(functools.partial(attend_back_kernel, behind=all_rows - rows,...  53.6 us
    select_n x10, other arithmetic, in_order(): jnp.where(bit == 1, jnp.stack([other, own], axis), jnp.stack([own, other]...  53.2 us
  transfers between devices with their start and end apart: 86, of which 32 were waited for; matrix products, arithmetic and copies ran while one was open for 32% of the time, Pallas kernels for 16%

profile of v2, /device:TPU:0, one launch (start us, length us, event | category | flops | bytes accessed | tf_op | source)
XLA Modules:
  0.0 1517.7 jit_solution(5983497221471629593)
XLA Ops:
  74.6 42.8 %collective-permute-done.15 = bf16[2,64,2048]{2,1,0:T(8,128)(2,1)S(1)} collective-permute-done((bf16[2,64,2048]{2,1,0:T(8,128)(2,1)}, bf16[2,64,2048]{2,1,0:T(8,128)(2,1)S(1)}, u32[]{:S(2)}, u32[]{:S(2)}) %collective-permute-start.15) | collective-permute-done | bytes 524320 | tf_op jit(solution)/shard_map/ppermute | solution.py:831
  117.4 37.0 %collective-permute-start.10 = (bf16[2,64,2048]{2,1,0:T(8,128)(2,1)}, bf16[2,64,2048]{2,1,0:T(8,128)(2,1)S(1)}, u32[]{:S(2)}, u32[]{:S(2)}) collective-permute-start(bf16[2,64,2048]{2,1,0:T(8,128)(2,1)} %pad_maximum_fusion.24), channel_id=1, source_target_pairs={{0,3},{1,0},{2,1},{3,2},{4,7},{5,4},{6,5},{7,6},{8,11},{9,8},{10,9... | collective-permute-start | bytes 1572872 | tf_op jit(solution)/shard_map/ppermute | solution.py:831
  195.8 31.8 %collective-permute-done.7 = bf16[2,2,4,10,64]{4,2,1,3,0:T(4,128)(2,1)S(1)} collective-permute-done((bf16[2,2,4,10,64]{4,2,1,3,0:T(4,128)(2,1)S(1)}, bf16[2,2,4,10,64]{4,2,1,3,0:T(4,128)(2,1)S(1)}, u32[]{:S(2)}, u32[]{:S(2)}) %collective-permute-start.7) | collective-permute-done | bytes 20512 | tf_op jit(solution)/shard_map/ppermute | solution.py:826
  240.7 16.4 %collective-permute-done.25 = bf16[256,2048]{1,0:T(8,128)(2,1)S(1)} collective-permute-done((bf16[256,2048]{1,0:T(8,128)(2,1)S(1)}, bf16[256,2048]{1,0:T(8,128)(2,1)S(1)}, u32[]{:S(2)}, u32[]{:S(2)}) %collective-permute-start.25) | collective-permute-done | bytes 1048608 | tf_op jit(solution)/shard_map/ppermute | solution.py:826
  264.9 35.6 %collective-permute-done.35 = bf16[768,2048]{1,0:T(8,128)(2,1)S(1)} collective-permute-done((bf16[768,2048]{1,0:T(8,128)(2,1)S(1)}, bf16[768,2048]{1,0:T(8,128)(2,1)S(1)}, u32[]{:S(2)}, u32[]{:S(2)}) %collective-permute-start.35) | collective-permute-done | bytes 3145760 | tf_op jit(solution)/shard_map/ppermute | solution.py:842
  303.3 17.4 %collective-permute-start.22 = (bf16[1024,2048]{1,0:T(8,128)(2,1)}, bf16[1024,2048]{1,0:T(8,128)(2,1)}, u32[]{:S(2)}, u32[]{:S(2)}) collective-permute-start(bf16[1024,2048]{1,0:T(8,128)(2,1)} %pad_maximum_fusion.5.a_ref.va), channel_id=1, source_target_pairs={{0,4},{4,0},{8,12},{12,8},{16,20},{20,16},{24,28},{28,24},{1,5},{5... | collective-permute-start | bytes 12582920 | tf_op jit(solution)/shard_map/ppermute | solution.py:826
  355.0 19.6 %shard_map.282 = (f32[1536,2048]{1,0:T(8,128)}, f32[1536,1]{1,0:T(8,128)}) custom-call(bf16[2,1536,1024]{2,1,0:T(8,128)(2,1)} %get-tuple-element.34.low_ref.high_ref, bf16[2,1536,1024]{2,1,0:T(8,128)(2,1)} %get-tuple-element.34.low_ref.high_ref, bf16[1024,2048]{1,0:T(8,128)(2,1)} %pad_maximum_fusion.4.a_ref.ka, ...), custom_call_target="tpu_custom_call" | custom-call | flops 12884901888 | bytes 16777216 | tf_op jit(solution)/shard_map/pallas_call | solution.py:472
  374.7 23.6 %collective-permute-done.36 = bf16[768,2048]{1,0:T(8,128)(2,1)} collective-permute-done((bf16[768,2048]{1,0:T(8,128)(2,1)}, bf16[768,2048]{1,0:T(8,128)(2,1)}, u32[]{:S(2)}, u32[]{:S(2)}) %collective-permute-start.36) | collective-permute-done | bytes 3145760 | tf_op jit(solution)/shard_map/ppermute | solution.py:826
  407.8 19.4 %shard_map.283 = (bf16[1536,2048]{1,0:T(8,128)(2,1)}, f32[1536,1]{1,0:T(8,128)}) custom-call(bf16[2,1536,1024]{2,1,0:T(8,128)(2,1)} %get-tuple-element.34.low_ref.high_ref, bf16[2,1536,1024]{2,1,0:T(8,128)(2,1)} %get-tuple-element.34.low_ref.high_ref, bf16[1024,2048]{1,0:T(8,128)(2,1)} %pad_maximum_fusion.5.a_ref.va, ...), custom_call_target="tpu_custom_call" | custom-call | flops 12884901888 | bytes 16777216 | tf_op jit(solution)/shard_map/pallas_call | solution.py:472
  448.6 35.8 %shard_map.284 = (bf16[2,512,1024]{2,1,0:T(8,128)(2,1)}, f32[16,1,512]{2,1,0:T(1,128)}) custom-call(s32[1]{0:T(128)} %bitcast.rank, f32[512,2048]{1,0:T(8,128)} %get-tuple-element.35.q_ref.lin_ref, f32[1536,2048]{1,0:T(8,128)} %get-tuple-element.36.k_ref.lin_ref, bf16[1536,2048]{1,0:T(8,128)(2,1)} %get-tuple-element.37.v_ref, ...), custom_call_target="tpu_custom_call" | custom-call | flops 4831838208 | bytes 25165824 | tf_op jit(solution)/shard_map/pallas_call | solution.py:669
  517.2 28.3 %collective-permute-done.37 = bf16[2,768,2048]{2,1,0:T(8,128)(2,1)} collective-permute-done((bf16[2,768,2048]{2,1,0:T(8,128)(2,1)}, bf16[2,768,2048]{2,1,0:T(8,128)(2,1)}, u32[]{:S(2)}, u32[]{:S(2)}) %collective-permute-start.37) | collective-permute-done | bytes 6291488 | tf_op jit(solution)/shard_map/ppermute | solution.py:826
  593.4 14.3 fusion.179
  679.5 13.8 multiply_convert_fusion.5
  693.3 14.7 fusion.46
  828.5 53.6 %shard_map.286 = (bf16[512,2048]{1,0:T(8,128)(2,1)}, bf16[1536,2048]{1,0:T(8,128)(2,1)}, bf16[1536,2048]{1,0:T(8,128)(2,1)}) custom-call(s32[1]{0:T(128)} %bitcast.rank, f32[512,2048]{1,0:T(8,128)} %get-tuple-element.35.q_ref.lin_ref, f32[1536,2048]{1,0:T(8,128)} %get-tuple-element.36.k_ref.lin_ref, bf16[1536,2048]{1,0:T(8,128)(2,1)} %get-tuple-element.37.v_ref, ...), custom_call_target="tpu_custom_call" | custom-call | flops 13421772800 | bytes 37748736 | tf_op jit(solution)/shard_map/pallas_call | solution.py:745
  891.4 21.6 %shard_map.287 = (bf16[1536,2048]{1,0:T(8,128)(2,1)}, f32[1,2048]{1,0:T(1,128)}) custom-call(bf16[1536,2048]{1,0:T(8,128)(2,1)} %get-tuple-element.43.g_ref, f32[1536,2048]{1,0:T(8,128)} %get-tuple-element.36.k_ref.lin_ref, f32[1536,1]{1,0:T(8,128)} %add_rsqrt_fusion.sk_ref.scale_ref, f32[1,2048]{1,0:T(1,128)} %reshape.1333.gk_ref.gain_ref, ...), custom_call_target="tpu_custom_call" | custom-call | flops 31457280 | bytes 25165824 | tf_op jit(solution)/shard_map/pallas_call | solution.py:809
  928.5 50.8 %shard_map.289.g_ref = f32[2,1536,1024]{2,1,0:T(8,128)} custom-call(bf16[1536,2048]{1,0:T(8,128)(2,1)} %get-tuple-element.44.k_ref, bf16[1536,2048]{1,0:T(8,128)(2,1)} %get-tuple-element.45.v_ref, bf16[512,2048]{1,0:T(8,128)(2,1)} %get-tuple-element.47.q_ref, bf16[1024,2048]{1,0:T(8,128)(2,1)} %pad_maximum_fusion.4.a_ref.ka, ...), custom_call_target="tpu_custom_call" | custom-call | flops 28991029248 | bytes 67108864 | tf_op jit(solution)/shard_map/pallas_call | solution.py:525
  1031.3 31.2 %collective-permute-done.80 = bf16[768,2048]{1,0:T(8,128)(2,1)} collective-permute-done((bf16[768,2048]{1,0:T(8,128)(2,1)S(1)}, bf16[768,2048]{1,0:T(8,128)(2,1)}, u32[]{:S(2)}, u32[]{:S(2)}) %collective-permute-start.80) | collective-permute-done | bytes 3145760 | tf_op jit(solution)/shard_map/ppermute | solution.py:826
  1115.3 14.9 collective-permute-done.60
  1167.3 26.0 %collective-permute-start.76 = (bf16[2,64,1024]{2,1,0:T(8,128)(2,1)S(1)}, bf16[2,64,1024]{2,1,0:T(8,128)(2,1)S(1)}, u32[]{:S(2)}, u32[]{:S(2)}) collective-permute-start(bf16[2,64,1024]{2,1,0:T(8,128)(2,1)S(1)} %get-tuple-element.96), channel_id=1, source_target_pairs={{0,3},{1,0},{2,1},{3,2},{4,7},{5,4},{6,5},{7,6},{8,11},{9,8},{10,9... | collective-permute-start | bytes 786440 | tf_op jit(solution)/shard_map/ppermute | solution.py:831
  1197.4 91.7 %collective-permute-start.74 = (bf16[2,64,1024]{2,1,0:T(8,128)(2,1)S(1)}, bf16[2,64,1024]{2,1,0:T(8,128)(2,1)S(1)}, u32[]{:S(2)}, u32[]{:S(2)}) collective-permute-start(bf16[2,64,1024]{2,1,0:T(8,128)(2,1)S(1)} %get-tuple-element.94), channel_id=1, source_target_pairs={{0,1},{1,2},{2,3},{3,0},{4,5},{5,6},{6,7},{7,4},{8,9},{9,10},{10,1... | collective-permute-start | bytes 786440 | tf_op jit(solution)/shard_map/ppermute | solution.py:831
  1325.0 23.0 %collective-permute-done.43.c_ref = bf16[2,512,1024]{2,1,0:T(8,128)(2,1)S(1)} collective-permute-done((bf16[2,512,1024]{2,1,0:T(8,128)(2,1)S(1)}, bf16[2,512,1024]{2,1,0:T(8,128)(2,1)S(1)}, u32[]{:S(2)}, u32[]{:S(2)}) %collective-permute-start.43) | collective-permute-done | bytes 2097184 | tf_op jit(solution)/shard_map/ppermute | solution.py:24
  1390.7 32.8 %collective-permute-done.46 = f32[9,2048]{1,0:T(8,128)S(1)} collective-permute-done((f32[9,2048]{1,0:T(8,128)S(1)}, f32[9,2048]{1,0:T(8,128)S(1)}, u32[]{:S(2)}, u32[]{:S(2)}) %collective-permute-start.46) | collective-permute-done | bytes 73760 | tf_op jit(solution)/shard_map/ppermute | solution.py:826
  1480.6 29.6 %collective-permute-done.57 = bf16[2,64,2048]{2,1,0:T(8,128)(2,1)} collective-permute-done((bf16[2,64,2048]{2,1,0:T(8,128)(2,1)}, bf16[2,64,2048]{2,1,0:T(8,128)(2,1)}, u32[]{:S(2)}, u32[]{:S(2)}) %collective-permute-start.57) | collective-permute-done | bytes 524320 | tf_op jit(solution)/shard_map/ppermute | solution.py:831
  (623 shorter events, 782.9 us)
Async XLA Ops:
  15.1 144.1 %collective-permute-start.8 = (bf16[2,64,2048]{2,1,0:T(8,128)(2,1)}, bf16[2,64,2048]{2,1,0:T(8,128)(2,1)}, u32[]{:S(2)}, u32[]{:S(2)}) collective-permute-start(bf16[2,64,2048]{2,1,0:T(8,128)(2,1)} %pad_maximum_fusion.24), channel_id=1, source_target_pairs={{0,1},{1,2},{2,3},{3,0},{4,5},{5,6},{6,7},{7,4},{8,9},{9,10},{10,1... | collective-permute-start | bytes 1572872 | tf_op jit(solution)/shard_map/ppermute | solution.py:831
  42.5 120.1 %collective-permute-start.9 = (bf16[2,64,2048]{2,1,0:T(8,128)(2,1)}, bf16[2,64,2048]{2,1,0:T(8,128)(2,1)}, u32[]{:S(2)}, u32[]{:S(2)}) collective-permute-start(bf16[2,64,2048]{2,1,0:T(8,128)(2,1)} %pad_maximum_fusion.24), channel_id=1, source_target_pairs={{0,2},{1,3},{2,0},{3,1},{4,6},{5,7},{6,4},{7,5},{8,10},{9,11},{10,... | collective-permute-start | bytes 1572872 | tf_op jit(solution)/shard_map/ppermute | solution.py:831
  46.0 113.7 %collective-permute-start.30 = (bf16[768,2048]{1,0:T(8,128)(2,1)}, bf16[768,2048]{1,0:T(8,128)(2,1)}, u32[]{:S(2)}, u32[]{:S(2)}) collective-permute-start(bf16[768,2048]{1,0:T(8,128)(2,1)} %pad_maximum_fusion.10), channel_id=1, source_target_pairs={{0,1},{1,2},{7,6},{6,5},{8,9},{9,10},{15,14},{14,13},{16,17},{17,1... | collective-permute-start | bytes 9437192 | tf_op jit(solution)/shard_map/ppermute | solution.py:842
  72.7 82.5 %collective-permute-start.16 = (bf16[2,64,2048]{2,1,0:T(8,128)(2,1)}, bf16[2,64,2048]{2,1,0:T(8,128)(2,1)S(1)}, u32[]{:S(2)}, u32[]{:S(2)}) collective-permute-start(bf16[2,64,2048]{2,1,0:T(8,128)(2,1)} %pad_maximum_fusion.25), channel_id=1, source_target_pairs={{0,3},{1,0},{2,1},{3,2},{4,7},{5,4},{6,5},{7,6},{8,11},{9,8},{10,9... | collective-permute-start | bytes 1572872 | tf_op jit(solution)/shard_map/ppermute | solution.py:831
  258.6 96.1 %collective-permute-start.19 = (bf16[1024,2048]{1,0:T(8,128)(2,1)}, bf16[1024,2048]{1,0:T(8,128)(2,1)}, u32[]{:S(2)}, u32[]{:S(2)}) collective-permute-start(bf16[1024,2048]{1,0:T(8,128)(2,1)} %pad_maximum_fusion.4.a_ref.ka), channel_id=1, source_target_pairs={{0,4},{4,0},{8,12},{12,8},{16,20},{20,16},{24,28},{28,24},{1,5},{5... | collective-permute-start | bytes 12582920 | tf_op jit(solution)/shard_map/ppermute | solution.py:826
  303.3 104.4 %collective-permute-start.22 = (bf16[1024,2048]{1,0:T(8,128)(2,1)}, bf16[1024,2048]{1,0:T(8,128)(2,1)}, u32[]{:S(2)}, u32[]{:S(2)}) collective-permute-start(bf16[1024,2048]{1,0:T(8,128)(2,1)} %pad_maximum_fusion.5.a_ref.va), channel_id=1, source_target_pairs={{0,4},{4,0},{8,12},{12,8},{16,20},{20,16},{24,28},{28,24},{1,5},{5... | collective-permute-start | bytes 12582920 | tf_op jit(solution)/shard_map/ppermute | solution.py:826
  335.4 100.6 %collective-permute-start.13 = (bf16[1024,2048]{1,0:T(8,128)(2,1)}, bf16[1024,2048]{1,0:T(8,128)(2,1)}, u32[]{:S(2)}, u32[]{:S(2)}) collective-permute-start(bf16[1024,2048]{1,0:T(8,128)(2,1)} %pad_maximum_fusion.3.a_ref.qa), channel_id=1, source_target_pairs={{0,4},{4,0},{8,12},{12,8},{16,20},{20,16},{24,28},{28,24},{1,5},{5... | collective-permute-start | bytes 12582920 | tf_op jit(solution)/shard_map/ppermute | solution.py:826
  340.3 86.9 %collective-permute-start.33 = (bf16[768,2048]{1,0:T(8,128)(2,1)S(1)}, bf16[768,2048]{1,0:T(8,128)(2,1)}, u32[]{:S(2)}, u32[]{:S(2)}) collective-permute-start(bf16[768,2048]{1,0:T(8,128)(2,1)S(1)} %get-tuple-element.72), channel_id=1, source_target_pairs={{0,8},{4,12},{8,0},{12,4},{16,24},{20,28},{24,16},{28,20},{1,9},{5... | collective-permute-start | bytes 9437192 | tf_op jit(solution)/shard_map/ppermute | solution.py:826
  354.7 129.7 %collective-permute-start.27 = (bf16[1024,2048]{1,0:T(8,128)(2,1)}, bf16[1024,2048]{1,0:T(8,128)(2,1)}, u32[]{:S(2)}, u32[]{:S(2)}) collective-permute-start(bf16[1024,2048]{1,0:T(8,128)(2,1)} %pad_maximum_fusion.6.a_ref), channel_id=1, source_target_pairs={{0,4},{4,0},{8,12},{12,8},{16,20},{20,16},{24,28},{28,24},{1,5},{5... | collective-permute-start | bytes 12582920 | tf_op jit(solution)/shard_map/ppermute | solution.py:826
  407.5 138.1 %collective-permute-start.37 = (bf16[2,768,2048]{2,1,0:T(8,128)(2,1)}, bf16[2,768,2048]{2,1,0:T(8,128)(2,1)}, u32[]{:S(2)}, u32[]{:S(2)}) collective-permute-start(bf16[2,768,2048]{2,1,0:T(8,128)(2,1)} %maximum_select_fusion.4), channel_id=1, source_target_pairs={{0,8},{4,12},{8,0},{12,4},{16,24},{20,28},{24,16},{28,20},{1,9},{5... | collective-permute-start | bytes 18874376 | tf_op jit(solution)/shard_map/ppermute | solution.py:826
  434.5 136.6 %collective-permute-start.34 = (bf16[2,768,2048]{2,1,0:T(8,128)(2,1)}, bf16[2,768,2048]{2,1,0:T(8,128)(2,1)}, u32[]{:S(2)}, u32[]{:S(2)}) collective-permute-start(bf16[2,768,2048]{2,1,0:T(8,128)(2,1)} %maximum_select_fusion.2), channel_id=1, source_target_pairs={{0,16},{4,20},{8,24},{12,28},{16,0},{20,4},{24,8},{28,12},{1,17},{... | collective-permute-start | bytes 18874376 | tf_op jit(solution)/shard_map/ppermute | solution.py:826
  502.2 91.2 %collective-permute-start.29 = (bf16[512,2048]{1,0:T(8,128)(2,1)}, bf16[512,2048]{1,0:T(8,128)(2,1)}, u32[]{:S(2)}, u32[]{:S(2)}) collective-permute-start(bf16[512,2048]{1,0:T(8,128)(2,1)} %multiply_convert_fusion.8), channel_id=1, source_target_pairs={{0,4},{4,0},{8,12},{12,8},{16,20},{20,16},{24,28},{28,24},{1,5},{5... | collective-permute-start | bytes 6291464 | tf_op jit(solution)/shard_map/ppermute | solution.py:826
  679.0 122.3 %collective-permute-start.41 = (f32[512,2]{0,1:T(2,128)S(1)}, f32[512,2]{0,1:T(2,128)S(1)}, u32[]{:S(2)}, u32[]{:S(2)}) collective-permute-start(f32[512,2]{0,1:T(2,128)S(1)} %pad_maximum_fusion.30), channel_id=1, source_target_pairs={{0,4},{4,0},{8,12},{12,8},{16,20},{20,16},{24,28},{28,24},{1,5},{5... | collective-permute-start | bytes 12296 | tf_op jit(solution)/shard_map/ppermute | solution.py:826
  768.9 210.5 %collective-permute-start.79 = (bf16[2,768,2048]{2,1,0:T(8,128)(2,1)}, bf16[2,768,2048]{2,1,0:T(8,128)(2,1)}, u32[]{:S(2)}, u32[]{:S(2)}) collective-permute-start(bf16[2,768,2048]{2,1,0:T(8,128)(2,1)} %fusion.6), channel_id=1, source_target_pairs={{0,16},{4,20},{8,24},{12,28},{16,0},{20,4},{24,8},{28,12},{1,17},{... | collective-permute-start | bytes 18874376 | tf_op jit(solution)/shard_map/ppermute | solution.py:826
  799.6 193.4 %collective-permute-start.77 = (bf16[2,768,2048]{2,1,0:T(8,128)(2,1)}, bf16[2,768,2048]{2,1,0:T(8,128)(2,1)}, u32[]{:S(2)}, u32[]{:S(2)}) collective-permute-start(bf16[2,768,2048]{2,1,0:T(8,128)(2,1)} %fusion.10), channel_id=1, source_target_pairs={{0,8},{4,12},{8,0},{12,4},{16,24},{20,28},{24,16},{28,20},{1,9},{5... | collective-permute-start | bytes 18874376 | tf_op jit(solution)/shard_map/ppermute | solution.py:826
  815.9 210.5 %collective-permute-start.68 = (bf16[1024,1024]{1,0:T(8,128)(2,1)}, bf16[1024,1024]{1,0:T(8,128)(2,1)}, u32[]{:S(2)}, u32[]{:S(2)}) collective-permute-start(bf16[1024,1024]{1,0:T(8,128)(2,1)} %convolution_convert_fusion.9), channel_id=1, source_target_pairs={{0,4},{4,0},{8,12},{12,8},{16,20},{20,16},{24,28},{28,24},{1,5},{5... | collective-permute-start | bytes 6291464 | tf_op jit(solution)/shard_map/ppermute | solution.py:826
  1015.8 151.5 %collective-permute-start.42 = (bf16[2,512,1024]{2,1,0:T(8,128)(2,1)}, bf16[2,512,1024]{2,1,0:T(8,128)(2,1)}, u32[]{:S(2)}, u32[]{:S(2)}) collective-permute-start(bf16[2,512,1024]{2,1,0:T(8,128)(2,1)} %slice.824), channel_id=1, source_target_pairs={{1,0},{2,1},{3,2},{5,4},{6,5},{7,6},{9,8},{10,9},{11,10},{13,12},{... | collective-permute-start | bytes 6291464 | tf_op jit(solution)/shard_map/ppermute | solution.py:24
  1080.7 78.4 %collective-permute-start.81 = (bf16[2,768,2048]{2,1,0:T(8,128)(2,1)}, bf16[2,768,2048]{2,1,0:T(8,128)(2,1)S(1)}, u32[]{:S(2)}, u32[]{:S(2)}) collective-permute-start(bf16[2,768,2048]{2,1,0:T(8,128)(2,1)} %pad_maximum_fusion.2), channel_id=1, source_target_pairs={{3,2},{4,5},{11,10},{12,13},{19,18},{20,21},{27,26},{28,29}} | collective-permute-start | bytes 18874376 | tf_op jit(solution)/shard_map/ppermute | solution.py:842
  1114.8 200.4 %collective-permute-start.50 = (bf16[1024,2048]{1,0:T(8,128)(2,1)}, bf16[1024,2048]{1,0:T(8,128)(2,1)}, u32[]{:S(2)}, u32[]{:S(2)}) collective-permute-start(bf16[1024,2048]{1,0:T(8,128)(2,1)} %convolution_convert_fusion.3), channel_id=1, source_target_pairs={{0,4},{4,0},{8,12},{12,8},{16,20},{20,16},{24,28},{28,24},{1,5},{5... | collective-permute-start | bytes 12582920 | tf_op jit(solution)/shard_map/ppermute | solution.py:826
  1147.4 212.2 %collective-permute-start.53 = (bf16[1024,2048]{1,0:T(8,128)(2,1)}, bf16[1024,2048]{1,0:T(8,128)(2,1)}, u32[]{:S(2)}, u32[]{:S(2)}) collective-permute-start(bf16[1024,2048]{1,0:T(8,128)(2,1)} %convolution_convert_fusion.2), channel_id=1, source_target_pairs={{0,4},{4,0},{8,12},{12,8},{16,20},{20,16},{24,28},{28,24},{1,5},{5... | collective-permute-start | bytes 12582920 | tf_op jit(solution)/shard_map/ppermute | solution.py:826
  1163.9 217.9 %collective-permute-start.82 = (bf16[2,768,2048]{2,1,0:T(8,128)(2,1)}, bf16[2,768,2048]{2,1,0:T(8,128)(2,1)}, u32[]{:S(2)}, u32[]{:S(2)}) collective-permute-start(bf16[2,768,2048]{2,1,0:T(8,128)(2,1)} %add_convert_fusion), channel_id=1, source_target_pairs={{2,1},{5,6},{10,9},{13,14},{18,17},{21,22},{26,25},{29,30}} | collective-permute-start | bytes 18874376 | tf_op jit(solution)/shard_map/ppermute | solution.py:842
  1193.4 98.7 %collective-permute-start.75 = (bf16[2,64,1024]{2,1,0:T(8,128)(2,1)S(1)}, bf16[2,64,1024]{2,1,0:T(8,128)(2,1)S(1)}, u32[]{:S(2)}, u32[]{:S(2)}) collective-permute-start(bf16[2,64,1024]{2,1,0:T(8,128)(2,1)S(1)} %get-tuple-element.95), channel_id=1, source_target_pairs={{0,2},{1,3},{2,0},{3,1},{4,6},{5,7},{6,4},{7,5},{8,10},{9,11},{10,... | collective-permute-start | bytes 786440 | tf_op jit(solution)/shard_map/ppermute | solution.py:831
  1197.4 97.9 %collective-permute-start.74 = (bf16[2,64,1024]{2,1,0:T(8,128)(2,1)S(1)}, bf16[2,64,1024]{2,1,0:T(8,128)(2,1)S(1)}, u32[]{:S(2)}, u32[]{:S(2)}) collective-permute-start(bf16[2,64,1024]{2,1,0:T(8,128)(2,1)S(1)} %get-tuple-element.94), channel_id=1, source_target_pairs={{0,1},{1,2},{2,3},{3,0},{4,5},{5,6},{6,7},{7,4},{8,9},{9,10},{10,1... | collective-permute-start | bytes 786440 | tf_op jit(solution)/shard_map/ppermute | solution.py:831
  1323.3 109.1 %collective-permute-start.51 = (bf16[2,256,2048]{2,1,0:T(8,128)(2,1)}, bf16[2,256,2048]{2,1,0:T(8,128)(2,1)}, u32[]{:S(2)}, u32[]{:S(2)}) collective-permute-start(bf16[2,256,2048]{2,1,0:T(8,128)(2,1)} %slice_bitcast_fusion.2), channel_id=1, source_target_pairs={{0,8},{4,12},{8,0},{12,4},{16,24},{20,28},{24,16},{28,20},{1,9},{5... | collective-permute-start | bytes 6291464 | tf_op jit(solution)/shard_map/ppermute | solution.py:826
  (180 other events, 6140.3 us)

commit v3 on v2

--- a/solution.py
+++ b/solution.py
@@ -416,24 +416,25 @@
     return code % 2 * (blocks // 2) + code // 2
 
 
-def norm_kernel(rank, x_ref, gain_ref, o_ref, scale_ref, *, blocks):
+def norm_kernel(rank, x_ref, gain_ref, o_ref, scale_ref, *, codes):
     value = x_ref[...].astype(jnp.float32)
     scale = lax.rsqrt(jnp.mean(value * value, axis=1, keepdims=True) + norm_eps)
     scale_ref[...] = scale
-    block = x_ref.shape[1] // blocks
-    for place in range(blocks):
-        start = pl.multiple_of((rank[0] ^ code_of(place, blocks)) * block, block)
+    half = len(codes) // 2
+    block = x_ref.shape[1] // len(codes)
+    for place, code in enumerate(codes):
+        start = pl.multiple_of((rank[0] ^ code) * block, block)
         piece = x_ref[:, pl.ds(start, block)].astype(jnp.float32)
         piece = piece * scale * gain_ref[:, pl.ds(start, block)]
-        at = place % (blocks // 2) * block
-        o_ref[place // (blocks // 2), :, at : at + block] = piece.astype(jnp.bfloat16)
-
-
-def norm_rows(rank, value, gain, blocks):
+        at = place % half * block
+        o_ref[place // half, :, at : at + block] = piece.astype(jnp.bfloat16)
+
+
+def norm_rows(rank, value, gain, codes):
     rows, width = value.shape
     tile = 256
     return kernel_call(
-        functools.partial(norm_kernel, blocks=blocks),
+        functools.partial(norm_kernel, codes=codes),
         grid_spec=pltpu.PrefetchScalarGridSpec(
             num_scalar_prefetch=1,
             grid=(rows // tile,),
@@ -492,13 +493,14 @@
     )(halves, halves, a, b)
 
 
-def project_back_kernel(k_ref, v_ref, q_ref, ka, kb, va, vb, qa, qb, o_ref, *, own):
+def project_back_kernel(k_ref, v_ref, w_ref, q_ref, ka, kb, va, vb, qa, qb, o_ref, *, own):
     i, j = pl.program_id(0), pl.program_id(1)
     half = pl.num_programs(1) // 2
 
     def part(key, value, query):
-        total = dot_t(k_ref[...], key[...]) + dot_t(v_ref[...], value[...])
-        o_ref[0] = total
+        half_width = v_ref.shape[1]
+        total = dot_t(k_ref[...], key[...]) + dot_t(v_ref[...], value[:, :half_width])
+        o_ref[0] = total + dot_t(w_ref[...], value[:, half_width:])
 
         @pl.when(i >= own)
         def _():
@@ -513,13 +515,14 @@
         part(kb, vb, qb)
 
 
-def project_back(key, value, query, key_w, value_w, query_w):
+def project_back(key, value, value_high, query, key_w, value_w, query_w):
     rows, width = key.shape
     depth = key_w[0].shape[0]
     tile, step = 512, 512
     half = depth // step
     own = (rows - query.shape[0]) // tile
     x_spec = pl.BlockSpec((tile, width), lambda i, j: (i, 0))
+    half_spec = pl.BlockSpec((tile, width // 2), lambda i, j: (i, 0))
     low = pl.BlockSpec((step, width), lambda i, j: (jnp.minimum(j, half - 1), 0))
     high = pl.BlockSpec((step, width), lambda i, j: (jnp.maximum(j - half, 0), 0))
     return kernel_call(
@@ -527,7 +530,8 @@
         grid=(rows // tile, 2 * half),
         in_specs=[
             x_spec,
-            x_spec,
+            half_spec,
+            half_spec,
             pl.BlockSpec((tile, width), lambda i, j: (jnp.maximum(i - own, 0), 0)),
         ]
         + [low, high] * 3,
@@ -536,7 +540,7 @@
         cost_estimate=pl.CostEstimate(
             flops=9 * rows * depth * width, bytes_accessed=32 * depth * width, transcendentals=0
         ),
-    )(key, value, query, *key_w, *value_w, *query_w)
+    )(key, value, value_high, query, *key_w, *value_w, *query_w)
 
 
 def tokens_back_kernel(
@@ -609,8 +613,8 @@
     return place // (HEADS // 2), 0, place % (HEADS // 2)
 
 
-def attention_specs(rows, all_rows, bias):
-    head = lambda h, rank: (0, h)
+def attention_specs(rows, all_rows, bias, first=0):
+    head = lambda h, rank: (0, h + first)
     fixed = lambda h, rank: (0, 0)
     return [
         pl.BlockSpec((rows, HEAD_DIM), head),
@@ -737,8 +741,9 @@
     dv_ref[...] = value_total[...].astype(jnp.bfloat16)
 
 
-def attend_back(rank, operands, bias, grad, lse):
+def attend_back(rank, operands, bias, grad, lse, first):
     rows, width = operands[0].shape
+    width = width // 2
     all_rows = operands[1].shape[0]
     tiles, span, tile = bias.shape
     head = lambda h, rank: (0, h)
@@ -746,11 +751,11 @@
         functools.partial(attend_back_kernel, behind=all_rows - rows, tile=tile, span=span),
         grid_spec=pltpu.PrefetchScalarGridSpec(
             num_scalar_prefetch=1,
-            grid=(HEADS,),
-            in_specs=attention_specs(rows, all_rows, bias)
+            grid=(HEADS // 2,),
+            in_specs=attention_specs(rows, all_rows, bias, first)
             + [
-                pl.BlockSpec((1, rows, HEAD_DIM), moved_head),
-                pl.BlockSpec((1, 1, rows), lambda h, rank: (h, 0, 0)),
+                pl.BlockSpec((1, rows, HEAD_DIM), lambda h, rank: moved_head(h + first, rank)),
+                pl.BlockSpec((1, 1, rows), lambda h, rank: (h + first, 0, 0)),
             ],
             out_specs=[
                 pl.BlockSpec((rows, HEAD_DIM), head),
@@ -770,12 +775,12 @@
         cost_estimate=pl.CostEstimate(
             flops=10 * rows * span * width,
             bytes_accessed=12 * all_rows * width,
-            transcendentals=rows * span * HEADS,
+            transcendentals=rows * span * HEADS // 2,
         ),
     )(rank, *operands, bias, grad, lse)
 
 
-def lin_back_kernel(g_ref, lin_ref, scale_ref, gain_ref, cos_ref, sin_ref, o_ref, gain_grad_ref):
+def lin_back_kernel(low_ref, high_ref, lin_ref, scale_ref, gain_ref, cos_ref, sin_ref, o_ref, gain_grad_ref):
     scale = scale_ref[...]
     cosine, sine = cos_ref[...], -sin_ref[...]
     inner = jnp.zeros_like(scale)
@@ -784,10 +789,13 @@
     def _():
         gain_grad_ref[...] = jnp.zeros_like(gain_grad_ref)
 
-    turned = []
+    def grad_of(h):
+        ref = low_ref if h < HEADS // 2 else high_ref
+        return ref[:, h % (HEADS // 2) * HEAD_DIM : (h % (HEADS // 2) + 1) * HEAD_DIM]
+
     for h in range(HEADS):
         at = slice(h * HEAD_DIM, (h + 1) * HEAD_DIM)
-        grad = turn(g_ref[:, at].astype(jnp.float32), cosine, sine)
+        grad = turn(grad_of(h).astype(jnp.float32), cosine, sine)
         lin = lin_ref[:, at]
         product = grad * lin
         gain_grad_ref[:, at] += jnp.sum(product * scale, axis=0, keepdims=True)
@@ -795,21 +803,22 @@
     inner = inner * (1.0 / (HEADS * HEAD_DIM)) * (scale * scale * scale)
     for h in range(HEADS):
         at = slice(h * HEAD_DIM, (h + 1) * HEAD_DIM)
-        grad = turn(g_ref[:, at].astype(jnp.float32), cosine, sine)
+        grad = turn(grad_of(h).astype(jnp.float32), cosine, sine)
         value = scale * (grad * gain_ref[:, at]) - lin_ref[:, at] * inner
         o_ref[:, at] = value.astype(jnp.bfloat16)
 
 
-def lin_back(grad, lin, scale, gain, cosine, sine):
+def lin_back(low, high, lin, scale, gain, cosine, sine):
     rows, width = lin.shape
     tile = 256
     wide = pl.BlockSpec((tile, width), lambda i: (i, 0))
     one = pl.BlockSpec((1, width), lambda i: (0, 0))
+    half = pl.BlockSpec((tile, width // 2), lambda i: (i, 0))
     table = pl.BlockSpec((tile, HEAD_DIM), lambda i: (i, 0))
     return kernel_call(
         lin_back_kernel,
         grid=(rows // tile,),
-        in_specs=[wide, wide, pl.BlockSpec((tile, 1), lambda i: (i, 0)), one, table, table],
+        in_specs=[half, half, wide, pl.BlockSpec((tile, 1), lambda i: (i, 0)), one, table, table],
         out_specs=[wide, one],
         out_shape=[
             jax.ShapeDtypeStruct((rows, width), jnp.bfloat16),
@@ -818,7 +827,239 @@
         cost_estimate=pl.CostEstimate(
             flops=10 * rows * width, bytes_accessed=8 * rows * width, transcendentals=0
         ),
-    )(grad, lin, scale, gain, cosine, sine)
+    )(low, high, lin, scale, gain, cosine, sine)
+
+
+def dynamic_block(index, block):
+    return pl.ds(pl.multiple_of(index * block, block), block)
+
+
+def experts_up_kernel(rank, x_ref, z_ref, ga, gb, ua, ub, g_ref, u_ref, my_ref, mx_ref, middle_ref):
+    gate = matmul(x_ref[0], ga[...]) + matmul(x_ref[1], gb[...])
+    up = matmul(z_ref[0], ua[...]) + matmul(z_ref[1], ub[...])
+    g_ref[...] = gate
+    u_ref[...] = up
+    middle_ref[...] = (gate * jax.nn.sigmoid(gate) * up).astype(jnp.bfloat16)
+    block = gate.shape[1] // 4
+    for j in range(4):
+        piece = middle_ref[:, dynamic_block(rank[0] ^ j, block)]
+        dy, dx = j // 2, j % 2
+        my_ref[dy, :, dx * block : (dx + 1) * block] = piece
+        mx_ref[dx, :, dy * block : (dy + 1) * block] = piece
+
+
+def experts_up(rank, by_y, by_x, weights):
+    _, rows, depth = by_y.shape
+    hidden = weights[0].shape[1]
+    tile = 256
+    x_spec = pl.BlockSpec((2, tile, depth), lambda i, rank: (0, i, 0))
+    w_spec = pl.BlockSpec((depth, hidden), lambda i, rank: (0, 0))
+    wide = pl.BlockSpec((tile, hidden), lambda i, rank: (i, 0))
+    half = pl.BlockSpec((2, tile, hidden // 2), lambda i, rank: (0, i, 0))
+    return kernel_call(
+        experts_up_kernel,
+        grid_spec=pltpu.PrefetchScalarGridSpec(
+            num_scalar_prefetch=1,
+            grid=(rows // tile,),
+            in_specs=[x_spec, x_spec] + [w_spec] * 4,
+            out_specs=[wide, wide, half, half],
+            scratch_shapes=[pltpu.VMEM((tile, hidden), jnp.bfloat16)],
+        ),
+        out_shape=[jax.ShapeDtypeStruct((rows, hidden), jnp.float32)] * 2
+        + [jax.ShapeDtypeStruct((2, rows, hidden // 2), jnp.bfloat16)] * 2,
+        cost_estimate=pl.CostEstimate(
+            flops=8 * rows * depth * hidden, bytes_accessed=30 * rows * hidden, transcendentals=0
+        ),
+    )(rank, by_y, by_x, *weights)
+
+
+def experts_down_kernel(*refs):
+    gates, slots, outs = refs[:2], (refs[2:8], refs[8:14]), refs[14:]
+    half = outs[0].shape[1] // 2
+    for side in range(2):
+        at = slice(side * half, (side + 1) * half)
+        mixture = 0.0
+        for slot, (my, mx, la, lb, ra, rb) in enumerate(slots):
+            if side == 0:
+                out = matmul(my[0], la[...]) + matmul(my[1], lb[...])
+            else:
+                out = matmul(mx[0], ra[...]) + matmul(mx[1], rb[...])
+            out = out.astype(jnp.bfloat16)
+            outs[slot][:, at] = out
+            mixture += gates[slot][...] * out.astype(jnp.float32)
+        outs[2][:, at] = mixture
+
+
+def experts_down(gates, slots):
+    _, rows, depth = slots[0][0].shape
+    half = slots[0][2].shape[1]
+    tile = 256
+    x_spec = pl.BlockSpec((2, tile, depth), lambda i: (0, i, 0))
+    w_spec = pl.BlockSpec((depth, half), lambda i: (0, 0))
+    wide = pl.BlockSpec((tile, 2 * half), lambda i: (i, 0))
+    column = pl.BlockSpec((tile, 1), lambda i: (i, 0))
+    return kernel_call(
+        experts_down_kernel,
+        grid=(rows // tile,),
+        in_specs=[column] * 2 + ([x_spec] * 2 + [w_spec] * 4) * 2,
+        out_specs=[wide] * 3,
+        out_shape=[
+            jax.ShapeDtypeStruct((rows, 2 * half), jnp.bfloat16),
+            jax.ShapeDtypeStruct((rows, 2 * half), jnp.bfloat16),
+            jax.ShapeDtypeStruct((rows, 2 * half), jnp.float32),
+        ],
+        cost_estimate=pl.CostEstimate(
+            flops=16 * rows * depth * half, bytes_accessed=24 * rows * half, transcendentals=0
+        ),
+    )(*gates, *slots[0], *slots[1])
+
+
+def experts_back_kernel(
+    rank, r_ref, out_ref, gate_ref, g_ref, u_ref, la, lb, ra, rb, p_ref, dg_ref, du_ref, gg_ref
+):
+    grad = r_ref[...]
+    gg_ref[...] = jnp.sum(grad * out_ref[...].astype(jnp.float32), axis=1, keepdims=True)
+    p_ref[...] = (gate_ref[...] * grad).astype(jnp.bfloat16)
+    half = grad.shape[1] // 2
+    left, right = p_ref[:, :half], p_ref[:, half:]
+    block = la.shape[0] // 2
+    first, second = slice(0, block), slice(block, 2 * block)
+    for j in range(4):
+        dy, dx = j // 2, j % 2
+        left_w = (la, lb)[dy][(first, second)[dx], :]
+        right_w = (ra, rb)[dx][(first, second)[dy], :]
+        middle_grad = dot_t(left, left_w) + dot_t(right, right_w)
+        at = dynamic_block(rank[0] ^ j, block)
+        gate_pre, up_pre = g_ref[:, at], u_ref[:, at]
+        sigma = jax.nn.sigmoid(gate_pre)
+        change = middle_grad * up_pre * sigma * (1.0 + gate_pre * (1.0 - sigma))
+        dg_ref[:, at] = change.astype(jnp.bfloat16)
+        du_ref[:, at] = (middle_grad * (gate_pre * sigma)).astype(jnp.bfloat16)
+
+
+def experts_back(rank, result_grad, out, gate, gate_pre, up_pre, weights):
+    rows, width = result_grad.shape
+    hidden = gate_pre.shape[1]
+    tile = 256
+    wide = pl.BlockSpec((tile, width), lambda i, rank: (i, 0))
+    narrow = pl.BlockSpec((tile, hidden), lambda i, rank: (i, 0))
+    column = pl.BlockSpec((tile, 1), lambda i, rank: (i, 0))
+    w_spec = pl.BlockSpec(weights[0].shape, lambda i, rank: (0, 0))
+    return kernel_call(
+        experts_back_kernel,
+        grid_spec=pltpu.PrefetchScalarGridSpec(
+            num_scalar_prefetch=1,
+            grid=(rows // tile,),
+            in_specs=[wide, wide, column, narrow, narrow] + [w_spec] * 4,
+            out_specs=[wide, narrow, narrow, column],
+        ),
+        out_shape=[
+            jax.ShapeDtypeStruct((rows, width), jnp.bfloat16),
+            jax.ShapeDtypeStruct((rows, hidden), jnp.bfloat16),
+            jax.ShapeDtypeStruct((rows, hidden), jnp.bfloat16),
+            jax.ShapeDtypeStruct((rows, 1), jnp.float32),
+        ],
+        cost_estimate=pl.CostEstimate(
+            flops=2 * rows * width * hidden, bytes_accessed=26 * rows * hidden, transcendentals=0
+        ),
+    )(rank, result_grad, out, gate, gate_pre, up_pre, *weights)
+
+
+def experts_input_kernel(*refs):
+    o_ref = refs[-1]
+    depth = o_ref.shape[2]
+    first, second = slice(0, depth), slice(depth, 2 * depth)
+    for j in range(4):
+        dy, dx = j // 2, j % 2
+        total = 0.0
+        for dg, du, ga, gb, ua, ub in (refs[:6], refs[6:12]):
+            gate_w = (ga, gb)[dy][(first, second)[dx], :]
+            up_w = (ua, ub)[dx][(first, second)[dy], :]
+            part = dot_t(dg[...], gate_w) + dot_t(du[...], up_w)
+            total += part.astype(jnp.bfloat16).astype(jnp.float32)
+        o_ref[j] = total
+
+
+def experts_input(slots):
+    rows, hidden = slots[0][0].shape
+    depth = slots[0][2].shape[0] // 2
+    tile = 256
+    narrow = pl.BlockSpec((tile, hidden), lambda i: (i, 0))
+    w_spec = pl.BlockSpec((2 * depth, hidden), lambda i: (0, 0))
+    return kernel_call(
+        experts_input_kernel,
+        grid=(rows // tile,),
+        in_specs=([narrow] * 2 + [w_spec] * 4) * 2,
+        out_specs=pl.BlockSpec((4, tile, depth), lambda i: (0, i, 0)),
+        out_shape=jax.ShapeDtypeStruct((4, rows, depth), jnp.float32),
+        cost_estimate=pl.CostEstimate(
+            flops=32 * rows * depth * hidden, bytes_accessed=48 * rows * depth, transcendentals=0
+        ),
+    )(*slots[0], *slots[1])
+
+
+def residual_back_kernel(
+    rank, a_ref, b_ref, lg_ref, wr_ref, x_ref, r_ref, scale_ref, gain_ref, o_ref, c_ref, gg_ref
+):
+    scale = scale_ref[...]
+    block = a_ref.shape[2]
+
+    @pl.when(pl.program_id(0) == 0)
+    def _():
+        gg_ref[...] = jnp.zeros_like(gg_ref)
+
+    inner = jnp.zeros_like(scale)
+    for j in range(4):
+        at = dynamic_block(rank[0] ^ j, block)
+        grad = a_ref[j] + b_ref[j]
+        for e in range(wr_ref.shape[0]):
+            grad += lg_ref[:, e : e + 1] * wr_ref[e : e + 1, at]
+        o_ref[:, at] = grad
+        product = grad * x_ref[:, at]
+        inner += jnp.sum(product * gain_ref[:, at], axis=1, keepdims=True)
+        gg_ref[:, at] += jnp.sum(product * scale, axis=0, keepdims=True)
+    inner = inner * (1.0 / x_ref.shape[1]) * (scale * scale * scale)
+    for j in range(4):
+        at = slice(j * block, (j + 1) * block)
+        value = scale * (o_ref[:, at] * gain_ref[:, at]) - x_ref[:, at] * inner
+        value = r_ref[:, at] + value
+        o_ref[:, at] = value
+        c_ref[:, at] = value.astype(jnp.bfloat16)
+
+
+def residual_back(rank, own, other, logit_grad, router, residual, result_grad, scale, gain):
+    rows, width = residual.shape
+    tile = 128
+    wide = pl.BlockSpec((tile, width), lambda i, rank: (i, 0))
+    piece = pl.BlockSpec((4, tile, width // 4), lambda i, rank: (0, i, 0))
+    one = pl.BlockSpec((1, width), lambda i, rank: (0, 0))
+    experts = logit_grad.shape[1]
+    return kernel_call(
+        residual_back_kernel,
+        grid_spec=pltpu.PrefetchScalarGridSpec(
+            num_scalar_prefetch=1,
+            grid=(rows // tile,),
+            in_specs=[
+                piece,
+                piece,
+                pl.BlockSpec((tile, experts), lambda i, rank: (i, 0)),
+                pl.BlockSpec((experts, width), lambda i, rank: (0, 0)),
+                wide,
+                wide,
+                pl.BlockSpec((tile, 1), lambda i, rank: (i, 0)),
+                one,
+            ],
+            out_specs=[wide, wide, one],
+        ),
+        out_shape=[
+            jax.ShapeDtypeStruct((rows, width), jnp.float32),
+            jax.ShapeDtypeStruct((rows, width), jnp.bfloat16),
+            jax.ShapeDtypeStruct((1, width), jnp.float32),
+        ],
+        cost_estimate=pl.CostEstimate(
+            flops=20 * rows * width, bytes_accessed=22 * rows * width, transcendentals=0
+        ),
+    )(rank, own, other, logit_grad, router, residual, result_grad, scale, gain[None])
 
 
 def across(value, bit):
@@ -862,14 +1103,6 @@
     return parts
 
 
-def gather_small(value, place):
-    y_bit, x_bit, core, shard = place
-    value = over_ep(value, place)
-    value = in_order(value, across(value, 1), core, 0)
-    value = in_order(value, across(value, 2), x_bit, 0)
-    return in_order(value, across(value, 4), y_bit, 0)
-
-
 def sum_small(value, place):
     value = value + across(value, 1)
     value = value + across(value, 2)
@@ -877,30 +1110,16 @@
     return jnp.sum(over_ep(value, place), axis=0)
 
 
-def gather_pair(left, right, place):
-    width = left.shape[1]
-    parts = over_ep(jnp.stack([left, right]), place)
-    a, b = parts[:, 0].reshape(-1, width), parts[:, 1].reshape(-1, width)
-    a_x, b_y = across(a, 2), across(b, 4)
-    a = jnp.concatenate([a, a_x], 0)
-    b_both = jnp.stack([b, b_y])
-    a_y, b_x = across(a, 4), across(b_both, 2)
-    a = jnp.concatenate([a, a_y], 0)
-    b = jnp.concatenate([b, b_x[0], b_y, b_x[1]], 0)
-    return (a, across(a, 1)), (b, across(b, 1))
-
-
-def half_step(value, bit, axis, link):
-    sent = across(pick(value, 1 - bit, axis), link)
-    kept = pick(value, bit, axis)
-    return (kept.astype(jnp.float32) + sent.astype(jnp.float32)).astype(jnp.bfloat16)
-
-
-def plane_sum(left, right, place):
-    y_bit, x_bit, core, shard = place
-    a = half_step(left, x_bit, 1, 2)
-    b = half_step(right, y_bit, 0, 4)
-    return half_step(a, y_bit, 0, 4), half_step(b, x_bit, 0, 2)
+def hold(*values):
+    return lax.optimization_barrier(values)
+
+
+def both_ways(value):
+    return across(value[0], 2), across(value[1], 4)
+
+
+def other_ways(first, second):
+    return across(first, 4), across(second, 2)
 
 
 def chip_sum(halves, grad):
@@ -913,50 +1132,23 @@
     return (left.astype(jnp.float32) + right.astype(jnp.float32)).astype(jnp.bfloat16)
 
 
-def scatter_pair(a, b, place):
+def over_ep_sum(both, place):
     shard = place[3]
     experts = lax.axis_size("ep")
-    a_x, b_y = across(a[:, 1], 2), across(b[1], 4)
-    a, b = add(a[:, 0], a_x), add(b[0], b_y)
-    a_y, b_x = across(a[1], 4), across(b[1], 2)
-    a, b = add(a[0], a_y), add(b[0], b_x)
-    both = jnp.stack([a, b])
     both = both.reshape(2, experts, both.shape[1] // experts, both.shape[2])
     total = pick(both, shard, 1).astype(jnp.float32)
     for steps in range(1, experts):
         total = total + along(pick(both, lax.rem(shard + steps, experts), 1), steps)
-    return total[0], total[1]
-
-
-def gather_experts(quarter, place):
-    y_bit, x_bit, core, shard = place
-    m = jnp.where(core == 0, shard, lax.axis_size("ep") - 1 - shard)
-    one = mirrored(quarter, [(0, 1), (1, 2)])
-    two = mirrored(jnp.where(m == 2, one, quarter), [(1, 0), (2, 3)])
-    three = mirrored(one, [(1, 2)])
-    four = mirrored(three, [(2, 3)])
-    a = jnp.where(m == 0, quarter, jnp.where(m == 1, one, jnp.where(m == 2, three, four)))
-    b = jnp.where(m == 1, quarter, jnp.where(m == 2, one, two))
-    a_x, b_y = across(a, 2), across(b, 4)
-    a, b = in_order(a, a_x, x_bit, 0), in_order(b, b_y, y_bit, 0)
-    a_y, b_x = across(a, 4), across(b, 2)
-    return in_order(a, a_y, y_bit, 0), in_order(b, b_x, x_bit, 1)
-
-
-def scatter_experts(left, right, place):
-    y_bit, x_bit, core, shard = place
-    m = jnp.where(core == 0, shard, lax.axis_size("ep") - 1 - shard)
-    a, b = plane_sum(left, right, place)
-    both = jnp.stack([a, b])
-    up = mirrored(b, [(0, 1)])
-    got = mirrored(both, [(3, 2)])
-    both = (both.astype(jnp.float32) + got.astype(jnp.float32)).astype(jnp.bfloat16)
-    got = mirrored(both, [(2, 1)])
-    both = both.astype(jnp.float32) + got.astype(jnp.float32)
-    a, b = both[0], both[1]
-    got = mirrored(a.astype(jnp.bfloat16), [(1, 0)])
-    mine = jnp.where(m == 0, a + got.astype(jnp.float32), b + up.astype(jnp.float32))
-    return mine, m
+    return total
+
+
+def part_sum(left, grad):
+    return t_dot(left, grad).astype(jnp.bfloat16)
+
+
+def kept_sum(left, grad, got):
+    total = t_dot(left, grad) + got.astype(jnp.float32)
+    return total.astype(jnp.bfloat16).reshape(2, -1, grad.shape[1])
 
 
 def body(
@@ -1000,44 +1192,100 @@
         ],
         1,
     )
-    small = gather_small(small.T, place)
+    small = small.T
+    rank = rep.astype(jnp.int32)[None]
+    quarter = rep // 2
+    quarter_rank = quarter.astype(jnp.int32)[None]
+    order = tuple(code_of(j, reps) for j in range(reps))
+    half = width // 2
+    behind = reach * local_rows
+    all_rows = local_rows + behind
+    m = jnp.where(core == 0, shard, experts - 1 - shard)
+    quarter_rows = w_gate.shape[1] // 4
+    quarter_down = w_down.shape[1] // 4
+    own_gu = jnp.stack(
+        [
+            lax.dynamic_slice_in_dim(w[0], quarter * quarter_rows, quarter_rows, 0)
+            for w in (w_gate, w_up)
+        ]
+    )
+    own_d = lax.dynamic_slice_in_dim(w_down[0], quarter * quarter_down, quarter_down, 0)
+    own_d = jnp.stack([own_d[:, :half], own_d[:, half:]])
+    segments = segment_ids.reshape(local_rows)
+
+    small = over_ep(small, place)
+    kv = over_ep(jnp.stack([w_key, w_value]), place)
+    gu_1 = mirrored(own_gu, [(0, 1), (1, 2)])
+    segment_parts = [segments]
+    for back in range(reach):
+        segment_parts.insert(0, from_behind(segment_parts[0], "ep", 1))
+    qo = jnp.stack([w_query, w_out])
+    small, kv, gu_1, qo, tokens_1, own_gu = hold(small, kv, gu_1, qo, tokens, own_gu)
+
+    qo = over_ep(qo, place)
+    k_w, v_w = kv[:, 0].reshape(-1, width), kv[:, 1].reshape(-1, width)
+    k_x, v_y = both_ways((k_w, v_w))
+    small = in_order(small, across(small, 1), core, 0)
+    small = in_order(small, across(small, 2), place[1], 0)
+    small = in_order(small, across(small, 4), place[0], 0)
+    qo, k_w, k_x, v_w, v_y, tokens_1, gu_1, own_gu, own_d = hold(
+        qo, k_w, k_x, v_w, v_y, tokens_1, gu_1, own_gu, own_d
+    )
+
+    k_w = jnp.concatenate([k_w, k_x], 0)
+    k_y, v_x = other_ways(k_w, jnp.stack([v_w, v_y]))
+    k_w = jnp.concatenate([k_w, k_y], 0)
+    v_w = jnp.concatenate([v_w, v_x[0], v_y, v_x[1]], 0)
+    token_parts = [from_behind(tokens_1, "ep", 1), tokens]
+    gu_2 = mirrored(jnp.where(m == 2, gu_1, own_gu), [(1, 0), (2, 3)])
+    qo, k_w, v_w, token_1, gu_1, gu_2, own_d = hold(
+        qo, k_w, v_w, token_parts[0], gu_1, gu_2, own_d
+    )
+
+    token_parts[0] = token_1
+    for back in range(reach - 1):
+        token_parts.insert(0, from_behind(token_parts[0], "ep", 1))
+    key_w, value_w = (k_w, across(k_w, 1)), (v_w, across(v_w, 1))
+    q_w, o_w = qo[:, 0].reshape(-1, width), qo[:, 1].reshape(-1, width)
+    q_x, o_y = both_ways((q_w, o_w))
+    gu_b = jnp.where(m == 1, own_gu, jnp.where(m == 2, gu_1, gu_2))
+    b_x, b_y = both_ways(gu_b)
+    gu_3 = mirrored(gu_1, [(1, 2)])
+    d_1 = mirrored(own_d, [(0, 1), (1, 2)])
+    token_0, key_w, value_w, q_w, q_x, o_w, o_y, gu_b, b_x, b_y, gu_3, d_1, own_d = hold(
+        token_parts[0], key_w, value_w, q_w, q_x, o_w, o_y, gu_b, b_x, b_y, gu_3, d_1, own_d
+    )
+    token_parts[0] = token_0
+
+    q_w = jnp.concatenate([q_w, q_x], 0)
+    q_y, o_x = other_ways(q_w, jnp.stack([o_w, o_y]))
+    q_w = jnp.concatenate([q_w, q_y], 0)
+    o_w = jnp.concatenate([o_w, o_x[0], o_y, o_x[1]], 0)
+    gate_b, up_b = jnp.stack([gu_b[0], b_x]), jnp.stack([gu_b[1], b_y])
+    gate_b2, up_b2 = other_ways(gate_b, up_b)
+    gu_4 = mirrored(gu_3, [(2, 3)])
+    d_2 = mirrored(jnp.where(m == 2, d_1, own_d), [(1, 0), (2, 3)])
     small = jnp.moveaxis(small, 4, 0).reshape(small.shape[4], -1)
     gain_attn, gain_query, gain_key, gain_moe = [small[i].astype(f32) for i in range(4)]
     weight_router = small[4 : 4 + experts].T
     counts = small[4 + experts :, :: attn_gain.shape[0]].astype(f32)
     count = jnp.sum(counts[0]) * 16.0 + jnp.sum(counts[1])
 
-    key_w, value_w = gather_pair(w_key, w_value, place)
-    query_w, out_w = gather_pair(w_query, w_out, place)
-    rank = rep.astype(jnp.int32)[None]
-    blocks = reps
-
-    moved, moved_segments = tokens, segment_ids.reshape(local_rows)
-    token_parts, segment_parts = [tokens], [moved_segments]
-    for back in range(reach):
-        moved = from_behind(moved, "ep", 1)
-        moved_segments = from_behind(moved_segments, "ep", 1)
-        token_parts.insert(0, moved)
-        segment_parts.insert(0, moved_segments)
-    behind = reach * local_rows
     tokens_all = jnp.concatenate(token_parts, 0)
     key_segments = jnp.concatenate(segment_parts, 0)
-    inputs = tokens.astype(f32)
-
-    quarter_rows = w_gate.shape[1] // 4
-    quarter_down = w_down.shape[1] // 4
-    quarter = rep // 2
-    quarter_gate = lax.dynamic_slice_in_dim(w_gate[0], quarter * quarter_rows, quarter_rows, 0)
-    quarter_up = lax.dynamic_slice_in_dim(w_up[0], quarter * quarter_rows, quarter_rows, 0)
-    quarter_down_w = lax.dynamic_slice_in_dim(w_down[0], quarter * quarter_down, quarter_down, 0)
-    own_quarter = jnp.concatenate(
-        [jnp.concatenate([quarter_gate, quarter_up], 1), quarter_down_w], 0
-    )
-
-    all_rows = local_rows + behind
-    normed, scale_all = norm_rows(rank, tokens_all, gain_attn, blocks)
+    normed, scale_all = norm_rows(rank, tokens_all, gain_attn, order)
     key_lin, key_squares = project(normed, *key_w, f32)
     value_all, _ = project(normed, *value_w, bf16)
+    q_w, o_w, gate_b2, up_b2, gu_4, d_2, normed, key_lin, value_all = hold(
+        q_w, o_w, gate_b2, up_b2, gu_4, d_2, normed, key_lin, value_all
+    )
+
+    query_w, out_w = (q_w, across(q_w, 1)), (o_w, across(o_w, 1))
+    gu_a = jnp.where(
+        m == 0, own_gu, jnp.where(m == 1, gu_1, jnp.where(m == 2, gu_3, gu_4))
+    )
+    a_x, a_y = both_ways(gu_a)
+    d_3 = mirrored(d_1, [(1, 2)])
     query_lin, query_squares = project(normed, *query_w, f32, behind)
     scale_key = lax.rsqrt(key_squares / width + norm_eps)
     scale_query = lax.rsqrt(query_squares / width + norm_eps)
@@ -1076,39 +1324,65 @@
         sine,
     )
     mixed, lse = attend(rank, operands, mask_of(local_rows // 4))
+    mixed, lse, out_w, gu_a, a_x, a_y, d_3, d_1, d_2, own_d = hold(
+        mixed, lse, out_w, gu_a, a_x, a_y, d_3, d_1, d_2, own_d
+    )
+
+    gate_a, up_a = jnp.stack([gu_a[0], a_x]), jnp.stack([gu_a[1], a_y])
+    gate_a2, up_a2 = other_ways(gate_a, up_a)
+    d_4 = mirrored(d_3, [(2, 3)])
+    d_b = jnp.where(m == 1, own_d, jnp.where(m == 2, d_1, d_2))
+    b_x, b_y = both_ways(d_b)
     branch, _ = project(mixed, *out_w, f32)
-    residual = inputs + branch
-    scale_moe = rms_scale(residual)
-    normed_moe = (residual * scale_moe * gain_moe).astype(bf16)
-    partner_moe = across(normed_moe, 1)
-    router_probs = jax.nn.softmax(matmul(normed_moe, weight_router), axis=-1)
+    residual = tokens.astype(f32) + branch
+    moe, scale_moe = norm_rows(quarter_rank, residual, gain_moe, (0, 1, 2, 3))
+    moe_y = jnp.concatenate([moe, across(moe, 1)], 1)
+    piece = half // 2
+    moe_x = jnp.stack(
+        [
+            jnp.concatenate([moe_y[0, :, i : i + piece], moe_y[1, :, i : i + piece]], 1)
+            for i in (0, piece)
+        ]
+    )
+    router_parts = weight_router.reshape(4, -1, experts)
+    router_rel = jnp.concatenate([pick(router_parts, quarter ^ j, 0) for j in range(4)], 0)
+    router_probs = jax.nn.softmax(
+        matmul(moe[0], router_rel[:half]) + matmul(moe[1], router_rel[half:]), axis=-1
+    )
     chosen = jnp.sum(
         (routes[:, :, None] == jnp.arange(experts, dtype=jnp.int32)).astype(f32), axis=1
     )
     gates = router_probs * chosen
-    ends = ((0, experts - 1), (1, experts - 2))
-
-    def slot_of(value, slot, of_core):
-        low, high = ends[slot]
-        return jnp.where(of_core == 0, value[:, low], value[:, high])
-
     gates_both = jnp.concatenate([gates, across(gates, 1)], 0)
-    moe_both = jnp.concatenate([normed_moe, partner_moe], 0)
-
-    experts_a, experts_b = gather_experts(own_quarter, place)
-    slots = []
-    mixture = 0.0
-    for slot, pieces in enumerate((experts_a, experts_b)):
-        weight_gu = pieces[:, :, :quarter_rows].reshape(4 * quarter_rows, width)
-        weight_down = pieces[:, :, quarter_rows:].reshape(4 * quarter_down, width)
-        hidden = width // 2
-        pre = matmul(moe_both, weight_gu)
-        gate_pre, up_pre = pre[:, :hidden], pre[:, hidden:]
-        middle = (jax.nn.silu(gate_pre) * up_pre).astype(bf16)
-        expert_out = matmul(middle, weight_down).astype(bf16)
-        gate = slot_of(gates_both, slot, core)
-        mixture = mixture + gate[:, None] * expert_out
-        slots.append((weight_gu, weight_down, gate_pre, up_pre, middle, expert_out, gate))
+    gates_a = jnp.where(core == 0, gates_both[:, :1], gates_both[:, -1:])
+    gates_b = jnp.where(core == 0, gates_both[:, 1:2], gates_both[:, -2:-1])
+    gate_a2, up_a2, d_4, d_b, b_x, b_y, moe_y, moe_x = hold(
+        gate_a2, up_a2, d_4, d_b, b_x, b_y, moe_y, moe_x
+    )
+
+    def flat(value):
+        return value.reshape(-1, value.shape[-1])
+
+    left_b, right_b = jnp.stack([d_b[0], b_x]), jnp.stack([d_b[1], b_y])
+    left_b2, right_b2 = other_ways(left_b, right_b)
+    d_a = jnp.where(m == 0, own_d, jnp.where(m == 1, d_1, jnp.where(m == 2, d_3, d_4)))
+    a_x, a_y = both_ways(d_a)
+    gu_weights_b = (flat(gate_b), flat(gate_b2), flat(up_b), flat(up_b2))
+    gate_pre_b, up_pre_b, my_b, mx_b = experts_up(quarter_rank, moe_y, moe_x, gu_weights_b)
+    left_b2, right_b2, d_a, a_x, a_y, my_b, mx_b, gate_a = hold(
+        left_b2, right_b2, d_a, a_x, a_y, my_b, mx_b, gate_a
+    )
+
+    left_a, right_a = jnp.stack([d_a[0], a_x]), jnp.stack([d_a[1], a_y])
+    left_a2, right_a2 = other_ways(left_a, right_a)
+    gu_weights_a = (flat(gate_a), flat(gate_a2), flat(up_a), flat(up_a2))
+    gate_pre_a, up_pre_a, my_a, mx_a = experts_up(quarter_rank, moe_y, moe_x, gu_weights_a)
+    left_a2, right_a2, my_a, mx_a = hold(left_a2, right_a2, my_a, mx_a)
+    d_weights_a = (flat(left_a), flat(left_a2), flat(right_a), flat(right_a2))
+    d_weights_b = (flat(left_b), flat(left_b2), flat(right_b), flat(right_b2))
+    expert_out_a, expert_out_b, mixture = experts_down(
+        (gates_a, gates_b), ((my_a, mx_a) + d_weights_a, (my_b, mx_b) + d_weights_b)
+    )
     result = residual + (mixture[:local_rows] + across(mixture[local_rows:], 1))
     output = result.astype(bf16)
     error = result - teacher.astype(f32)
@@ -1116,44 +1390,30 @@
     result_grad = total_tokens / count * valid[:, None] * error
     result_grad_both = jnp.concatenate([result_grad, across(result_grad, 1)], 0)
 
-    input_grad = 0.0
-    gate_grads, expert_grads = [], []
-    for weight_gu, weight_down, gate_pre, up_pre, middle, expert_out, gate in slots:
-        gate_grads.append(jnp.sum(result_grad_both * expert_out, axis=1))
-        pair_grad = (gate[:, None] * result_grad_both).astype(bf16)
-        down_local = matmul(middle.T, pair_grad).astype(bf16)
-        middle_grad = matmul(pair_grad, weight_down.T)
-        sigma = jax.nn.sigmoid(gate_pre)
-        active = gate_pre * sigma
-        gate_pre_grad = (middle_grad * up_pre * sigma * (1.0 + gate_pre * (1.0 - sigma))).astype(
-            bf16
-        )
-        up_pre_grad = (middle_grad * active).astype(bf16)
-        pre_grad = jnp.concatenate([gate_pre_grad, up_pre_grad], 1)
-        gu_local = matmul(moe_both.T, pre_grad).astype(bf16)
-        input_grad = input_grad + matmul(pre_grad, weight_gu.T).astype(bf16).astype(f32)
-        expert_grads.append(
-            jnp.concatenate(
-                [
-                    gu_local.reshape(2, 2, quarter_rows, width),
-                    down_local.reshape(2, 2, quarter_down, width),
-                ],
-                2,
-            )
-        )
-    expert_mine, m = scatter_experts(expert_grads[0], expert_grads[1], place)
-    half_rows, half_down = quarter_rows // 2, quarter_down // 2
-    gu_halves = expert_mine[:quarter_rows].reshape(2, half_rows, width)
-    down_halves = expert_mine[quarter_rows:].reshape(2, half_down, width)
-    halves = jnp.concatenate([gu_halves, down_halves], 1)
-    from_holder = across(pick(halves, 1 - core, 0), 1)
-    expert_half = jnp.where(m < 2, pick(halves, core, 0), from_holder)
-    gate_out = expert_half[None, :half_rows, : width // 2]
-    up_out = expert_half[None, :half_rows, width // 2 :]
-    down_out = expert_half[None, half_rows:]
-
-    input_grad = input_grad[:local_rows] + across(input_grad[local_rows:], 1)
-    slot_grads = jnp.stack(gate_grads, 1)
+    pair_b, dg_b, du_b, gate_grad_b = experts_back(
+        quarter_rank, result_grad_both, expert_out_b, gates_b, gate_pre_b, up_pre_b, d_weights_b
+    )
+    pair_a, dg_a, du_a, gate_grad_a = experts_back(
+        quarter_rank, result_grad_both, expert_out_a, gates_a, gate_pre_a, up_pre_a, d_weights_a
+    )
+    sent = [
+        part_sum(mx[1], pair[:, :half])
+        for mx, pair in ((mx_a, pair_a), (mx_b, pair_b))
+    ] + [
+        part_sum(my[1], pair[:, half:])
+        for my, pair in ((my_a, pair_a), (my_b, pair_b))
+    ]
+    sent, dg_a, du_a, dg_b, du_b, gate_grad_a, pair_a, pair_b = hold(
+        sent, dg_a, du_a, dg_b, du_b, gate_grad_a, pair_a, pair_b
+    )
+
+    got_d = [across(sent[0], 2), across(sent[1], 2), across(sent[2], 4), across(sent[3], 4)]
+    sent_gu = [part_sum(moe_x[1], grad) for grad in (dg_a, dg_b)] + [
+        part_sum(moe_y[1], grad) for grad in (du_a, du_b)
+    ]
+    input_grad = experts_input(((dg_a, du_a) + gu_weights_a, (dg_b, du_b) + gu_weights_b))
+    input_other = across(input_grad[:, local_rows:], 1)
+    slot_grads = jnp.concatenate([gate_grad_a, gate_grad_b], 1)
     own_slots, partner_slots = slot_grads[:local_rows], across(slot_grads[local_rows:], 1)
     from_low = jnp.where(core == 0, own_slots, partner_slots)
     from_high = jnp.where(core == 0, partner_slots, own_slots)
@@ -1161,69 +1421,274 @@
     logit_grad = router_probs * (
         prob_grad - jnp.sum(prob_grad * router_probs, axis=-1, keepdims=True)
     )
-    router_local = jnp.dot(
-        normed_moe.T, logit_grad, precision=highest, preferred_element_type=f32
-    )
-    normed_moe_grad = input_grad + jnp.dot(
-        logit_grad, weight_router.T, precision=highest, preferred_element_type=f32
-    )
-    residual_part, moe_gain_local = norm_back(residual, scale_moe, gain_moe, normed_moe_grad)
-    residual_grad = result_grad + residual_part
-    branch_grad = residual_grad.astype(bf16)
-    half = width // 2
-    out_a, out_b = scatter_pair(
-        chip_sum(mixed, branch_grad[:, :half]), chip_sum(mixed, branch_grad[:, half:]), place
-    )
-    out_out = jnp.concatenate([out_a, out_b], 1)
+    got_d, sent_gu, input_grad, input_other, logit_grad = hold(
+        got_d, sent_gu, input_grad, input_other, logit_grad
+    )
+
+    got_gu = [
+        across(sent_gu[0], 2),
+        across(sent_gu[1], 2),
+        across(sent_gu[2], 4),
+        across(sent_gu[3], 4),
+    ]
+    kept_d = [
+        kept_sum(mx_a[0], pair_a[:, :half], got_d[0]),
+        kept_sum(mx_b[0], pair_b[:, :half], got_d[1]),
+        kept_sum(my_a[0], pair_a[:, half:], got_d[2]),
+        kept_sum(my_b[0], pair_b[:, half:], got_d[3]),
+    ]
+    got_d = [
+        across(kept_d[0][1], 4),
+        across(kept_d[1][1], 4),
+        across(kept_d[2][1], 2),
+        across(kept_d[3][1], 2),
+    ]
+    router_local = jnp.concatenate(
+        [
+            jnp.dot(part.T.astype(f32), logit_grad, precision=highest, preferred_element_type=f32)
+            for part in (moe[0], moe[1])
+        ],
+        0,
+    )
+    router_local = router_local.reshape(4, -1, experts)
+    router_local = jnp.concatenate([pick(router_local, quarter ^ j, 0) for j in range(4)], 0)
+    residual_grad, branch_grad, moe_gain_local = residual_back(
+        quarter_rank,
+        input_grad,
+        input_other,
+        logit_grad,
+        weight_router.astype(f32).T,
+        residual,
+        result_grad,
+        scale_moe,
+        gain_moe,
+    )
+    out_a = chip_sum(mixed, branch_grad[:, :half])
+    out_b = chip_sum(mixed, branch_grad[:, half:])
     mixed_grad = jnp.stack([dot_t(branch_grad, weight).astype(bf16) for weight in out_w])
-    query_row_grad, key_row_grad, value_row_grad = attend_back(
-        rank, operands, mask_of(local_rows // 2), mixed_grad, lse
-    )
-    value_a, value_b = scatter_pair(
-        chip_sum(normed, value_row_grad[:, :half]),
-        chip_sum(normed, value_row_grad[:, half:]),
-        place,
-    )
-    value_out = jnp.concatenate([value_a, value_b], 1)
+    bias = mask_of(local_rows // 2)
+    dq_0, dk_0, dv_0 = attend_back(rank, operands, bias, mixed_grad, lse, 0)
+    got_gu, kept_d, got_d, out_a, out_b, mixed_grad, dq_0, dk_0, dv_0 = hold(
+        got_gu, kept_d, got_d, out_a, out_b, mixed_grad, dq_0, dk_0, dv_0
+    )
+
+    def ends(kept, got):
+        total = [add(k[0], g) for k, g in zip(kept, got)]
+        return jnp.stack([jnp.stack([total[0], total[2]]), jnp.stack([total[1], total[3]])])
+
+    def first_move(both):
+        return mirrored(both, [(3, 2)]), mirrored(both[1], [(0, 1)])
+
+    kept_gu = [
+        kept_sum(moe_x[0], dg_a, got_gu[0]),
+        kept_sum(moe_x[0], dg_b, got_gu[1]),
+        kept_sum(moe_y[0], du_a, got_gu[2]),
+        kept_sum(moe_y[0], du_b, got_gu[3]),
+    ]
+    got_gu = [
+        across(kept_gu[0][1], 4),
+        across(kept_gu[1][1], 4),
+        across(kept_gu[2][1], 2),
+        across(kept_gu[3][1], 2),
+    ]
+    out_x, out_y = across(out_a[:, 1], 2), across(out_b[1], 4)
+    both_d = ends(kept_d, got_d)
+    d_3, d_1 = first_move(both_d)
+    dq_1, dk_1, dv_1 = attend_back(rank, operands, bias, mixed_grad, lse, HEADS // 2)
     query_lin_grad, q_gain_local = lin_back(
-        query_row_grad,
-        query_lin,
-        scale_query,
-        gain_query[None],
-        cosine[behind:],
-        sine[behind:],
+        dq_0, dq_1, query_lin, scale_query, gain_query[None], cosine[behind:], sine[behind:]
     )
     key_lin_grad, k_gain_local = lin_back(
-        key_row_grad, key_lin, scale_key, gain_key[None], cosine, sine
-    )
-    query_out, key_out = scatter_pair(
-        chip_sum(normed[:, behind:], query_lin_grad), chip_sum(normed, key_lin_grad), place
-    )
+        dk_0, dk_1, key_lin, scale_key, gain_key[None], cosine, sine
+    )
+    (
+        kept_gu,
+        got_gu,
+        out_a,
+        out_b,
+        out_x,
+        out_y,
+        both_d,
+        d_3,
+        d_1,
+        dv_0,
+        dv_1,
+        query_lin_grad,
+        key_lin_grad,
+    ) = hold(
+        kept_gu,
+        got_gu,
+        out_a,
+        out_b,
+        out_x,
+        out_y,
+        both_d,
+        d_3,
+        d_1,
+        dv_0,
+        dv_1,
+        query_lin_grad,
+        key_lin_grad,
+    )
+
+    out_a, out_b = add(out_a[:, 0], out_x), add(out_b[0], out_y)
+    out_x, out_y = across(out_b[1], 2), across(out_a[1], 4)
+    both_d = add(both_d, d_3)
+    d_2 = mirrored(both_d, [(2, 1)])
+    both_gu = ends(kept_gu, got_gu)
+    gu_3, gu_1 = first_move(both_gu)
+    value_a, value_b = chip_sum(normed, dv_0), chip_sum(normed, dv_1)
     normed_grad = project_back(
-        key_lin_grad, value_row_grad, query_lin_grad, key_w, value_w, query_w
-    )
-    carried = jnp.zeros((2, local_rows, width // 2), f32)
-    for back in range(reach):
-        carried = carried + normed_grad[:, back * local_rows : (back + 1) * local_rows]
-        carried = from_behind(carried.astype(bf16), "ep", -1).astype(f32)
+        key_lin_grad, dv_0, dv_1, query_lin_grad, key_w, value_w, query_w
+    )
+    (
+        out_a,
+        out_b,
+        out_x,
+        out_y,
+        both_d,
+        d_2,
+        both_gu,
+        gu_3,
+        gu_1,
+        value_a,
+        value_b,
+        normed_grad,
+        query_lin_grad,
+        key_lin_grad,
+    ) = hold(
+        out_a,
+        out_b,
+        out_x,
+        out_y,
+        both_d,
+        d_2,
+        both_gu,
+        gu_3,
+        gu_1,
+        value_a,
+        value_b,
+        normed_grad,
+        query_lin_grad,
+        key_lin_grad,
+    )
+
+    value_x, value_y = across(value_a[:, 1], 2), across(value_b[1], 4)
+    query_sum = chip_sum(normed[:, behind:], query_lin_grad)
+    key_sum = chip_sum(normed, key_lin_grad)
+    carried = normed_grad[:, :local_rows].astype(bf16)
+    carried = from_behind(carried, "ep", -1)
+    d_a, d_b = both_d[0] + d_2[0].astype(f32), both_d[1] + d_2[1].astype(f32)
+    d_0 = mirrored(d_a.astype(bf16), [(1, 0)])
+    both_gu = add(both_gu, gu_3)
+    gu_2 = mirrored(both_gu, [(2, 1)])
+    out_total = over_ep_sum(jnp.stack([add(out_a[0], out_y), add(out_b[0], out_x)]), place)
+    (
+        value_a,
+        value_b,
+        value_x,
+        value_y,
+        query_sum,
+        key_sum,
+        carried,
+        d_a,
+        d_b,
+        d_0,
+        both_gu,
+        gu_2,
+        out_total,
+    ) = hold(
+        value_a,
+        value_b,
+        value_x,
+        value_y,
+        query_sum,
+        key_sum,
+        carried,
+        d_a,
+        d_b,
+        d_0,
+        both_gu,
+        gu_2,
+        out_total,
+    )
+
+    def own_half(mine):
+        halves = mine.reshape(2, 2, -1, mine.shape[2])
+        other = across(pick(halves, 1 - core, 1), 1)
+        return jnp.where(m < 2, pick(halves, core, 1), other)
+
+    query_x, key_y = across(query_sum[:, 1], 2), across(key_sum[1], 4)
+    value_a, value_b = add(value_a[:, 0], value_x), add(value_b[0], value_y)
+    value_x, value_y = across(value_b[1], 2), across(value_a[1], 4)
+    for back in range(1, reach):
+        here = normed_grad[:, back * local_rows : (back + 1) * local_rows] + carried.astype(f32)
+        carried = from_behind(here.astype(bf16), "ep", -1)
+    down_mine = jnp.where(m == 0, d_a + d_0.astype(f32), d_b + d_1.astype(f32))
+    gu_a, gu_b = both_gu[0] + gu_2[0].astype(f32), both_gu[1] + gu_2[1].astype(f32)
+    gu_0 = mirrored(gu_a.astype(bf16), [(1, 0)])
+    (
+        query_sum,
+        key_sum,
+        query_x,
+        key_y,
+        value_a,
+        value_b,
+        value_x,
+        value_y,
+        carried,
+        gu_a,
+        gu_b,
+        gu_0,
+        down_mine,
+    ) = hold(
+        query_sum,
+        key_sum,
+        query_x,
+        key_y,
+        value_a,
+        value_b,
+        value_x,
+        value_y,
+        carried,
+        gu_a,
+        gu_b,
+        gu_0,
+        down_mine,
+    )
+
+    query_sum, key_sum = add(query_sum[:, 0], query_x), add(key_sum[0], key_y)
+    query_y, key_x = across(query_sum[1], 4), across(key_sum[1], 2)
+    value_total = over_ep_sum(
+        jnp.stack([add(value_a[0], value_y), add(value_b[0], value_x)]), place
+    )
+    gu_mine = jnp.where(m == 0, gu_a + gu_0.astype(f32), gu_b + gu_1.astype(f32))
     tokens_grad, attn_gain_local = tokens_back(
         rank,
         normed_grad,
-        carried.astype(bf16),
+        carried,
         tokens,
         residual_grad,
         scale_all,
         gain_attn,
-        blocks,
-    )
-
+        reps,
+    )
+    query_sum, key_sum, query_y, key_x, value_total, gu_mine, attn_gain_local = hold(
+        query_sum, key_sum, query_y, key_x, value_total, gu_mine, attn_gain_local
+    )
+
+    qk_total = over_ep_sum(jnp.stack([add(query_sum[0], query_y), add(key_sum[0], key_x)]), place)
+    gu_half, down_half = own_half(gu_mine), own_half(down_mine)
+    down_out = jnp.concatenate([down_half[0], down_half[1]], 1)
+    out_out = jnp.concatenate([out_total[0], out_total[1]], 1)
+    value_out = jnp.concatenate([value_total[0], value_total[1]], 1)
     packed = jnp.concatenate(
         [
             jnp.broadcast_to(squares, (1, width)),
             attn_gain_local,
             q_gain_local,
             k_gain_local,
-            moe_gain_local[None],
+            moe_gain_local,
             router_local.T,
         ],
         0,
@@ -1240,14 +1705,14 @@
         mine[2],
         mine[3],
         mine[4],
-        query_out,
-        key_out,
+        qk_total[0],
+        qk_total[1],
         value_out,
         out_out,
         mine[5:].T,
-        gate_out,
-        up_out,
-        down_out,
+        gu_half[0][None],
+        gu_half[1][None],
+        down_out[None],
     )
 
 

time: 1530 us -> 1550 us (1.013)
  Pallas kernels: 246 us -> 366 us
  matrix products: 227 us -> 133 us
  starting transfers between devices: 263 us -> 344 us
  other arithmetic: 236 us -> 158 us
    dot_general x13 -> x2, matrix products: 140 us -> 3.38 us  [matmul(): return jnp.dot(left, right, preferred_element_type=jnp.float32)]
    pallas_call x3 -> x11, Pallas kernels: 39.5 us -> 155 us  [the longest x2 30.5 us: experts_up(): kernel_call(experts_up_kernel, grid_spec=pltpu.PrefetchScalarGridSpec(num...]
    ppermute x6, starting transfers between devices: 15.1 us -> 103 us  [from_behind(): lax.ppermute(value, axis, [(source, source + steps) for source in range(l...]
    ppermute x21, starting transfers between devices: 179 us -> 99.4 us  [along(): lax.ppermute(value, 'ep', [(place, (place + steps) % count) for place in...]
    dot_general x12 -> x28, matrix products: 67.2 us -> 121 us  [t_dot(): lax.dot_general(left, right, (((0,), (0,)), ((), ())), preferred_element_...]
    select_n x10 -> x4, other arithmetic: 53.2 us -> 0.13 us  [in_order(): jnp.where(bit == 1, jnp.stack([other, own], axis), jnp.stack([own, other]...]
    ppermute x51 -> x76, starting transfers between devices: 51.2 us -> 102 us  [across(): lax.ppermute(value, 'rep', [(place, place ^ bit) for place in range(count)])]
    ppermute x51 -> x76, waiting for transfers between devices: 261 us -> 293 us  [across(): lax.ppermute(value, 'rep', [(place, place ^ bit) for place in range(count)])]
  transfers between devices with their start and end apart: 86 -> 119, of which waited for: 32 -> 38; matrix products, arithmetic and copies ran while one was open for 32% -> 18% of each run, Pallas kernels for 16% -> 17%
where the time goes in v3:
time: 1550 us; the launch traced here: 1540 us
  waiting for transfers between devices  448 us (29%)
  Pallas kernels  366 us (24%)
  starting transfers between devices  344 us (22%)
  other arithmetic  158 us (10%)
  matrix products  133 us (9%)
  local copies, waits for them, and re-layouts  84.9 us (5%)
    ppermute x76, waiting for transfers between devices, across(): lax.ppermute(value, 'rep', [(place, place ^ bit) for place in range(count)])  293 us
    dot_general x28, matrix products, t_dot(): lax.dot_general(left, right, (((0,), (0,)), ((), ())), preferred_element_...  121 us
    ppermute x6, starting transfers between devices, from_behind(): lax.ppermute(value, axis, [(source, source + steps) for source in range(l...  103 us
    ppermute x76, starting transfers between devices, across(): lax.ppermute(value, 'rep', [(place, place ^ bit) for place in range(count)])  102 us
    ppermute x21, starting transfers between devices, along(): lax.ppermute(value, 'ep', [(place, (place + steps) % count) for place in...  99.4 us
    ppermute x21, waiting for transfers between devices, along(): lax.ppermute(value, 'ep', [(place, (place + steps) % count) for place in...  88.3 us
    ppermute x16, waiting for transfers between devices, mirrored(): return lax.ppermute(value, ('rep', 'ep'), pairs)  66 us
    pallas_call x4, Pallas kernels, project(): kernel_call(project_kernel, grid=(rows // tile,), in_specs=[pl.BlockSpec(...  59.6 us
  transfers between devices with their start and end apart: 119, of which 38 were waited for; matrix products, arithmetic and copies ran while one was open for 18% of the time, Pallas kernels for 17%

profile of v3, /device:TPU:0, one launch (start us, length us, event | category | flops | bytes accessed | tf_op | source)
XLA Modules:
  0.0 1542.7 jit_solution(7571502944350618594)
XLA Ops:
  27.0 37.4 %collective-permute-done.2 = bf16[10,64]{1,0:T(8,128)(2,1)S(1)} collective-permute-done((bf16[10,64]{1,0:T(8,128)(2,1)S(1)}, bf16[10,64]{1,0:T(8,128)(2,1)S(1)}, u32[]{:S(2)}, u32[]{:S(2)}) %collective-permute-start.2) | collective-permute-done | bytes 1312 | tf_op jit(solution)/shard_map/ppermute | solution.py:1072
  126.9 25.6 %collective-permute-start.31 = (bf16[4,10,64]{2,0,1:T(4,128)(2,1)S(1)}, bf16[4,10,64]{2,0,1:T(4,128)(2,1)S(1)}, u32[]{:S(2)}, u32[]{:S(2)}) collective-permute-start(bf16[4,10,64]{2,0,1:T(4,128)(2,1)S(1)} %dynamic_update_slice.54), channel_id=1, source_target_pairs={{0,4},{4,0},{8,12},{12,8},{16,20},{20,16},{24,28},{28,24},{1,5},{5... | collective-permute-start | bytes 15368 | tf_op jit(solution)/shard_map/ppermute | solution.py:1067
  189.7 18.8 %collective-permute-done.19 = bf16[256,2048]{1,0:T(8,128)(2,1)} collective-permute-done((bf16[256,2048]{1,0:T(8,128)(2,1)}, bf16[256,2048]{1,0:T(8,128)(2,1)}, u32[]{:S(2)}, u32[]{:S(2)}) %collective-permute-start.19) | collective-permute-done | bytes 1048608 | tf_op jit(solution)/shard_map/ppermute | solution.py:1067
  210.6 47.2 %collective-permute-start.16 = (bf16[512,2048]{1,0:T(8,128)(2,1)}, bf16[512,2048]{1,0:T(8,128)(2,1)}, u32[]{:S(2)}, u32[]{:S(2)}) collective-permute-start(bf16[512,2048]{1,0:T(8,128)(2,1)} %collective-permute-done.14), channel_id=1, source_target_pairs={{0,1},{1,2},{2,3},{4,5},{5,6},{6,7},{8,9},{9,10},{10,11},{12,13},{... | collective-permute-start | bytes 6291464 | tf_op jit(solution)/shard_map/ppermute | solution.py:24
  262.8 21.4 %collective-permute-done.22 = bf16[512,1024]{1,0:T(8,128)(2,1)} collective-permute-done((bf16[512,1024]{1,0:T(8,128)(2,1)}, bf16[512,1024]{1,0:T(8,128)(2,1)}, u32[]{:S(2)}, u32[]{:S(2)}) %collective-permute-start.22) | collective-permute-done | bytes 1048608 | tf_op jit(solution)/shard_map/ppermute | solution.py:1067
  327.8 19.7 %shard_map.281 = (f32[1536,2048]{1,0:T(8,128)}, f32[1536,1]{1,0:T(8,128)}) custom-call(bf16[2,1536,1024]{2,1,0:T(8,128)(2,1)} %get-tuple-element.284.low_ref.high_ref, bf16[2,1536,1024]{2,1,0:T(8,128)(2,1)} %get-tuple-element.284.low_ref.high_ref, bf16[1024,2048]{1,0:T(8,128)(2,1)} %pad_maximum_fusion.2.a_ref.ka, ...), custom_call_target="tpu_custom_call" | custom-call | flops 12884901888 | bytes 16777216 | tf_op jit(solution)/shard_map/pallas_call | solution.py:473
  348.5 19.3 %shard_map.282 = (bf16[1536,2048]{1,0:T(8,128)(2,1)}, f32[1536,1]{1,0:T(8,128)}) custom-call(bf16[2,1536,1024]{2,1,0:T(8,128)(2,1)} %get-tuple-element.284.low_ref.high_ref, bf16[2,1536,1024]{2,1,0:T(8,128)(2,1)} %get-tuple-element.284.low_ref.high_ref, bf16[1024,2048]{1,0:T(8,128)(2,1)} %pad_maximum_fusion.3.a_ref.va, ...), custom_call_target="tpu_custom_call" | custom-call | flops 12884901888 | bytes 16777216 | tf_op jit(solution)/shard_map/pallas_call | solution.py:473
  372.9 37.3 %collective-permute-start.35 = (s32[512]{0:T(512)S(1)}, s32[512]{0:T(512)S(1)}, u32[]{:S(2)}, u32[]{:S(2)}) collective-permute-start(s32[512]{0:T(512)S(1)} %bitcast.637), channel_id=1, source_target_pairs={{0,1},{1,2},{2,3},{4,5},{5,6},{6,7},{8,9},{9,10},{10,11},{12,13},{... | collective-permute-start | bytes 6152 | tf_op jit(solution)/shard_map/ppermute | solution.py:24
  450.3 35.3 %shard_map.284 = (bf16[2,512,1024]{2,1,0:T(8,128)(2,1)}, f32[16,1,512]{2,1,0:T(1,128)}) custom-call(s32[1]{0:T(128)} %bitcast.rank, f32[512,2048]{1,0:T(8,128)} %get-tuple-element.286.q_ref.lin_ref, f32[1536,2048]{1,0:T(8,128)} %get-tuple-element.287.k_ref.lin_ref, bf16[1536,2048]{1,0:T(8,128)(2,1)} %get-tuple-element.288.v_ref, ...), custom_call_target="tpu_custom_call" | custom-call | flops 4831838208 | bytes 25165824 | tf_op jit(solution)/shard_map/pallas_call | solution.py:673
  536.3 37.4 %collective-permute-done.45 = bf16[256,1024]{1,0:T(8,128)(2,1)} collective-permute-done((bf16[256,1024]{1,0:T(8,128)(2,1)}, bf16[256,1024]{1,0:T(8,128)(2,1)}, u32[]{:S(2)}, u32[]{:S(2)}) %collective-permute-start.45) | collective-permute-done | bytes 524320 | tf_op jit(solution)/shard_map/ppermute | solution.py:1067
  727.5 26.7 %shard_map.292.a_ref = f32[4,1024,512]{2,1,0:T(8,128)} custom-call(bf16[1024,1024]{1,0:T(8,128)(2,1)} %get-tuple-element.348.refs_0_, bf16[1024,1024]{1,0:T(8,128)(2,1)} %get-tuple-element.354.refs_1_, bf16[1024,1024]{1,0:T(8,128)(2,1)} %bitcast.99.ga.refs_2_, bf16[1024,1024]{1,0:T(8,128)(2,1)} %bitcast.100.gb.refs_3_, ...), custom_call_target="tpu_custom_call" | custom-call | flops 17179869184 | bytes 25165824 | tf_op jit(solution)/shard_map/pallas_call | solution.py:989
  786.4 17.0 %collective-permute-done.56 = bf16[512,1024]{1,0:T(8,128)(2,1)} collective-permute-done((bf16[512,1024]{1,0:T(8,128)(2,1)}, bf16[512,1024]{1,0:T(8,128)(2,1)}, u32[]{:S(2)}, u32[]{:S(2)}) %collective-permute-start.56) | collective-permute-done | bytes 1048608 | tf_op jit(solution)/shard_map/ppermute | solution.py:1067
  803.4 21.6 %collective-permute-done.57 = bf16[512,1024]{1,0:T(8,128)(2,1)} collective-permute-done((bf16[512,1024]{1,0:T(8,128)(2,1)}, bf16[512,1024]{1,0:T(8,128)(2,1)}, u32[]{:S(2)}, u32[]{:S(2)}) %collective-permute-start.57) | collective-permute-done | bytes 1048608 | tf_op jit(solution)/shard_map/ppermute | solution.py:1067
  886.2 29.2 %shard_map.294 = (bf16[512,1024]{1,0:T(8,128)(2,1)}, bf16[1536,1024]{1,0:T(8,128)(2,1)}, bf16[1536,1024]{1,0:T(8,128)(2,1)}) custom-call(s32[1]{0:T(128)} %bitcast.rank, f32[512,2048]{1,0:T(8,128)} %get-tuple-element.286.q_ref.lin_ref, f32[1536,2048]{1,0:T(8,128)} %get-tuple-element.287.k_ref.lin_ref, bf16[1536,2048]{1,0:T(8,128)(2,1)} %get-tuple-element.288.v_ref, ...), custom_call_target="tpu_custom_call" | custom-call | flops 6710886400 | bytes 18874368 | tf_op jit(solution)/shard_map/pallas_call | solution.py:750
  923.6 46.7 %collective-permute-done.69 = bf16[256,1024]{1,0:T(8,128)(2,1)S(1)} collective-permute-done((bf16[256,1024]{1,0:T(8,128)(2,1)S(1)}, bf16[256,1024]{1,0:T(8,128)(2,1)S(1)}, u32[]{:S(2)}, u32[]{:S(2)}) %collective-permute-start.69) | collective-permute-done | bytes 524320 | tf_op jit(solution)/shard_map/ppermute | solution.py:1067
  1011.6 18.9 %collective-permute-done.73 = bf16[512,1024]{1,0:T(8,128)(2,1)S(1)} collective-permute-done((bf16[512,1024]{1,0:T(8,128)(2,1)S(1)}, bf16[512,1024]{1,0:T(8,128)(2,1)S(1)}, u32[]{:S(2)}, u32[]{:S(2)}) %collective-permute-start.73) | collective-permute-done | bytes 1048608 | tf_op jit(solution)/shard_map/ppermute | solution.py:1067
  1040.4 28.8 %shard_map.295 = (bf16[512,1024]{1,0:T(8,128)(2,1)}, bf16[1536,1024]{1,0:T(8,128)(2,1)}, bf16[1536,1024]{1,0:T(8,128)(2,1)}) custom-call(s32[1]{0:T(128)} %bitcast.rank, f32[512,2048]{1,0:T(8,128)} %get-tuple-element.286.q_ref.lin_ref, f32[1536,2048]{1,0:T(8,128)} %get-tuple-element.287.k_ref.lin_ref, bf16[1536,2048]{1,0:T(8,128)(2,1)} %get-tuple-element.288.v_ref, ...), custom_call_target="tpu_custom_call" | custom-call | flops 6710886400 | bytes 18874368 | tf_op jit(solution)/shard_map/pallas_call | solution.py:750
  1078.1 20.8 %shard_map.297 = (bf16[1536,2048]{1,0:T(8,128)(2,1)}, f32[1,2048]{1,0:T(1,128)}) custom-call(bf16[1536,1024]{1,0:T(8,128)(2,1)} %get-tuple-element.397.low_ref, bf16[1536,1024]{1,0:T(8,128)(2,1)} %get-tuple-element.398.high_ref, f32[1536,2048]{1,0:T(8,128)} %get-tuple-element.287.k_ref.lin_ref, f32[1536,1]{1,0:T(8,128)} %add_rsqrt_fusion.sk_ref.scale_ref, ...), custom_call_target="tpu_custom_call" | custom-call | flops 31457280 | bytes 25165824 | tf_op jit(solution)/shard_map/pallas_call | solution.py:818
  1128.5 50.5 %shard_map.298.g_ref = f32[2,1536,1024]{2,1,0:T(8,128)} custom-call(bf16[1536,2048]{1,0:T(8,128)(2,1)} %get-tuple-element.421.k_ref, bf16[1536,1024]{1,0:T(8,128)(2,1)} %get-tuple-element.414.v_ref, bf16[1536,1024]{1,0:T(8,128)(2,1)} %get-tuple-element.415.w_ref, bf16[512,2048]{1,0:T(8,128)(2,1)} %get-tuple-element.420.q_ref, ...), custom_call_target="tpu_custom_call" | custom-call | flops 28991029248 | bytes 67108864 | tf_op jit(solution)/shard_map/pallas_call | solution.py:528
  1249.6 51.7 %collective-permute-start.94 = (bf16[2,64,1024]{2,1,0:T(8,128)(2,1)S(1)}, bf16[2,64,1024]{2,1,0:T(8,128)(2,1)S(1)}, u32[]{:S(2)}, u32[]{:S(2)}) collective-permute-start(bf16[2,64,1024]{2,1,0:T(8,128)(2,1)S(1)} %get-tuple-element.525), channel_id=1, source_target_pairs={{0,1},{1,2},{2,3},{3,0},{4,5},{5,6},{6,7},{7,4},{8,9},{9,10},{10,1... | collective-permute-start | bytes 786440 | tf_op jit(solution)/shard_map/ppermute | solution.py:1072
  1326.8 38.4 %collective-permute-done.92 = bf16[2,256,1024]{2,1,0:T(8,128)(2,1)S(1)} collective-permute-done((bf16[2,256,1024]{2,1,0:T(8,128)(2,1)}, bf16[2,256,1024]{2,1,0:T(8,128)(2,1)S(1)}, u32[]{:S(2)}, u32[]{:S(2)}) %collective-permute-start.92) | collective-permute-done | bytes 1048608 | tf_op jit(solution)/shard_map/ppermute | solution.py:1083
  1383.1 20.1 %collective-permute-done.99 = bf16[256,1024]{1,0:T(8,128)(2,1)S(1)} collective-permute-done((bf16[256,1024]{1,0:T(8,128)(2,1)S(1)}, bf16[256,1024]{1,0:T(8,128)(2,1)S(1)}, u32[]{:S(2)}, u32[]{:S(2)}) %collective-permute-start.99) | collective-permute-done | bytes 524320 | tf_op jit(solution)/shard_map/ppermute | solution.py:1067
  1418.1 18.9 %collective-permute-done.102 = bf16[2,512,1024]{2,1,0:T(8,128)(2,1)S(1)} collective-permute-done((bf16[2,512,1024]{2,1,0:T(8,128)(2,1)S(1)}, bf16[2,512,1024]{2,1,0:T(8,128)(2,1)S(1)}, u32[]{:S(2)}, u32[]{:S(2)}) %collective-permute-start.102) | collective-permute-done | bytes 2097184 | tf_op jit(solution)/shard_map/ppermute | solution.py:1083
  1487.7 22.0 %collective-permute-done.111 = f32[9,2048]{1,0:T(8,128)S(1)} collective-permute-done((f32[9,2048]{1,0:T(8,128)S(1)}, f32[9,2048]{1,0:T(8,128)S(1)}, u32[]{:S(2)}, u32[]{:S(2)}) %collective-permute-start.111) | collective-permute-done | bytes 73760 | tf_op jit(solution)/shard_map/ppermute | solution.py:1072
  (803 shorter events, 822.3 us)
Async XLA Ops:
  166.3 131.5 %collective-permute-start.17 = (bf16[1024,2048]{1,0:T(8,128)(2,1)}, bf16[1024,2048]{1,0:T(8,128)(2,1)}, u32[]{:S(2)}, u32[]{:S(2)}) collective-permute-start(bf16[1024,2048]{1,0:T(8,128)(2,1)} %pad_maximum_fusion.2.a_ref.ka), channel_id=1, source_target_pairs={{0,4},{4,0},{8,12},{12,8},{16,20},{20,16},{24,28},{28,24},{1,5},{5... | collective-permute-start | bytes 12582920 | tf_op jit(solution)/shard_map/ppermute | solution.py:1067
  180.6 117.2 %collective-permute-start.18 = (bf16[1024,2048]{1,0:T(8,128)(2,1)}, bf16[1024,2048]{1,0:T(8,128)(2,1)}, u32[]{:S(2)}, u32[]{:S(2)}) collective-permute-start(bf16[1024,2048]{1,0:T(8,128)(2,1)} %pad_maximum_fusion.3.a_ref.va), channel_id=1, source_target_pairs={{0,4},{4,0},{8,12},{12,8},{16,20},{20,16},{24,28},{28,24},{1,5},{5... | collective-permute-start | bytes 12582920 | tf_op jit(solution)/shard_map/ppermute | solution.py:1067
  188.3 69.5 %collective-permute-start.21 = (bf16[512,1024]{1,0:T(8,128)(2,1)}, bf16[512,1024]{1,0:T(8,128)(2,1)}, u32[]{:S(2)}, u32[]{:S(2)}) collective-permute-start(bf16[512,1024]{1,0:T(8,128)(2,1)} %get-tuple-element.511), channel_id=1, source_target_pairs={{0,8},{4,12},{8,0},{12,4},{16,24},{20,28},{24,16},{28,20},{1,9},{5... | collective-permute-start | bytes 3145736 | tf_op jit(solution)/shard_map/ppermute | solution.py:1067
  208.6 89.3 %collective-permute-start.23 = (bf16[2,512,1024]{2,1,0:T(8,128)(2,1)}, bf16[2,512,1024]{2,1,0:T(8,128)(2,1)}, u32[]{:S(2)}, u32[]{:S(2)}) collective-permute-start(bf16[2,512,1024]{2,1,0:T(8,128)(2,1)} %collective-permute-done.6), channel_id=1, source_target_pairs={{1,2},{6,5},{9,10},{14,13},{17,18},{22,21},{25,26},{30,29}} | collective-permute-start | bytes 6291464 | tf_op jit(solution)/shard_map/ppermute | solution.py:1083
  210.6 87.2 %collective-permute-start.16 = (bf16[512,2048]{1,0:T(8,128)(2,1)}, bf16[512,2048]{1,0:T(8,128)(2,1)}, u32[]{:S(2)}, u32[]{:S(2)}) collective-permute-start(bf16[512,2048]{1,0:T(8,128)(2,1)} %collective-permute-done.14), channel_id=1, source_target_pairs={{0,1},{1,2},{2,3},{4,5},{5,6},{6,7},{8,9},{9,10},{10,11},{12,13},{... | collective-permute-start | bytes 6291464 | tf_op jit(solution)/shard_map/ppermute | solution.py:24
  306.8 110.7 %collective-permute-start.27 = (bf16[2,512,1024]{2,1,0:T(8,128)(2,1)S(1)}, bf16[2,512,1024]{2,1,0:T(8,128)(2,1)}, u32[]{:S(2)}, u32[]{:S(2)}) collective-permute-start(bf16[2,512,1024]{2,1,0:T(8,128)(2,1)S(1)} %pad_maximum_fusion.15), channel_id=1, source_target_pairs={{0,16},{4,20},{8,24},{12,28},{16,0},{20,4},{24,8},{28,12},{1,17},{... | collective-permute-start | bytes 6291464 | tf_op jit(solution)/shard_map/ppermute | solution.py:1067
  310.0 107.5 %collective-permute-start.28 = (bf16[2,512,1024]{2,1,0:T(8,128)(2,1)S(1)}, bf16[2,512,1024]{2,1,0:T(8,128)(2,1)}, u32[]{:S(2)}, u32[]{:S(2)}) collective-permute-start(bf16[2,512,1024]{2,1,0:T(8,128)(2,1)S(1)} %pad_maximum_fusion.16), channel_id=1, source_target_pairs={{0,8},{4,12},{8,0},{12,4},{16,24},{20,28},{24,16},{28,20},{1,9},{5... | collective-permute-start | bytes 6291464 | tf_op jit(solution)/shard_map/ppermute | solution.py:1067
  311.6 106.9 %collective-permute-start.29 = (bf16[2,512,1024]{2,1,0:T(8,128)(2,1)}, bf16[2,512,1024]{2,1,0:T(8,128)(2,1)}, u32[]{:S(2)}, u32[]{:S(2)}) collective-permute-start(bf16[2,512,1024]{2,1,0:T(8,128)(2,1)} %collective-permute-done.23), channel_id=1, source_target_pairs={{2,3},{5,4},{10,11},{13,12},{18,19},{21,20},{26,27},{29,28}} | collective-permute-start | bytes 6291464 | tf_op jit(solution)/shard_map/ppermute | solution.py:1083
  842.2 73.2 %collective-permute-start.71 = (bf16[1024,1024]{1,0:T(8,128)(2,1)}, bf16[1024,1024]{1,0:T(8,128)(2,1)}, u32[]{:S(2)}, u32[]{:S(2)}) collective-permute-start(bf16[1024,1024]{1,0:T(8,128)(2,1)} %convolution_convert_fusion.2), channel_id=1, source_target_pairs={{0,4},{4,0},{8,12},{12,8},{16,20},{20,16},{24,28},{28,24},{1,5},{5... | collective-permute-start | bytes 6291464 | tf_op jit(solution)/shard_map/ppermute | solution.py:1067
  869.0 101.4 %collective-permute-start.62 = (bf16[1024,1024]{1,0:T(8,128)(2,1)}, bf16[1024,1024]{1,0:T(8,128)(2,1)}, u32[]{:S(2)}, u32[]{:S(2)}) collective-permute-start(bf16[1024,1024]{1,0:T(8,128)(2,1)} %fusion.61), channel_id=1, source_target_pairs={{0,8},{4,12},{8,0},{12,4},{16,24},{20,28},{24,16},{28,20},{1,9},{5... | collective-permute-start | bytes 6291464 | tf_op jit(solution)/shard_map/ppermute | solution.py:1067
  878.8 91.6 %collective-permute-start.63 = (bf16[1024,1024]{1,0:T(8,128)(2,1)}, bf16[1024,1024]{1,0:T(8,128)(2,1)}, u32[]{:S(2)}, u32[]{:S(2)}) collective-permute-start(bf16[1024,1024]{1,0:T(8,128)(2,1)} %fusion.64), channel_id=1, source_target_pairs={{0,8},{4,12},{8,0},{12,4},{16,24},{20,28},{24,16},{28,20},{1,9},{5... | collective-permute-start | bytes 6291464 | tf_op jit(solution)/shard_map/ppermute | solution.py:1067
  880.3 90.1 %collective-permute-start.64 = (bf16[1024,1024]{1,0:T(8,128)(2,1)}, bf16[1024,1024]{1,0:T(8,128)(2,1)}, u32[]{:S(2)}, u32[]{:S(2)}) collective-permute-start(bf16[1024,1024]{1,0:T(8,128)(2,1)} %fusion.67), channel_id=1, source_target_pairs={{0,16},{4,20},{8,24},{12,28},{16,0},{20,4},{24,8},{28,12},{1,17},{... | collective-permute-start | bytes 6291464 | tf_op jit(solution)/shard_map/ppermute | solution.py:1067
  880.8 90.7 %collective-permute-start.65 = (bf16[1024,1024]{1,0:T(8,128)(2,1)}, bf16[1024,1024]{1,0:T(8,128)(2,1)}, u32[]{:S(2)}, u32[]{:S(2)}) collective-permute-start(bf16[1024,1024]{1,0:T(8,128)(2,1)} %fusion.70), channel_id=1, source_target_pairs={{0,16},{4,20},{8,24},{12,28},{16,0},{20,4},{24,8},{28,12},{1,17},{... | collective-permute-start | bytes 6291464 | tf_op jit(solution)/shard_map/ppermute | solution.py:1067
  990.0 109.0 %collective-permute-start.78 = (bf16[2,2,256,1024]{3,2,1,0:T(8,128)(2,1)S(1)}, bf16[2,2,256,1024]{3,2,1,0:T(8,128)(2,1)S(1)}, u32[]{:S(2)}, u32[]{:S(2)}) collective-permute-start(bf16[2,2,256,1024]{3,2,1,0:T(8,128)(2,1)S(1)} %pad_maximum_fusion.20), channel_id=1, source_target_pairs={{3,2},{4,5},{11,10},{12,13},{19,18},{20,21},{27,26},{28,29}} | collective-permute-start | bytes 6291464 | tf_op jit(solution)/shard_map/ppermute | solution.py:1083
  996.6 102.4 %collective-permute-start.75 = (bf16[512,1024]{1,0:T(8,128)(2,1)}, bf16[512,1024]{1,0:T(8,128)(2,1)}, u32[]{:S(2)}, u32[]{:S(2)}) collective-permute-start(bf16[512,1024]{1,0:T(8,128)(2,1)} %slice.781), channel_id=1, source_target_pairs={{0,8},{4,12},{8,0},{12,4},{16,24},{20,28},{24,16},{28,20},{1,9},{5... | collective-permute-start | bytes 3145736 | tf_op jit(solution)/shard_map/ppermute | solution.py:1067
  1011.1 87.9 %collective-permute-start.76 = (bf16[2,256,1024]{2,1,0:T(8,128)(2,1)}, bf16[2,256,1024]{2,1,0:T(8,128)(2,1)}, u32[]{:S(2)}, u32[]{:S(2)}) collective-permute-start(bf16[2,256,1024]{2,1,0:T(8,128)(2,1)} %slice_bitcast_fusion.5), channel_id=1, source_target_pairs={{0,8},{4,12},{8,0},{12,4},{16,24},{20,28},{24,16},{28,20},{1,9},{5... | collective-permute-start | bytes 3145736 | tf_op jit(solution)/shard_map/ppermute | solution.py:1067
  1030.5 68.5 %collective-permute-start.77 = (bf16[2,256,1024]{2,1,0:T(8,128)(2,1)}, bf16[2,256,1024]{2,1,0:T(8,128)(2,1)}, u32[]{:S(2)}, u32[]{:S(2)}) collective-permute-start(bf16[2,256,1024]{2,1,0:T(8,128)(2,1)} %slice_bitcast_fusion.19), channel_id=1, source_target_pairs={{0,16},{4,20},{8,24},{12,28},{16,0},{20,4},{24,8},{28,12},{1,17},{... | collective-permute-start | bytes 3145736 | tf_op jit(solution)/shard_map/ppermute | solution.py:1067
  1101.4 103.0 %collective-permute-start.82 = (bf16[2,2,256,1024]{3,2,1,0:T(8,128)(2,1)}, bf16[2,2,256,1024]{3,2,1,0:T(8,128)(2,1)}, u32[]{:S(2)}, u32[]{:S(2)}) collective-permute-start(bf16[2,2,256,1024]{3,2,1,0:T(8,128)(2,1)} %add_convert_fusion.6), channel_id=1, source_target_pairs={{2,1},{5,6},{10,9},{13,14},{18,17},{21,22},{26,25},{29,30}} | collective-permute-start | bytes 6291464 | tf_op jit(solution)/shard_map/ppermute | solution.py:1083
  1112.9 91.5 %collective-permute-start.83 = (bf16[2,2,512,1024]{3,2,1,0:T(8,128)(2,1)}, bf16[2,2,512,1024]{3,2,1,0:T(8,128)(2,1)}, u32[]{:S(2)}, u32[]{:S(2)}) collective-permute-start(bf16[2,2,512,1024]{3,2,1,0:T(8,128)(2,1)} %pad_maximum_fusion.7), channel_id=1, source_target_pairs={{3,2},{4,5},{11,10},{12,13},{19,18},{20,21},{27,26},{28,29}} | collective-permute-start | bytes 12582920 | tf_op jit(solution)/shard_map/ppermute | solution.py:1083
  1115.7 88.7 %collective-permute-start.84 = (bf16[2,512,1024]{2,1,0:T(8,128)(2,1)}, bf16[2,512,1024]{2,1,0:T(8,128)(2,1)}, u32[]{:S(2)}, u32[]{:S(2)}) collective-permute-start(bf16[2,512,1024]{2,1,0:T(8,128)(2,1)} %get-tuple-element.500), channel_id=1, source_target_pairs={{0,1},{7,6},{8,9},{15,14},{16,17},{23,22},{24,25},{31,30}} | collective-permute-start | bytes 6291464 | tf_op jit(solution)/shard_map/ppermute | solution.py:1083
  1208.9 97.9 %collective-permute-start.89 = (bf16[1024,2048]{1,0:T(8,128)(2,1)}, bf16[1024,2048]{1,0:T(8,128)(2,1)}, u32[]{:S(2)}, u32[]{:S(2)}) collective-permute-start(bf16[1024,2048]{1,0:T(8,128)(2,1)} %convolution_convert_fusion.1), channel_id=1, source_target_pairs={{0,4},{4,0},{8,12},{12,8},{16,20},{20,16},{24,28},{28,24},{1,5},{5... | collective-permute-start | bytes 12582920 | tf_op jit(solution)/shard_map/ppermute | solution.py:1067
  1217.7 90.5 %collective-permute-start.90 = (bf16[1024,2048]{1,0:T(8,128)(2,1)}, bf16[1024,2048]{1,0:T(8,128)(2,1)}, u32[]{:S(2)}, u32[]{:S(2)}) collective-permute-start(bf16[1024,2048]{1,0:T(8,128)(2,1)} %convolution_convert_fusion), channel_id=1, source_target_pairs={{0,4},{4,0},{8,12},{12,8},{16,20},{20,16},{24,28},{28,24},{1,5},{5... | collective-permute-start | bytes 12582920 | tf_op jit(solution)/shard_map/ppermute | solution.py:1067
  1233.2 132.0 %collective-permute-start.93 = (bf16[2,2,512,1024]{3,2,1,0:T(8,128)(2,1)S(1)}, bf16[2,2,512,1024]{3,2,1,0:T(8,128)(2,1)S(1)}, u32[]{:S(2)}, u32[]{:S(2)}) collective-permute-start(bf16[2,2,512,1024]{3,2,1,0:T(8,128)(2,1)S(1)} %add_convert_fusion), channel_id=1, source_target_pairs={{2,1},{5,6},{10,9},{13,14},{18,17},{21,22},{26,25},{29,30}} | collective-permute-start | bytes 12582920 | tf_op jit(solution)/shard_map/ppermute | solution.py:1083
  1467.8 68.7 %collective-permute-start.116 = (bf16[2,64,2048]{2,1,0:T(8,128)(2,1)}, bf16[2,64,2048]{2,1,0:T(8,128)(2,1)S(1)}, u32[]{:S(2)}, u32[]{:S(2)}) collective-permute-start(bf16[2,64,2048]{2,1,0:T(8,128)(2,1)} %get-tuple-element.499), channel_id=1, source_target_pairs={{0,3},{1,0},{2,1},{3,2},{4,7},{5,4},{6,5},{7,6},{8,11},{9,8},{10,9... | collective-permute-start | bytes 1572872 | tf_op jit(solution)/shard_map/ppermute | solution.py:1072
  (239 other events, 4893.9 us)

commit v4 on v3

--- a/solution.py
+++ b/solution.py
@@ -451,9 +451,6 @@
             jax.ShapeDtypeStruct((2, rows, width // 2), jnp.bfloat16),
             jax.ShapeDtypeStruct((rows, 1), jnp.float32),
         ],
-        cost_estimate=pl.CostEstimate(
-            flops=8 * rows * width, bytes_accessed=4 * rows * width, transcendentals=0
-        ),
     )(rank, value, gain[None])
 
 
@@ -487,24 +484,23 @@
             jax.ShapeDtypeStruct((rows, width), dtype),
             jax.ShapeDtypeStruct((rows, 1), jnp.float32),
         ],
-        cost_estimate=pl.CostEstimate(
-            flops=4 * rows * depth * width, bytes_accessed=8 * depth * width, transcendentals=0
-        ),
     )(halves, halves, a, b)
 
 
-def project_back_kernel(k_ref, v_ref, w_ref, q_ref, ka, kb, va, vb, qa, qb, o_ref, *, own):
-    i, j = pl.program_id(0), pl.program_id(1)
-    half = pl.num_programs(1) // 2
+def project_back_kernel(k_ref, v_ref, w_ref, q_ref, ka, kb, va, vb, qa, qb, o_ref, *, tile):
+    j = pl.program_id(0)
+    half = pl.num_programs(0) // 2
+    half_width = v_ref.shape[1]
+    own = k_ref.shape[0] - q_ref.shape[0]
 
     def part(key, value, query):
-        half_width = v_ref.shape[1]
-        total = dot_t(k_ref[...], key[...]) + dot_t(v_ref[...], value[:, :half_width])
-        o_ref[0] = total + dot_t(w_ref[...], value[:, half_width:])
-
-        @pl.when(i >= own)
-        def _():
-            o_ref[0] += dot_t(q_ref[...], query[...])
+        for start in range(0, k_ref.shape[0], tile):
+            at = slice(start, start + tile)
+            total = dot_t(k_ref[at, :], key[...]) + dot_t(v_ref[at, :], value[:, :half_width])
+            total += dot_t(w_ref[at, :], value[:, half_width:])
+            if start >= own:
+                total += dot_t(q_ref[start - own : start - own + tile, :], query[...])
+            o_ref[0, at, :] = total
 
     @pl.when(j < half)
     def _():
@@ -517,42 +513,27 @@
 
 def project_back(key, value, value_high, query, key_w, value_w, query_w):
     rows, width = key.shape
-    depth = key_w[0].shape[0]
-    tile, step = 512, 512
+    depth = value_w[0].shape[0]
+    step = 256
     half = depth // step
-    own = (rows - query.shape[0]) // tile
-    x_spec = pl.BlockSpec((tile, width), lambda i, j: (i, 0))
-    half_spec = pl.BlockSpec((tile, width // 2), lambda i, j: (i, 0))
-    low = pl.BlockSpec((step, width), lambda i, j: (jnp.minimum(j, half - 1), 0))
-    high = pl.BlockSpec((step, width), lambda i, j: (jnp.maximum(j - half, 0), 0))
+    whole = lambda value: pl.BlockSpec(value.shape, lambda j: (0, 0), pipeline_mode=pl.Buffered(1))
+    low = pl.BlockSpec((step, width), lambda j: (jnp.minimum(j, half - 1), 0))
+    high = pl.BlockSpec((step, width), lambda j: (jnp.maximum(j - half, 0), 0))
     return kernel_call(
-        functools.partial(project_back_kernel, own=own),
-        grid=(rows // tile, 2 * half),
-        in_specs=[
-            x_spec,
-            half_spec,
-            half_spec,
-            pl.BlockSpec((tile, width), lambda i, j: (jnp.maximum(i - own, 0), 0)),
-        ]
-        + [low, high] * 3,
-        out_specs=pl.BlockSpec((1, tile, step), lambda i, j: (j // half, i, j % half)),
+        functools.partial(project_back_kernel, tile=512),
+        grid=(2 * half,),
+        in_specs=[whole(key), whole(value), whole(value_high), whole(query)] + [low, high] * 3,
+        out_specs=pl.BlockSpec((1, rows, step), lambda j: (j // half, 0, j % half)),
         out_shape=jax.ShapeDtypeStruct((2, rows, depth), jnp.float32),
-        cost_estimate=pl.CostEstimate(
-            flops=9 * rows * depth * width, bytes_accessed=32 * depth * width, transcendentals=0
-        ),
     )(key, value, value_high, query, *key_w, *value_w, *query_w)
 
 
 def tokens_back_kernel(
-    rank, g_ref, c_ref, x_ref, res_ref, scale_ref, gain_ref, o_ref, gain_grad_ref, *, blocks
+    rank, g_ref, c_ref, x_ref, res_ref, scale_ref, gain_ref, o_ref, *, blocks
 ):
     scale = scale_ref[...]
     block = x_ref.shape[1] // blocks
     half = blocks // 2
-
-    @pl.when(pl.program_id(0) == 0)
-    def _():
-        gain_grad_ref[...] = jnp.zeros_like(gain_grad_ref)
 
     def pieces(place):
         start = pl.multiple_of((rank[0] ^ code_of(place, blocks)) * block, block)
@@ -564,9 +545,7 @@
     inner = jnp.zeros_like(scale)
     for place in range(blocks):
         columns, grad, value, gain = pieces(place)
-        product = grad * value
-        inner += jnp.sum(product * gain, axis=1, keepdims=True)
-        gain_grad_ref[:, columns] += jnp.sum(product * scale, axis=0, keepdims=True)
+        inner += jnp.sum(grad * value * gain, axis=1, keepdims=True)
     inner = inner * (1.0 / x_ref.shape[1]) * (scale * scale * scale)
     for place in range(blocks):
         columns, grad, value, gain = pieces(place)
@@ -592,15 +571,9 @@
                 pl.BlockSpec((tile, 1), lambda i, rank: (i + first, 0)),
                 one,
             ],
-            out_specs=[wide, one],
+            out_specs=wide,
         ),
-        out_shape=[
-            jax.ShapeDtypeStruct((rows, width), jnp.float32),
-            jax.ShapeDtypeStruct((1, width), jnp.float32),
-        ],
-        cost_estimate=pl.CostEstimate(
-            flops=10 * rows * width, bytes_accessed=16 * rows * width, transcendentals=0
-        ),
+        out_shape=jax.ShapeDtypeStruct((rows, width), jnp.float32),
     )(rank, grad, carried, tokens, residual_grad, scale, gain[None])
 
 
@@ -642,13 +615,12 @@
     cos_ref,
     sin_ref,
     bias_ref,
-    o_ref,
-    lse_ref,
-    *,
+    *refs,
     behind,
     tile,
     span,
 ):
+    o_ref, lse_ref = refs[-2:]
     rows = q_ref.shape[0]
     cosine, sine = cos_ref[...], sin_ref[...]
     keys = head_rows(k_ref[...], sk_ref[...], gk_ref[...], cosine, sine)
@@ -666,7 +638,7 @@
         lse_ref[0, :, at] = peak + jnp.log(total)
 
 
-def attend(rank, operands, bias):
+def attend(rank, operands, bias, first, into=()):
     rows, width = operands[0].shape
     all_rows = operands[1].shape[0]
     tiles, span, tile = bias.shape
@@ -674,23 +646,20 @@
         functools.partial(attend_kernel, behind=all_rows - rows, tile=tile, span=span),
         grid_spec=pltpu.PrefetchScalarGridSpec(
             num_scalar_prefetch=1,
-            grid=(HEADS,),
-            in_specs=attention_specs(rows, all_rows, bias),
+            grid=(HEADS // 2,),
+            in_specs=attention_specs(rows, all_rows, bias, first)
+            + [pl.BlockSpec(memory_space=pl.ANY)] * len(into),
             out_specs=[
-                pl.BlockSpec((1, rows, HEAD_DIM), moved_head),
+                pl.BlockSpec((1, rows, HEAD_DIM), lambda h, rank: moved_head(h + first, rank)),
                 pl.BlockSpec((1, 1, rows), lambda h, rank: (h, 0, 0)),
             ],
         ),
+        input_output_aliases={2 + len(operands): 0} if into else {},
         out_shape=[
             jax.ShapeDtypeStruct((2, rows, width // 2), jnp.bfloat16),
-            jax.ShapeDtypeStruct((HEADS, 1, rows), jnp.float32),
+            jax.ShapeDtypeStruct((HEADS // 2, 1, rows), jnp.float32),
         ],
-        cost_estimate=pl.CostEstimate(
-            flops=4 * rows * span * width,
-            bytes_accessed=8 * all_rows * width,
-            transcendentals=rows * span * HEADS,
-        ),
-    )(rank, *operands, bias)
+    )(rank, *operands, bias, *into)
 
 
 def attend_back_kernel(
@@ -755,7 +724,7 @@
             in_specs=attention_specs(rows, all_rows, bias, first)
             + [
                 pl.BlockSpec((1, rows, HEAD_DIM), lambda h, rank: moved_head(h + first, rank)),
-                pl.BlockSpec((1, 1, rows), lambda h, rank: (h + first, 0, 0)),
+                pl.BlockSpec((1, 1, rows), lambda h, rank: (h, 0, 0)),
             ],
             out_specs=[
                 pl.BlockSpec((rows, HEAD_DIM), head),
@@ -772,40 +741,36 @@
             jax.ShapeDtypeStruct((all_rows, width), jnp.bfloat16),
             jax.ShapeDtypeStruct((all_rows, width), jnp.bfloat16),
         ],
-        cost_estimate=pl.CostEstimate(
-            flops=10 * rows * span * width,
-            bytes_accessed=12 * all_rows * width,
-            transcendentals=rows * span * HEADS // 2,
-        ),
     )(rank, *operands, bias, grad, lse)
 
 
-def lin_back_kernel(low_ref, high_ref, lin_ref, scale_ref, gain_ref, cos_ref, sin_ref, o_ref, gain_grad_ref):
-    scale = scale_ref[...]
+def lin_back_kernel(
+    low_ref, high_ref, lin_ref, scale_ref, gain_ref, cos_ref, sin_ref, o_ref, gain_grad_ref, kept
+):
+    rows = scale_ref.shape[0]
+    scale = jnp.broadcast_to(scale_ref[...], (rows, HEAD_DIM))
     cosine, sine = cos_ref[...], -sin_ref[...]
-    inner = jnp.zeros_like(scale)
 
     @pl.when(pl.program_id(0) == 0)
     def _():
         gain_grad_ref[...] = jnp.zeros_like(gain_grad_ref)
 
-    def grad_of(h):
-        ref = low_ref if h < HEADS // 2 else high_ref
-        return ref[:, h % (HEADS // 2) * HEAD_DIM : (h % (HEADS // 2) + 1) * HEAD_DIM]
-
+    inner = jnp.zeros((rows, HEAD_DIM), jnp.float32)
     for h in range(HEADS):
         at = slice(h * HEAD_DIM, (h + 1) * HEAD_DIM)
-        grad = turn(grad_of(h).astype(jnp.float32), cosine, sine)
-        lin = lin_ref[:, at]
-        product = grad * lin
+        ref = low_ref if h < HEADS // 2 else high_ref
+        here = slice(h % (HEADS // 2) * HEAD_DIM, (h % (HEADS // 2) + 1) * HEAD_DIM)
+        grad = turn(ref[:, here].astype(jnp.float32), cosine, sine)
+        product = grad * lin_ref[:, at]
+        gain = gain_ref[:, at]
         gain_grad_ref[:, at] += jnp.sum(product * scale, axis=0, keepdims=True)
-        inner += jnp.sum(product * gain_ref[:, at], axis=1, keepdims=True)
-    inner = inner * (1.0 / (HEADS * HEAD_DIM)) * (scale * scale * scale)
+        inner += product * gain
+        kept[:, at] = grad * gain * scale
+    inner = jnp.sum(inner, axis=1, keepdims=True) * (1.0 / (HEADS * HEAD_DIM))
+    inner = jnp.broadcast_to(inner, (rows, HEAD_DIM)) * (scale * scale * scale)
     for h in range(HEADS):
         at = slice(h * HEAD_DIM, (h + 1) * HEAD_DIM)
-        grad = turn(grad_of(h).astype(jnp.float32), cosine, sine)
-        value = scale * (grad * gain_ref[:, at]) - lin_ref[:, at] * inner
-        o_ref[:, at] = value.astype(jnp.bfloat16)
+        o_ref[:, at] = (kept[:, at] - lin_ref[:, at] * inner).astype(jnp.bfloat16)
 
 
 def lin_back(low, high, lin, scale, gain, cosine, sine):
@@ -820,14 +785,24 @@
         grid=(rows // tile,),
         in_specs=[half, half, wide, pl.BlockSpec((tile, 1), lambda i: (i, 0)), one, table, table],
         out_specs=[wide, one],
+        scratch_shapes=[pltpu.VMEM((tile, width), jnp.float32)],
         out_shape=[
             jax.ShapeDtypeStruct((rows, width), jnp.bfloat16),
             jax.ShapeDtypeStruct((1, width), jnp.float32),
         ],
-        cost_estimate=pl.CostEstimate(
-            flops=10 * rows * width, bytes_accessed=8 * rows * width, transcendentals=0
-        ),
     )(low, high, lin, scale, gain, cosine, sine)
+
+
+def flat(ref):
+    return ref[...].reshape(-1, ref.shape[-1])
+
+
+def gu_spec(weights):
+    return pl.BlockSpec((2, weights.shape[1] // 3 * 2, weights.shape[2]), lambda i, *_: (0, 0, 0))
+
+
+def d_spec(weights):
+    return pl.BlockSpec((2, weights.shape[1] // 3, weights.shape[2]), lambda i, *_: (0, 2, 0))
 
 
 def dynamic_block(index, block):
@@ -835,8 +810,8 @@
 
 
 def experts_up_kernel(rank, x_ref, z_ref, ga, gb, ua, ub, g_ref, u_ref, my_ref, mx_ref, middle_ref):
-    gate = matmul(x_ref[0], ga[...]) + matmul(x_ref[1], gb[...])
-    up = matmul(z_ref[0], ua[...]) + matmul(z_ref[1], ub[...])
+    gate = matmul(x_ref[0], flat(ga)) + matmul(x_ref[1], flat(gb))
+    up = matmul(z_ref[0], flat(ua)) + matmul(z_ref[1], flat(ub))
     g_ref[...] = gate
     u_ref[...] = up
     middle_ref[...] = (gate * jax.nn.sigmoid(gate) * up).astype(jnp.bfloat16)
@@ -850,10 +825,10 @@
 
 def experts_up(rank, by_y, by_x, weights):
     _, rows, depth = by_y.shape
-    hidden = weights[0].shape[1]
+    hidden = weights[0].shape[2]
     tile = 256
     x_spec = pl.BlockSpec((2, tile, depth), lambda i, rank: (0, i, 0))
-    w_spec = pl.BlockSpec((depth, hidden), lambda i, rank: (0, 0))
+    w_spec = gu_spec(weights[0])
     wide = pl.BlockSpec((tile, hidden), lambda i, rank: (i, 0))
     half = pl.BlockSpec((2, tile, hidden // 2), lambda i, rank: (0, i, 0))
     return kernel_call(
@@ -867,67 +842,77 @@
         ),
         out_shape=[jax.ShapeDtypeStruct((rows, hidden), jnp.float32)] * 2
         + [jax.ShapeDtypeStruct((2, rows, hidden // 2), jnp.bfloat16)] * 2,
-        cost_estimate=pl.CostEstimate(
-            flops=8 * rows * depth * hidden, bytes_accessed=30 * rows * hidden, transcendentals=0
-        ),
     )(rank, by_y, by_x, *weights)
 
 
 def experts_down_kernel(*refs):
     gates, slots, outs = refs[:2], (refs[2:8], refs[8:14]), refs[14:]
     half = outs[0].shape[1] // 2
+    mixtures = []
     for side in range(2):
         at = slice(side * half, (side + 1) * half)
         mixture = 0.0
         for slot, (my, mx, la, lb, ra, rb) in enumerate(slots):
             if side == 0:
-                out = matmul(my[0], la[...]) + matmul(my[1], lb[...])
+                out = matmul(my[0], flat(la)) + matmul(my[1], flat(lb))
             else:
-                out = matmul(mx[0], ra[...]) + matmul(mx[1], rb[...])
+                out = matmul(mx[0], flat(ra)) + matmul(mx[1], flat(rb))
             out = out.astype(jnp.bfloat16)
             outs[slot][:, at] = out
             mixture += gates[slot][...] * out.astype(jnp.float32)
-        outs[2][:, at] = mixture
+        mixtures.append(mixture)
+
+    @pl.when(pl.program_id(0) < pl.num_programs(0) // 2)
+    def _():
+        outs[2][:, :half], outs[2][:, half:] = mixtures
+
+    @pl.when(pl.program_id(0) >= pl.num_programs(0) // 2)
+    def _():
+        outs[3][:, :half], outs[3][:, half:] = mixtures
 
 
 def experts_down(gates, slots):
     _, rows, depth = slots[0][0].shape
-    half = slots[0][2].shape[1]
+    half = slots[0][2].shape[2]
     tile = 256
     x_spec = pl.BlockSpec((2, tile, depth), lambda i: (0, i, 0))
-    w_spec = pl.BlockSpec((depth, half), lambda i: (0, 0))
+    w_spec = d_spec(slots[0][2])
     wide = pl.BlockSpec((tile, 2 * half), lambda i: (i, 0))
     column = pl.BlockSpec((tile, 1), lambda i: (i, 0))
+    steps = rows // tile // 2
     return kernel_call(
         experts_down_kernel,
         grid=(rows // tile,),
         in_specs=[column] * 2 + ([x_spec] * 2 + [w_spec] * 4) * 2,
-        out_specs=[wide] * 3,
+        out_specs=[
+            wide,
+            wide,
+            pl.BlockSpec((tile, 2 * half), lambda i: (jnp.minimum(i, steps - 1), 0)),
+            pl.BlockSpec((tile, 2 * half), lambda i: (jnp.maximum(i - steps, 0), 0)),
+        ],
         out_shape=[
             jax.ShapeDtypeStruct((rows, 2 * half), jnp.bfloat16),
             jax.ShapeDtypeStruct((rows, 2 * half), jnp.bfloat16),
-            jax.ShapeDtypeStruct((rows, 2 * half), jnp.float32),
+            jax.ShapeDtypeStruct((rows // 2, 2 * half), jnp.float32),
+            jax.ShapeDtypeStruct((rows // 2, 2 * half), jnp.float32),
         ],
-        cost_estimate=pl.CostEstimate(
-            flops=16 * rows * depth * half, bytes_accessed=24 * rows * half, transcendentals=0
-        ),
     )(*gates, *slots[0], *slots[1])
 
 
 def experts_back_kernel(
-    rank, r_ref, out_ref, gate_ref, g_ref, u_ref, la, lb, ra, rb, p_ref, dg_ref, du_ref, gg_ref
+    rank, own_ref, other_ref, out_ref, gate_ref, g_ref, u_ref, la, lb, ra, rb, p_ref, dg_ref, du_ref, gg_ref
 ):
-    grad = r_ref[...]
+    own = pl.program_id(0) < pl.num_programs(0) // 2
+    grad = jnp.where(own, own_ref[...], other_ref[...])
     gg_ref[...] = jnp.sum(grad * out_ref[...].astype(jnp.float32), axis=1, keepdims=True)
     p_ref[...] = (gate_ref[...] * grad).astype(jnp.bfloat16)
     half = grad.shape[1] // 2
     left, right = p_ref[:, :half], p_ref[:, half:]
-    block = la.shape[0] // 2
-    first, second = slice(0, block), slice(block, 2 * block)
+    block = la.shape[1]
     for j in range(4):
         dy, dx = j // 2, j % 2
-        left_w = (la, lb)[dy][(first, second)[dx], :]
-        right_w = (ra, rb)[dx][(first, second)[dy], :]
+        left_w = (la, lb)[dy][dx]
+        right_w = (ra, rb)[dx][dy]
         middle_grad = dot_t(left, left_w) + dot_t(right, right_w)
         at = dynamic_block(rank[0] ^ j, block)
         gate_pre, up_pre = g_ref[:, at], u_ref[:, at]
@@ -937,20 +922,25 @@
         du_ref[:, at] = (middle_grad * (gate_pre * sigma)).astype(jnp.bfloat16)
 
 
-def experts_back(rank, result_grad, out, gate, gate_pre, up_pre, weights):
-    rows, width = result_grad.shape
+def experts_back(rank, own, other, out, gate, gate_pre, up_pre, weights):
+    rows, width = out.shape
     hidden = gate_pre.shape[1]
     tile = 256
     wide = pl.BlockSpec((tile, width), lambda i, rank: (i, 0))
     narrow = pl.BlockSpec((tile, hidden), lambda i, rank: (i, 0))
     column = pl.BlockSpec((tile, 1), lambda i, rank: (i, 0))
-    w_spec = pl.BlockSpec(weights[0].shape, lambda i, rank: (0, 0))
+    w_spec = d_spec(weights[0])
+    steps = rows // tile // 2
     return kernel_call(
         experts_back_kernel,
         grid_spec=pltpu.PrefetchScalarGridSpec(
             num_scalar_prefetch=1,
             grid=(rows // tile,),
-            in_specs=[wide, wide, column, narrow, narrow] + [w_spec] * 4,
+            in_specs=[
+                pl.BlockSpec((tile, width), lambda i, rank: (jnp.minimum(i, steps - 1), 0)),
+                pl.BlockSpec((tile, width), lambda i, rank: (jnp.maximum(i - steps, 0), 0)),
+                wide, column, narrow, narrow
+            ] + [w_spec] * 4,
             out_specs=[wide, narrow, narrow, column],
         ),
         out_shape=[
@@ -959,42 +949,48 @@
             jax.ShapeDtypeStruct((rows, hidden), jnp.bfloat16),
             jax.ShapeDtypeStruct((rows, 1), jnp.float32),
         ],
-        cost_estimate=pl.CostEstimate(
-            flops=2 * rows * width * hidden, bytes_accessed=26 * rows * hidden, transcendentals=0
-        ),
-    )(rank, result_grad, out, gate, gate_pre, up_pre, *weights)
+    )(rank, own, other, out, gate, gate_pre, up_pre, *weights)
 
 
 def experts_input_kernel(*refs):
-    o_ref = refs[-1]
-    depth = o_ref.shape[2]
-    first, second = slice(0, depth), slice(depth, 2 * depth)
+    totals = []
     for j in range(4):
         dy, dx = j // 2, j % 2
         total = 0.0
         for dg, du, ga, gb, ua, ub in (refs[:6], refs[6:12]):
-            gate_w = (ga, gb)[dy][(first, second)[dx], :]
-            up_w = (ua, ub)[dx][(first, second)[dy], :]
+            gate_w = (ga, gb)[dy][dx]
+            up_w = (ua, ub)[dx][dy]
             part = dot_t(dg[...], gate_w) + dot_t(du[...], up_w)
             total += part.astype(jnp.bfloat16).astype(jnp.float32)
-        o_ref[j] = total
+        totals.append(total)
+
+    @pl.when(pl.program_id(0) < pl.num_programs(0) // 2)
+    def _():
+        for j in range(4):
+            refs[-2][j] = totals[j]
+
+    @pl.when(pl.program_id(0) >= pl.num_programs(0) // 2)
+    def _():
+        for j in range(4):
+            refs[-1][j] = totals[j]
 
 
 def experts_input(slots):
     rows, hidden = slots[0][0].shape
-    depth = slots[0][2].shape[0] // 2
+    depth = slots[0][2].shape[1] // 3 * 2
     tile = 256
     narrow = pl.BlockSpec((tile, hidden), lambda i: (i, 0))
-    w_spec = pl.BlockSpec((2 * depth, hidden), lambda i: (0, 0))
+    w_spec = gu_spec(slots[0][2])
+    steps = rows // tile // 2
     return kernel_call(
         experts_input_kernel,
         grid=(rows // tile,),
         in_specs=([narrow] * 2 + [w_spec] * 4) * 2,
-        out_specs=pl.BlockSpec((4, tile, depth), lambda i: (0, i, 0)),
-        out_shape=jax.ShapeDtypeStruct((4, rows, depth), jnp.float32),
-        cost_estimate=pl.CostEstimate(
-            flops=32 * rows * depth * hidden, bytes_accessed=48 * rows * depth, transcendentals=0
-        ),
+        out_specs=[
+            pl.BlockSpec((4, tile, depth), lambda i: (0, jnp.minimum(i, steps - 1), 0)),
+            pl.BlockSpec((4, tile, depth), lambda i: (0, jnp.maximum(i - steps, 0), 0)),
+        ],
+        out_shape=[jax.ShapeDtypeStruct((4, rows // 2, depth), jnp.float32)] * 2,
     )(*slots[0], *slots[1])
 
 
@@ -1056,10 +1052,116 @@
             jax.ShapeDtypeStruct((rows, width), jnp.bfloat16),
             jax.ShapeDtypeStruct((1, width), jnp.float32),
         ],
-        cost_estimate=pl.CostEstimate(
-            flops=20 * rows * width, bytes_accessed=22 * rows * width, transcendentals=0
+    )(rank, own, other, logit_grad, router, residual, result_grad, scale, gain[None])
+
+
+def experts_grad_kernel(x_ref, d_ref, m_ref, p_ref, *refs):
+    o_ref = refs[-1]
+    rows, down_rows = x_ref.shape[2], m_ref.shape[2]
+    top, bottom = t_dot(x_ref[0], d_ref[...]), t_dot(m_ref[0], p_ref[...])
+    if len(refs) == 2:
+        top += refs[0][0, :rows].astype(jnp.float32)
+        bottom += refs[0][0, rows:].astype(jnp.float32)
+    o_ref[0, :rows] = top.astype(jnp.bfloat16)
+    o_ref[0, rows:] = bottom.astype(jnp.bfloat16)
+
+
+def experts_grad(inputs, pre_grad, middle, pair, part, side, got=()):
+    _, rows, depth = inputs.shape
+    hidden, down = pre_grad.shape[1], middle.shape[2]
+    step = hidden // 2
+    piece = pl.BlockSpec((1, (depth + down) // 2, step), lambda q, j: (q, 0, j))
+    return kernel_call(
+        experts_grad_kernel,
+        grid=(2, 2),
+        in_specs=[
+            pl.BlockSpec((1, rows, depth // 2), lambda q, j: (part, 0, q)),
+            pl.BlockSpec((rows, step), lambda q, j: (0, j)),
+            pl.BlockSpec((1, rows, down // 2), lambda q, j: (part, 0, q)),
+            pl.BlockSpec((rows, step), lambda q, j: (0, j + 2 * side)),
+        ]
+        + [piece] * len(got),
+        out_specs=piece,
+        out_shape=jax.ShapeDtypeStruct((2, (depth + down) // 2, hidden), jnp.bfloat16),
+    )(inputs, pre_grad, middle, pair, *got)
+
+
+def gain_grad_kernel(rank, g_ref, x_ref, scale_ref, o_ref, *, codes):
+    half = len(codes) // 2
+    block = x_ref.shape[1] // len(codes)
+
+    @pl.when(pl.program_id(0) == 0)
+    def _():
+        o_ref[...] = jnp.zeros_like(o_ref)
+
+    for place, code in enumerate(codes):
+        columns = dynamic_block(rank[0] ^ code, block)
+        grad = g_ref[place // half, :, place % half * block : (place % half + 1) * block]
+        product = grad * (x_ref[:, columns].astype(jnp.float32) * scale_ref[...])
+        o_ref[:, columns] += jnp.sum(product, axis=0, keepdims=True)
+
+
+def gain_grad(rank, grad, value, scale, codes):
+    rows, width = value.shape
+    tile = 256
+    return kernel_call(
+        functools.partial(gain_grad_kernel, codes=codes),
+        grid_spec=pltpu.PrefetchScalarGridSpec(
+            num_scalar_prefetch=1,
+            grid=(rows // tile,),
+            in_specs=[
+                pl.BlockSpec((2, tile, width // 2), lambda i, rank: (0, i, 0)),
+                pl.BlockSpec((tile, width), lambda i, rank: (i, 0)),
+                pl.BlockSpec((tile, 1), lambda i, rank: (i, 0)),
+            ],
+            out_specs=pl.BlockSpec((1, width), lambda i, rank: (0, 0)),
         ),
-    )(rank, own, other, logit_grad, router, residual, result_grad, scale, gain[None])
+        out_shape=jax.ShapeDtypeStruct((1, width), jnp.float32),
+    )(rank, grad, value, scale)
+
+
+def chip_grad_kernel(x_ref, g_ref, *refs):
+    total = t_dot(x_ref[0], g_ref[...])
+    if len(refs) == 2:
+        total += refs[0][...].astype(jnp.float32)
+    refs[-1][...] = total.astype(jnp.bfloat16)
+
+
+def chip_grad(halves, part, grad, start=0, got=()):
+    depth = halves.shape[2]
+    rows, width = grad.shape
+    tile, step = 512, 512
+    piece = pl.BlockSpec((tile, step), lambda i, j: (i, j))
+    return kernel_call(
+        chip_grad_kernel,
+        grid=(depth // tile, width // step),
+        in_specs=[
+            pl.BlockSpec((1, rows, tile), lambda i, j: (part, start // rows, i)),
+            pl.BlockSpec((rows, step), lambda i, j: (0, j)),
+        ]
+        + [piece] * len(got),
+        out_specs=piece,
+        out_shape=jax.ShapeDtypeStruct((depth, width), jnp.bfloat16),
+    )(halves, grad, *got)
+
+
+def mixed_back_kernel(g_ref, a_ref, b_ref, o_ref):
+    for half, ref in enumerate((a_ref, b_ref)):
+        o_ref[half] = dot_t(g_ref[...], ref[...]).astype(jnp.bfloat16)
+
+
+def mixed_back(grad, weights):
+    rows, width = grad.shape
+    depth = weights[0].shape[0]
+    step = 256
+    weight = pl.BlockSpec((step, width), lambda j: (j, 0))
+    return kernel_call(
+        mixed_back_kernel,
+        grid=(depth // step,),
+        in_specs=[pl.BlockSpec((rows, width), lambda j: (0, 0)), weight, weight],
+        out_specs=pl.BlockSpec((2, rows, step), lambda j: (0, 0, j)),
+        out_shape=jax.ShapeDtypeStruct((2, rows, depth), jnp.bfloat16),
+    )(grad, *weights)
 
 
 def across(value, bit):
@@ -1103,13 +1205,6 @@
     return parts
 
 
-def sum_small(value, place):
-    value = value + across(value, 1)
-    value = value + across(value, 2)
-    value = value + across(value, 4)
-    return jnp.sum(over_ep(value, place), axis=0)
-
-
 def hold(*values):
     return lax.optimization_barrier(values)
 
@@ -1122,33 +1217,12 @@
     return across(first, 4), across(second, 2)
 
 
-def chip_sum(halves, grad):
-    sent = across(t_dot(halves[1], grad).astype(jnp.bfloat16), 1)
-    kept = t_dot(halves[0], grad) + sent.astype(jnp.float32)
-    return kept.astype(jnp.bfloat16).reshape(2, 2, -1, grad.shape[1])
-
-
 def add(left, right):
     return (left.astype(jnp.float32) + right.astype(jnp.float32)).astype(jnp.bfloat16)
 
 
-def over_ep_sum(both, place):
-    shard = place[3]
-    experts = lax.axis_size("ep")
-    both = both.reshape(2, experts, both.shape[1] // experts, both.shape[2])
-    total = pick(both, shard, 1).astype(jnp.float32)
-    for steps in range(1, experts):
-        total = total + along(pick(both, lax.rem(shard + steps, experts), 1), steps)
-    return total
-
-
-def part_sum(left, grad):
-    return t_dot(left, grad).astype(jnp.bfloat16)
-
-
-def kept_sum(left, grad, got):
-    total = t_dot(left, grad) + got.astype(jnp.float32)
-    return total.astype(jnp.bfloat16).reshape(2, -1, grad.shape[1])
+def ep_sum(both):
+    return lax.psum_scatter(both, "ep", scatter_dimension=1, tiled=True).astype(jnp.float32)
 
 
 def body(
@@ -1192,7 +1266,6 @@
         ],
         1,
     )
-    small = small.T
     rank = rep.astype(jnp.int32)[None]
     quarter = rep // 2
     quarter_rank = quarter.astype(jnp.int32)[None]
@@ -1203,89 +1276,85 @@
     m = jnp.where(core == 0, shard, experts - 1 - shard)
     quarter_rows = w_gate.shape[1] // 4
     quarter_down = w_down.shape[1] // 4
-    own_gu = jnp.stack(
+
+    def own_part(weight, rows):
+        return lax.dynamic_slice_in_dim(weight[0], quarter * rows, rows, 0)
+
+    down = own_part(w_down, quarter_down)
+    own = jnp.stack(
         [
-            lax.dynamic_slice_in_dim(w[0], quarter * quarter_rows, quarter_rows, 0)
-            for w in (w_gate, w_up)
+            jnp.concatenate([own_part(w_gate, quarter_rows), down[:, :half]], 0),
+            jnp.concatenate([own_part(w_up, quarter_rows), down[:, half:]], 0),
         ]
     )
-    own_d = lax.dynamic_slice_in_dim(w_down[0], quarter * quarter_down, quarter_down, 0)
-    own_d = jnp.stack([own_d[:, :half], own_d[:, half:]])
     segments = segment_ids.reshape(local_rows)
+    shard_rows = w_key.shape[0]
+    columns = small.shape[1]
+    small = small.T
 
     small = over_ep(small, place)
-    kv = over_ep(jnp.stack([w_key, w_value]), place)
-    gu_1 = mirrored(own_gu, [(0, 1), (1, 2)])
-    segment_parts = [segments]
-    for back in range(reach):
-        segment_parts.insert(0, from_behind(segment_parts[0], "ep", 1))
+    parts = over_ep(jnp.stack([w_key, w_value]), place)
+    segments_1 = from_behind(segments, "ep", 1)
+    parts, small, own, tokens_1, segments_1 = hold(parts, small, own, tokens, segments_1)
     qo = jnp.stack([w_query, w_out])
-    small, kv, gu_1, qo, tokens_1, own_gu = hold(small, kv, gu_1, qo, tokens, own_gu)
-
-    qo = over_ep(qo, place)
-    k_w, v_w = kv[:, 0].reshape(-1, width), kv[:, 1].reshape(-1, width)
+
+    qo, parts = hold(qo, parts)
+    qo = lax.all_gather(qo, "ep", axis=0)
+    block = shard_rows * experts
+    k_w, v_w = parts[:, 0].reshape(block, width), parts[:, 1].reshape(block, width)
+    e_1 = mirrored(own, [(0, 1), (1, 2)])
+    small = small.reshape(-1)
+    small = jnp.pad(small, (0, 16 * width - small.shape[0])).reshape(16, width)
+    k_w = jnp.concatenate([k_w, small], 0)
     k_x, v_y = both_ways((k_w, v_w))
-    small = in_order(small, across(small, 1), core, 0)
-    small = in_order(small, across(small, 2), place[1], 0)
-    small = in_order(small, across(small, 4), place[0], 0)
-    qo, k_w, k_x, v_w, v_y, tokens_1, gu_1, own_gu, own_d = hold(
-        qo, k_w, k_x, v_w, v_y, tokens_1, gu_1, own_gu, own_d
-    )
-
-    k_w = jnp.concatenate([k_w, k_x], 0)
+    segments_2 = from_behind(segments_1, "ep", 1)
+    k_w, k_x, v_w, v_y, tokens_1, segments_2 = hold(k_w, k_x, v_w, v_y, tokens_1, segments_2)
+
+    k_w = jnp.stack([k_w, k_x])
     k_y, v_x = other_ways(k_w, jnp.stack([v_w, v_y]))
-    k_w = jnp.concatenate([k_w, k_y], 0)
+    tokens_1 = from_behind(tokens_1, "ep", 1)
+    qo, k_w, k_y, v_w, v_y, v_x, tokens_1 = hold(qo, k_w, k_y, v_w, v_y, v_x, tokens_1)
+
+    small = jnp.concatenate([k_w[:, block : block + 2], k_y[:, block : block + 2]], 0)
+    small = jnp.pad(small.reshape(-1, width), ((0, 8), (0, 0)))
+    k_w = jnp.concatenate([k_w[0, :block], k_w[1, :block], k_y[0, :block], k_y[1, :block], small], 0)
     v_w = jnp.concatenate([v_w, v_x[0], v_y, v_x[1]], 0)
-    token_parts = [from_behind(tokens_1, "ep", 1), tokens]
-    gu_2 = mirrored(jnp.where(m == 2, gu_1, own_gu), [(1, 0), (2, 3)])
-    qo, k_w, v_w, token_1, gu_1, gu_2, own_d = hold(
-        qo, k_w, v_w, token_parts[0], gu_1, gu_2, own_d
-    )
-
-    token_parts[0] = token_1
-    for back in range(reach - 1):
-        token_parts.insert(0, from_behind(token_parts[0], "ep", 1))
     key_w, value_w = (k_w, across(k_w, 1)), (v_w, across(v_w, 1))
     q_w, o_w = qo[:, 0].reshape(-1, width), qo[:, 1].reshape(-1, width)
     q_x, o_y = both_ways((q_w, o_w))
-    gu_b = jnp.where(m == 1, own_gu, jnp.where(m == 2, gu_1, gu_2))
-    b_x, b_y = both_ways(gu_b)
-    gu_3 = mirrored(gu_1, [(1, 2)])
-    d_1 = mirrored(own_d, [(0, 1), (1, 2)])
-    token_0, key_w, value_w, q_w, q_x, o_w, o_y, gu_b, b_x, b_y, gu_3, d_1, own_d = hold(
-        token_parts[0], key_w, value_w, q_w, q_x, o_w, o_y, gu_b, b_x, b_y, gu_3, d_1, own_d
-    )
-    token_parts[0] = token_0
+    tokens_2 = from_behind(tokens_1, "ep", 1)
+    key_w, value_w, q_w, q_x, o_w, o_y, tokens_2, tokens_1, e_1, own = hold(
+        key_w, value_w, q_w, q_x, o_w, o_y, tokens_2, tokens_1, e_1, own
+    )
 
     q_w = jnp.concatenate([q_w, q_x], 0)
     q_y, o_x = other_ways(q_w, jnp.stack([o_w, o_y]))
     q_w = jnp.concatenate([q_w, q_y], 0)
     o_w = jnp.concatenate([o_w, o_x[0], o_y, o_x[1]], 0)
-    gate_b, up_b = jnp.stack([gu_b[0], b_x]), jnp.stack([gu_b[1], b_y])
-    gate_b2, up_b2 = other_ways(gate_b, up_b)
-    gu_4 = mirrored(gu_3, [(2, 3)])
-    d_2 = mirrored(jnp.where(m == 2, d_1, own_d), [(1, 0), (2, 3)])
-    small = jnp.moveaxis(small, 4, 0).reshape(small.shape[4], -1)
+    e_2 = mirrored(jnp.where(m == 2, e_1, own), [(1, 0), (2, 3)])
+    small = jnp.stack([weight[4 * block : 4 * block + 8] for weight in key_w])
+    small = small.reshape(2, 2, 2, -1)[..., : experts * columns * shard_rows]
+    for axis, bit in enumerate((core, place[0], place[1])):
+        small = jnp.where(bit == 1, jnp.flip(small, axis), small)
+    small = small.reshape(2, 2, 2, experts, columns, shard_rows)
+    small = jnp.transpose(small, (4, 1, 2, 0, 3, 5)).reshape(columns, -1)
     gain_attn, gain_query, gain_key, gain_moe = [small[i].astype(f32) for i in range(4)]
     weight_router = small[4 : 4 + experts].T
-    counts = small[4 + experts :, :: attn_gain.shape[0]].astype(f32)
+    counts = small[4 + experts :, ::shard_rows].astype(f32)
     count = jnp.sum(counts[0]) * 16.0 + jnp.sum(counts[1])
-
-    tokens_all = jnp.concatenate(token_parts, 0)
-    key_segments = jnp.concatenate(segment_parts, 0)
+    tokens_all = jnp.concatenate([tokens_2, tokens_1, tokens], 0)
+    key_segments = jnp.concatenate([segments_2, segments_1, segments], 0)
     normed, scale_all = norm_rows(rank, tokens_all, gain_attn, order)
     key_lin, key_squares = project(normed, *key_w, f32)
     value_all, _ = project(normed, *value_w, bf16)
-    q_w, o_w, gate_b2, up_b2, gu_4, d_2, normed, key_lin, value_all = hold(
-        q_w, o_w, gate_b2, up_b2, gu_4, d_2, normed, key_lin, value_all
+    q_w, o_w, e_2, e_1, own, normed, key_lin, value_all = hold(
+        q_w, o_w, e_2, e_1, own, normed, key_lin, value_all
     )
 
     query_w, out_w = (q_w, across(q_w, 1)), (o_w, across(o_w, 1))
-    gu_a = jnp.where(
-        m == 0, own_gu, jnp.where(m == 1, gu_1, jnp.where(m == 2, gu_3, gu_4))
-    )
-    a_x, a_y = both_ways(gu_a)
-    d_3 = mirrored(d_1, [(1, 2)])
+    e_b = jnp.where(m == 1, own, jnp.where(m == 2, e_1, e_2))
+    b_x, b_y = both_ways(e_b)
+    e_3 = mirrored(e_1, [(1, 2)])
     query_lin, query_squares = project(normed, *query_w, f32, behind)
     scale_key = lax.rsqrt(key_squares / width + norm_eps)
     scale_query = lax.rsqrt(query_squares / width + norm_eps)
@@ -1323,16 +1392,14 @@
         cosine,
         sine,
     )
-    mixed, lse = attend(rank, operands, mask_of(local_rows // 4))
-    mixed, lse, out_w, gu_a, a_x, a_y, d_3, d_1, d_2, own_d = hold(
-        mixed, lse, out_w, gu_a, a_x, a_y, d_3, d_1, d_2, own_d
-    )
-
-    gate_a, up_a = jnp.stack([gu_a[0], a_x]), jnp.stack([gu_a[1], a_y])
-    gate_a2, up_a2 = other_ways(gate_a, up_a)
-    d_4 = mirrored(d_3, [(2, 3)])
-    d_b = jnp.where(m == 1, own_d, jnp.where(m == 2, d_1, d_2))
-    b_x, b_y = both_ways(d_b)
+    bias_small = mask_of(local_rows // 4)
+    mixed, lse_0 = attend(rank, operands, bias_small, 0)
+    mixed, out_w, e_b, b_x, b_y, e_3, e_1, own = hold(mixed, out_w, e_b, b_x, b_y, e_3, e_1, own)
+
+    b_0, b_1 = jnp.stack([e_b[0], b_x]), jnp.stack([e_b[1], b_y])
+    b_2, b_3 = other_ways(b_0, b_1)
+    e_4 = mirrored(e_3, [(2, 3)])
+    mixed, lse_1 = attend(rank, operands, bias_small, HEADS // 2, (mixed,))
     branch, _ = project(mixed, *out_w, f32)
     residual = tokens.astype(f32) + branch
     moe, scale_moe = norm_rows(quarter_rank, residual, gain_moe, (0, 1, 2, 3))
@@ -1356,63 +1423,60 @@
     gates_both = jnp.concatenate([gates, across(gates, 1)], 0)
     gates_a = jnp.where(core == 0, gates_both[:, :1], gates_both[:, -1:])
     gates_b = jnp.where(core == 0, gates_both[:, 1:2], gates_both[:, -2:-1])
-    gate_a2, up_a2, d_4, d_b, b_x, b_y, moe_y, moe_x = hold(
-        gate_a2, up_a2, d_4, d_b, b_x, b_y, moe_y, moe_x
-    )
-
-    def flat(value):
-        return value.reshape(-1, value.shape[-1])
-
-    left_b, right_b = jnp.stack([d_b[0], b_x]), jnp.stack([d_b[1], b_y])
-    left_b2, right_b2 = other_ways(left_b, right_b)
-    d_a = jnp.where(m == 0, own_d, jnp.where(m == 1, d_1, jnp.where(m == 2, d_3, d_4)))
-    a_x, a_y = both_ways(d_a)
-    gu_weights_b = (flat(gate_b), flat(gate_b2), flat(up_b), flat(up_b2))
-    gate_pre_b, up_pre_b, my_b, mx_b = experts_up(quarter_rank, moe_y, moe_x, gu_weights_b)
-    left_b2, right_b2, d_a, a_x, a_y, my_b, mx_b, gate_a = hold(
-        left_b2, right_b2, d_a, a_x, a_y, my_b, mx_b, gate_a
-    )
-
-    left_a, right_a = jnp.stack([d_a[0], a_x]), jnp.stack([d_a[1], a_y])
-    left_a2, right_a2 = other_ways(left_a, right_a)
-    gu_weights_a = (flat(gate_a), flat(gate_a2), flat(up_a), flat(up_a2))
-    gate_pre_a, up_pre_a, my_a, mx_a = experts_up(quarter_rank, moe_y, moe_x, gu_weights_a)
-    left_a2, right_a2, my_a, mx_a = hold(left_a2, right_a2, my_a, mx_a)
-    d_weights_a = (flat(left_a), flat(left_a2), flat(right_a), flat(right_a2))
-    d_weights_b = (flat(left_b), flat(left_b2), flat(right_b), flat(right_b2))
-    expert_out_a, expert_out_b, mixture = experts_down(
-        (gates_a, gates_b), ((my_a, mx_a) + d_weights_a, (my_b, mx_b) + d_weights_b)
-    )
-    result = residual + (mixture[:local_rows] + across(mixture[local_rows:], 1))
+    b_0, b_1, b_2, b_3, e_4, e_3, e_1, own, moe_y, moe_x = hold(
+        b_0, b_1, b_2, b_3, e_4, e_3, e_1, own, moe_y, moe_x
+    )
+
+    e_a = jnp.where(m == 0, own, jnp.where(m == 1, e_1, jnp.where(m == 2, e_3, e_4)))
+    a_x, a_y = both_ways(e_a)
+    weights_b = (b_0, b_2, b_1, b_3)
+    gate_pre_b, up_pre_b, my_b, mx_b = experts_up(quarter_rank, moe_y, moe_x, weights_b)
+    e_a, a_x, a_y, my_b, mx_b, moe_y, moe_x = hold(e_a, a_x, a_y, my_b, mx_b, moe_y, moe_x)
+
+    a_0, a_1 = jnp.stack([e_a[0], a_x]), jnp.stack([e_a[1], a_y])
+    a_2, a_3 = other_ways(a_0, a_1)
+    weights_a = (a_0, a_2, a_1, a_3)
+    gate_pre_a, up_pre_a, my_a, mx_a = experts_up(quarter_rank, moe_y, moe_x, weights_a)
+    expert_out_a, expert_out_b, mixture, mixture_other = experts_down(
+        (gates_a, gates_b), ((my_a, mx_a) + weights_a, (my_b, mx_b) + weights_b)
+    )
+    result = residual + (mixture + across(mixture_other, 1))
     output = result.astype(bf16)
     error = result - teacher.astype(f32)
     squares = jnp.sum(valid * jnp.sum(error * error, axis=1))
     result_grad = total_tokens / count * valid[:, None] * error
-    result_grad_both = jnp.concatenate([result_grad, across(result_grad, 1)], 0)
+    result_other = across(result_grad, 1)
 
     pair_b, dg_b, du_b, gate_grad_b = experts_back(
-        quarter_rank, result_grad_both, expert_out_b, gates_b, gate_pre_b, up_pre_b, d_weights_b
-    )
+        quarter_rank,
+        result_grad,
+        result_other,
+        expert_out_b,
+        gates_b,
+        gate_pre_b,
+        up_pre_b,
+        weights_b,
+    )
+    sent_x = experts_grad(moe_x, dg_b, mx_b, pair_b, 1, 0)
+    sent_y = experts_grad(moe_y, du_b, my_b, pair_b, 1, 1)
+    sent_x, sent_y, expert_out_a = hold(sent_x, sent_y, expert_out_a)
+
+    b_x, b_y = both_ways((sent_x, sent_y))
     pair_a, dg_a, du_a, gate_grad_a = experts_back(
-        quarter_rank, result_grad_both, expert_out_a, gates_a, gate_pre_a, up_pre_a, d_weights_a
-    )
-    sent = [
-        part_sum(mx[1], pair[:, :half])
-        for mx, pair in ((mx_a, pair_a), (mx_b, pair_b))
-    ] + [
-        part_sum(my[1], pair[:, half:])
-        for my, pair in ((my_a, pair_a), (my_b, pair_b))
-    ]
-    sent, dg_a, du_a, dg_b, du_b, gate_grad_a, pair_a, pair_b = hold(
-        sent, dg_a, du_a, dg_b, du_b, gate_grad_a, pair_a, pair_b
-    )
-
-    got_d = [across(sent[0], 2), across(sent[1], 2), across(sent[2], 4), across(sent[3], 4)]
-    sent_gu = [part_sum(moe_x[1], grad) for grad in (dg_a, dg_b)] + [
-        part_sum(moe_y[1], grad) for grad in (du_a, du_b)
-    ]
-    input_grad = experts_input(((dg_a, du_a) + gu_weights_a, (dg_b, du_b) + gu_weights_b))
-    input_other = across(input_grad[:, local_rows:], 1)
+        quarter_rank,
+        result_grad,
+        result_other,
+        expert_out_a,
+        gates_a,
+        gate_pre_a,
+        up_pre_a,
+        weights_a,
+    )
+    sent_x = experts_grad(moe_x, dg_a, mx_a, pair_a, 1, 0)
+    sent_y = experts_grad(moe_y, du_a, my_a, pair_a, 1, 1)
+    input_grad, input_other = experts_input(
+        ((dg_a, du_a) + weights_a, (dg_b, du_b) + weights_b)
+    )
     slot_grads = jnp.concatenate([gate_grad_a, gate_grad_b], 1)
     own_slots, partner_slots = slot_grads[:local_rows], across(slot_grads[local_rows:], 1)
     from_low = jnp.where(core == 0, own_slots, partner_slots)
@@ -1421,28 +1485,15 @@
     logit_grad = router_probs * (
         prob_grad - jnp.sum(prob_grad * router_probs, axis=-1, keepdims=True)
     )
-    got_d, sent_gu, input_grad, input_other, logit_grad = hold(
-        got_d, sent_gu, input_grad, input_other, logit_grad
-    )
-
-    got_gu = [
-        across(sent_gu[0], 2),
-        across(sent_gu[1], 2),
-        across(sent_gu[2], 4),
-        across(sent_gu[3], 4),
-    ]
-    kept_d = [
-        kept_sum(mx_a[0], pair_a[:, :half], got_d[0]),
-        kept_sum(mx_b[0], pair_b[:, :half], got_d[1]),
-        kept_sum(my_a[0], pair_a[:, half:], got_d[2]),
-        kept_sum(my_b[0], pair_b[:, half:], got_d[3]),
-    ]
-    got_d = [
-        across(kept_d[0][1], 4),
-        across(kept_d[1][1], 4),
-        across(kept_d[2][1], 2),
-        across(kept_d[3][1], 2),
-    ]
+    b_x, b_y, sent_x, sent_y, input_grad, input_other, logit_grad = hold(
+        b_x, b_y, sent_x, sent_y, input_grad, input_other, logit_grad
+    )
+
+    input_other = across(input_other, 1)
+    a_x, a_y = both_ways((sent_x, sent_y))
+    b_0 = experts_grad(moe_x, dg_b, mx_b, pair_b, 0, 0, (b_x,))
+    b_1 = experts_grad(moe_y, du_b, my_b, pair_b, 0, 1, (b_y,))
+    b_y, b_x = other_ways(b_0[1], b_1[1])
     router_local = jnp.concatenate(
         [
             jnp.dot(part.T.astype(f32), logit_grad, precision=highest, preferred_element_type=f32)
@@ -1463,225 +1514,58 @@
         scale_moe,
         gain_moe,
     )
-    out_a = chip_sum(mixed, branch_grad[:, :half])
-    out_b = chip_sum(mixed, branch_grad[:, half:])
-    mixed_grad = jnp.stack([dot_t(branch_grad, weight).astype(bf16) for weight in out_w])
+    out_sent = across(chip_grad(mixed, 1, branch_grad), 1)
+    out_sum = chip_grad(mixed, 0, branch_grad, 0, (out_sent,)).reshape(2, 2, -1, width)
+    mixed_grad = mixed_back(branch_grad, out_w)
     bias = mask_of(local_rows // 2)
-    dq_0, dk_0, dv_0 = attend_back(rank, operands, bias, mixed_grad, lse, 0)
-    got_gu, kept_d, got_d, out_a, out_b, mixed_grad, dq_0, dk_0, dv_0 = hold(
-        got_gu, kept_d, got_d, out_a, out_b, mixed_grad, dq_0, dk_0, dv_0
-    )
-
-    def ends(kept, got):
-        total = [add(k[0], g) for k, g in zip(kept, got)]
-        return jnp.stack([jnp.stack([total[0], total[2]]), jnp.stack([total[1], total[3]])])
-
-    def first_move(both):
-        return mirrored(both, [(3, 2)]), mirrored(both[1], [(0, 1)])
-
-    kept_gu = [
-        kept_sum(moe_x[0], dg_a, got_gu[0]),
-        kept_sum(moe_x[0], dg_b, got_gu[1]),
-        kept_sum(moe_y[0], du_a, got_gu[2]),
-        kept_sum(moe_y[0], du_b, got_gu[3]),
-    ]
-    got_gu = [
-        across(kept_gu[0][1], 4),
-        across(kept_gu[1][1], 4),
-        across(kept_gu[2][1], 2),
-        across(kept_gu[3][1], 2),
-    ]
-    out_x, out_y = across(out_a[:, 1], 2), across(out_b[1], 4)
-    both_d = ends(kept_d, got_d)
-    d_3, d_1 = first_move(both_d)
-    dq_1, dk_1, dv_1 = attend_back(rank, operands, bias, mixed_grad, lse, HEADS // 2)
+    dq_0, dk_0, dv_0 = attend_back(rank, operands, bias, mixed_grad, lse_0, 0)
+    dq_1, dk_1, dv_1 = attend_back(rank, operands, bias, mixed_grad, lse_1, HEADS // 2)
+    a_x, a_y, b_0, b_1, b_x, b_y, out_sum, dq_0, dk_0, dv_0, dq_1, dk_1, dv_1 = hold(
+        a_x, a_y, b_0, b_1, b_x, b_y, out_sum, dq_0, dk_0, dv_0, dq_1, dk_1, dv_1
+    )
+
+    a_0 = experts_grad(moe_x, dg_a, mx_a, pair_a, 0, 0, (a_x,))
+    a_1 = experts_grad(moe_y, du_a, my_a, pair_a, 0, 1, (a_y,))
+    a_y, a_x = other_ways(a_0[1], a_1[1])
+    out_x, out_y = across(out_sum[:, 1, :, :half], 2), across(out_sum[1, :, :, half:], 4)
+    b_end = jnp.stack([add(b_0[0], b_y), add(b_1[0], b_x)])
+    b_got = mirrored(b_end, [(3, 2), (0, 1)])
     query_lin_grad, q_gain_local = lin_back(
         dq_0, dq_1, query_lin, scale_query, gain_query[None], cosine[behind:], sine[behind:]
     )
     key_lin_grad, k_gain_local = lin_back(
         dk_0, dk_1, key_lin, scale_key, gain_key[None], cosine, sine
     )
+    value_sent = (chip_grad(normed, 1, dv_0), chip_grad(normed, 1, dv_1))
     (
-        kept_gu,
-        got_gu,
-        out_a,
-        out_b,
-        out_x,
-        out_y,
-        both_d,
-        d_3,
-        d_1,
-        dv_0,
-        dv_1,
-        query_lin_grad,
-        key_lin_grad,
+        a_0, a_1, a_x, a_y, out_sum, out_x, out_y, b_end, b_got, query_lin_grad, key_lin_grad,
+        value_sent, dv_0, dv_1,
     ) = hold(
-        kept_gu,
-        got_gu,
-        out_a,
-        out_b,
-        out_x,
-        out_y,
-        both_d,
-        d_3,
-        d_1,
-        dv_0,
-        dv_1,
-        query_lin_grad,
-        key_lin_grad,
-    )
-
-    out_a, out_b = add(out_a[:, 0], out_x), add(out_b[0], out_y)
+        a_0, a_1, a_x, a_y, out_sum, out_x, out_y, b_end, b_got, query_lin_grad, key_lin_grad,
+        value_sent, dv_0, dv_1,
+    )
+
+    out_a, out_b = add(out_sum[:, 0, :, :half], out_x), add(out_sum[0, :, :, half:], out_y)
     out_x, out_y = across(out_b[1], 2), across(out_a[1], 4)
-    both_d = add(both_d, d_3)
-    d_2 = mirrored(both_d, [(2, 1)])
-    both_gu = ends(kept_gu, got_gu)
-    gu_3, gu_1 = first_move(both_gu)
-    value_a, value_b = chip_sum(normed, dv_0), chip_sum(normed, dv_1)
+    b_low = add(b_end, b_got)
+    b_got_2 = mirrored(b_low, [(2, 1)])
+    a_end = jnp.stack([add(a_0[0], a_y), add(a_1[0], a_x)])
+    a_got = mirrored(a_end, [(3, 2)])
     normed_grad = project_back(
         key_lin_grad, dv_0, dv_1, query_lin_grad, key_w, value_w, query_w
     )
-    (
-        out_a,
-        out_b,
-        out_x,
-        out_y,
-        both_d,
-        d_2,
-        both_gu,
-        gu_3,
-        gu_1,
-        value_a,
-        value_b,
-        normed_grad,
-        query_lin_grad,
-        key_lin_grad,
-    ) = hold(
-        out_a,
-        out_b,
-        out_x,
-        out_y,
-        both_d,
-        d_2,
-        both_gu,
-        gu_3,
-        gu_1,
-        value_a,
-        value_b,
-        normed_grad,
-        query_lin_grad,
-        key_lin_grad,
-    )
-
-    value_x, value_y = across(value_a[:, 1], 2), across(value_b[1], 4)
-    query_sum = chip_sum(normed[:, behind:], query_lin_grad)
-    key_sum = chip_sum(normed, key_lin_grad)
-    carried = normed_grad[:, :local_rows].astype(bf16)
-    carried = from_behind(carried, "ep", -1)
-    d_a, d_b = both_d[0] + d_2[0].astype(f32), both_d[1] + d_2[1].astype(f32)
-    d_0 = mirrored(d_a.astype(bf16), [(1, 0)])
-    both_gu = add(both_gu, gu_3)
-    gu_2 = mirrored(both_gu, [(2, 1)])
-    out_total = over_ep_sum(jnp.stack([add(out_a[0], out_y), add(out_b[0], out_x)]), place)
-    (
-        value_a,
-        value_b,
-        value_x,
-        value_y,
-        query_sum,
-        key_sum,
-        carried,
-        d_a,
-        d_b,
-        d_0,
-        both_gu,
-        gu_2,
-        out_total,
-    ) = hold(
-        value_a,
-        value_b,
-        value_x,
-        value_y,
-        query_sum,
-        key_sum,
-        carried,
-        d_a,
-        d_b,
-        d_0,
-        both_gu,
-        gu_2,
-        out_total,
-    )
-
-    def own_half(mine):
-        halves = mine.reshape(2, 2, -1, mine.shape[2])
-        other = across(pick(halves, 1 - core, 1), 1)
-        return jnp.where(m < 2, pick(halves, core, 1), other)
-
-    query_x, key_y = across(query_sum[:, 1], 2), across(key_sum[1], 4)
-    value_a, value_b = add(value_a[:, 0], value_x), add(value_b[0], value_y)
-    value_x, value_y = across(value_b[1], 2), across(value_a[1], 4)
-    for back in range(1, reach):
-        here = normed_grad[:, back * local_rows : (back + 1) * local_rows] + carried.astype(f32)
-        carried = from_behind(here.astype(bf16), "ep", -1)
-    down_mine = jnp.where(m == 0, d_a + d_0.astype(f32), d_b + d_1.astype(f32))
-    gu_a, gu_b = both_gu[0] + gu_2[0].astype(f32), both_gu[1] + gu_2[1].astype(f32)
-    gu_0 = mirrored(gu_a.astype(bf16), [(1, 0)])
-    (
-        query_sum,
-        key_sum,
-        query_x,
-        key_y,
-        value_a,
-        value_b,
-        value_x,
-        value_y,
-        carried,
-        gu_a,
-        gu_b,
-        gu_0,
-        down_mine,
-    ) = hold(
-        query_sum,
-        key_sum,
-        query_x,
-        key_y,
-        value_a,
-        value_b,
-        value_x,
-        value_y,
-        carried,
-        gu_a,
-        gu_b,
-        gu_0,
-        down_mine,
-    )
-
-    query_sum, key_sum = add(query_sum[:, 0], query_x), add(key_sum[0], key_y)
-    query_y, key_x = across(query_sum[1], 4), across(key_sum[1], 2)
-    value_total = over_ep_sum(
-        jnp.stack([add(value_a[0], value_y), add(value_b[0], value_x)]), place
-    )
-    gu_mine = jnp.where(m == 0, gu_a + gu_0.astype(f32), gu_b + gu_1.astype(f32))
-    tokens_grad, attn_gain_local = tokens_back(
-        rank,
-        normed_grad,
-        carried,
-        tokens,
-        residual_grad,
-        scale_all,
-        gain_attn,
-        reps,
-    )
-    query_sum, key_sum, query_y, key_x, value_total, gu_mine, attn_gain_local = hold(
-        query_sum, key_sum, query_y, key_x, value_total, gu_mine, attn_gain_local
-    )
-
-    qk_total = over_ep_sum(jnp.stack([add(query_sum[0], query_y), add(key_sum[0], key_x)]), place)
-    gu_half, down_half = own_half(gu_mine), own_half(down_mine)
-    down_out = jnp.concatenate([down_half[0], down_half[1]], 1)
-    out_out = jnp.concatenate([out_total[0], out_total[1]], 1)
-    value_out = jnp.concatenate([value_total[0], value_total[1]], 1)
+    out_a, out_b, out_x, out_y, normed_grad, value_sent, query_lin_grad, key_lin_grad = hold(
+        out_a, out_b, out_x, out_y, normed_grad, value_sent, query_lin_grad, key_lin_grad
+    )
+
+    carried = from_behind(normed_grad[:, :local_rows].astype(bf16), "ep", -1)
+    value_got = across(value_sent[0], 1), across(value_sent[1], 1)
+    out_total = ep_sum(jnp.stack([add(out_a[0], out_y), add(out_b[0], out_x)]))
+    attn_gain_local = gain_grad(rank, normed_grad, tokens_all, scale_all, order)
+    query_sent = chip_grad(normed, 1, query_lin_grad, behind)
+    key_sent = chip_grad(normed, 1, key_lin_grad)
+    value_a = chip_grad(normed, 0, dv_0, 0, (value_got[0],)).reshape(2, 2, -1, half)
+    value_b = chip_grad(normed, 0, dv_1, 0, (value_got[1],)).reshape(2, 2, -1, half)
     packed = jnp.concatenate(
         [
             jnp.broadcast_to(squares, (1, width)),
@@ -1693,25 +1577,82 @@
         ],
         0,
     )
-    packed = sum_small(packed, place)
+    carried, value_a, value_b, query_sent, key_sent, query_lin_grad, key_lin_grad, packed = hold(
+        carried, value_a, value_b, query_sent, key_sent, query_lin_grad, key_lin_grad, packed
+    )
+
+    query_got, key_got = across(query_sent, 1), across(key_sent, 1)
+    value_x, value_y = across(value_a[:, 1], 2), across(value_b[1], 4)
+    for back in range(1, reach):
+        here = normed_grad[:, back * local_rows : (back + 1) * local_rows] + carried.astype(f32)
+        carried = from_behind(here.astype(bf16), "ep", -1)
+    query_sum = chip_grad(normed, 0, query_lin_grad, behind, (query_got,))
+    key_sum = chip_grad(normed, 0, key_lin_grad, 0, (key_got,))
+    query_sum = query_sum.reshape(2, 2, -1, width)
+    key_sum = key_sum.reshape(2, 2, -1, width)
+    packed = packed + across(packed, 1)
+    carried, value_a, value_b, value_x, value_y, query_sum, key_sum, packed, a_end, a_got = hold(
+        carried, value_a, value_b, value_x, value_y, query_sum, key_sum, packed, a_end, a_got
+    )
+
+    query_x, key_y = across(query_sum[:, 1], 2), across(key_sum[1], 4)
+    value_a, value_b = add(value_a[:, 0], value_x), add(value_b[0], value_y)
+    value_x, value_y = across(value_b[1], 2), across(value_a[1], 4)
+    a_low = add(a_end, a_got)
+    a_got = mirrored(a_low, [(2, 1)])
+    packed = packed + across(packed, 2)
+    tokens_grad = tokens_back(
+        rank, normed_grad, carried, tokens, residual_grad, scale_all, gain_attn, reps
+    )
+    query_sum, key_sum, query_x, key_y, value_a, value_b, value_x, value_y, packed, a_low, a_got = hold(
+        query_sum, key_sum, query_x, key_y, value_a, value_b, value_x, value_y, packed, a_low, a_got
+    )
+
+    query_sum, key_sum = add(query_sum[:, 0], query_x), add(key_sum[0], key_y)
+    query_y, key_x = across(query_sum[1], 4), across(key_sum[1], 2)
+    value_total = ep_sum(jnp.stack([add(value_a[0], value_y), add(value_b[0], value_x)]))
+    packed = packed + across(packed, 4)
+    a_low = a_low.astype(f32) + a_got.astype(f32)
+    a_got = mirrored(a_low.astype(bf16), [(1, 0)])
+    query_sum, key_sum, query_y, key_x, packed, a_low, a_got = hold(
+        query_sum, key_sum, query_y, key_x, packed, a_low, a_got
+    )
+
+    qk_total = ep_sum(jnp.stack([add(query_sum[0], query_y), add(key_sum[0], key_x)]))
+    packed = jnp.sum(over_ep(packed, place), axis=0)
+    b_total = b_end.astype(f32) + b_got.astype(f32) + b_got_2.astype(f32)
+    mine = jnp.where(m == 0, a_low + a_got.astype(f32), b_total)
+
+    def own_half(piece):
+        return piece.reshape(2, 2, -1, piece.shape[2])
+
+    tops, bottoms = own_half(mine[:, :quarter_rows]), own_half(mine[:, quarter_rows:])
+    halves = jnp.concatenate([tops, bottoms], 2)
+    other = across(pick(halves, 1 - core, 1), 1)
+    mine = jnp.where(m < 2, pick(halves, core, 1), other)
+    top = quarter_rows // 2
+    down_out = jnp.concatenate([mine[0, top:], mine[1, top:]], 1)
+    out_out = jnp.concatenate([out_total[0], out_total[1]], 1)
+    value_out = jnp.concatenate([value_total[0], value_total[1]], 1)
     loss = packed[0, 0] / (2.0 * count * width)
-    own_rows = attn_gain.shape[0]
-    mine = lax.dynamic_slice_in_dim(packed, (rep * experts + shard) * own_rows, own_rows, 1)
+    shares = lax.dynamic_slice_in_dim(
+        packed, (rep * experts + shard) * shard_rows, shard_rows, 1
+    )
     return (
         output,
         loss,
         tokens_grad,
-        mine[1],
-        mine[2],
-        mine[3],
-        mine[4],
+        shares[1],
+        shares[2],
+        shares[3],
+        shares[4],
         qk_total[0],
         qk_total[1],
         value_out,
         out_out,
-        mine[5:].T,
-        gu_half[0][None],
-        gu_half[1][None],
+        shares[5:].T,
+        mine[0, :top][None],
+        mine[1, :top][None],
         down_out[None],
     )
 

time: 1550 us -> 1410 us (0.910)
  starting transfers between devices: 344 us -> 129 us
  Pallas kernels: 366 us -> 539 us
  matrix products: 133 us -> 4.35 us
  local copies, waits for them, and re-layouts: 84.9 us -> 120 us
  waiting for transfers between devices: 448 us -> 419 us
    pallas_call x1 -> x21, Pallas kernels: 50.5 us -> 226 us  [the longest x10 95.7 us: chip_grad(): kernel_call(chip_grad_kernel, grid=(depth // tile, width // step), in_spe...]
    dot_general x30 -> x0, matrix products: 129 us -> none  [the longest x28 121 us: t_dot(): lax.dot_general(left, right, (((0,), (0,)), ((), ())), preferred_element_...]
    ppermute x21 -> x9, starting transfers between devices: 99.4 us -> 14.8 us  [along(): lax.ppermute(value, 'ep', [(place, (place + steps) % count) for place in...]
    ppermute x6, starting transfers between devices: 103 us -> 35.2 us  [from_behind(): lax.ppermute(value, axis, [(source, source + steps) for source in range(l...]
    ppermute x6, waiting for transfers between devices: 0.4 us -> 56.2 us  [from_behind(): lax.ppermute(value, axis, [(source, source + steps) for source in range(l...]
    ppermute x21 -> x9, waiting for transfers between devices: 88.3 us -> 35 us  [along(): lax.ppermute(value, 'ep', [(place, (place + steps) % count) for place in...]
    ppermute x76 -> x55, starting transfers between devices: 102 us -> 49.2 us  [across(): lax.ppermute(value, 'rep', [(place, place ^ bit) for place in range(count)])]
    ppermute x16 -> x9, waiting for transfers between devices: 66 us -> 33 us  [mirrored(): return lax.ppermute(value, ('rep', 'ep'), pairs)]
  transfers between devices with their start and end apart: 119 -> 83, of which waited for: 38 -> 38; matrix products, arithmetic and copies ran while one was open for 18% -> 17% of each run, Pallas kernels for 17% -> 30%
where the time goes in v4:
time: 1410 us; the launch traced here: 1400 us
  Pallas kernels  539 us (38%)
  waiting for transfers between devices  419 us (30%)
  other arithmetic  168 us (12%)
  starting transfers between devices  129 us (9%)
  local copies, waits for them, and re-layouts  120 us (9%)
  between operations  21.4 us (2%)
    ppermute x55, waiting for transfers between devices, across(): lax.ppermute(value, 'rep', [(place, place ^ bit) for place in range(count)])  262 us
    pallas_call x10, Pallas kernels, chip_grad(): kernel_call(chip_grad_kernel, grid=(depth // tile, width // step), in_spe...  95.7 us
    pallas_call x8, Pallas kernels, experts_grad(): kernel_call(experts_grad_kernel, grid=(2, 2), in_specs=[pl.BlockSpec((1,...  71.4 us
    pallas_call x4, Pallas kernels, project(): kernel_call(project_kernel, grid=(rows // tile,), in_specs=[pl.BlockSpec(...  59.2 us
    pallas_call x2, Pallas kernels, attend_back(): kernel_call(functools.partial(attend_back_kernel, behind=all_rows - rows,...  57.8 us
    ppermute x6, waiting for transfers between devices, from_behind(): lax.ppermute(value, axis, [(source, source + steps) for source in range(l...  56.2 us
    ppermute x55, starting transfers between devices, across(): lax.ppermute(value, 'rep', [(place, place ^ bit) for place in range(count)])  49.2 us
    pallas_call x1, Pallas kernels, project_back(): kernel_call(functools.partial(project_back_kernel, tile=512), grid=(2 * h...  41.2 us
  transfers between devices with their start and end apart: 83, of which 38 were waited for; matrix products, arithmetic and copies ran while one was open for 17% of the time, Pallas kernels for 30%

profile of v4, /device:TPU:0, one launch (start us, length us, event | category | flops | bytes accessed | tf_op | source)
XLA Modules:
  0.0 1400.1 jit_solution(502268633365891165)
XLA Ops:
  40.0 18.7 %collective-permute-done.1 = bf16[2,64,2048]{2,1,0:T(8,128)(2,1)} collective-permute-done((bf16[2,64,2048]{2,1,0:T(8,128)(2,1)}, bf16[2,64,2048]{2,1,0:T(8,128)(2,1)}, u32[]{:S(2)}, u32[]{:S(2)}) %collective-permute-start.1) | collective-permute-done | bytes 524320 | tf_op jit(solution)/shard_map/ppermute | solution.py:1174
  125.5 19.8 %collective-permute-done.11 = bf16[2,256,2048]{2,1,0:T(8,128)(2,1)} collective-permute-done((bf16[2,256,2048]{2,1,0:T(8,128)(2,1)}, bf16[2,256,2048]{2,1,0:T(8,128)(2,1)}, u32[]{:S(2)}, u32[]{:S(2)}) %collective-permute-start.11) | collective-permute-done | bytes 2097184 | tf_op jit(solution)/shard_map/ppermute | solution.py:1169
  145.4 18.6 %collective-permute-done.12 = bf16[512,2048]{1,0:T(8,128)(2,1)} collective-permute-done((bf16[512,2048]{1,0:T(8,128)(2,1)}, bf16[512,2048]{1,0:T(8,128)(2,1)}, u32[]{:S(2)}, u32[]{:S(2)}) %collective-permute-start.12) | collective-permute-done | bytes 2097184 | tf_op jit(solution)/shard_map/ppermute | solution.py:24
  222.3 20.3 %collective-permute-done.17 = bf16[512,2048]{1,0:T(8,128)(2,1)} collective-permute-done((bf16[512,2048]{1,0:T(8,128)(2,1)}, bf16[512,2048]{1,0:T(8,128)(2,1)}, u32[]{:S(2)}, u32[]{:S(2)}) %collective-permute-start.17) | collective-permute-done | bytes 2097184 | tf_op jit(solution)/shard_map/ppermute | solution.py:24
  276.4 19.7 %shard_map.281 = (f32[1536,2048]{1,0:T(8,128)}, f32[1536,1]{1,0:T(8,128)}) custom-call(bf16[2,1536,1024]{2,1,0:T(8,128)(2,1)} %get-tuple-element.247.low_ref.high_ref.x_ref, bf16[2,1536,1024]{2,1,0:T(8,128)(2,1)} %get-tuple-element.247.low_ref.high_ref.x_ref, bf16[1040,2048]{1,0:T(8,128)(2,1)} %pad_dynamic-update-slice_fusion.a_ref.ka, ...), custom_call_target="tpu_custom_call" | custom-call | tf_op jit(solution)/shard_map/pallas_call | solution.py:470
  296.0 19.3 %shard_map.282 = (bf16[1536,2048]{1,0:T(8,128)(2,1)}, f32[1536,1]{1,0:T(8,128)}) custom-call(bf16[2,1536,1024]{2,1,0:T(8,128)(2,1)} %get-tuple-element.247.low_ref.high_ref.x_ref, bf16[2,1536,1024]{2,1,0:T(8,128)(2,1)} %get-tuple-element.247.low_ref.high_ref.x_ref, bf16[1024,2048]{1,0:T(8,128)(2,1)} %pad_maximum_fusion.a_ref.va, ...), custom_call_target="tpu_custom_call" | custom-call | tf_op jit(solution)/shard_map/pallas_call | solution.py:470
  353.4 19.6 %shard_map.284 = (bf16[2,512,1024]{2,1,0:T(8,128)(2,1)}, f32[8,1,512]{2,1,0:T(1,128)}) custom-call(s32[1]{0:T(128)} %bitcast.rank, f32[512,2048]{1,0:T(8,128)} %get-tuple-element.249.q_ref.lin_ref, f32[1536,2048]{1,0:T(8,128)} %get-tuple-element.250.k_ref.lin_ref, bf16[1536,2048]{1,0:T(8,128)(2,1)} %get-tuple-element.251.v_ref, ...), custom_call_target="tpu_custom_call" | custom-call | tf_op jit(solution)/shard_map/pallas_call | solution.py:645
  373.0 20.6 %shard_map.285 = (bf16[2,512,1024]{2,1,0:T(8,128)(2,1)}, f32[8,1,512]{2,1,0:T(1,128)}) custom-call(s32[1]{0:T(128)} %bitcast.rank, f32[512,2048]{1,0:T(8,128)} %get-tuple-element.249.q_ref.lin_ref, f32[1536,2048]{1,0:T(8,128)} %get-tuple-element.250.k_ref.lin_ref, bf16[1536,2048]{1,0:T(8,128)(2,1)} %get-tuple-element.251.v_ref, ...), custom_call_target="tpu_custom_call", output_to_operand_aliasing={{0}: (11, {})} | custom-call | tf_op jit(solution)/shard_map/pallas_call | solution.py:645
  430.8 53.7 %collective-permute-done.29.ub.refs_13_.rb.refs_11_ = bf16[2,768,1024]{2,1,0:T(8,128)(2,1)} collective-permute-done((bf16[2,768,1024]{2,1,0:T(8,128)(2,1)S(1)}, bf16[2,768,1024]{2,1,0:T(8,128)(2,1)}, u32[]{:S(2)}, u32[]{:S(2)}) %collective-permute-start.29) | collective-permute-done | bytes 3145760 | tf_op jit(solution)/shard_map/ppermute | solution.py:1169
  495.2 15.4 %shard_map.288 = (f32[1024,1024]{1,0:T(8,128)}, f32[1024,1024]{1,0:T(8,128)}, bf16[2,1024,512]{2,1,0:T(8,128)(2,1)}, bf16[2,1024,512]{2,1,0:T(8,128)(2,1)}) custom-call(s32[1]{0:T(128)} %bitcast.56.rank, bf16[2,1024,1024]{2,1,0:T(8,128)(2,1)} %copy-done, bf16[2,1024,1024]{2,1,0:T(8,128)(2,1)} %pad_maximum_fusion.3.z_ref.x_ref, ...), custom_call_target="tpu_custom_call" | custom-call | tf_op jit(solution)/shard_map/pallas_call | solution.py:834
  510.6 16.9 %collective-permute-done.32 = bf16[768,1024]{1,0:T(8,128)(2,1)S(1)} collective-permute-done((bf16[768,1024]{1,0:T(8,128)(2,1)}, bf16[768,1024]{1,0:T(8,128)(2,1)S(1)}, u32[]{:S(2)}, u32[]{:S(2)}) %collective-permute-start.32) | collective-permute-done | bytes 1572896 | tf_op jit(solution)/shard_map/ppermute | solution.py:1169
  552.9 46.1 %collective-permute-done.35.ub.refs_7_.rb.refs_5_ = bf16[2,768,1024]{2,1,0:T(8,128)(2,1)} collective-permute-done((bf16[2,768,1024]{2,1,0:T(8,128)(2,1)S(1)}, bf16[2,768,1024]{2,1,0:T(8,128)(2,1)}, u32[]{:S(2)}, u32[]{:S(2)}) %collective-permute-start.35) | collective-permute-done | bytes 3145760 | tf_op jit(solution)/shard_map/ppermute | solution.py:1169
  602.0 15.2 %shard_map.289 = (f32[1024,1024]{1,0:T(8,128)}, f32[1024,1024]{1,0:T(8,128)}, bf16[2,1024,512]{2,1,0:T(8,128)(2,1)}, bf16[2,1024,512]{2,1,0:T(8,128)(2,1)}) custom-call(s32[1]{0:T(128)} %bitcast.56.rank, bf16[2,1024,1024]{2,1,0:T(8,128)(2,1)} %copy-done, bf16[2,1024,1024]{2,1,0:T(8,128)(2,1)} %pad_maximum_fusion.3.z_ref.x_ref, ...), custom_call_target="tpu_custom_call" | custom-call | tf_op jit(solution)/shard_map/pallas_call | solution.py:834
  617.2 17.8 %shard_map.290 = (bf16[1024,2048]{1,0:T(8,128)(2,1)}, bf16[1024,2048]{1,0:T(8,128)(2,1)}, f32[512,2048]{1,0:T(8,128)}, f32[512,2048]{1,0:T(8,128)}) custom-call(f32[1024,1]{1,0:T(8,128)} %broadcast_select_fusion.2.refs_0_.gate_ref, f32[1024,1]{1,0:T(8,128)} %broadcast_select_fusion.1.refs_1_.gate_ref, ...), custom_call_target="tpu_custom_call" | custom-call | tf_op jit(solution)/shard_map/pallas_call | solution.py:883
  660.4 14.5 %shard_map.291 = (bf16[1024,2048]{1,0:T(8,128)(2,1)}, bf16[1024,1024]{1,0:T(8,128)(2,1)}, bf16[1024,1024]{1,0:T(8,128)(2,1)}, f32[1024,1]{1,0:T(8,128)}) custom-call(s32[1]{0:T(128)} %bitcast.56.rank, f32[512,2048]{1,0:T(8,128)} %copy-done.3, f32[512,2048]{1,0:T(8,128)} %copy-done.10, bf16[1024,2048]{1,0:T(8,128)(2,1)} %get-tuple-element.295.out_ref, ...), custom_call_target="tpu_custom_call" | custom-call | tf_op jit(solution)/shard_map/pallas_call | solution.py:934
  694.5 14.3 %shard_map.294 = (bf16[1024,2048]{1,0:T(8,128)(2,1)}, bf16[1024,1024]{1,0:T(8,128)(2,1)}, bf16[1024,1024]{1,0:T(8,128)(2,1)}, f32[1024,1]{1,0:T(8,128)}) custom-call(s32[1]{0:T(128)} %bitcast.56.rank, f32[512,2048]{1,0:T(8,128)} %copy-done.3, f32[512,2048]{1,0:T(8,128)} %copy-done.10, bf16[1024,2048]{1,0:T(8,128)(2,1)} %get-tuple-element.302.out_ref, ...), custom_call_target="tpu_custom_call" | custom-call | tf_op jit(solution)/shard_map/pallas_call | solution.py:934
  728.8 27.6 %shard_map.297 = (f32[4,512,512]{2,1,0:T(8,128)}, f32[4,512,512]{2,1,0:T(8,128)}) custom-call(bf16[1024,1024]{1,0:T(8,128)(2,1)} %get-tuple-element.305.d_ref.refs_0_, bf16[1024,1024]{1,0:T(8,128)(2,1)} %get-tuple-element.309.d_ref.refs_1_, bf16[2,768,1024]{2,1,0:T(8,128)(2,1)} %pad_maximum_fusion.7.ga.refs_4_.la.refs_2_, ...), custom_call_target="tpu_custom_call" | custom-call | tf_op jit(solution)/shard_map/pallas_call | solution.py:985
  831.5 28.9 %shard_map.305 = (bf16[512,1024]{1,0:T(8,128)(2,1)}, bf16[1536,1024]{1,0:T(8,128)(2,1)}, bf16[1536,1024]{1,0:T(8,128)(2,1)}) custom-call(s32[1]{0:T(128)} %bitcast.rank, f32[512,2048]{1,0:T(8,128)} %get-tuple-element.249.q_ref.lin_ref, f32[1536,2048]{1,0:T(8,128)} %get-tuple-element.250.k_ref.lin_ref, bf16[1536,2048]{1,0:T(8,128)(2,1)} %get-tuple-element.251.v_ref, ...), custom_call_target="tpu_custom_call" | custom-call | tf_op jit(solution)/shard_map/pallas_call | solution.py:719
  860.4 28.9 %shard_map.304 = (bf16[512,1024]{1,0:T(8,128)(2,1)}, bf16[1536,1024]{1,0:T(8,128)(2,1)}, bf16[1536,1024]{1,0:T(8,128)(2,1)}) custom-call(s32[1]{0:T(128)} %bitcast.rank, f32[512,2048]{1,0:T(8,128)} %get-tuple-element.249.q_ref.lin_ref, f32[1536,2048]{1,0:T(8,128)} %get-tuple-element.250.k_ref.lin_ref, bf16[1536,2048]{1,0:T(8,128)(2,1)} %get-tuple-element.251.v_ref, ...), custom_call_target="tpu_custom_call" | custom-call | tf_op jit(solution)/shard_map/pallas_call | solution.py:719
  1005.7 41.2 %shard_map.312.g_ref = f32[2,1536,1024]{2,1,0:T(8,128)} custom-call(bf16[1536,2048]{1,0:T(8,128)(2,1)} %get-tuple-element.369.k_ref.g_ref, bf16[1536,1024]{1,0:T(8,128)(2,1)} %get-tuple-element.350.g_ref.v_ref, bf16[1536,1024]{1,0:T(8,128)(2,1)} %get-tuple-element.351.g_ref.w_ref, bf16[512,2048]{1,0:T(8,128)(2,1)} %get-tuple-element.367.q_ref.g_ref, ...), custom_call_target="tpu_custom_call" | custom-call | tf_op jit(solution)/shard_map/pallas_call | solution.py:522
  1124.3 13.9 shard_map.319
  1148.8 16.0 %collective-permute-done.57.c_ref = bf16[2,512,1024]{2,1,0:T(8,128)(2,1)} collective-permute-done((bf16[2,512,1024]{2,1,0:T(8,128)(2,1)}, bf16[2,512,1024]{2,1,0:T(8,128)(2,1)}, u32[]{:S(2)}, u32[]{:S(2)}) %collective-permute-start.57) | collective-permute-done | bytes 2097184 | tf_op jit(solution)/shard_map/ppermute | solution.py:24
  1188.8 36.5 %collective-permute-done.68 = f32[9,2048]{1,0:T(8,128)S(1)} collective-permute-done((f32[9,2048]{1,0:T(8,128)S(1)}, f32[9,2048]{1,0:T(8,128)S(1)}, u32[]{:S(2)}, u32[]{:S(2)}) %collective-permute-start.68) | collective-permute-done | bytes 73760 | tf_op jit(solution)/shard_map/ppermute | solution.py:1169
  1286.9 27.1 %collective-permute-done.73 = bf16[2,768,1024]{2,1,0:T(8,128)(2,1)} collective-permute-done((bf16[2,768,1024]{2,1,0:T(8,128)(2,1)}, bf16[2,768,1024]{2,1,0:T(8,128)(2,1)}, u32[]{:S(2)}, u32[]{:S(2)}) %collective-permute-start.73) | collective-permute-done | bytes 3145760 | tf_op jit(solution)/shard_map/ppermute | solution.py:1185
  (565 shorter events, 808.1 us)
Async XLA Ops:
  7.2 118.4 %all-gather.3.cloned.1.call-start = ((), (), s32[]{:S(2)}) async-start(), calls=%async_computation.6 | async-start | bytes 2621440 | tf_op jit(solution)/shard_map/all_gather | solution.py:1302
  70.0 1198.9 %reduce-scatter.8.cloned.1.call-start = ((), (), s32[]{:S(2)}) async-start(), calls=%async_computation.5 | async-start | bytes 1310720 | tf_op jit(solution)/shard_map/reduce_scatter | solution.py:1225
  95.7 68.2 %collective-permute-start.10 = (bf16[2,272,2048]{2,1,0:T(8,128)(2,1)}, bf16[2,272,2048]{2,1,0:T(8,128)(2,1)}, u32[]{:S(2)}, u32[]{:S(2)}) collective-permute-start(bf16[2,272,2048]{2,1,0:T(8,128)(2,1)} %pad_maximum_fusion.13), channel_id=1, source_target_pairs={{0,16},{4,20},{8,24},{12,28},{16,0},{20,4},{24,8},{28,12},{1,17},{... | collective-permute-start | bytes 6684680 | tf_op jit(solution)/shard_map/ppermute | solution.py:1169
  114.5 88.7 %collective-permute-start.18 = (bf16[2,768,1024]{2,1,0:T(8,128)(2,1)S(1)}, bf16[2,768,1024]{2,1,0:T(8,128)(2,1)}, u32[]{:S(2)}, u32[]{:S(2)}) collective-permute-start(bf16[2,768,1024]{2,1,0:T(8,128)(2,1)S(1)} %pad_maximum_fusion.4), channel_id=1, source_target_pairs={{0,1},{1,2},{7,6},{6,5},{8,9},{9,10},{15,14},{14,13},{16,17},{17,1... | collective-permute-start | bytes 9437192 | tf_op jit(solution)/shard_map/ppermute | solution.py:1185
  246.2 78.0 %collective-permute-start.21 = (bf16[2,768,1024]{2,1,0:T(8,128)(2,1)}, bf16[2,768,1024]{2,1,0:T(8,128)(2,1)}, u32[]{:S(2)}, u32[]{:S(2)}) collective-permute-start(bf16[2,768,1024]{2,1,0:T(8,128)(2,1)} %broadcast_select_fusion), channel_id=1, source_target_pairs={{1,0},{2,3},{6,7},{5,4},{9,8},{10,11},{14,15},{13,12},{17,16},{18,... | collective-permute-start | bytes 9437192 | tf_op jit(solution)/shard_map/ppermute | solution.py:1185
  250.6 68.5 %collective-permute-start.20 = (bf16[2,256,2048]{2,1,0:T(8,128)(2,1)}, bf16[2,256,2048]{2,1,0:T(8,128)(2,1)}, u32[]{:S(2)}, u32[]{:S(2)}) collective-permute-start(bf16[2,256,2048]{2,1,0:T(8,128)(2,1)} %pad_maximum_fusion.16), channel_id=1, source_target_pairs={{0,8},{4,12},{8,0},{12,4},{16,24},{20,28},{24,16},{28,20},{1,9},{5... | collective-permute-start | bytes 6291464 | tf_op jit(solution)/shard_map/ppermute | solution.py:1169
  414.8 69.7 %collective-permute-start.29 = (bf16[2,768,1024]{2,1,0:T(8,128)(2,1)S(1)}, bf16[2,768,1024]{2,1,0:T(8,128)(2,1)}, u32[]{:S(2)}, u32[]{:S(2)}) collective-permute-start(bf16[2,768,1024]{2,1,0:T(8,128)(2,1)S(1)} %pad_maximum_fusion.6.ua.refs_12_.ra.refs_10_), channel_id=1, source_target_pairs={{0,8},{4,12},{8,0},{12,4},{16,24},{20,28},{24,16},{28,20},{1,9},{5... | collective-permute-start | bytes 9437192 | tf_op jit(solution)/shard_map/ppermute | solution.py:1169
  418.2 69.8 %collective-permute-start.28 = (bf16[2,768,1024]{2,1,0:T(8,128)(2,1)}, bf16[2,768,1024]{2,1,0:T(8,128)(2,1)}, u32[]{:S(2)}, u32[]{:S(2)}) collective-permute-start(bf16[2,768,1024]{2,1,0:T(8,128)(2,1)} %pad_maximum_fusion.5.ga.refs_10_.la.refs_8_), channel_id=1, source_target_pairs={{0,16},{4,20},{8,24},{12,28},{16,0},{20,4},{24,8},{28,12},{1,17},{... | collective-permute-start | bytes 9437192 | tf_op jit(solution)/shard_map/ppermute | solution.py:1169
  419.7 68.4 %collective-permute-start.30 = (bf16[2,768,1024]{2,1,0:T(8,128)(2,1)}, bf16[2,768,1024]{2,1,0:T(8,128)(2,1)}, u32[]{:S(2)}, u32[]{:S(2)}) collective-permute-start(bf16[2,768,1024]{2,1,0:T(8,128)(2,1)} %collective-permute-done.26), channel_id=1, source_target_pairs={{2,3},{5,4},{10,11},{13,12},{18,19},{21,20},{26,27},{29,28}} | collective-permute-start | bytes 9437192 | tf_op jit(solution)/shard_map/ppermute | solution.py:1185
  531.4 67.6 %collective-permute-start.35 = (bf16[2,768,1024]{2,1,0:T(8,128)(2,1)S(1)}, bf16[2,768,1024]{2,1,0:T(8,128)(2,1)}, u32[]{:S(2)}, u32[]{:S(2)}) collective-permute-start(bf16[2,768,1024]{2,1,0:T(8,128)(2,1)S(1)} %pad_maximum_fusion.8.ua.refs_6_.ra.refs_4_), channel_id=1, source_target_pairs={{0,8},{4,12},{8,0},{12,4},{16,24},{20,28},{24,16},{28,20},{1,9},{5... | collective-permute-start | bytes 9437192 | tf_op jit(solution)/shard_map/ppermute | solution.py:1169
  534.3 67.7 %collective-permute-start.34 = (bf16[2,768,1024]{2,1,0:T(8,128)(2,1)}, bf16[2,768,1024]{2,1,0:T(8,128)(2,1)}, u32[]{:S(2)}, u32[]{:S(2)}) collective-permute-start(bf16[2,768,1024]{2,1,0:T(8,128)(2,1)} %pad_maximum_fusion.7.ga.refs_4_.la.refs_2_), channel_id=1, source_target_pairs={{0,16},{4,20},{8,24},{12,28},{16,0},{20,4},{24,8},{28,12},{1,17},{... | collective-permute-start | bytes 9437192 | tf_op jit(solution)/shard_map/ppermute | solution.py:1169
  692.2 70.3 %collective-permute-start.38 = (bf16[2,768,1024]{2,1,0:T(8,128)(2,1)}, bf16[2,768,1024]{2,1,0:T(8,128)(2,1)S(1)}, u32[]{:S(2)}, u32[]{:S(2)}) collective-permute-start(bf16[2,768,1024]{2,1,0:T(8,128)(2,1)} %shard_map.292), channel_id=1, source_target_pairs={{0,8},{4,12},{8,0},{12,4},{16,24},{20,28},{24,16},{28,20},{1,9},{5... | collective-permute-start | bytes 9437192 | tf_op jit(solution)/shard_map/ppermute | solution.py:1169
  693.1 70.2 %collective-permute-start.39 = (bf16[2,768,1024]{2,1,0:T(8,128)(2,1)}, bf16[2,768,1024]{2,1,0:T(8,128)(2,1)}, u32[]{:S(2)}, u32[]{:S(2)}) collective-permute-start(bf16[2,768,1024]{2,1,0:T(8,128)(2,1)} %shard_map.293), channel_id=1, source_target_pairs={{0,16},{4,20},{8,24},{12,28},{16,0},{20,4},{24,8},{28,12},{1,17},{... | collective-permute-start | bytes 9437192 | tf_op jit(solution)/shard_map/ppermute | solution.py:1169
  791.8 97.5 %collective-permute-start.46 = (bf16[1024,2048]{1,0:T(8,128)(2,1)}, bf16[1024,2048]{1,0:T(8,128)(2,1)S(1)}, u32[]{:S(2)}, u32[]{:S(2)}) collective-permute-start(bf16[1024,2048]{1,0:T(8,128)(2,1)} %shard_map.301), channel_id=1, source_target_pairs={{0,4},{4,0},{8,12},{12,8},{16,20},{20,16},{24,28},{28,24},{1,5},{5... | collective-permute-start | bytes 12582920 | tf_op jit(solution)/shard_map/ppermute | solution.py:1169
  792.0 109.1 %collective-permute-start.41 = (bf16[2,768,1024]{2,1,0:T(8,128)(2,1)}, bf16[2,768,1024]{2,1,0:T(8,128)(2,1)}, u32[]{:S(2)}, u32[]{:S(2)}) collective-permute-start(bf16[2,768,1024]{2,1,0:T(8,128)(2,1)} %shard_map.295), channel_id=1, source_target_pairs={{0,8},{4,12},{8,0},{12,4},{16,24},{20,28},{24,16},{28,20},{1,9},{5... | collective-permute-start | bytes 9437192 | tf_op jit(solution)/shard_map/ppermute | solution.py:1169
  793.1 107.9 %collective-permute-start.42 = (bf16[2,768,1024]{2,1,0:T(8,128)(2,1)}, bf16[2,768,1024]{2,1,0:T(8,128)(2,1)}, u32[]{:S(2)}, u32[]{:S(2)}) collective-permute-start(bf16[2,768,1024]{2,1,0:T(8,128)(2,1)} %shard_map.296), channel_id=1, source_target_pairs={{0,16},{4,20},{8,24},{12,28},{16,0},{20,4},{24,8},{28,12},{1,17},{... | collective-permute-start | bytes 9437192 | tf_op jit(solution)/shard_map/ppermute | solution.py:1169
  806.5 94.5 %collective-permute-start.43 = (bf16[768,1024]{1,0:T(8,128)(2,1)}, bf16[768,1024]{1,0:T(8,128)(2,1)}, u32[]{:S(2)}, u32[]{:S(2)}) collective-permute-start(bf16[768,1024]{1,0:T(8,128)(2,1)} %slice_bitcast_fusion.6), channel_id=1, source_target_pairs={{0,8},{4,12},{8,0},{12,4},{16,24},{20,28},{24,16},{28,20},{1,9},{5... | collective-permute-start | bytes 4718600 | tf_op jit(solution)/shard_map/ppermute | solution.py:1169
  819.3 81.7 %collective-permute-start.44 = (bf16[768,1024]{1,0:T(8,128)(2,1)}, bf16[768,1024]{1,0:T(8,128)(2,1)}, u32[]{:S(2)}, u32[]{:S(2)}) collective-permute-start(bf16[768,1024]{1,0:T(8,128)(2,1)} %slice_bitcast_fusion.5), channel_id=1, source_target_pairs={{0,16},{4,20},{8,24},{12,28},{16,0},{20,4},{24,8},{28,12},{1,17},{... | collective-permute-start | bytes 4718600 | tf_op jit(solution)/shard_map/ppermute | solution.py:1169
  905.8 93.9 %collective-permute-start.51 = (bf16[2,768,1024]{2,1,0:T(8,128)(2,1)S(1)}, bf16[2,768,1024]{2,1,0:T(8,128)(2,1)}, u32[]{:S(2)}, u32[]{:S(2)}) collective-permute-start(bf16[2,768,1024]{2,1,0:T(8,128)(2,1)S(1)} %pad_maximum_fusion.9), channel_id=1, source_target_pairs={{3,2},{0,1},{4,5},{7,6},{11,10},{8,9},{12,13},{15,14},{19,18},{16,... | collective-permute-start | bytes 9437192 | tf_op jit(solution)/shard_map/ppermute | solution.py:1185
  928.7 71.0 %collective-permute-start.47 = (bf16[768,1024]{1,0:T(8,128)(2,1)}, bf16[768,1024]{1,0:T(8,128)(2,1)}, u32[]{:S(2)}, u32[]{:S(2)}) collective-permute-start(bf16[768,1024]{1,0:T(8,128)(2,1)} %slice_bitcast_fusion.4), channel_id=1, source_target_pairs={{0,8},{4,12},{8,0},{12,4},{16,24},{20,28},{24,16},{28,20},{1,9},{5... | collective-permute-start | bytes 4718600 | tf_op jit(solution)/shard_map/ppermute | solution.py:1169
  1170.2 69.2 %collective-permute-start.69 = (bf16[2,768,1024]{2,1,0:T(8,128)(2,1)}, bf16[2,768,1024]{2,1,0:T(8,128)(2,1)}, u32[]{:S(2)}, u32[]{:S(2)}) collective-permute-start(bf16[2,768,1024]{2,1,0:T(8,128)(2,1)} %add_convert_fusion), channel_id=1, source_target_pairs={{2,1},{5,6},{10,9},{13,14},{18,17},{21,22},{26,25},{29,30}} | collective-permute-start | bytes 9437192 | tf_op jit(solution)/shard_map/ppermute | solution.py:1185
  1227.3 120.2 %reduce-scatter.6.cloned.1.call-start = ((), (), s32[]{:S(2)}) async-start(), calls=%async_computation.4 | async-start | bytes 1310720 | tf_op jit(solution)/shard_map/reduce_scatter | solution.py:1225
  1236.6 77.4 %collective-permute-start.77 = (bf16[2,768,1024]{2,1,0:T(8,128)(2,1)}, bf16[2,768,1024]{2,1,0:T(8,128)(2,1)}, u32[]{:S(2)}, u32[]{:S(2)}) collective-permute-start(bf16[2,768,1024]{2,1,0:T(8,128)(2,1)} %fusion), channel_id=1, source_target_pairs={{2,1},{5,6},{10,9},{13,14},{18,17},{21,22},{26,25},{29,30}} | collective-permute-start | bytes 9437192 | tf_op jit(solution)/shard_map/ppermute | solution.py:1185
  1276.1 114.0 %reduce-scatter.4.cloned.1.call-start = ((), (), s32[]{:S(2)}) async-start(), calls=%async_computation.3 | async-start | bytes 2621440 | tf_op jit(solution)/shard_map/reduce_scatter | solution.py:1225
  (134 other events, 3051.0 us)
Sparse Core Ops, SparseCore 0:
  70.1 55.3 all-gather.2
  1227.4 41.4 reduce-scatter.7
  1276.2 31.4 reduce-scatter.5
  1338.7 51.2 reduce-scatter.3

commit v5 on v4

--- a/solution.py
+++ b/solution.py
@@ -797,12 +797,13 @@
     return ref[...].reshape(-1, ref.shape[-1])
 
 
-def gu_spec(weights):
-    return pl.BlockSpec((2, weights.shape[1] // 3 * 2, weights.shape[2]), lambda i, *_: (0, 0, 0))
-
-
-def d_spec(weights):
-    return pl.BlockSpec((2, weights.shape[1] // 3, weights.shape[2]), lambda i, *_: (0, 2, 0))
+def gu_spec(weights, rows):
+    return pl.BlockSpec((2, rows, weights.shape[2]), lambda i, *_: (0, 0, 0))
+
+
+def d_spec(weights, rows):
+    last = weights.shape[1] // rows - 1
+    return pl.BlockSpec((2, rows, weights.shape[2]), lambda i, *_: (0, last, 0))
 
 
 def dynamic_block(index, block):
@@ -828,7 +829,7 @@
     hidden = weights[0].shape[2]
     tile = 256
     x_spec = pl.BlockSpec((2, tile, depth), lambda i, rank: (0, i, 0))
-    w_spec = gu_spec(weights[0])
+    w_specs = [gu_spec(weight, depth // 2) for weight in weights]
     wide = pl.BlockSpec((tile, hidden), lambda i, rank: (i, 0))
     half = pl.BlockSpec((2, tile, hidden // 2), lambda i, rank: (0, i, 0))
     return kernel_call(
@@ -836,7 +837,7 @@
         grid_spec=pltpu.PrefetchScalarGridSpec(
             num_scalar_prefetch=1,
             grid=(rows // tile,),
-            in_specs=[x_spec, x_spec] + [w_spec] * 4,
+            in_specs=[x_spec, x_spec] + w_specs,
             out_specs=[wide, wide, half, half],
             scratch_shapes=[pltpu.VMEM((tile, hidden), jnp.bfloat16)],
         ),
@@ -876,14 +877,14 @@
     half = slots[0][2].shape[2]
     tile = 256
     x_spec = pl.BlockSpec((2, tile, depth), lambda i: (0, i, 0))
-    w_spec = d_spec(slots[0][2])
+    w_specs = [d_spec(weight, depth // 2) for weight in slots[0][2:]]
     wide = pl.BlockSpec((tile, 2 * half), lambda i: (i, 0))
     column = pl.BlockSpec((tile, 1), lambda i: (i, 0))
     steps = rows // tile // 2
     return kernel_call(
         experts_down_kernel,
         grid=(rows // tile,),
-        in_specs=[column] * 2 + ([x_spec] * 2 + [w_spec] * 4) * 2,
+        in_specs=[column] * 2 + ([x_spec] * 2 + w_specs) * 2,
         out_specs=[
             wide,
             wide,
@@ -929,7 +930,7 @@
     wide = pl.BlockSpec((tile, width), lambda i, rank: (i, 0))
     narrow = pl.BlockSpec((tile, hidden), lambda i, rank: (i, 0))
     column = pl.BlockSpec((tile, 1), lambda i, rank: (i, 0))
-    w_spec = d_spec(weights[0])
+    w_specs = [d_spec(weight, hidden // 4) for weight in weights]
     steps = rows // tile // 2
     return kernel_call(
         experts_back_kernel,
@@ -940,7 +941,7 @@
                 pl.BlockSpec((tile, width), lambda i, rank: (jnp.minimum(i, steps - 1), 0)),
                 pl.BlockSpec((tile, width), lambda i, rank: (jnp.maximum(i - steps, 0), 0)),
                 wide, column, narrow, narrow
-            ] + [w_spec] * 4,
+            ] + w_specs,
             out_specs=[wide, narrow, narrow, column],
         ),
         out_shape=[
@@ -980,12 +981,12 @@
     depth = slots[0][2].shape[1] // 3 * 2
     tile = 256
     narrow = pl.BlockSpec((tile, hidden), lambda i: (i, 0))
-    w_spec = gu_spec(slots[0][2])
+    w_specs = [gu_spec(weight, depth) for weight in slots[0][2:]]
     steps = rows // tile // 2
     return kernel_call(
         experts_input_kernel,
         grid=(rows // tile,),
-        in_specs=([narrow] * 2 + [w_spec] * 4) * 2,
+        in_specs=([narrow] * 2 + w_specs) * 2,
         out_specs=[
             pl.BlockSpec((4, tile, depth), lambda i: (0, jnp.minimum(i, steps - 1), 0)),
             pl.BlockSpec((4, tile, depth), lambda i: (0, jnp.maximum(i - steps, 0), 0)),
@@ -1069,16 +1070,15 @@
 def experts_grad(inputs, pre_grad, middle, pair, part, side, got=()):
     _, rows, depth = inputs.shape
     hidden, down = pre_grad.shape[1], middle.shape[2]
-    step = hidden // 2
-    piece = pl.BlockSpec((1, (depth + down) // 2, step), lambda q, j: (q, 0, j))
+    piece = pl.BlockSpec((1, (depth + down) // 2, hidden), lambda q: (q, 0, 0))
     return kernel_call(
         experts_grad_kernel,
-        grid=(2, 2),
+        grid=(2,),
         in_specs=[
-            pl.BlockSpec((1, rows, depth // 2), lambda q, j: (part, 0, q)),
-            pl.BlockSpec((rows, step), lambda q, j: (0, j)),
-            pl.BlockSpec((1, rows, down // 2), lambda q, j: (part, 0, q)),
-            pl.BlockSpec((rows, step), lambda q, j: (0, j + 2 * side)),
+            pl.BlockSpec((1, rows, depth // 2), lambda q: (part, 0, q)),
+            pl.BlockSpec((rows, hidden), lambda q: (0, 0)),
+            pl.BlockSpec((1, rows, down // 2), lambda q: (part, 0, q)),
+            pl.BlockSpec((rows, hidden), lambda q: (0, side)),
         ]
         + [piece] * len(got),
         out_specs=piece,
@@ -1086,63 +1086,32 @@
     )(inputs, pre_grad, middle, pair, *got)
 
 
-def gain_grad_kernel(rank, g_ref, x_ref, scale_ref, o_ref, *, codes):
-    half = len(codes) // 2
-    block = x_ref.shape[1] // len(codes)
-
-    @pl.when(pl.program_id(0) == 0)
-    def _():
-        o_ref[...] = jnp.zeros_like(o_ref)
-
-    for place, code in enumerate(codes):
-        columns = dynamic_block(rank[0] ^ code, block)
-        grad = g_ref[place // half, :, place % half * block : (place % half + 1) * block]
-        product = grad * (x_ref[:, columns].astype(jnp.float32) * scale_ref[...])
-        o_ref[:, columns] += jnp.sum(product, axis=0, keepdims=True)
-
-
-def gain_grad(rank, grad, value, scale, codes):
-    rows, width = value.shape
+def chip_grad_kernel(x_ref, *refs, count):
+    o_ref = refs[-1]
+    width = o_ref.shape[1] // count
+    for i in range(count):
+        at = slice(i * width, (i + 1) * width)
+        total = t_dot(x_ref[0], refs[i][...])
+        if len(refs) > count + 1:
+            total += refs[count][:, at].astype(jnp.float32)
+        o_ref[:, at] = total.astype(jnp.bfloat16)
+
+
+def chip_grad(halves, part, grads, start=0, got=()):
+    depth = halves.shape[2]
+    rows = grads[0].shape[0]
+    width = sum(grad.shape[1] for grad in grads)
     tile = 256
+    piece = pl.BlockSpec((tile, width), lambda i: (i, 0))
     return kernel_call(
-        functools.partial(gain_grad_kernel, codes=codes),
-        grid_spec=pltpu.PrefetchScalarGridSpec(
-            num_scalar_prefetch=1,
-            grid=(rows // tile,),
-            in_specs=[
-                pl.BlockSpec((2, tile, width // 2), lambda i, rank: (0, i, 0)),
-                pl.BlockSpec((tile, width), lambda i, rank: (i, 0)),
-                pl.BlockSpec((tile, 1), lambda i, rank: (i, 0)),
-            ],
-            out_specs=pl.BlockSpec((1, width), lambda i, rank: (0, 0)),
-        ),
-        out_shape=jax.ShapeDtypeStruct((1, width), jnp.float32),
-    )(rank, grad, value, scale)
-
-
-def chip_grad_kernel(x_ref, g_ref, *refs):
-    total = t_dot(x_ref[0], g_ref[...])
-    if len(refs) == 2:
-        total += refs[0][...].astype(jnp.float32)
-    refs[-1][...] = total.astype(jnp.bfloat16)
-
-
-def chip_grad(halves, part, grad, start=0, got=()):
-    depth = halves.shape[2]
-    rows, width = grad.shape
-    tile, step = 512, 512
-    piece = pl.BlockSpec((tile, step), lambda i, j: (i, j))
-    return kernel_call(
-        chip_grad_kernel,
-        grid=(depth // tile, width // step),
-        in_specs=[
-            pl.BlockSpec((1, rows, tile), lambda i, j: (part, start // rows, i)),
-            pl.BlockSpec((rows, step), lambda i, j: (0, j)),
-        ]
+        functools.partial(chip_grad_kernel, count=len(grads)),
+        grid=(depth // tile,),
+        in_specs=[pl.BlockSpec((1, rows, tile), lambda i: (part, start // rows, i))]
+        + [pl.BlockSpec(grad.shape, lambda i: (0, 0)) for grad in grads]
         + [piece] * len(got),
         out_specs=piece,
         out_shape=jax.ShapeDtypeStruct((depth, width), jnp.bfloat16),
-    )(halves, grad, *got)
+    )(halves, *grads, *got)
 
 
 def mixed_back_kernel(g_ref, a_ref, b_ref, o_ref):
@@ -1397,7 +1366,7 @@
     mixed, out_w, e_b, b_x, b_y, e_3, e_1, own = hold(mixed, out_w, e_b, b_x, b_y, e_3, e_1, own)
 
     b_0, b_1 = jnp.stack([e_b[0], b_x]), jnp.stack([e_b[1], b_y])
-    b_2, b_3 = other_ways(b_0, b_1)
+    b_2, b_3 = other_ways(b_0[:, :quarter_rows], b_1[:, :quarter_rows])
     e_4 = mirrored(e_3, [(2, 3)])
     mixed, lse_1 = attend(rank, operands, bias_small, HEADS // 2, (mixed,))
     branch, _ = project(mixed, *out_w, f32)
@@ -1429,16 +1398,20 @@
 
     e_a = jnp.where(m == 0, own, jnp.where(m == 1, e_1, jnp.where(m == 2, e_3, e_4)))
     a_x, a_y = both_ways(e_a)
-    weights_b = (b_0, b_2, b_1, b_3)
-    gate_pre_b, up_pre_b, my_b, mx_b = experts_up(quarter_rank, moe_y, moe_x, weights_b)
+    b_4, b_5 = other_ways(b_0[:, quarter_rows:], b_1[:, quarter_rows:])
+    up_weights_b, down_weights_b = (b_0, b_2, b_1, b_3), (b_0, b_4, b_1, b_5)
+    gate_pre_b, up_pre_b, my_b, mx_b = experts_up(quarter_rank, moe_y, moe_x, up_weights_b)
     e_a, a_x, a_y, my_b, mx_b, moe_y, moe_x = hold(e_a, a_x, a_y, my_b, mx_b, moe_y, moe_x)
 
     a_0, a_1 = jnp.stack([e_a[0], a_x]), jnp.stack([e_a[1], a_y])
-    a_2, a_3 = other_ways(a_0, a_1)
-    weights_a = (a_0, a_2, a_1, a_3)
-    gate_pre_a, up_pre_a, my_a, mx_a = experts_up(quarter_rank, moe_y, moe_x, weights_a)
+    a_2, a_3 = other_ways(a_0[:, :quarter_rows], a_1[:, :quarter_rows])
+    a_0, a_1, a_2, a_3 = hold(a_0, a_1, a_2, a_3)
+
+    a_4, a_5 = other_ways(a_0[:, quarter_rows:], a_1[:, quarter_rows:])
+    up_weights_a, down_weights_a = (a_0, a_2, a_1, a_3), (a_0, a_4, a_1, a_5)
+    gate_pre_a, up_pre_a, my_a, mx_a = experts_up(quarter_rank, moe_y, moe_x, up_weights_a)
     expert_out_a, expert_out_b, mixture, mixture_other = experts_down(
-        (gates_a, gates_b), ((my_a, mx_a) + weights_a, (my_b, mx_b) + weights_b)
+        (gates_a, gates_b), ((my_a, mx_a) + down_weights_a, (my_b, mx_b) + down_weights_b)
     )
     result = residual + (mixture + across(mixture_other, 1))
     output = result.astype(bf16)
@@ -1455,7 +1428,7 @@
         gates_b,
         gate_pre_b,
         up_pre_b,
-        weights_b,
+        down_weights_b,
     )
     sent_x = experts_grad(moe_x, dg_b, mx_b, pair_b, 1, 0)
     sent_y = experts_grad(moe_y, du_b, my_b, pair_b, 1, 1)
@@ -1470,12 +1443,12 @@
         gates_a,
         gate_pre_a,
         up_pre_a,
-        weights_a,
+        down_weights_a,
     )
     sent_x = experts_grad(moe_x, dg_a, mx_a, pair_a, 1, 0)
     sent_y = experts_grad(moe_y, du_a, my_a, pair_a, 1, 1)
     input_grad, input_other = experts_input(
-        ((dg_a, du_a) + weights_a, (dg_b, du_b) + weights_b)
+        ((dg_a, du_a) + up_weights_a, (dg_b, du_b) + up_weights_b)
     )
     slot_grads = jnp.concatenate([gate_grad_a, gate_grad_b], 1)
     own_slots, partner_slots = slot_grads[:local_rows], across(slot_grads[local_rows:], 1)
@@ -1493,7 +1466,6 @@
     a_x, a_y = both_ways((sent_x, sent_y))
     b_0 = experts_grad(moe_x, dg_b, mx_b, pair_b, 0, 0, (b_x,))
     b_1 = experts_grad(moe_y, du_b, my_b, pair_b, 0, 1, (b_y,))
-    b_y, b_x = other_ways(b_0[1], b_1[1])
     router_local = jnp.concatenate(
         [
             jnp.dot(part.T.astype(f32), logit_grad, precision=highest, preferred_element_type=f32)
@@ -1514,39 +1486,66 @@
         scale_moe,
         gain_moe,
     )
-    out_sent = across(chip_grad(mixed, 1, branch_grad), 1)
-    out_sum = chip_grad(mixed, 0, branch_grad, 0, (out_sent,)).reshape(2, 2, -1, width)
+    out_sent = across(chip_grad(mixed, 1, (branch_grad,)), 1)
+    out_sum = chip_grad(mixed, 0, (branch_grad,), 0, (out_sent,)).reshape(2, 2, -1, width)
     mixed_grad = mixed_back(branch_grad, out_w)
+    b_0, b_1, out_sum, mixed_grad, branch_grad = hold(b_0, b_1, out_sum, mixed_grad, branch_grad)
+
+    b_y, b_x = other_ways(b_0[1], b_1[1])
+    out_x, out_y = across(out_sum[:, 1, :, :half], 2), across(out_sum[1, :, :, half:], 4)
     bias = mask_of(local_rows // 2)
     dq_0, dk_0, dv_0 = attend_back(rank, operands, bias, mixed_grad, lse_0, 0)
     dq_1, dk_1, dv_1 = attend_back(rank, operands, bias, mixed_grad, lse_1, HEADS // 2)
-    a_x, a_y, b_0, b_1, b_x, b_y, out_sum, dq_0, dk_0, dv_0, dq_1, dk_1, dv_1 = hold(
-        a_x, a_y, b_0, b_1, b_x, b_y, out_sum, dq_0, dk_0, dv_0, dq_1, dk_1, dv_1
+    a_x, a_y, b_0, b_1, b_x, b_y, out_sum, out_x, out_y, dq_0, dk_0, dv_0, dq_1, dk_1, dv_1 = hold(
+        a_x, a_y, b_0, b_1, b_x, b_y, out_sum, out_x, out_y, dq_0, dk_0, dv_0, dq_1, dk_1, dv_1
     )
 
     a_0 = experts_grad(moe_x, dg_a, mx_a, pair_a, 0, 0, (a_x,))
     a_1 = experts_grad(moe_y, du_a, my_a, pair_a, 0, 1, (a_y,))
     a_y, a_x = other_ways(a_0[1], a_1[1])
-    out_x, out_y = across(out_sum[:, 1, :, :half], 2), across(out_sum[1, :, :, half:], 4)
+    out_a, out_b = add(out_sum[:, 0, :, :half], out_x), add(out_sum[0, :, :, half:], out_y)
+    out_x, out_y = across(out_b[1], 2), across(out_a[1], 4)
     b_end = jnp.stack([add(b_0[0], b_y), add(b_1[0], b_x)])
     b_got = mirrored(b_end, [(3, 2), (0, 1)])
+    value_sent = chip_grad(normed, 1, (dv_0, dv_1))
+    value_got = across(value_sent, 1)
+    value_sum = chip_grad(normed, 0, (dv_0, dv_1), 0, (value_got,)).reshape(2, 2, -1, width)
+    value_x = across(value_sum[:, 1, :, :half], 2)
+    value_y = across(value_sum[1, :, :, half:], 4)
     query_lin_grad, q_gain_local = lin_back(
         dq_0, dq_1, query_lin, scale_query, gain_query[None], cosine[behind:], sine[behind:]
     )
     key_lin_grad, k_gain_local = lin_back(
         dk_0, dk_1, key_lin, scale_key, gain_key[None], cosine, sine
     )
-    value_sent = (chip_grad(normed, 1, dv_0), chip_grad(normed, 1, dv_1))
+    query_sent = chip_grad(normed, 1, (query_lin_grad,), behind)
+    key_sent = chip_grad(normed, 1, (key_lin_grad,))
+    packed = jnp.concatenate(
+        [
+            jnp.broadcast_to(squares, (1, width)),
+            q_gain_local,
+            k_gain_local,
+            moe_gain_local,
+            router_local.T,
+        ],
+        0,
+    )
     (
-        a_0, a_1, a_x, a_y, out_sum, out_x, out_y, b_end, b_got, query_lin_grad, key_lin_grad,
-        value_sent, dv_0, dv_1,
+        a_0, a_1, a_x, a_y, out_a, out_b, out_x, out_y, b_end, b_got, query_lin_grad, key_lin_grad,
+        value_sum, value_x, value_y, query_sent, key_sent, packed,
     ) = hold(
-        a_0, a_1, a_x, a_y, out_sum, out_x, out_y, b_end, b_got, query_lin_grad, key_lin_grad,
-        value_sent, dv_0, dv_1,
-    )
-
-    out_a, out_b = add(out_sum[:, 0, :, :half], out_x), add(out_sum[0, :, :, half:], out_y)
-    out_x, out_y = across(out_b[1], 2), across(out_a[1], 4)
+        a_0, a_1, a_x, a_y, out_a, out_b, out_x, out_y, b_end, b_got, query_lin_grad, key_lin_grad,
+        value_sum, value_x, value_y, query_sent, key_sent, packed,
+    )
+
+    query_got, key_got = across(query_sent, 1), across(key_sent, 1)
+    value_a = add(value_sum[:, 0, :, :half], value_x)
+    value_b = add(value_sum[0, :, :, half:], value_y)
+    for link in (1, 2, 4):
+        packed = packed + across(packed, link)
+    value_a, value_b, packed = hold(value_a, value_b, packed)
+    value_x, value_y = across(value_b[1], 2), across(value_a[1], 4)
+    out_total = ep_sum(jnp.stack([add(out_a[0], out_y), add(out_b[0], out_x)]))
     b_low = add(b_end, b_got)
     b_got_2 = mirrored(b_low, [(2, 1)])
     a_end = jnp.stack([add(a_0[0], a_y), add(a_1[0], a_x)])
@@ -1554,74 +1553,45 @@
     normed_grad = project_back(
         key_lin_grad, dv_0, dv_1, query_lin_grad, key_w, value_w, query_w
     )
-    out_a, out_b, out_x, out_y, normed_grad, value_sent, query_lin_grad, key_lin_grad = hold(
-        out_a, out_b, out_x, out_y, normed_grad, value_sent, query_lin_grad, key_lin_grad
-    )
-
+    query_sum = chip_grad(normed, 0, (query_lin_grad,), behind, (query_got,))
+    key_sum = chip_grad(normed, 0, (key_lin_grad,), 0, (key_got,))
+    (
+        normed_grad, query_sum, key_sum, value_a, value_b, value_x, value_y, b_got_2, a_end, a_got,
+        packed,
+    ) = hold(
+        normed_grad, query_sum, key_sum, value_a, value_b, value_x, value_y, b_got_2, a_end, a_got,
+        packed,
+    )
+
+    query_sum = query_sum.reshape(2, 2, -1, width)
+    key_sum = key_sum.reshape(2, 2, -1, width)
+    query_x, key_y = across(query_sum[:, 1], 2), across(key_sum[1], 4)
     carried = from_behind(normed_grad[:, :local_rows].astype(bf16), "ep", -1)
-    value_got = across(value_sent[0], 1), across(value_sent[1], 1)
-    out_total = ep_sum(jnp.stack([add(out_a[0], out_y), add(out_b[0], out_x)]))
-    attn_gain_local = gain_grad(rank, normed_grad, tokens_all, scale_all, order)
-    query_sent = chip_grad(normed, 1, query_lin_grad, behind)
-    key_sent = chip_grad(normed, 1, key_lin_grad)
-    value_a = chip_grad(normed, 0, dv_0, 0, (value_got[0],)).reshape(2, 2, -1, half)
-    value_b = chip_grad(normed, 0, dv_1, 0, (value_got[1],)).reshape(2, 2, -1, half)
-    packed = jnp.concatenate(
-        [
-            jnp.broadcast_to(squares, (1, width)),
-            attn_gain_local,
-            q_gain_local,
-            k_gain_local,
-            moe_gain_local,
-            router_local.T,
-        ],
-        0,
-    )
-    carried, value_a, value_b, query_sent, key_sent, query_lin_grad, key_lin_grad, packed = hold(
-        carried, value_a, value_b, query_sent, key_sent, query_lin_grad, key_lin_grad, packed
-    )
-
-    query_got, key_got = across(query_sent, 1), across(key_sent, 1)
-    value_x, value_y = across(value_a[:, 1], 2), across(value_b[1], 4)
+    a_low = add(a_end, a_got)
+    a_got = mirrored(a_low, [(2, 1)])
+    value_total = ep_sum(jnp.stack([add(value_a[0], value_y), add(value_b[0], value_x)]))
+    b_total = (b_end.astype(f32) + b_got.astype(f32) + b_got_2.astype(f32)).astype(bf16)
+    query_sum, key_sum, query_x, key_y, carried, a_low, a_got, packed, b_total = hold(
+        query_sum, key_sum, query_x, key_y, carried, a_low, a_got, packed, b_total
+    )
+
+    query_sum, key_sum = add(query_sum[:, 0], query_x), add(key_sum[0], key_y)
+    query_y, key_x = across(query_sum[1], 4), across(key_sum[1], 2)
     for back in range(1, reach):
         here = normed_grad[:, back * local_rows : (back + 1) * local_rows] + carried.astype(f32)
         carried = from_behind(here.astype(bf16), "ep", -1)
-    query_sum = chip_grad(normed, 0, query_lin_grad, behind, (query_got,))
-    key_sum = chip_grad(normed, 0, key_lin_grad, 0, (key_got,))
-    query_sum = query_sum.reshape(2, 2, -1, width)
-    key_sum = key_sum.reshape(2, 2, -1, width)
-    packed = packed + across(packed, 1)
-    carried, value_a, value_b, value_x, value_y, query_sum, key_sum, packed, a_end, a_got = hold(
-        carried, value_a, value_b, value_x, value_y, query_sum, key_sum, packed, a_end, a_got
-    )
-
-    query_x, key_y = across(query_sum[:, 1], 2), across(key_sum[1], 4)
-    value_a, value_b = add(value_a[:, 0], value_x), add(value_b[0], value_y)
-    value_x, value_y = across(value_b[1], 2), across(value_a[1], 4)
-    a_low = add(a_end, a_got)
-    a_got = mirrored(a_low, [(2, 1)])
-    packed = packed + across(packed, 2)
+    a_low = add(a_low, a_got)
+    a_got = mirrored(a_low, [(1, 0)])
+    query_sum, key_sum, query_y, key_x, carried, packed, a_low, a_got = hold(
+        query_sum, key_sum, query_y, key_x, carried, packed, a_low, a_got
+    )
+
+    qk_total = ep_sum(jnp.stack([add(query_sum[0], query_y), add(key_sum[0], key_x)]))
+    packed = jnp.sum(over_ep(packed, place), axis=0)
     tokens_grad = tokens_back(
         rank, normed_grad, carried, tokens, residual_grad, scale_all, gain_attn, reps
     )
-    query_sum, key_sum, query_x, key_y, value_a, value_b, value_x, value_y, packed, a_low, a_got = hold(
-        query_sum, key_sum, query_x, key_y, value_a, value_b, value_x, value_y, packed, a_low, a_got
-    )
-
-    query_sum, key_sum = add(query_sum[:, 0], query_x), add(key_sum[0], key_y)
-    query_y, key_x = across(query_sum[1], 4), across(key_sum[1], 2)
-    value_total = ep_sum(jnp.stack([add(value_a[0], value_y), add(value_b[0], value_x)]))
-    packed = packed + across(packed, 4)
-    a_low = a_low.astype(f32) + a_got.astype(f32)
-    a_got = mirrored(a_low.astype(bf16), [(1, 0)])
-    query_sum, key_sum, query_y, key_x, packed, a_low, a_got = hold(
-        query_sum, key_sum, query_y, key_x, packed, a_low, a_got
-    )
-
-    qk_total = ep_sum(jnp.stack([add(query_sum[0], query_y), add(key_sum[0], key_x)]))
-    packed = jnp.sum(over_ep(packed, place), axis=0)
-    b_total = b_end.astype(f32) + b_got.astype(f32) + b_got_2.astype(f32)
-    mine = jnp.where(m == 0, a_low + a_got.astype(f32), b_total)
+    mine = jnp.where(m == 0, add(a_low, a_got), b_total)
 
     def own_half(piece):
         return piece.reshape(2, 2, -1, piece.shape[2])
@@ -1629,12 +1599,17 @@
     tops, bottoms = own_half(mine[:, :quarter_rows]), own_half(mine[:, quarter_rows:])
     halves = jnp.concatenate([tops, bottoms], 2)
     other = across(pick(halves, 1 - core, 1), 1)
-    mine = jnp.where(m < 2, pick(halves, core, 1), other)
+    mine = jnp.where(m < 2, pick(halves, core, 1), other).astype(f32)
     top = quarter_rows // 2
     down_out = jnp.concatenate([mine[0, top:], mine[1, top:]], 1)
     out_out = jnp.concatenate([out_total[0], out_total[1]], 1)
     value_out = jnp.concatenate([value_total[0], value_total[1]], 1)
     loss = packed[0, 0] / (2.0 * count * width)
+    attn_gain_out = (
+        jnp.sum(w_query.astype(f32) * qk_total[0], axis=1)
+        + jnp.sum(w_key.astype(f32) * qk_total[1], axis=1)
+        + jnp.sum(w_value.astype(f32) * value_out, axis=1)
+    ) / attn_gain.astype(f32)
     shares = lax.dynamic_slice_in_dim(
         packed, (rep * experts + shard) * shard_rows, shard_rows, 1
     )
@@ -1642,15 +1617,15 @@
         output,
         loss,
         tokens_grad,
+        attn_gain_out,
         shares[1],
         shares[2],
         shares[3],
-        shares[4],
         qk_total[0],
         qk_total[1],
         value_out,
         out_out,
-        shares[5:].T,
+        shares[4:].T,
         mine[0, :top][None],
         mine[1, :top][None],
         down_out[None],

time: 1410 us -> 1380 us (0.979)
  Pallas kernels: 539 us -> 498 us
    ppermute x6, waiting for transfers between devices: 56.2 us -> 126 us  [from_behind(): lax.ppermute(value, axis, [(source, source + steps) for source in range(l...]
    pallas_call x19 -> x16, Pallas kernels: 176 us -> 137 us  [the longest x8 74.3 us: chip_grad(): kernel_call(functools.partial(chip_grad_kernel, count=len(grads)), grid=(...]
    ppermute x9, waiting for transfers between devices: 33 us -> 5.76 us  [mirrored(): return lax.ppermute(value, ('rep', 'ep'), pairs)]
    ppermute x55 -> x58, waiting for transfers between devices: 262 us -> 244 us  [across(): lax.ppermute(value, 'rep', [(place, place ^ bit) for place in range(count)])]
    ppermute x9, waiting for transfers between devices: 35 us -> 19.9 us  [along(): lax.ppermute(value, 'ep', [(place, (place + steps) % count) for place in...]
    unnamed x161 -> x167, local copies, waits for them, and re-layouts: 31.9 us -> 28.2 us
    ppermute x55 -> x58, starting transfers between devices: 49.2 us -> 50.8 us  [across(): lax.ppermute(value, 'rep', [(place, place ^ bit) for place in range(count)])]
  transfers between devices with their start and end apart: 83 -> 86, of which waited for: 38 -> 36; matrix products, arithmetic and copies ran while one was open for 17% -> 17% of each run, Pallas kernels for 30% -> 28%
where the time goes in v5:
time: 1380 us; the launch traced here: 1370 us
  Pallas kernels  498 us (36%)
  waiting for transfers between devices  421 us (31%)
  other arithmetic  178 us (13%)
  starting transfers between devices  136 us (10%)
  local copies, waits for them, and re-layouts  113 us (8%)
  between operations  21.7 us (2%)
    ppermute x58, waiting for transfers between devices, across(): lax.ppermute(value, 'rep', [(place, place ^ bit) for place in range(count)])  244 us
    ppermute x6, waiting for transfers between devices, from_behind(): lax.ppermute(value, axis, [(source, source + steps) for source in range(l...  126 us
    pallas_call x8, Pallas kernels, chip_grad(): kernel_call(functools.partial(chip_grad_kernel, count=len(grads)), grid=(...  74.3 us
    pallas_call x8, Pallas kernels, experts_grad(): kernel_call(experts_grad_kernel, grid=(2,), in_specs=[pl.BlockSpec((1, ro...  63.1 us
    pallas_call x4, Pallas kernels, project(): kernel_call(project_kernel, grid=(rows // tile,), in_specs=[pl.BlockSpec(...  58.8 us
    pallas_call x2, Pallas kernels, attend_back(): kernel_call(functools.partial(attend_back_kernel, behind=all_rows - rows,...  57.7 us
    ppermute x58, starting transfers between devices, across(): lax.ppermute(value, 'rep', [(place, place ^ bit) for place in range(count)])  50.8 us
    pallas_call x1, Pallas kernels, project_back(): kernel_call(functools.partial(project_back_kernel, tile=512), grid=(2 * h...  41 us
  transfers between devices with their start and end apart: 86, of which 36 were waited for; matrix products, arithmetic and copies ran while one was open for 17% of the time, Pallas kernels for 28%

profile of v5, /device:TPU:0, one launch (start us, length us, event | category | flops | bytes accessed | tf_op | source)
XLA Modules:
  0.0 1373.5 jit_solution(10127748544341497454)
XLA Ops:
  40.0 18.7 %collective-permute-done.1 = bf16[2,64,2048]{2,1,0:T(8,128)(2,1)} collective-permute-done((bf16[2,64,2048]{2,1,0:T(8,128)(2,1)}, bf16[2,64,2048]{2,1,0:T(8,128)(2,1)}, u32[]{:S(2)}, u32[]{:S(2)}) %collective-permute-start.1) | collective-permute-done | bytes 524320 | tf_op jit(solution)/shard_map/ppermute | solution.py:1143
  125.5 19.8 %collective-permute-done.11 = bf16[2,256,2048]{2,1,0:T(8,128)(2,1)} collective-permute-done((bf16[2,256,2048]{2,1,0:T(8,128)(2,1)}, bf16[2,256,2048]{2,1,0:T(8,128)(2,1)}, u32[]{:S(2)}, u32[]{:S(2)}) %collective-permute-start.11) | collective-permute-done | bytes 2097184 | tf_op jit(solution)/shard_map/ppermute | solution.py:1138
  145.4 18.6 %collective-permute-done.12 = bf16[512,2048]{1,0:T(8,128)(2,1)} collective-permute-done((bf16[512,2048]{1,0:T(8,128)(2,1)}, bf16[512,2048]{1,0:T(8,128)(2,1)}, u32[]{:S(2)}, u32[]{:S(2)}) %collective-permute-start.12) | collective-permute-done | bytes 2097184 | tf_op jit(solution)/shard_map/ppermute | solution.py:24
  222.4 20.2 %collective-permute-done.17 = bf16[512,2048]{1,0:T(8,128)(2,1)} collective-permute-done((bf16[512,2048]{1,0:T(8,128)(2,1)}, bf16[512,2048]{1,0:T(8,128)(2,1)}, u32[]{:S(2)}, u32[]{:S(2)}) %collective-permute-start.17) | collective-permute-done | bytes 2097184 | tf_op jit(solution)/shard_map/ppermute | solution.py:24
  272.7 19.7 %shard_map.281 = (f32[1536,2048]{1,0:T(8,128)}, f32[1536,1]{1,0:T(8,128)}) custom-call(bf16[2,1536,1024]{2,1,0:T(8,128)(2,1)} %get-tuple-element.246.low_ref.high_ref.x_ref, bf16[2,1536,1024]{2,1,0:T(8,128)(2,1)} %get-tuple-element.246.low_ref.high_ref.x_ref, bf16[1040,2048]{1,0:T(8,128)(2,1)} %pad_dynamic-update-slice_fusion.a_ref.ka, ...), custom_call_target="tpu_custom_call" | custom-call | tf_op jit(solution)/shard_map/pallas_call | solution.py:470
  292.4 19.3 %shard_map.282 = (bf16[1536,2048]{1,0:T(8,128)(2,1)}, f32[1536,1]{1,0:T(8,128)}) custom-call(bf16[2,1536,1024]{2,1,0:T(8,128)(2,1)} %get-tuple-element.246.low_ref.high_ref.x_ref, bf16[2,1536,1024]{2,1,0:T(8,128)(2,1)} %get-tuple-element.246.low_ref.high_ref.x_ref, bf16[1024,2048]{1,0:T(8,128)(2,1)} %pad_maximum_fusion.1.a_ref.va, ...), custom_call_target="tpu_custom_call" | custom-call | tf_op jit(solution)/shard_map/pallas_call | solution.py:470
  349.8 19.6 %shard_map.284 = (bf16[2,512,1024]{2,1,0:T(8,128)(2,1)}, f32[8,1,512]{2,1,0:T(1,128)}) custom-call(s32[1]{0:T(128)} %bitcast.rank, f32[512,2048]{1,0:T(8,128)} %get-tuple-element.248.q_ref.lin_ref, f32[1536,2048]{1,0:T(8,128)} %get-tuple-element.249.k_ref.lin_ref, bf16[1536,2048]{1,0:T(8,128)(2,1)} %get-tuple-element.250.v_ref, ...), custom_call_target="tpu_custom_call" | custom-call | tf_op jit(solution)/shard_map/pallas_call | solution.py:645
  369.4 19.7 %shard_map.285 = (bf16[2,512,1024]{2,1,0:T(8,128)(2,1)}, f32[8,1,512]{2,1,0:T(1,128)}) custom-call(s32[1]{0:T(128)} %bitcast.rank, f32[512,2048]{1,0:T(8,128)} %get-tuple-element.248.q_ref.lin_ref, f32[1536,2048]{1,0:T(8,128)} %get-tuple-element.249.k_ref.lin_ref, bf16[1536,2048]{1,0:T(8,128)(2,1)} %get-tuple-element.250.v_ref, ...), custom_call_target="tpu_custom_call", output_to_operand_aliasing={{0}: (11, {})} | custom-call | tf_op jit(solution)/shard_map/pallas_call | solution.py:645
  436.1 26.2 %collective-permute-done.29.ub.refs_11_ = bf16[2,512,1024]{2,1,0:T(8,128)(2,1)} collective-permute-done((bf16[2,512,1024]{2,1,0:T(8,128)(2,1)}, bf16[2,512,1024]{2,1,0:T(8,128)(2,1)}, u32[]{:S(2)}, u32[]{:S(2)}) %collective-permute-start.29) | collective-permute-done | bytes 2097184 | tf_op jit(solution)/shard_map/ppermute | solution.py:1138
  472.0 15.2 %shard_map.288 = (f32[1024,1024]{1,0:T(8,128)}, f32[1024,1024]{1,0:T(8,128)}, bf16[2,1024,512]{2,1,0:T(8,128)(2,1)}, bf16[2,1024,512]{2,1,0:T(8,128)(2,1)}) custom-call(s32[1]{0:T(128)} %bitcast.56.rank, bf16[2,1024,1024]{2,1,0:T(8,128)(2,1)} %copy-done, bf16[2,1024,1024]{2,1,0:T(8,128)(2,1)} %pad_maximum_fusion.4.z_ref.x_ref, ...), custom_call_target="tpu_custom_call" | custom-call | tf_op jit(solution)/shard_map/pallas_call | solution.py:835
  487.2 17.5 %collective-permute-done.32 = bf16[768,1024]{1,0:T(8,128)(2,1)S(1)} collective-permute-done((bf16[768,1024]{1,0:T(8,128)(2,1)}, bf16[768,1024]{1,0:T(8,128)(2,1)S(1)}, u32[]{:S(2)}, u32[]{:S(2)}) %collective-permute-start.32) | collective-permute-done | bytes 1572896 | tf_op jit(solution)/shard_map/ppermute | solution.py:1138
  524.4 33.7 %collective-permute-done.35.ub.refs_5_ = bf16[2,512,1024]{2,1,0:T(8,128)(2,1)} collective-permute-done((bf16[2,512,1024]{2,1,0:T(8,128)(2,1)}, bf16[2,512,1024]{2,1,0:T(8,128)(2,1)}, u32[]{:S(2)}, u32[]{:S(2)}) %collective-permute-start.35) | collective-permute-done | bytes 2097184 | tf_op jit(solution)/shard_map/ppermute | solution.py:1138
  572.3 15.2 %shard_map.289 = (f32[1024,1024]{1,0:T(8,128)}, f32[1024,1024]{1,0:T(8,128)}, bf16[2,1024,512]{2,1,0:T(8,128)(2,1)}, bf16[2,1024,512]{2,1,0:T(8,128)(2,1)}) custom-call(s32[1]{0:T(128)} %bitcast.56.rank, bf16[2,1024,1024]{2,1,0:T(8,128)(2,1)} %copy-done, bf16[2,1024,1024]{2,1,0:T(8,128)(2,1)} %pad_maximum_fusion.4.z_ref.x_ref, ...), custom_call_target="tpu_custom_call" | custom-call | tf_op jit(solution)/shard_map/pallas_call | solution.py:835
  602.6 18.0 %shard_map.290 = (bf16[1024,2048]{1,0:T(8,128)(2,1)}, bf16[1024,2048]{1,0:T(8,128)(2,1)}, f32[512,2048]{1,0:T(8,128)}, f32[512,2048]{1,0:T(8,128)}) custom-call(f32[1024,1]{1,0:T(8,128)} %broadcast_select_fusion.2.refs_0_.gate_ref, f32[1024,1]{1,0:T(8,128)} %broadcast_select_fusion.1.refs_1_.gate_ref, ...), custom_call_target="tpu_custom_call" | custom-call | tf_op jit(solution)/shard_map/pallas_call | solution.py:884
  694.4 27.9 %shard_map.297 = (f32[4,512,512]{2,1,0:T(8,128)}, f32[4,512,512]{2,1,0:T(8,128)}) custom-call(bf16[1024,1024]{1,0:T(8,128)(2,1)} %get-tuple-element.308.d_ref.refs_0_, bf16[1024,1024]{1,0:T(8,128)(2,1)} %get-tuple-element.312.d_ref.refs_1_, bf16[2,768,1024]{2,1,0:T(8,128)(2,1)} %copy-done.2, bf16[2,512,1024]{2,1,0:T(8,128)(2,1)} %collective-permute-done.34.gb.refs_3_, ...), custom_call_target="tpu_custom_call" | custom-call | tf_op jit(solution)/shard_map/pallas_call | solution.py:986
  819.1 24.7 %collective-permute-done.45.refs_0_ = bf16[2,768,1024]{2,1,0:T(8,128)(2,1)} collective-permute-done((bf16[2,768,1024]{2,1,0:T(8,128)(2,1)}, bf16[2,768,1024]{2,1,0:T(8,128)(2,1)}, u32[]{:S(2)}, u32[]{:S(2)}) %collective-permute-start.45) | collective-permute-done | bytes 3145760 | tf_op jit(solution)/shard_map/ppermute | solution.py:1138
  848.1 28.8 %shard_map.305 = (bf16[512,1024]{1,0:T(8,128)(2,1)}, bf16[1536,1024]{1,0:T(8,128)(2,1)}, bf16[1536,1024]{1,0:T(8,128)(2,1)}) custom-call(s32[1]{0:T(128)} %bitcast.rank, f32[512,2048]{1,0:T(8,128)} %get-tuple-element.248.q_ref.lin_ref, f32[1536,2048]{1,0:T(8,128)} %get-tuple-element.249.k_ref.lin_ref, bf16[1536,2048]{1,0:T(8,128)(2,1)} %get-tuple-element.250.v_ref, ...), custom_call_target="tpu_custom_call" | custom-call | tf_op jit(solution)/shard_map/pallas_call | solution.py:719
  876.9 28.9 %shard_map.304 = (bf16[512,1024]{1,0:T(8,128)(2,1)}, bf16[1536,1024]{1,0:T(8,128)(2,1)}, bf16[1536,1024]{1,0:T(8,128)(2,1)}) custom-call(s32[1]{0:T(128)} %bitcast.rank, f32[512,2048]{1,0:T(8,128)} %get-tuple-element.248.q_ref.lin_ref, f32[1536,2048]{1,0:T(8,128)} %get-tuple-element.249.k_ref.lin_ref, bf16[1536,2048]{1,0:T(8,128)(2,1)} %get-tuple-element.250.v_ref, ...), custom_call_target="tpu_custom_call" | custom-call | tf_op jit(solution)/shard_map/pallas_call | solution.py:719
  924.5 16.7 %collective-permute-start.57 = (bf16[2,768,1024]{2,1,0:T(8,128)(2,1)S(1)}, bf16[2,768,1024]{2,1,0:T(8,128)(2,1)}, u32[]{:S(2)}, u32[]{:S(2)}) collective-permute-start(bf16[2,768,1024]{2,1,0:T(8,128)(2,1)S(1)} %pad_maximum_fusion.10), channel_id=1, source_target_pairs={{3,2},{0,1},{4,5},{7,6},{11,10},{8,9},{12,13},{15,14},{19,18},{16,... | collective-permute-start | bytes 9437192 | tf_op jit(solution)/shard_map/ppermute | solution.py:1154
  1059.5 41.0 %shard_map.314.g_ref = f32[2,1536,1024]{2,1,0:T(8,128)} custom-call(bf16[1536,2048]{1,0:T(8,128)(2,1)} %get-tuple-element.358.refs_0_.k_ref, bf16[1536,1024]{1,0:T(8,128)(2,1)} %get-tuple-element.353.refs_0_.v_ref, bf16[1536,1024]{1,0:T(8,128)(2,1)} %get-tuple-element.354.refs_1_.w_ref, bf16[512,2048]{1,0:T(8,128)(2,1)} %get-tuple-element.359.refs_0_.q_ref, ...), custom_call_target="tpu_custom_call" | custom-call | tf_op jit(solution)/shard_map/pallas_call | solution.py:522
  1150.8 27.7 %collective-permute-done.70 = bf16[2,256,2048]{2,1,0:T(8,128)(2,1)} collective-permute-done((bf16[2,256,2048]{2,1,0:T(8,128)(2,1)}, bf16[2,256,2048]{2,1,0:T(8,128)(2,1)}, u32[]{:S(2)}, u32[]{:S(2)}) %collective-permute-start.70) | collective-permute-done | bytes 2097184 | tf_op jit(solution)/shard_map/ppermute | solution.py:1138
  1180.8 33.2 %collective-permute-done.72 = bf16[2,512,1024]{2,1,0:T(8,128)(2,1)} collective-permute-done((bf16[2,512,1024]{2,1,0:T(8,128)(2,1)}, bf16[2,512,1024]{2,1,0:T(8,128)(2,1)}, u32[]{:S(2)}, u32[]{:S(2)}) %collective-permute-start.72) | collective-permute-done | bytes 2097184 | tf_op jit(solution)/shard_map/ppermute | solution.py:24
  1261.5 52.4 %collective-permute-done.76.c_ref = bf16[2,512,1024]{2,1,0:T(8,128)(2,1)} collective-permute-done((bf16[2,512,1024]{2,1,0:T(8,128)(2,1)}, bf16[2,512,1024]{2,1,0:T(8,128)(2,1)}, u32[]{:S(2)}, u32[]{:S(2)}) %collective-permute-start.76) | collective-permute-done | bytes 2097184 | tf_op jit(solution)/shard_map/ppermute | solution.py:24
  1345.1 17.4 %reduce-scatter.4.cloned.1.call-done = bf16[2,64,2048]{2,1,0:T(8,128)(2,1)} async-done(((bf16[2,256,2048]{2,1,0:T(8,128)(2,1)}), bf16[2,64,2048]{2,1,0:T(8,128)(2,1)}) %reduce-scatter.4.cloned.1.call-update) | async-done | bytes 524304 | tf_op jit(solution)/shard_map/reduce_scatter | solution.py:1194
  (584 shorter events, 771.8 us)
Async XLA Ops:
  7.2 118.4 %all-gather.3.cloned.1.call-start = ((), (), s32[]{:S(2)}) async-start(), calls=%async_computation.6 | async-start | bytes 2621440 | tf_op jit(solution)/shard_map/all_gather | solution.py:1271
  70.0 1167.8 %reduce-scatter.8.cloned.1.call-start = ((), (), s32[]{:S(2)}) async-start(), calls=%async_computation.5 | async-start | bytes 1310720 | tf_op jit(solution)/shard_map/reduce_scatter | solution.py:1194
  95.7 68.2 %collective-permute-start.10 = (bf16[2,272,2048]{2,1,0:T(8,128)(2,1)}, bf16[2,272,2048]{2,1,0:T(8,128)(2,1)}, u32[]{:S(2)}, u32[]{:S(2)}) collective-permute-start(bf16[2,272,2048]{2,1,0:T(8,128)(2,1)} %pad_maximum_fusion.14), channel_id=1, source_target_pairs={{0,16},{4,20},{8,24},{12,28},{16,0},{20,4},{24,8},{28,12},{1,17},{... | collective-permute-start | bytes 6684680 | tf_op jit(solution)/shard_map/ppermute | solution.py:1138
  114.5 88.8 %collective-permute-start.18 = (bf16[2,768,1024]{2,1,0:T(8,128)(2,1)S(1)}, bf16[2,768,1024]{2,1,0:T(8,128)(2,1)}, u32[]{:S(2)}, u32[]{:S(2)}) collective-permute-start(bf16[2,768,1024]{2,1,0:T(8,128)(2,1)S(1)} %pad_maximum_fusion.9), channel_id=1, source_target_pairs={{0,1},{1,2},{7,6},{6,5},{8,9},{9,10},{15,14},{14,13},{16,17},{17,1... | collective-permute-start | bytes 9437192 | tf_op jit(solution)/shard_map/ppermute | solution.py:1154
  246.2 74.4 %collective-permute-start.21 = (bf16[2,768,1024]{2,1,0:T(8,128)(2,1)}, bf16[2,768,1024]{2,1,0:T(8,128)(2,1)}, u32[]{:S(2)}, u32[]{:S(2)}) collective-permute-start(bf16[2,768,1024]{2,1,0:T(8,128)(2,1)} %broadcast_select_fusion), channel_id=1, source_target_pairs={{1,0},{2,3},{6,7},{5,4},{9,8},{10,11},{14,15},{13,12},{17,16},{18,... | collective-permute-start | bytes 9437192 | tf_op jit(solution)/shard_map/ppermute | solution.py:1154
  522.3 65.2 %collective-permute-start.38 = (bf16[2,256,1024]{2,1,0:T(8,128)(2,1)}, bf16[2,256,1024]{2,1,0:T(8,128)(2,1)}, u32[]{:S(2)}, u32[]{:S(2)}) collective-permute-start(bf16[2,256,1024]{2,1,0:T(8,128)(2,1)} %slice.490), channel_id=1, source_target_pairs={{0,16},{4,20},{8,24},{12,28},{16,0},{20,4},{24,8},{28,12},{1,17},{... | collective-permute-start | bytes 3145736 | tf_op jit(solution)/shard_map/ppermute | solution.py:1138
  675.3 70.3 %collective-permute-start.42 = (bf16[2,768,1024]{2,1,0:T(8,128)(2,1)}, bf16[2,768,1024]{2,1,0:T(8,128)(2,1)S(1)}, u32[]{:S(2)}, u32[]{:S(2)}) collective-permute-start(bf16[2,768,1024]{2,1,0:T(8,128)(2,1)} %shard_map.292), channel_id=1, source_target_pairs={{0,8},{4,12},{8,0},{12,4},{16,24},{20,28},{24,16},{28,20},{1,9},{5... | collective-permute-start | bytes 9437192 | tf_op jit(solution)/shard_map/ppermute | solution.py:1138
  676.1 70.2 %collective-permute-start.43 = (bf16[2,768,1024]{2,1,0:T(8,128)(2,1)}, bf16[2,768,1024]{2,1,0:T(8,128)(2,1)}, u32[]{:S(2)}, u32[]{:S(2)}) collective-permute-start(bf16[2,768,1024]{2,1,0:T(8,128)(2,1)} %shard_map.293), channel_id=1, source_target_pairs={{0,16},{4,20},{8,24},{12,28},{16,0},{20,4},{24,8},{28,12},{1,17},{... | collective-permute-start | bytes 9437192 | tf_op jit(solution)/shard_map/ppermute | solution.py:1138
  772.5 71.2 %collective-permute-start.45 = (bf16[2,768,1024]{2,1,0:T(8,128)(2,1)}, bf16[2,768,1024]{2,1,0:T(8,128)(2,1)}, u32[]{:S(2)}, u32[]{:S(2)}) collective-permute-start(bf16[2,768,1024]{2,1,0:T(8,128)(2,1)} %shard_map.295), channel_id=1, source_target_pairs={{0,8},{4,12},{8,0},{12,4},{16,24},{20,28},{24,16},{28,20},{1,9},{5... | collective-permute-start | bytes 9437192 | tf_op jit(solution)/shard_map/ppermute | solution.py:1138
  773.8 132.0 %collective-permute-start.46 = (bf16[2,768,1024]{2,1,0:T(8,128)(2,1)}, bf16[2,768,1024]{2,1,0:T(8,128)(2,1)}, u32[]{:S(2)}, u32[]{:S(2)}) collective-permute-start(bf16[2,768,1024]{2,1,0:T(8,128)(2,1)} %shard_map.296), channel_id=1, source_target_pairs={{0,16},{4,20},{8,24},{12,28},{16,0},{20,4},{24,8},{28,12},{1,17},{... | collective-permute-start | bytes 9437192 | tf_op jit(solution)/shard_map/ppermute | solution.py:1138
  811.7 94.1 %collective-permute-start.49 = (bf16[768,1024]{1,0:T(8,128)(2,1)}, bf16[768,1024]{1,0:T(8,128)(2,1)}, u32[]{:S(2)}, u32[]{:S(2)}) collective-permute-start(bf16[768,1024]{1,0:T(8,128)(2,1)} %slice_bitcast_fusion.9), channel_id=1, source_target_pairs={{0,8},{4,12},{8,0},{12,4},{16,24},{20,28},{24,16},{28,20},{1,9},{5... | collective-permute-start | bytes 4718600 | tf_op jit(solution)/shard_map/ppermute | solution.py:1138
  815.2 90.6 %collective-permute-start.50 = (bf16[768,1024]{1,0:T(8,128)(2,1)}, bf16[768,1024]{1,0:T(8,128)(2,1)}, u32[]{:S(2)}, u32[]{:S(2)}) collective-permute-start(bf16[768,1024]{1,0:T(8,128)(2,1)} %slice_bitcast_fusion.8), channel_id=1, source_target_pairs={{0,16},{4,20},{8,24},{12,28},{16,0},{20,4},{24,8},{28,12},{1,17},{... | collective-permute-start | bytes 4718600 | tf_op jit(solution)/shard_map/ppermute | solution.py:1138
  816.8 89.0 %collective-permute-start.51 = (bf16[2,256,1024]{2,1,0:T(8,128)(2,1)}, bf16[2,256,1024]{2,1,0:T(8,128)(2,1)}, u32[]{:S(2)}, u32[]{:S(2)}) collective-permute-start(bf16[2,256,1024]{2,1,0:T(8,128)(2,1)} %slice_bitcast_fusion.14), channel_id=1, source_target_pairs={{0,8},{4,12},{8,0},{12,4},{16,24},{20,28},{24,16},{28,20},{1,9},{5... | collective-permute-start | bytes 3145736 | tf_op jit(solution)/shard_map/ppermute | solution.py:1138
  924.5 105.0 %collective-permute-start.57 = (bf16[2,768,1024]{2,1,0:T(8,128)(2,1)S(1)}, bf16[2,768,1024]{2,1,0:T(8,128)(2,1)}, u32[]{:S(2)}, u32[]{:S(2)}) collective-permute-start(bf16[2,768,1024]{2,1,0:T(8,128)(2,1)S(1)} %pad_maximum_fusion.10), channel_id=1, source_target_pairs={{3,2},{0,1},{4,5},{7,6},{11,10},{8,9},{12,13},{15,14},{19,18},{16,... | collective-permute-start | bytes 9437192 | tf_op jit(solution)/shard_map/ppermute | solution.py:1154
  958.4 71.1 %collective-permute-start.53 = (bf16[768,1024]{1,0:T(8,128)(2,1)}, bf16[768,1024]{1,0:T(8,128)(2,1)}, u32[]{:S(2)}, u32[]{:S(2)}) collective-permute-start(bf16[768,1024]{1,0:T(8,128)(2,1)} %slice_bitcast_fusion.3), channel_id=1, source_target_pairs={{0,8},{4,12},{8,0},{12,4},{16,24},{20,28},{24,16},{28,20},{1,9},{5... | collective-permute-start | bytes 4718600 | tf_op jit(solution)/shard_map/ppermute | solution.py:1138
  1029.7 82.9 %collective-permute-start.61 = (bf16[1024,2048]{1,0:T(8,128)(2,1)}, bf16[1024,2048]{1,0:T(8,128)(2,1)}, u32[]{:S(2)}, u32[]{:S(2)}) collective-permute-start(bf16[1024,2048]{1,0:T(8,128)(2,1)} %shard_map.312), channel_id=1, source_target_pairs={{0,4},{4,0},{8,12},{12,8},{16,20},{20,16},{24,28},{28,24},{1,5},{5... | collective-permute-start | bytes 12582920 | tf_op jit(solution)/shard_map/ppermute | solution.py:1138
  1035.4 84.3 %collective-permute-start.69 = (bf16[2,768,1024]{2,1,0:T(8,128)(2,1)S(1)}, bf16[2,768,1024]{2,1,0:T(8,128)(2,1)}, u32[]{:S(2)}, u32[]{:S(2)}) collective-permute-start(bf16[2,768,1024]{2,1,0:T(8,128)(2,1)S(1)} %pad_maximum_fusion.11), channel_id=1, source_target_pairs={{3,2},{4,5},{11,10},{12,13},{19,18},{20,21},{27,26},{28,29}} | collective-permute-start | bytes 9437192 | tf_op jit(solution)/shard_map/ppermute | solution.py:1154
  1043.0 76.7 %collective-permute-start.68 = (bf16[2,768,1024]{2,1,0:T(8,128)(2,1)}, bf16[2,768,1024]{2,1,0:T(8,128)(2,1)}, u32[]{:S(2)}, u32[]{:S(2)}) collective-permute-start(bf16[2,768,1024]{2,1,0:T(8,128)(2,1)} %fusion), channel_id=1, source_target_pairs={{2,1},{5,6},{10,9},{13,14},{18,17},{21,22},{26,25},{29,30}} | collective-permute-start | bytes 9437192 | tf_op jit(solution)/shard_map/ppermute | solution.py:1154
  1125.1 89.0 %collective-permute-start.73 = (bf16[2,768,1024]{2,1,0:T(8,128)(2,1)}, bf16[2,768,1024]{2,1,0:T(8,128)(2,1)}, u32[]{:S(2)}, u32[]{:S(2)}) collective-permute-start(bf16[2,768,1024]{2,1,0:T(8,128)(2,1)} %add_convert_fusion.3), channel_id=1, source_target_pairs={{2,1},{5,6},{10,9},{13,14},{18,17},{21,22},{26,25},{29,30}} | collective-permute-start | bytes 9437192 | tf_op jit(solution)/shard_map/ppermute | solution.py:1154
  1129.0 110.7 %reduce-scatter.6.cloned.1.call-start = ((), (), s32[]{:S(2)}) async-start(), calls=%async_computation.4 | async-start | bytes 1310720 | tf_op jit(solution)/shard_map/reduce_scatter | solution.py:1194
  1139.8 74.2 %collective-permute-start.72 = (bf16[2,512,1024]{2,1,0:T(8,128)(2,1)}, bf16[2,512,1024]{2,1,0:T(8,128)(2,1)}, u32[]{:S(2)}, u32[]{:S(2)}) collective-permute-start(bf16[2,512,1024]{2,1,0:T(8,128)(2,1)} %slice.803), channel_id=1, source_target_pairs={{1,0},{2,1},{3,2},{5,4},{6,5},{7,6},{9,8},{10,9},{11,10},{13,12},{... | collective-permute-start | bytes 6291464 | tf_op jit(solution)/shard_map/ppermute | solution.py:24
  1143.7 218.8 %reduce-scatter.4.cloned.1.call-start = ((), (), s32[]{:S(2)}) async-start(), calls=%async_computation.3 | async-start | bytes 2621440 | tf_op jit(solution)/shard_map/reduce_scatter | solution.py:1194
  1218.5 95.4 %collective-permute-start.77 = (bf16[2,768,1024]{2,1,0:T(8,128)(2,1)S(1)}, bf16[2,768,1024]{2,1,0:T(8,128)(2,1)}, u32[]{:S(2)}, u32[]{:S(2)}) collective-permute-start(bf16[2,768,1024]{2,1,0:T(8,128)(2,1)S(1)} %add_convert_fusion.1), channel_id=1, source_target_pairs={{1,0},{6,7},{9,8},{14,15},{17,16},{22,23},{25,24},{30,31}} | collective-permute-start | bytes 9437192 | tf_op jit(solution)/shard_map/ppermute | solution.py:1154
  1225.8 88.1 %collective-permute-start.76 = (bf16[2,512,1024]{2,1,0:T(8,128)(2,1)}, bf16[2,512,1024]{2,1,0:T(8,128)(2,1)}, u32[]{:S(2)}, u32[]{:S(2)}) collective-permute-start(bf16[2,512,1024]{2,1,0:T(8,128)(2,1)} %add_convert_fusion.4), channel_id=1, source_target_pairs={{1,0},{2,1},{3,2},{5,4},{6,5},{7,6},{9,8},{10,9},{11,10},{13,12},{... | collective-permute-start | bytes 6291464 | tf_op jit(solution)/shard_map/ppermute | solution.py:24
  (141 other events, 2892.1 us)
Sparse Core Ops, SparseCore 0:
  70.1 55.3 all-gather.2
  1129.1 34.7 reduce-scatter.7
  1166.9 43.6 reduce-scatter.5
  1319.2 43.2 reduce-scatter.3

commit v6 on v5

--- a/solution.py
+++ b/solution.py
@@ -1420,6 +1420,21 @@
     result_grad = total_tokens / count * valid[:, None] * error
     result_other = across(result_grad, 1)
 
+    pair_a, dg_a, du_a, gate_grad_a = experts_back(
+        quarter_rank,
+        result_grad,
+        result_other,
+        expert_out_a,
+        gates_a,
+        gate_pre_a,
+        up_pre_a,
+        down_weights_a,
+    )
+    sent_x = experts_grad(moe_x, dg_a, mx_a, pair_a, 1, 0)
+    sent_y = experts_grad(moe_y, du_a, my_a, pair_a, 1, 1)
+    sent_x, sent_y, expert_out_b = hold(sent_x, sent_y, expert_out_b)
+
+    a_x, a_y = both_ways((sent_x, sent_y))
     pair_b, dg_b, du_b, gate_grad_b = experts_back(
         quarter_rank,
         result_grad,
@@ -1432,23 +1447,8 @@
     )
     sent_x = experts_grad(moe_x, dg_b, mx_b, pair_b, 1, 0)
     sent_y = experts_grad(moe_y, du_b, my_b, pair_b, 1, 1)
-    sent_x, sent_y, expert_out_a = hold(sent_x, sent_y, expert_out_a)
-
-    b_x, b_y = both_ways((sent_x, sent_y))
-    pair_a, dg_a, du_a, gate_grad_a = experts_back(
-        quarter_rank,
-        result_grad,
-        result_other,
-        expert_out_a,
-        gates_a,
-        gate_pre_a,
-        up_pre_a,
-        down_weights_a,
-    )
-    sent_x = experts_grad(moe_x, dg_a, mx_a, pair_a, 1, 0)
-    sent_y = experts_grad(moe_y, du_a, my_a, pair_a, 1, 1)
     input_grad, input_other = experts_input(
-        ((dg_a, du_a) + up_weights_a, (dg_b, du_b) + up_weights_b)
+        ((dg_b, du_b) + up_weights_b, (dg_a, du_a) + up_weights_a)
     )
     slot_grads = jnp.concatenate([gate_grad_a, gate_grad_b], 1)
     own_slots, partner_slots = slot_grads[:local_rows], across(slot_grads[local_rows:], 1)
@@ -1458,14 +1458,14 @@
     logit_grad = router_probs * (
         prob_grad - jnp.sum(prob_grad * router_probs, axis=-1, keepdims=True)
     )
-    b_x, b_y, sent_x, sent_y, input_grad, input_other, logit_grad = hold(
-        b_x, b_y, sent_x, sent_y, input_grad, input_other, logit_grad
+    a_x, a_y, sent_x, sent_y, input_grad, input_other, logit_grad = hold(
+        a_x, a_y, sent_x, sent_y, input_grad, input_other, logit_grad
     )
 
     input_other = across(input_other, 1)
-    a_x, a_y = both_ways((sent_x, sent_y))
-    b_0 = experts_grad(moe_x, dg_b, mx_b, pair_b, 0, 0, (b_x,))
-    b_1 = experts_grad(moe_y, du_b, my_b, pair_b, 0, 1, (b_y,))
+    b_x, b_y = both_ways((sent_x, sent_y))
+    a_0 = experts_grad(moe_x, dg_a, mx_a, pair_a, 0, 0, (a_x,))
+    a_1 = experts_grad(moe_y, du_a, my_a, pair_a, 0, 1, (a_y,))
     router_local = jnp.concatenate(
         [
             jnp.dot(part.T.astype(f32), logit_grad, precision=highest, preferred_element_type=f32)
@@ -1489,24 +1489,20 @@
     out_sent = across(chip_grad(mixed, 1, (branch_grad,)), 1)
     out_sum = chip_grad(mixed, 0, (branch_grad,), 0, (out_sent,)).reshape(2, 2, -1, width)
     mixed_grad = mixed_back(branch_grad, out_w)
-    b_0, b_1, out_sum, mixed_grad, branch_grad = hold(b_0, b_1, out_sum, mixed_grad, branch_grad)
-
-    b_y, b_x = other_ways(b_0[1], b_1[1])
-    out_x, out_y = across(out_sum[:, 1, :, :half], 2), across(out_sum[1, :, :, half:], 4)
+    a_y, a_x = other_ways(a_0[1], a_1[1])
     bias = mask_of(local_rows // 2)
     dq_0, dk_0, dv_0 = attend_back(rank, operands, bias, mixed_grad, lse_0, 0)
     dq_1, dk_1, dv_1 = attend_back(rank, operands, bias, mixed_grad, lse_1, HEADS // 2)
-    a_x, a_y, b_0, b_1, b_x, b_y, out_sum, out_x, out_y, dq_0, dk_0, dv_0, dq_1, dk_1, dv_1 = hold(
-        a_x, a_y, b_0, b_1, b_x, b_y, out_sum, out_x, out_y, dq_0, dk_0, dv_0, dq_1, dk_1, dv_1
-    )
-
-    a_0 = experts_grad(moe_x, dg_a, mx_a, pair_a, 0, 0, (a_x,))
-    a_1 = experts_grad(moe_y, du_a, my_a, pair_a, 0, 1, (a_y,))
-    a_y, a_x = other_ways(a_0[1], a_1[1])
-    out_a, out_b = add(out_sum[:, 0, :, :half], out_x), add(out_sum[0, :, :, half:], out_y)
-    out_x, out_y = across(out_b[1], 2), across(out_a[1], 4)
-    b_end = jnp.stack([add(b_0[0], b_y), add(b_1[0], b_x)])
-    b_got = mirrored(b_end, [(3, 2), (0, 1)])
+    b_x, b_y, a_0, a_1, a_x, a_y, out_sum, dq_0, dk_0, dv_0, dq_1, dk_1, dv_1 = hold(
+        b_x, b_y, a_0, a_1, a_x, a_y, out_sum, dq_0, dk_0, dv_0, dq_1, dk_1, dv_1
+    )
+
+    b_0 = experts_grad(moe_x, dg_b, mx_b, pair_b, 0, 0, (b_x,))
+    b_1 = experts_grad(moe_y, du_b, my_b, pair_b, 0, 1, (b_y,))
+    b_y, b_x = other_ways(b_0[1], b_1[1])
+    out_x, out_y = across(out_sum[:, 1, :, :half], 2), across(out_sum[1, :, :, half:], 4)
+    a_end = jnp.stack([add(a_0[0], a_y), add(a_1[0], a_x)])
+    a_got = mirrored(a_end, [(3, 2)])
     value_sent = chip_grad(normed, 1, (dv_0, dv_1))
     value_got = across(value_sent, 1)
     value_sum = chip_grad(normed, 0, (dv_0, dv_1), 0, (value_got,)).reshape(2, 2, -1, width)
@@ -1531,10 +1527,10 @@
         0,
     )
     (
-        a_0, a_1, a_x, a_y, out_a, out_b, out_x, out_y, b_end, b_got, query_lin_grad, key_lin_grad,
+        b_0, b_1, b_x, b_y, out_sum, out_x, out_y, a_end, a_got, query_lin_grad, key_lin_grad,
         value_sum, value_x, value_y, query_sent, key_sent, packed,
     ) = hold(
-        a_0, a_1, a_x, a_y, out_a, out_b, out_x, out_y, b_end, b_got, query_lin_grad, key_lin_grad,
+        b_0, b_1, b_x, b_y, out_sum, out_x, out_y, a_end, a_got, query_lin_grad, key_lin_grad,
         value_sum, value_x, value_y, query_sent, key_sent, packed,
     )
 
@@ -1543,36 +1539,39 @@
     value_b = add(value_sum[0, :, :, half:], value_y)
     for link in (1, 2, 4):
         packed = packed + across(packed, link)
-    value_a, value_b, packed = hold(value_a, value_b, packed)
-    value_x, value_y = across(value_b[1], 2), across(value_a[1], 4)
-    out_total = ep_sum(jnp.stack([add(out_a[0], out_y), add(out_b[0], out_x)]))
-    b_low = add(b_end, b_got)
-    b_got_2 = mirrored(b_low, [(2, 1)])
-    a_end = jnp.stack([add(a_0[0], a_y), add(a_1[0], a_x)])
-    a_got = mirrored(a_end, [(3, 2)])
+    out_a, out_b = add(out_sum[:, 0, :, :half], out_x), add(out_sum[0, :, :, half:], out_y)
+    value_a, value_b, packed, out_a, out_b = hold(value_a, value_b, packed, out_a, out_b)
+    moved_x = across(jnp.stack([value_b[1], out_b[1]]), 2)
+    moved_y = across(jnp.stack([value_a[1], out_a[1]]), 4)
+    value_x, value_y, out_x, out_y = moved_x[0], moved_y[0], moved_x[1], moved_y[1]
+    four = [add(out_a[0], out_y), add(out_b[0], out_x)]
+    four += [add(value_a[0], value_y), add(value_b[0], value_x)]
+    four = ep_sum(jnp.stack(four))
+    out_total, value_total = four[:2], four[2:]
+    a_low = add(a_end, a_got)
+    a_got = mirrored(a_low, [(2, 1)])
+    b_end = jnp.stack([add(b_0[0], b_y), add(b_1[0], b_x)])
+    b_got = mirrored(b_end, [(3, 2), (0, 1)])
     normed_grad = project_back(
         key_lin_grad, dv_0, dv_1, query_lin_grad, key_w, value_w, query_w
     )
     query_sum = chip_grad(normed, 0, (query_lin_grad,), behind, (query_got,))
     key_sum = chip_grad(normed, 0, (key_lin_grad,), 0, (key_got,))
     (
-        normed_grad, query_sum, key_sum, value_a, value_b, value_x, value_y, b_got_2, a_end, a_got,
-        packed,
+        normed_grad, query_sum, key_sum, out_total, value_total, a_low, a_got, b_end, b_got, packed,
     ) = hold(
-        normed_grad, query_sum, key_sum, value_a, value_b, value_x, value_y, b_got_2, a_end, a_got,
-        packed,
+        normed_grad, query_sum, key_sum, out_total, value_total, a_low, a_got, b_end, b_got, packed,
     )
 
     query_sum = query_sum.reshape(2, 2, -1, width)
     key_sum = key_sum.reshape(2, 2, -1, width)
     query_x, key_y = across(query_sum[:, 1], 2), across(key_sum[1], 4)
     carried = from_behind(normed_grad[:, :local_rows].astype(bf16), "ep", -1)
-    a_low = add(a_end, a_got)
-    a_got = mirrored(a_low, [(2, 1)])
-    value_total = ep_sum(jnp.stack([add(value_a[0], value_y), add(value_b[0], value_x)]))
-    b_total = (b_end.astype(f32) + b_got.astype(f32) + b_got_2.astype(f32)).astype(bf16)
-    query_sum, key_sum, query_x, key_y, carried, a_low, a_got, packed, b_total = hold(
-        query_sum, key_sum, query_x, key_y, carried, a_low, a_got, packed, b_total
+    a_low = add(a_low, a_got)
+    a_got = mirrored(a_low, [(1, 0)])
+    b_got_2 = mirrored(add(b_end, b_got), [(2, 1)])
+    query_sum, key_sum, query_x, key_y, carried, a_low, a_got, packed, b_got_2 = hold(
+        query_sum, key_sum, query_x, key_y, carried, a_low, a_got, packed, b_got_2
     )
 
     query_sum, key_sum = add(query_sum[:, 0], query_x), add(key_sum[0], key_y)
@@ -1580,10 +1579,17 @@
     for back in range(1, reach):
         here = normed_grad[:, back * local_rows : (back + 1) * local_rows] + carried.astype(f32)
         carried = from_behind(here.astype(bf16), "ep", -1)
-    a_low = add(a_low, a_got)
-    a_got = mirrored(a_low, [(1, 0)])
-    query_sum, key_sum, query_y, key_x, carried, packed, a_low, a_got = hold(
-        query_sum, key_sum, query_y, key_x, carried, packed, a_low, a_got
+    b_total = (b_end.astype(f32) + b_got.astype(f32) + b_got_2.astype(f32)).astype(bf16)
+    mine = jnp.where(m == 0, add(a_low, a_got), b_total)
+
+    def own_half(piece):
+        return piece.reshape(2, 2, -1, piece.shape[2])
+
+    tops, bottoms = own_half(mine[:, :quarter_rows]), own_half(mine[:, quarter_rows:])
+    halves = jnp.concatenate([tops, bottoms], 2)
+    other = across(pick(halves, 1 - core, 1), 1)
+    query_sum, key_sum, query_y, key_x, carried, packed, other = hold(
+        query_sum, key_sum, query_y, key_x, carried, packed, other
     )
 
     qk_total = ep_sum(jnp.stack([add(query_sum[0], query_y), add(key_sum[0], key_x)]))
@@ -1591,14 +1597,6 @@
     tokens_grad = tokens_back(
         rank, normed_grad, carried, tokens, residual_grad, scale_all, gain_attn, reps
     )
-    mine = jnp.where(m == 0, add(a_low, a_got), b_total)
-
-    def own_half(piece):
-        return piece.reshape(2, 2, -1, piece.shape[2])
-
-    tops, bottoms = own_half(mine[:, :quarter_rows]), own_half(mine[:, quarter_rows:])
-    halves = jnp.concatenate([tops, bottoms], 2)
-    other = across(pick(halves, 1 - core, 1), 1)
     mine = jnp.where(m < 2, pick(halves, core, 1), other).astype(f32)
     top = quarter_rows // 2
     down_out = jnp.concatenate([mine[0, top:], mine[1, top:]], 1)

time: 1380 us -> 1380 us (level)
    ppermute x6, waiting for transfers between devices: 126 us -> 84.7 us  [from_behind(): lax.ppermute(value, axis, [(source, source + steps) for source in range(l...]
    ppermute x9, waiting for transfers between devices: 5.76 us -> 29.5 us  [mirrored(): return lax.ppermute(value, ('rep', 'ep'), pairs)]
    ppermute x58 -> x56, waiting for transfers between devices: 244 us -> 256 us  [across(): lax.ppermute(value, 'rep', [(place, place ^ bit) for place in range(count)])]
    ppermute x58 -> x56, starting transfers between devices: 50.8 us -> 60 us  [across(): lax.ppermute(value, 'rep', [(place, place ^ bit) for place in range(count)])]
    convert_element_type x7 -> x10, other arithmetic: 24.6 us -> 28.1 us  [add(): (left.astype(jnp.float32) + right.astype(jnp.float32)).astype(jnp.bfloat16)]
    unnamed x167 -> x147, local copies, waits for them, and re-layouts: 28.2 us -> 25.7 us
  transfers between devices with their start and end apart: 86 -> 83, of which waited for: 36 -> 39; matrix products, arithmetic and copies ran while one was open for 17% -> 16% of each run, Pallas kernels for 28% -> 28%
where the time goes in v6:
time: 1380 us
  Pallas kernels  499 us (36%)
  waiting for transfers between devices  423 us (31%)
  other arithmetic  174 us (13%)
  starting transfers between devices  141 us (10%)
  local copies, waits for them, and re-layouts  112 us (8%)
  between operations  21.5 us (2%)
    ppermute x56, waiting for transfers between devices, across(): lax.ppermute(value, 'rep', [(place, place ^ bit) for place in range(count)])  256 us
    ppermute x6, waiting for transfers between devices, from_behind(): lax.ppermute(value, axis, [(source, source + steps) for source in range(l...  84.7 us
    pallas_call x8, Pallas kernels, chip_grad(): kernel_call(functools.partial(chip_grad_kernel, count=len(grads)), grid=(...  75.1 us
    pallas_call x8, Pallas kernels, experts_grad(): kernel_call(experts_grad_kernel, grid=(2,), in_specs=[pl.BlockSpec((1, ro...  63.3 us
    ppermute x56, starting transfers between devices, across(): lax.ppermute(value, 'rep', [(place, place ^ bit) for place in range(count)])  60 us
    pallas_call x4, Pallas kernels, project(): kernel_call(project_kernel, grid=(rows // tile,), in_specs=[pl.BlockSpec(...  58.8 us
    pallas_call x2, Pallas kernels, attend_back(): kernel_call(functools.partial(attend_back_kernel, behind=all_rows - rows,...  57.7 us
    pallas_call x1, Pallas kernels, project_back(): kernel_call(functools.partial(project_back_kernel, tile=512), grid=(2 * h...  41.3 us
  transfers between devices with their start and end apart: 83, of which 39 were waited for; matrix products, arithmetic and copies ran while one was open for 16% of the time, Pallas kernels for 28%

profile of v6, /device:TPU:0, one launch (start us, length us, event | category | flops | bytes accessed | tf_op | source)
XLA Modules:
  0.0 1375.4 jit_solution(12379077162613057660)
XLA Ops:
  40.0 18.7 %collective-permute-done.1 = bf16[2,64,2048]{2,1,0:T(8,128)(2,1)} collective-permute-done((bf16[2,64,2048]{2,1,0:T(8,128)(2,1)}, bf16[2,64,2048]{2,1,0:T(8,128)(2,1)}, u32[]{:S(2)}, u32[]{:S(2)}) %collective-permute-start.1) | collective-permute-done | bytes 524320 | tf_op jit(solution)/shard_map/ppermute | solution.py:1143
  125.5 19.8 %collective-permute-done.11 = bf16[2,256,2048]{2,1,0:T(8,128)(2,1)} collective-permute-done((bf16[2,256,2048]{2,1,0:T(8,128)(2,1)}, bf16[2,256,2048]{2,1,0:T(8,128)(2,1)}, u32[]{:S(2)}, u32[]{:S(2)}) %collective-permute-start.11) | collective-permute-done | bytes 2097184 | tf_op jit(solution)/shard_map/ppermute | solution.py:1138
  145.4 18.6 %collective-permute-done.12 = bf16[512,2048]{1,0:T(8,128)(2,1)} collective-permute-done((bf16[512,2048]{1,0:T(8,128)(2,1)}, bf16[512,2048]{1,0:T(8,128)(2,1)}, u32[]{:S(2)}, u32[]{:S(2)}) %collective-permute-start.12) | collective-permute-done | bytes 2097184 | tf_op jit(solution)/shard_map/ppermute | solution.py:24
  222.5 20.0 %collective-permute-done.17 = bf16[512,2048]{1,0:T(8,128)(2,1)} collective-permute-done((bf16[512,2048]{1,0:T(8,128)(2,1)}, bf16[512,2048]{1,0:T(8,128)(2,1)}, u32[]{:S(2)}, u32[]{:S(2)}) %collective-permute-start.17) | collective-permute-done | bytes 2097184 | tf_op jit(solution)/shard_map/ppermute | solution.py:24
  272.8 19.7 %shard_map.281 = (f32[1536,2048]{1,0:T(8,128)}, f32[1536,1]{1,0:T(8,128)}) custom-call(bf16[2,1536,1024]{2,1,0:T(8,128)(2,1)} %get-tuple-element.239.low_ref.high_ref.x_ref, bf16[2,1536,1024]{2,1,0:T(8,128)(2,1)} %get-tuple-element.239.low_ref.high_ref.x_ref, bf16[1040,2048]{1,0:T(8,128)(2,1)} %pad_dynamic-update-slice_fusion.a_ref.ka, ...), custom_call_target="tpu_custom_call" | custom-call | tf_op jit(solution)/shard_map/pallas_call | solution.py:470
  292.4 19.3 %shard_map.282 = (bf16[1536,2048]{1,0:T(8,128)(2,1)}, f32[1536,1]{1,0:T(8,128)}) custom-call(bf16[2,1536,1024]{2,1,0:T(8,128)(2,1)} %get-tuple-element.239.low_ref.high_ref.x_ref, bf16[2,1536,1024]{2,1,0:T(8,128)(2,1)} %get-tuple-element.239.low_ref.high_ref.x_ref, bf16[1024,2048]{1,0:T(8,128)(2,1)} %pad_maximum_fusion.1.a_ref.va, ...), custom_call_target="tpu_custom_call" | custom-call | tf_op jit(solution)/shard_map/pallas_call | solution.py:470
  349.5 19.6 %shard_map.284 = (bf16[2,512,1024]{2,1,0:T(8,128)(2,1)}, f32[8,1,512]{2,1,0:T(1,128)}) custom-call(s32[1]{0:T(128)} %bitcast.rank, f32[512,2048]{1,0:T(8,128)} %get-tuple-element.241.q_ref.lin_ref, f32[1536,2048]{1,0:T(8,128)} %get-tuple-element.242.k_ref.lin_ref, bf16[1536,2048]{1,0:T(8,128)(2,1)} %get-tuple-element.243.v_ref, ...), custom_call_target="tpu_custom_call" | custom-call | tf_op jit(solution)/shard_map/pallas_call | solution.py:645
  369.1 19.7 %shard_map.285 = (bf16[2,512,1024]{2,1,0:T(8,128)(2,1)}, f32[8,1,512]{2,1,0:T(1,128)}) custom-call(s32[1]{0:T(128)} %bitcast.rank, f32[512,2048]{1,0:T(8,128)} %get-tuple-element.241.q_ref.lin_ref, f32[1536,2048]{1,0:T(8,128)} %get-tuple-element.242.k_ref.lin_ref, bf16[1536,2048]{1,0:T(8,128)(2,1)} %get-tuple-element.243.v_ref, ...), custom_call_target="tpu_custom_call", output_to_operand_aliasing={{0}: (11, {})} | custom-call | tf_op jit(solution)/shard_map/pallas_call | solution.py:645
  436.0 26.1 %collective-permute-done.29.ub.refs_5_ = bf16[2,512,1024]{2,1,0:T(8,128)(2,1)} collective-permute-done((bf16[2,512,1024]{2,1,0:T(8,128)(2,1)}, bf16[2,512,1024]{2,1,0:T(8,128)(2,1)}, u32[]{:S(2)}, u32[]{:S(2)}) %collective-permute-start.29) | collective-permute-done | bytes 2097184 | tf_op jit(solution)/shard_map/ppermute | solution.py:1138
  471.9 15.2 %shard_map.288 = (f32[1024,1024]{1,0:T(8,128)}, f32[1024,1024]{1,0:T(8,128)}, bf16[2,1024,512]{2,1,0:T(8,128)(2,1)}, bf16[2,1024,512]{2,1,0:T(8,128)(2,1)}) custom-call(s32[1]{0:T(128)} %bitcast.56.rank, bf16[2,1024,1024]{2,1,0:T(8,128)(2,1)} %copy-done, bf16[2,1024,1024]{2,1,0:T(8,128)(2,1)} %pad_maximum_fusion.4.z_ref.x_ref, ...), custom_call_target="tpu_custom_call" | custom-call | tf_op jit(solution)/shard_map/pallas_call | solution.py:835
  487.1 17.7 %collective-permute-done.32 = bf16[768,1024]{1,0:T(8,128)(2,1)S(1)} collective-permute-done((bf16[768,1024]{1,0:T(8,128)(2,1)}, bf16[768,1024]{1,0:T(8,128)(2,1)S(1)}, u32[]{:S(2)}, u32[]{:S(2)}) %collective-permute-start.32) | collective-permute-done | bytes 1572896 | tf_op jit(solution)/shard_map/ppermute | solution.py:1138
  524.2 33.8 %collective-permute-done.35.ub.refs_11_ = bf16[2,512,1024]{2,1,0:T(8,128)(2,1)} collective-permute-done((bf16[2,512,1024]{2,1,0:T(8,128)(2,1)}, bf16[2,512,1024]{2,1,0:T(8,128)(2,1)}, u32[]{:S(2)}, u32[]{:S(2)}) %collective-permute-start.35) | collective-permute-done | bytes 2097184 | tf_op jit(solution)/shard_map/ppermute | solution.py:1138
  572.2 15.2 %shard_map.289 = (f32[1024,1024]{1,0:T(8,128)}, f32[1024,1024]{1,0:T(8,128)}, bf16[2,1024,512]{2,1,0:T(8,128)(2,1)}, bf16[2,1024,512]{2,1,0:T(8,128)(2,1)}) custom-call(s32[1]{0:T(128)} %bitcast.56.rank, bf16[2,1024,1024]{2,1,0:T(8,128)(2,1)} %copy-done, bf16[2,1024,1024]{2,1,0:T(8,128)(2,1)} %pad_maximum_fusion.4.z_ref.x_ref, ...), custom_call_target="tpu_custom_call" | custom-call | tf_op jit(solution)/shard_map/pallas_call | solution.py:835
  602.7 18.2 %shard_map.290 = (bf16[1024,2048]{1,0:T(8,128)(2,1)}, bf16[1024,2048]{1,0:T(8,128)(2,1)}, f32[512,2048]{1,0:T(8,128)}, f32[512,2048]{1,0:T(8,128)}) custom-call(f32[1024,1]{1,0:T(8,128)} %broadcast_select_fusion.2.refs_0_.gate_ref, f32[1024,1]{1,0:T(8,128)} %broadcast_select_fusion.1.refs_1_.gate_ref, ...), custom_call_target="tpu_custom_call" | custom-call | tf_op jit(solution)/shard_map/pallas_call | solution.py:884
  694.9 27.8 %shard_map.297 = (f32[4,512,512]{2,1,0:T(8,128)}, f32[4,512,512]{2,1,0:T(8,128)}) custom-call(bf16[1024,1024]{1,0:T(8,128)(2,1)} %get-tuple-element.301.d_ref.refs_0_, bf16[1024,1024]{1,0:T(8,128)(2,1)} %get-tuple-element.305.d_ref.refs_1_, bf16[2,768,1024]{2,1,0:T(8,128)(2,1)} %pad_maximum_fusion.5.ga.refs_10_.la.refs_2_, ...), custom_call_target="tpu_custom_call" | custom-call | tf_op jit(solution)/shard_map/pallas_call | solution.py:986
  810.5 28.8 %shard_map.305 = (bf16[512,1024]{1,0:T(8,128)(2,1)}, bf16[1536,1024]{1,0:T(8,128)(2,1)}, bf16[1536,1024]{1,0:T(8,128)(2,1)}) custom-call(s32[1]{0:T(128)} %bitcast.rank, f32[512,2048]{1,0:T(8,128)} %get-tuple-element.241.q_ref.lin_ref, f32[1536,2048]{1,0:T(8,128)} %get-tuple-element.242.k_ref.lin_ref, bf16[1536,2048]{1,0:T(8,128)(2,1)} %get-tuple-element.243.v_ref, ...), custom_call_target="tpu_custom_call" | custom-call | tf_op jit(solution)/shard_map/pallas_call | solution.py:719
  839.3 28.9 %shard_map.304 = (bf16[512,1024]{1,0:T(8,128)(2,1)}, bf16[1536,1024]{1,0:T(8,128)(2,1)}, bf16[1536,1024]{1,0:T(8,128)(2,1)}) custom-call(s32[1]{0:T(128)} %bitcast.rank, f32[512,2048]{1,0:T(8,128)} %get-tuple-element.241.q_ref.lin_ref, f32[1536,2048]{1,0:T(8,128)} %get-tuple-element.242.k_ref.lin_ref, bf16[1536,2048]{1,0:T(8,128)(2,1)} %get-tuple-element.243.v_ref, ...), custom_call_target="tpu_custom_call" | custom-call | tf_op jit(solution)/shard_map/pallas_call | solution.py:719
  1013.9 20.4 %collective-permute-done.64 = bf16[2,256,1024]{2,1,0:T(8,128)(2,1)S(1)} collective-permute-done((bf16[2,256,1024]{2,1,0:T(8,128)(2,1)S(1)}, bf16[2,256,1024]{2,1,0:T(8,128)(2,1)S(1)}, u32[]{:S(2)}, u32[]{:S(2)}) %collective-permute-start.64) | collective-permute-done | bytes 1048608 | tf_op jit(solution)/shard_map/ppermute | solution.py:1138
  1062.9 41.3 %shard_map.314.g_ref = f32[2,1536,1024]{2,1,0:T(8,128)} custom-call(bf16[1536,2048]{1,0:T(8,128)(2,1)} %get-tuple-element.345.refs_0_.k_ref, bf16[1536,1024]{1,0:T(8,128)(2,1)} %get-tuple-element.340.refs_0_.v_ref, bf16[1536,1024]{1,0:T(8,128)(2,1)} %get-tuple-element.341.refs_1_.w_ref, bf16[512,2048]{1,0:T(8,128)(2,1)} %get-tuple-element.346.refs_0_.q_ref, ...), custom_call_target="tpu_custom_call" | custom-call | tf_op jit(solution)/shard_map/pallas_call | solution.py:522
  1125.3 24.0 %collective-permute-done.67 = bf16[2,768,1024]{2,1,0:T(8,128)(2,1)} collective-permute-done((bf16[2,768,1024]{2,1,0:T(8,128)(2,1)S(1)}, bf16[2,768,1024]{2,1,0:T(8,128)(2,1)}, u32[]{:S(2)}, u32[]{:S(2)}) %collective-permute-start.67) | collective-permute-done | bytes 3145760 | tf_op jit(solution)/shard_map/ppermute | solution.py:1154
  1176.1 37.8 %collective-permute-done.68 = bf16[2,256,2048]{2,1,0:T(8,128)(2,1)} collective-permute-done((bf16[2,256,2048]{2,1,0:T(8,128)(2,1)}, bf16[2,256,2048]{2,1,0:T(8,128)(2,1)}, u32[]{:S(2)}, u32[]{:S(2)}) %collective-permute-start.68) | collective-permute-done | bytes 2097184 | tf_op jit(solution)/shard_map/ppermute | solution.py:1138
  1216.8 30.8 %collective-permute-done.70 = bf16[2,512,1024]{2,1,0:T(8,128)(2,1)} collective-permute-done((bf16[2,512,1024]{2,1,0:T(8,128)(2,1)}, bf16[2,512,1024]{2,1,0:T(8,128)(2,1)}, u32[]{:S(2)}, u32[]{:S(2)}) %collective-permute-start.70) | collective-permute-done | bytes 2097184 | tf_op jit(solution)/shard_map/ppermute | solution.py:24
  1277.2 16.5 %collective-permute-done.74 = bf16[256,2048]{1,0:T(8,128)(2,1)} collective-permute-done((bf16[256,2048]{1,0:T(8,128)(2,1)}, bf16[256,2048]{1,0:T(8,128)(2,1)}, u32[]{:S(2)}, u32[]{:S(2)}) %collective-permute-start.74) | collective-permute-done | bytes 1048608 | tf_op jit(solution)/shard_map/ppermute | solution.py:1138
  1339.9 24.5 %reduce-scatter.5.cloned.1.call-done = bf16[2,64,2048]{2,1,0:T(8,128)(2,1)} async-done(((bf16[2,256,2048]{2,1,0:T(8,128)(2,1)}), bf16[2,64,2048]{2,1,0:T(8,128)(2,1)}) %reduce-scatter.5.cloned.1.call-update) | async-done | bytes 524304 | tf_op jit(solution)/shard_map/reduce_scatter | solution.py:1194
  (555 shorter events, 791.6 us)
Async XLA Ops:
  7.2 118.4 %all-gather.3.cloned.1.call-start = ((), (), s32[]{:S(2)}) async-start(), calls=%async_computation.4 | async-start | bytes 2621440 | tf_op jit(solution)/shard_map/all_gather | solution.py:1271
  70.0 1053.2 %reduce-scatter.3.cloned.1.call-start = ((), (), s32[]{:S(2)}) async-start(), calls=%async_computation.2 | async-start | bytes 2621440 | tf_op jit(solution)/shard_map/reduce_scatter | solution.py:1194
  95.7 68.2 %collective-permute-start.10 = (bf16[2,272,2048]{2,1,0:T(8,128)(2,1)}, bf16[2,272,2048]{2,1,0:T(8,128)(2,1)}, u32[]{:S(2)}, u32[]{:S(2)}) collective-permute-start(bf16[2,272,2048]{2,1,0:T(8,128)(2,1)} %pad_maximum_fusion.14), channel_id=1, source_target_pairs={{0,16},{4,20},{8,24},{12,28},{16,0},{20,4},{24,8},{28,12},{1,17},{... | collective-permute-start | bytes 6684680 | tf_op jit(solution)/shard_map/ppermute | solution.py:1138
  114.5 88.8 %collective-permute-start.18 = (bf16[2,768,1024]{2,1,0:T(8,128)(2,1)S(1)}, bf16[2,768,1024]{2,1,0:T(8,128)(2,1)}, u32[]{:S(2)}, u32[]{:S(2)}) collective-permute-start(bf16[2,768,1024]{2,1,0:T(8,128)(2,1)S(1)} %pad_maximum_fusion.9), channel_id=1, source_target_pairs={{0,1},{1,2},{7,6},{6,5},{8,9},{9,10},{15,14},{14,13},{16,17},{17,1... | collective-permute-start | bytes 9437192 | tf_op jit(solution)/shard_map/ppermute | solution.py:1154
  246.3 74.5 %collective-permute-start.21 = (bf16[2,768,1024]{2,1,0:T(8,128)(2,1)}, bf16[2,768,1024]{2,1,0:T(8,128)(2,1)}, u32[]{:S(2)}, u32[]{:S(2)}) collective-permute-start(bf16[2,768,1024]{2,1,0:T(8,128)(2,1)} %broadcast_select_fusion), channel_id=1, source_target_pairs={{1,0},{2,3},{6,7},{5,4},{9,8},{10,11},{14,15},{13,12},{17,16},{18,... | collective-permute-start | bytes 9437192 | tf_op jit(solution)/shard_map/ppermute | solution.py:1154
  250.6 64.9 %collective-permute-start.20 = (bf16[2,256,2048]{2,1,0:T(8,128)(2,1)}, bf16[2,256,2048]{2,1,0:T(8,128)(2,1)}, u32[]{:S(2)}, u32[]{:S(2)}) collective-permute-start(bf16[2,256,2048]{2,1,0:T(8,128)(2,1)} %pad_maximum_fusion.17), channel_id=1, source_target_pairs={{0,8},{4,12},{8,0},{12,4},{16,24},{20,28},{24,16},{28,20},{1,9},{5... | collective-permute-start | bytes 6291464 | tf_op jit(solution)/shard_map/ppermute | solution.py:1138
  522.2 65.1 %collective-permute-start.38 = (bf16[2,256,1024]{2,1,0:T(8,128)(2,1)}, bf16[2,256,1024]{2,1,0:T(8,128)(2,1)}, u32[]{:S(2)}, u32[]{:S(2)}) collective-permute-start(bf16[2,256,1024]{2,1,0:T(8,128)(2,1)} %slice.508), channel_id=1, source_target_pairs={{0,16},{4,20},{8,24},{12,28},{16,0},{20,4},{24,8},{28,12},{1,17},{... | collective-permute-start | bytes 3145736 | tf_op jit(solution)/shard_map/ppermute | solution.py:1138
  675.7 70.3 %collective-permute-start.42 = (bf16[2,768,1024]{2,1,0:T(8,128)(2,1)}, bf16[2,768,1024]{2,1,0:T(8,128)(2,1)S(1)}, u32[]{:S(2)}, u32[]{:S(2)}) collective-permute-start(bf16[2,768,1024]{2,1,0:T(8,128)(2,1)} %shard_map.292), channel_id=1, source_target_pairs={{0,8},{4,12},{8,0},{12,4},{16,24},{20,28},{24,16},{28,20},{1,9},{5... | collective-permute-start | bytes 9437192 | tf_op jit(solution)/shard_map/ppermute | solution.py:1138
  676.5 70.2 %collective-permute-start.43 = (bf16[2,768,1024]{2,1,0:T(8,128)(2,1)}, bf16[2,768,1024]{2,1,0:T(8,128)(2,1)}, u32[]{:S(2)}, u32[]{:S(2)}) collective-permute-start(bf16[2,768,1024]{2,1,0:T(8,128)(2,1)} %shard_map.293), channel_id=1, source_target_pairs={{0,16},{4,20},{8,24},{12,28},{16,0},{20,4},{24,8},{28,12},{1,17},{... | collective-permute-start | bytes 9437192 | tf_op jit(solution)/shard_map/ppermute | solution.py:1138
  772.6 95.6 %collective-permute-start.50 = (bf16[1024,2048]{1,0:T(8,128)(2,1)}, bf16[1024,2048]{1,0:T(8,128)(2,1)S(1)}, u32[]{:S(2)}, u32[]{:S(2)}) collective-permute-start(bf16[1024,2048]{1,0:T(8,128)(2,1)} %shard_map.301), channel_id=1, source_target_pairs={{0,4},{4,0},{8,12},{12,8},{16,20},{20,16},{24,28},{28,24},{1,5},{5... | collective-permute-start | bytes 12582920 | tf_op jit(solution)/shard_map/ppermute | solution.py:1138
  772.7 105.3 %collective-permute-start.45 = (bf16[2,768,1024]{2,1,0:T(8,128)(2,1)}, bf16[2,768,1024]{2,1,0:T(8,128)(2,1)S(1)}, u32[]{:S(2)}, u32[]{:S(2)}) collective-permute-start(bf16[2,768,1024]{2,1,0:T(8,128)(2,1)} %shard_map.295), channel_id=1, source_target_pairs={{0,8},{4,12},{8,0},{12,4},{16,24},{20,28},{24,16},{28,20},{1,9},{5... | collective-permute-start | bytes 9437192 | tf_op jit(solution)/shard_map/ppermute | solution.py:1138
  774.0 104.1 %collective-permute-start.46 = (bf16[2,768,1024]{2,1,0:T(8,128)(2,1)}, bf16[2,768,1024]{2,1,0:T(8,128)(2,1)}, u32[]{:S(2)}, u32[]{:S(2)}) collective-permute-start(bf16[2,768,1024]{2,1,0:T(8,128)(2,1)} %shard_map.296), channel_id=1, source_target_pairs={{0,16},{4,20},{8,24},{12,28},{16,0},{20,4},{24,8},{28,12},{1,17},{... | collective-permute-start | bytes 9437192 | tf_op jit(solution)/shard_map/ppermute | solution.py:1138
  786.3 91.0 %collective-permute-start.47 = (bf16[768,1024]{1,0:T(8,128)(2,1)}, bf16[768,1024]{1,0:T(8,128)(2,1)}, u32[]{:S(2)}, u32[]{:S(2)}) collective-permute-start(bf16[768,1024]{1,0:T(8,128)(2,1)} %slice_bitcast_fusion.5), channel_id=1, source_target_pairs={{0,8},{4,12},{8,0},{12,4},{16,24},{20,28},{24,16},{28,20},{1,9},{5... | collective-permute-start | bytes 4718600 | tf_op jit(solution)/shard_map/ppermute | solution.py:1138
  798.3 79.8 %collective-permute-start.48 = (bf16[768,1024]{1,0:T(8,128)(2,1)}, bf16[768,1024]{1,0:T(8,128)(2,1)}, u32[]{:S(2)}, u32[]{:S(2)}) collective-permute-start(bf16[768,1024]{1,0:T(8,128)(2,1)} %slice_bitcast_fusion.4), channel_id=1, source_target_pairs={{0,16},{4,20},{8,24},{12,28},{16,0},{20,4},{24,8},{28,12},{1,17},{... | collective-permute-start | bytes 4718600 | tf_op jit(solution)/shard_map/ppermute | solution.py:1138
  897.6 89.1 %collective-permute-start.55 = (bf16[2,768,1024]{2,1,0:T(8,128)(2,1)}, bf16[2,768,1024]{2,1,0:T(8,128)(2,1)}, u32[]{:S(2)}, u32[]{:S(2)}) collective-permute-start(bf16[2,768,1024]{2,1,0:T(8,128)(2,1)} %pad_maximum_fusion.10), channel_id=1, source_target_pairs={{3,2},{4,5},{11,10},{12,13},{19,18},{20,21},{27,26},{28,29}} | collective-permute-start | bytes 9437192 | tf_op jit(solution)/shard_map/ppermute | solution.py:1154
  915.6 71.0 %collective-permute-start.51 = (bf16[768,1024]{1,0:T(8,128)(2,1)}, bf16[768,1024]{1,0:T(8,128)(2,1)}, u32[]{:S(2)}, u32[]{:S(2)}) collective-permute-start(bf16[768,1024]{1,0:T(8,128)(2,1)} %slice_bitcast_fusion.3), channel_id=1, source_target_pairs={{0,8},{4,12},{8,0},{12,4},{16,24},{20,28},{24,16},{28,20},{1,9},{5... | collective-permute-start | bytes 4718600 | tf_op jit(solution)/shard_map/ppermute | solution.py:1138
  1013.4 90.7 %collective-permute-start.60 = (bf16[1024,2048]{1,0:T(8,128)(2,1)}, bf16[1024,2048]{1,0:T(8,128)(2,1)}, u32[]{:S(2)}, u32[]{:S(2)}) collective-permute-start(bf16[1024,2048]{1,0:T(8,128)(2,1)} %shard_map.313), channel_id=1, source_target_pairs={{0,4},{4,0},{8,12},{12,8},{16,20},{20,16},{24,28},{28,24},{1,5},{5... | collective-permute-start | bytes 12582920 | tf_op jit(solution)/shard_map/ppermute | solution.py:1138
  1013.4 102.8 %collective-permute-start.59 = (bf16[1024,2048]{1,0:T(8,128)(2,1)}, bf16[1024,2048]{1,0:T(8,128)(2,1)}, u32[]{:S(2)}, u32[]{:S(2)}) collective-permute-start(bf16[1024,2048]{1,0:T(8,128)(2,1)} %shard_map.312), channel_id=1, source_target_pairs={{0,4},{4,0},{8,12},{12,8},{16,20},{20,16},{24,28},{28,24},{1,5},{5... | collective-permute-start | bytes 12582920 | tf_op jit(solution)/shard_map/ppermute | solution.py:1138
  1036.9 327.4 %reduce-scatter.5.cloned.1.call-start = ((), (), s32[]{:S(2)}) async-start(), calls=%async_computation.3 | async-start | bytes 2621440 | tf_op jit(solution)/shard_map/reduce_scatter | solution.py:1194
  1041.9 107.4 %collective-permute-start.67 = (bf16[2,768,1024]{2,1,0:T(8,128)(2,1)S(1)}, bf16[2,768,1024]{2,1,0:T(8,128)(2,1)}, u32[]{:S(2)}, u32[]{:S(2)}) collective-permute-start(bf16[2,768,1024]{2,1,0:T(8,128)(2,1)S(1)} %pad_maximum_fusion.11), channel_id=1, source_target_pairs={{3,2},{0,1},{4,5},{7,6},{11,10},{8,9},{12,13},{15,14},{19,18},{16,... | collective-permute-start | bytes 9437192 | tf_op jit(solution)/shard_map/ppermute | solution.py:1154
  1060.6 88.7 %collective-permute-start.66 = (bf16[2,768,1024]{2,1,0:T(8,128)(2,1)}, bf16[2,768,1024]{2,1,0:T(8,128)(2,1)}, u32[]{:S(2)}, u32[]{:S(2)}) collective-permute-start(bf16[2,768,1024]{2,1,0:T(8,128)(2,1)} %add_convert_fusion.3), channel_id=1, source_target_pairs={{2,1},{5,6},{10,9},{13,14},{18,17},{21,22},{26,25},{29,30}} | collective-permute-start | bytes 9437192 | tf_op jit(solution)/shard_map/ppermute | solution.py:1154
  1154.4 93.2 %collective-permute-start.72 = (bf16[2,768,1024]{2,1,0:T(8,128)(2,1)}, bf16[2,768,1024]{2,1,0:T(8,128)(2,1)}, u32[]{:S(2)}, u32[]{:S(2)}) collective-permute-start(bf16[2,768,1024]{2,1,0:T(8,128)(2,1)} %fusion), channel_id=1, source_target_pairs={{2,1},{5,6},{10,9},{13,14},{18,17},{21,22},{26,25},{29,30}} | collective-permute-start | bytes 9437192 | tf_op jit(solution)/shard_map/ppermute | solution.py:1154
  1162.9 84.7 %collective-permute-start.71 = (bf16[2,768,1024]{2,1,0:T(8,128)(2,1)}, bf16[2,768,1024]{2,1,0:T(8,128)(2,1)}, u32[]{:S(2)}, u32[]{:S(2)}) collective-permute-start(bf16[2,768,1024]{2,1,0:T(8,128)(2,1)} %add_convert_fusion.2), channel_id=1, source_target_pairs={{1,0},{6,7},{9,8},{14,15},{17,16},{22,23},{25,24},{30,31}} | collective-permute-start | bytes 9437192 | tf_op jit(solution)/shard_map/ppermute | solution.py:1154
  1174.8 72.8 %collective-permute-start.70 = (bf16[2,512,1024]{2,1,0:T(8,128)(2,1)}, bf16[2,512,1024]{2,1,0:T(8,128)(2,1)}, u32[]{:S(2)}, u32[]{:S(2)}) collective-permute-start(bf16[2,512,1024]{2,1,0:T(8,128)(2,1)} %slice.832), channel_id=1, source_target_pairs={{1,0},{2,1},{3,2},{5,4},{6,5},{7,6},{9,8},{10,9},{11,10},{13,12},{... | collective-permute-start | bytes 6291464 | tf_op jit(solution)/shard_map/ppermute | solution.py:24
  (128 other events, 2605.8 us)
Sparse Core Ops, SparseCore 0:
  70.1 55.3 all-gather.2
  1037.0 80.9 reduce-scatter.2
  1318.4 45.9 reduce-scatter.4

commit v7 on v5

--- a/solution.py
+++ b/solution.py
@@ -1489,22 +1489,18 @@
     out_sent = across(chip_grad(mixed, 1, (branch_grad,)), 1)
     out_sum = chip_grad(mixed, 0, (branch_grad,), 0, (out_sent,)).reshape(2, 2, -1, width)
     mixed_grad = mixed_back(branch_grad, out_w)
-    b_0, b_1, out_sum, mixed_grad, branch_grad = hold(b_0, b_1, out_sum, mixed_grad, branch_grad)
-
     b_y, b_x = other_ways(b_0[1], b_1[1])
-    out_x, out_y = across(out_sum[:, 1, :, :half], 2), across(out_sum[1, :, :, half:], 4)
     bias = mask_of(local_rows // 2)
     dq_0, dk_0, dv_0 = attend_back(rank, operands, bias, mixed_grad, lse_0, 0)
     dq_1, dk_1, dv_1 = attend_back(rank, operands, bias, mixed_grad, lse_1, HEADS // 2)
-    a_x, a_y, b_0, b_1, b_x, b_y, out_sum, out_x, out_y, dq_0, dk_0, dv_0, dq_1, dk_1, dv_1 = hold(
-        a_x, a_y, b_0, b_1, b_x, b_y, out_sum, out_x, out_y, dq_0, dk_0, dv_0, dq_1, dk_1, dv_1
+    a_x, a_y, b_0, b_1, b_x, b_y, out_sum, dq_0, dk_0, dv_0, dq_1, dk_1, dv_1 = hold(
+        a_x, a_y, b_0, b_1, b_x, b_y, out_sum, dq_0, dk_0, dv_0, dq_1, dk_1, dv_1
     )
 
     a_0 = experts_grad(moe_x, dg_a, mx_a, pair_a, 0, 0, (a_x,))
     a_1 = experts_grad(moe_y, du_a, my_a, pair_a, 0, 1, (a_y,))
     a_y, a_x = other_ways(a_0[1], a_1[1])
-    out_a, out_b = add(out_sum[:, 0, :, :half], out_x), add(out_sum[0, :, :, half:], out_y)
-    out_x, out_y = across(out_b[1], 2), across(out_a[1], 4)
+    out_x, out_y = across(out_sum[:, 1, :, :half], 2), across(out_sum[1, :, :, half:], 4)
     b_end = jnp.stack([add(b_0[0], b_y), add(b_1[0], b_x)])
     b_got = mirrored(b_end, [(3, 2), (0, 1)])
     value_sent = chip_grad(normed, 1, (dv_0, dv_1))
@@ -1531,10 +1527,10 @@
         0,
     )
     (
-        a_0, a_1, a_x, a_y, out_a, out_b, out_x, out_y, b_end, b_got, query_lin_grad, key_lin_grad,
+        a_0, a_1, a_x, a_y, out_sum, out_x, out_y, b_end, b_got, query_lin_grad, key_lin_grad,
         value_sum, value_x, value_y, query_sent, key_sent, packed,
     ) = hold(
-        a_0, a_1, a_x, a_y, out_a, out_b, out_x, out_y, b_end, b_got, query_lin_grad, key_lin_grad,
+        a_0, a_1, a_x, a_y, out_sum, out_x, out_y, b_end, b_got, query_lin_grad, key_lin_grad,
         value_sum, value_x, value_y, query_sent, key_sent, packed,
     )
 
@@ -1543,9 +1539,15 @@
     value_b = add(value_sum[0, :, :, half:], value_y)
     for link in (1, 2, 4):
         packed = packed + across(packed, link)
-    value_a, value_b, packed = hold(value_a, value_b, packed)
-    value_x, value_y = across(value_b[1], 2), across(value_a[1], 4)
-    out_total = ep_sum(jnp.stack([add(out_a[0], out_y), add(out_b[0], out_x)]))
+    out_a, out_b = add(out_sum[:, 0, :, :half], out_x), add(out_sum[0, :, :, half:], out_y)
+    value_a, value_b, packed, out_a, out_b = hold(value_a, value_b, packed, out_a, out_b)
+    moved_x = across(jnp.stack([value_b[1], out_b[1]]), 2)
+    moved_y = across(jnp.stack([value_a[1], out_a[1]]), 4)
+    value_x, value_y, out_x, out_y = moved_x[0], moved_y[0], moved_x[1], moved_y[1]
+    four = [add(out_a[0], out_y), add(out_b[0], out_x)]
+    four += [add(value_a[0], value_y), add(value_b[0], value_x)]
+    four = ep_sum(jnp.stack(four))
+    out_total, value_total = four[:2], four[2:]
     b_low = add(b_end, b_got)
     b_got_2 = mirrored(b_low, [(2, 1)])
     a_end = jnp.stack([add(a_0[0], a_y), add(a_1[0], a_x)])
@@ -1556,11 +1558,9 @@
     query_sum = chip_grad(normed, 0, (query_lin_grad,), behind, (query_got,))
     key_sum = chip_grad(normed, 0, (key_lin_grad,), 0, (key_got,))
     (
-        normed_grad, query_sum, key_sum, value_a, value_b, value_x, value_y, b_got_2, a_end, a_got,
-        packed,
+        normed_grad, query_sum, key_sum, out_total, value_total, b_got_2, a_end, a_got, packed,
     ) = hold(
-        normed_grad, query_sum, key_sum, value_a, value_b, value_x, value_y, b_got_2, a_end, a_got,
-        packed,
+        normed_grad, query_sum, key_sum, out_total, value_total, b_got_2, a_end, a_got, packed,
     )
 
     query_sum = query_sum.reshape(2, 2, -1, width)
@@ -1569,7 +1569,6 @@
     carried = from_behind(normed_grad[:, :local_rows].astype(bf16), "ep", -1)
     a_low = add(a_end, a_got)
     a_got = mirrored(a_low, [(2, 1)])
-    value_total = ep_sum(jnp.stack([add(value_a[0], value_y), add(value_b[0], value_x)]))
     b_total = (b_end.astype(f32) + b_got.astype(f32) + b_got_2.astype(f32)).astype(bf16)
     query_sum, key_sum, query_x, key_y, carried, a_low, a_got, packed, b_total = hold(
         query_sum, key_sum, query_x, key_y, carried, a_low, a_got, packed, b_total

time: 1380 us -> 1360 us (0.986)
    ppermute x6, waiting for transfers between devices: 126 us -> 111 us  [from_behind(): lax.ppermute(value, axis, [(source, source + steps) for source in range(l...]
    ppermute x58 -> x56, waiting for transfers between devices: 244 us -> 250 us  [across(): lax.ppermute(value, 'rep', [(place, place ^ bit) for place in range(count)])]
    ppermute x58 -> x56, starting transfers between devices: 50.8 us -> 48.2 us  [across(): lax.ppermute(value, 'rep', [(place, place ^ bit) for place in range(count)])]
    unnamed x167 -> x151, local copies, waits for them, and re-layouts: 28.2 us -> 27.2 us
  transfers between devices with their start and end apart: 86 -> 83, of which waited for: 36 -> 39; matrix products, arithmetic and copies ran while one was open for 17% -> 16% of each run, Pallas kernels for 28% -> 29%
where the time goes in v7:
time: 1360 us; the launch traced here: 1350 us
  Pallas kernels  499 us (37%)
  waiting for transfers between devices  413 us (30%)
  other arithmetic  168 us (12%)
  starting transfers between devices  132 us (10%)
  local copies, waits for them, and re-layouts  111 us (8%)
  between operations  21.6 us (2%)
    ppermute x56, waiting for transfers between devices, across(): lax.ppermute(value, 'rep', [(place, place ^ bit) for place in range(count)])  250 us
    ppermute x6, waiting for transfers between devices, from_behind(): lax.ppermute(value, axis, [(source, source + steps) for source in range(l...  111 us
    pallas_call x8, Pallas kernels, chip_grad(): kernel_call(functools.partial(chip_grad_kernel, count=len(grads)), grid=(...  75 us
    pallas_call x8, Pallas kernels, experts_grad(): kernel_call(experts_grad_kernel, grid=(2,), in_specs=[pl.BlockSpec((1, ro...  63.4 us
    pallas_call x4, Pallas kernels, project(): kernel_call(project_kernel, grid=(rows // tile,), in_specs=[pl.BlockSpec(...  58.8 us
    pallas_call x2, Pallas kernels, attend_back(): kernel_call(functools.partial(attend_back_kernel, behind=all_rows - rows,...  57.7 us
    ppermute x56, starting transfers between devices, across(): lax.ppermute(value, 'rep', [(place, place ^ bit) for place in range(count)])  48.2 us
    pallas_call x1, Pallas kernels, project_back(): kernel_call(functools.partial(project_back_kernel, tile=512), grid=(2 * h...  41.3 us
  transfers between devices with their start and end apart: 83, of which 39 were waited for; matrix products, arithmetic and copies ran while one was open for 16% of the time, Pallas kernels for 29%

profile of v7, /device:TPU:0, one launch (start us, length us, event | category | flops | bytes accessed | tf_op | source)
XLA Modules:
  0.0 1349.0 jit_solution(11765404892184639036)
XLA Ops:
  40.0 18.7 %collective-permute-done.1 = bf16[2,64,2048]{2,1,0:T(8,128)(2,1)} collective-permute-done((bf16[2,64,2048]{2,1,0:T(8,128)(2,1)}, bf16[2,64,2048]{2,1,0:T(8,128)(2,1)}, u32[]{:S(2)}, u32[]{:S(2)}) %collective-permute-start.1) | collective-permute-done | bytes 524320 | tf_op jit(solution)/shard_map/ppermute | solution.py:1143
  125.5 19.8 %collective-permute-done.11 = bf16[2,256,2048]{2,1,0:T(8,128)(2,1)} collective-permute-done((bf16[2,256,2048]{2,1,0:T(8,128)(2,1)}, bf16[2,256,2048]{2,1,0:T(8,128)(2,1)}, u32[]{:S(2)}, u32[]{:S(2)}) %collective-permute-start.11) | collective-permute-done | bytes 2097184 | tf_op jit(solution)/shard_map/ppermute | solution.py:1138
  145.4 18.6 %collective-permute-done.12 = bf16[512,2048]{1,0:T(8,128)(2,1)} collective-permute-done((bf16[512,2048]{1,0:T(8,128)(2,1)}, bf16[512,2048]{1,0:T(8,128)(2,1)}, u32[]{:S(2)}, u32[]{:S(2)}) %collective-permute-start.12) | collective-permute-done | bytes 2097184 | tf_op jit(solution)/shard_map/ppermute | solution.py:24
  222.6 20.0 %collective-permute-done.17 = bf16[512,2048]{1,0:T(8,128)(2,1)} collective-permute-done((bf16[512,2048]{1,0:T(8,128)(2,1)}, bf16[512,2048]{1,0:T(8,128)(2,1)}, u32[]{:S(2)}, u32[]{:S(2)}) %collective-permute-start.17) | collective-permute-done | bytes 2097184 | tf_op jit(solution)/shard_map/ppermute | solution.py:24
  272.8 19.7 %shard_map.281 = (f32[1536,2048]{1,0:T(8,128)}, f32[1536,1]{1,0:T(8,128)}) custom-call(bf16[2,1536,1024]{2,1,0:T(8,128)(2,1)} %get-tuple-element.239.low_ref.high_ref.x_ref, bf16[2,1536,1024]{2,1,0:T(8,128)(2,1)} %get-tuple-element.239.low_ref.high_ref.x_ref, bf16[1040,2048]{1,0:T(8,128)(2,1)} %pad_dynamic-update-slice_fusion.a_ref.ka, ...), custom_call_target="tpu_custom_call" | custom-call | tf_op jit(solution)/shard_map/pallas_call | solution.py:470
  292.4 19.3 %shard_map.282 = (bf16[1536,2048]{1,0:T(8,128)(2,1)}, f32[1536,1]{1,0:T(8,128)}) custom-call(bf16[2,1536,1024]{2,1,0:T(8,128)(2,1)} %get-tuple-element.239.low_ref.high_ref.x_ref, bf16[2,1536,1024]{2,1,0:T(8,128)(2,1)} %get-tuple-element.239.low_ref.high_ref.x_ref, bf16[1024,2048]{1,0:T(8,128)(2,1)} %pad_maximum_fusion.1.a_ref.va, ...), custom_call_target="tpu_custom_call" | custom-call | tf_op jit(solution)/shard_map/pallas_call | solution.py:470
  349.4 19.6 %shard_map.284 = (bf16[2,512,1024]{2,1,0:T(8,128)(2,1)}, f32[8,1,512]{2,1,0:T(1,128)}) custom-call(s32[1]{0:T(128)} %bitcast.rank, f32[512,2048]{1,0:T(8,128)} %get-tuple-element.241.q_ref.lin_ref, f32[1536,2048]{1,0:T(8,128)} %get-tuple-element.242.k_ref.lin_ref, bf16[1536,2048]{1,0:T(8,128)(2,1)} %get-tuple-element.243.v_ref, ...), custom_call_target="tpu_custom_call" | custom-call | tf_op jit(solution)/shard_map/pallas_call | solution.py:645
  369.0 19.7 %shard_map.285 = (bf16[2,512,1024]{2,1,0:T(8,128)(2,1)}, f32[8,1,512]{2,1,0:T(1,128)}) custom-call(s32[1]{0:T(128)} %bitcast.rank, f32[512,2048]{1,0:T(8,128)} %get-tuple-element.241.q_ref.lin_ref, f32[1536,2048]{1,0:T(8,128)} %get-tuple-element.242.k_ref.lin_ref, bf16[1536,2048]{1,0:T(8,128)(2,1)} %get-tuple-element.243.v_ref, ...), custom_call_target="tpu_custom_call", output_to_operand_aliasing={{0}: (11, {})} | custom-call | tf_op jit(solution)/shard_map/pallas_call | solution.py:645
  435.7 26.1 %collective-permute-done.29.ub.refs_11_ = bf16[2,512,1024]{2,1,0:T(8,128)(2,1)} collective-permute-done((bf16[2,512,1024]{2,1,0:T(8,128)(2,1)}, bf16[2,512,1024]{2,1,0:T(8,128)(2,1)}, u32[]{:S(2)}, u32[]{:S(2)}) %collective-permute-start.29) | collective-permute-done | bytes 2097184 | tf_op jit(solution)/shard_map/ppermute | solution.py:1138
  471.6 15.2 %shard_map.288 = (f32[1024,1024]{1,0:T(8,128)}, f32[1024,1024]{1,0:T(8,128)}, bf16[2,1024,512]{2,1,0:T(8,128)(2,1)}, bf16[2,1024,512]{2,1,0:T(8,128)(2,1)}) custom-call(s32[1]{0:T(128)} %bitcast.56.rank, bf16[2,1024,1024]{2,1,0:T(8,128)(2,1)} %copy-done, bf16[2,1024,1024]{2,1,0:T(8,128)(2,1)} %pad_maximum_fusion.4.z_ref.x_ref, ...), custom_call_target="tpu_custom_call" | custom-call | tf_op jit(solution)/shard_map/pallas_call | solution.py:835
  486.8 17.6 %collective-permute-done.32 = bf16[768,1024]{1,0:T(8,128)(2,1)S(1)} collective-permute-done((bf16[768,1024]{1,0:T(8,128)(2,1)}, bf16[768,1024]{1,0:T(8,128)(2,1)S(1)}, u32[]{:S(2)}, u32[]{:S(2)}) %collective-permute-start.32) | collective-permute-done | bytes 1572896 | tf_op jit(solution)/shard_map/ppermute | solution.py:1138
  524.0 33.7 %collective-permute-done.35.ub.refs_5_ = bf16[2,512,1024]{2,1,0:T(8,128)(2,1)} collective-permute-done((bf16[2,512,1024]{2,1,0:T(8,128)(2,1)}, bf16[2,512,1024]{2,1,0:T(8,128)(2,1)}, u32[]{:S(2)}, u32[]{:S(2)}) %collective-permute-start.35) | collective-permute-done | bytes 2097184 | tf_op jit(solution)/shard_map/ppermute | solution.py:1138
  571.9 15.2 %shard_map.289 = (f32[1024,1024]{1,0:T(8,128)}, f32[1024,1024]{1,0:T(8,128)}, bf16[2,1024,512]{2,1,0:T(8,128)(2,1)}, bf16[2,1024,512]{2,1,0:T(8,128)(2,1)}) custom-call(s32[1]{0:T(128)} %bitcast.56.rank, bf16[2,1024,1024]{2,1,0:T(8,128)(2,1)} %copy-done, bf16[2,1024,1024]{2,1,0:T(8,128)(2,1)} %pad_maximum_fusion.4.z_ref.x_ref, ...), custom_call_target="tpu_custom_call" | custom-call | tf_op jit(solution)/shard_map/pallas_call | solution.py:835
  602.3 18.2 %shard_map.290 = (bf16[1024,2048]{1,0:T(8,128)(2,1)}, bf16[1024,2048]{1,0:T(8,128)(2,1)}, f32[512,2048]{1,0:T(8,128)}, f32[512,2048]{1,0:T(8,128)}) custom-call(f32[1024,1]{1,0:T(8,128)} %broadcast_select_fusion.2.refs_0_.gate_ref, f32[1024,1]{1,0:T(8,128)} %broadcast_select_fusion.1.refs_1_.gate_ref, ...), custom_call_target="tpu_custom_call" | custom-call | tf_op jit(solution)/shard_map/pallas_call | solution.py:884
  677.5 14.3 %shard_map.294 = (bf16[1024,2048]{1,0:T(8,128)(2,1)}, bf16[1024,1024]{1,0:T(8,128)(2,1)}, bf16[1024,1024]{1,0:T(8,128)(2,1)}, f32[1024,1]{1,0:T(8,128)}) custom-call(s32[1]{0:T(128)} %bitcast.56.rank, f32[512,2048]{1,0:T(8,128)} %copy-done.3, f32[512,2048]{1,0:T(8,128)} %copy-done.10, bf16[1024,2048]{1,0:T(8,128)(2,1)} %get-tuple-element.298.out_ref, ...), custom_call_target="tpu_custom_call" | custom-call | tf_op jit(solution)/shard_map/pallas_call | solution.py:935
  694.3 27.7 %shard_map.297 = (f32[4,512,512]{2,1,0:T(8,128)}, f32[4,512,512]{2,1,0:T(8,128)}) custom-call(bf16[1024,1024]{1,0:T(8,128)(2,1)} %get-tuple-element.301.d_ref.refs_0_, bf16[1024,1024]{1,0:T(8,128)(2,1)} %get-tuple-element.305.d_ref.refs_1_, bf16[2,768,1024]{2,1,0:T(8,128)(2,1)} %copy-done.2, bf16[2,512,1024]{2,1,0:T(8,128)(2,1)} %collective-permute-done.34.gb.refs_3_, ...), custom_call_target="tpu_custom_call" | custom-call | tf_op jit(solution)/shard_map/pallas_call | solution.py:986
  810.1 28.8 %shard_map.305 = (bf16[512,1024]{1,0:T(8,128)(2,1)}, bf16[1536,1024]{1,0:T(8,128)(2,1)}, bf16[1536,1024]{1,0:T(8,128)(2,1)}) custom-call(s32[1]{0:T(128)} %bitcast.rank, f32[512,2048]{1,0:T(8,128)} %get-tuple-element.241.q_ref.lin_ref, f32[1536,2048]{1,0:T(8,128)} %get-tuple-element.242.k_ref.lin_ref, bf16[1536,2048]{1,0:T(8,128)(2,1)} %get-tuple-element.243.v_ref, ...), custom_call_target="tpu_custom_call" | custom-call | tf_op jit(solution)/shard_map/pallas_call | solution.py:719
  839.0 28.9 %shard_map.304 = (bf16[512,1024]{1,0:T(8,128)(2,1)}, bf16[1536,1024]{1,0:T(8,128)(2,1)}, bf16[1536,1024]{1,0:T(8,128)(2,1)}) custom-call(s32[1]{0:T(128)} %bitcast.rank, f32[512,2048]{1,0:T(8,128)} %get-tuple-element.241.q_ref.lin_ref, f32[1536,2048]{1,0:T(8,128)} %get-tuple-element.242.k_ref.lin_ref, bf16[1536,2048]{1,0:T(8,128)(2,1)} %get-tuple-element.243.v_ref, ...), custom_call_target="tpu_custom_call" | custom-call | tf_op jit(solution)/shard_map/pallas_call | solution.py:719
  895.6 16.5 %collective-permute-start.55 = (bf16[2,768,1024]{2,1,0:T(8,128)(2,1)S(1)}, bf16[2,768,1024]{2,1,0:T(8,128)(2,1)}, u32[]{:S(2)}, u32[]{:S(2)}) collective-permute-start(bf16[2,768,1024]{2,1,0:T(8,128)(2,1)S(1)} %pad_maximum_fusion.10), channel_id=1, source_target_pairs={{3,2},{0,1},{4,5},{7,6},{11,10},{8,9},{12,13},{15,14},{19,18},{16,... | collective-permute-start | bytes 9437192 | tf_op jit(solution)/shard_map/ppermute | solution.py:1154
  1022.2 20.2 %collective-permute-done.64 = bf16[2,256,1024]{2,1,0:T(8,128)(2,1)S(1)} collective-permute-done((bf16[2,256,1024]{2,1,0:T(8,128)(2,1)S(1)}, bf16[2,256,1024]{2,1,0:T(8,128)(2,1)S(1)}, u32[]{:S(2)}, u32[]{:S(2)}) %collective-permute-start.64) | collective-permute-done | bytes 1048608 | tf_op jit(solution)/shard_map/ppermute | solution.py:1138
  1062.8 41.3 %shard_map.314.g_ref = f32[2,1536,1024]{2,1,0:T(8,128)} custom-call(bf16[1536,2048]{1,0:T(8,128)(2,1)} %get-tuple-element.345.refs_0_.k_ref, bf16[1536,1024]{1,0:T(8,128)(2,1)} %get-tuple-element.340.refs_0_.v_ref, bf16[1536,1024]{1,0:T(8,128)(2,1)} %get-tuple-element.341.refs_1_.w_ref, bf16[512,2048]{1,0:T(8,128)(2,1)} %get-tuple-element.346.refs_0_.q_ref, ...), custom_call_target="tpu_custom_call" | custom-call | tf_op jit(solution)/shard_map/pallas_call | solution.py:522
  1146.4 30.0 %collective-permute-done.68 = bf16[2,256,2048]{2,1,0:T(8,128)(2,1)S(1)} collective-permute-done((bf16[2,256,2048]{2,1,0:T(8,128)(2,1)S(1)}, bf16[2,256,2048]{2,1,0:T(8,128)(2,1)S(1)}, u32[]{:S(2)}, u32[]{:S(2)}) %collective-permute-start.68) | collective-permute-done | bytes 2097184 | tf_op jit(solution)/shard_map/ppermute | solution.py:1138
  1223.9 65.2 %collective-permute-done.74.c_ref = bf16[2,512,1024]{2,1,0:T(8,128)(2,1)} collective-permute-done((bf16[2,512,1024]{2,1,0:T(8,128)(2,1)}, bf16[2,512,1024]{2,1,0:T(8,128)(2,1)}, u32[]{:S(2)}, u32[]{:S(2)}) %collective-permute-start.74) | collective-permute-done | bytes 2097184 | tf_op jit(solution)/shard_map/ppermute | solution.py:24
  1319.6 18.2 %reduce-scatter.5.cloned.1.call-done = bf16[2,64,2048]{2,1,0:T(8,128)(2,1)} async-done(((bf16[2,256,2048]{2,1,0:T(8,128)(2,1)}), bf16[2,64,2048]{2,1,0:T(8,128)(2,1)}) %reduce-scatter.5.cloned.1.call-update) | async-done | bytes 524304 | tf_op jit(solution)/shard_map/reduce_scatter | solution.py:1194
  (560 shorter events, 754.8 us)
Async XLA Ops:
  7.2 118.4 %all-gather.3.cloned.1.call-start = ((), (), s32[]{:S(2)}) async-start(), calls=%async_computation.4 | async-start | bytes 2621440 | tf_op jit(solution)/shard_map/all_gather | solution.py:1271
  70.0 1053.1 %reduce-scatter.3.cloned.1.call-start = ((), (), s32[]{:S(2)}) async-start(), calls=%async_computation.2 | async-start | bytes 2621440 | tf_op jit(solution)/shard_map/reduce_scatter | solution.py:1194
  95.7 68.2 %collective-permute-start.10 = (bf16[2,272,2048]{2,1,0:T(8,128)(2,1)}, bf16[2,272,2048]{2,1,0:T(8,128)(2,1)}, u32[]{:S(2)}, u32[]{:S(2)}) collective-permute-start(bf16[2,272,2048]{2,1,0:T(8,128)(2,1)} %pad_maximum_fusion.14), channel_id=1, source_target_pairs={{0,16},{4,20},{8,24},{12,28},{16,0},{20,4},{24,8},{28,12},{1,17},{... | collective-permute-start | bytes 6684680 | tf_op jit(solution)/shard_map/ppermute | solution.py:1138
  114.5 88.8 %collective-permute-start.18 = (bf16[2,768,1024]{2,1,0:T(8,128)(2,1)S(1)}, bf16[2,768,1024]{2,1,0:T(8,128)(2,1)}, u32[]{:S(2)}, u32[]{:S(2)}) collective-permute-start(bf16[2,768,1024]{2,1,0:T(8,128)(2,1)S(1)} %pad_maximum_fusion.9), channel_id=1, source_target_pairs={{0,1},{1,2},{7,6},{6,5},{8,9},{9,10},{15,14},{14,13},{16,17},{17,1... | collective-permute-start | bytes 9437192 | tf_op jit(solution)/shard_map/ppermute | solution.py:1154
  246.2 74.4 %collective-permute-start.21 = (bf16[2,768,1024]{2,1,0:T(8,128)(2,1)}, bf16[2,768,1024]{2,1,0:T(8,128)(2,1)}, u32[]{:S(2)}, u32[]{:S(2)}) collective-permute-start(bf16[2,768,1024]{2,1,0:T(8,128)(2,1)} %broadcast_select_fusion), channel_id=1, source_target_pairs={{1,0},{2,3},{6,7},{5,4},{9,8},{10,11},{14,15},{13,12},{17,16},{18,... | collective-permute-start | bytes 9437192 | tf_op jit(solution)/shard_map/ppermute | solution.py:1154
  250.6 64.8 %collective-permute-start.20 = (bf16[2,256,2048]{2,1,0:T(8,128)(2,1)}, bf16[2,256,2048]{2,1,0:T(8,128)(2,1)}, u32[]{:S(2)}, u32[]{:S(2)}) collective-permute-start(bf16[2,256,2048]{2,1,0:T(8,128)(2,1)} %pad_maximum_fusion.17), channel_id=1, source_target_pairs={{0,8},{4,12},{8,0},{12,4},{16,24},{20,28},{24,16},{28,20},{1,9},{5... | collective-permute-start | bytes 6291464 | tf_op jit(solution)/shard_map/ppermute | solution.py:1138
  521.9 65.3 %collective-permute-start.38 = (bf16[2,256,1024]{2,1,0:T(8,128)(2,1)}, bf16[2,256,1024]{2,1,0:T(8,128)(2,1)}, u32[]{:S(2)}, u32[]{:S(2)}) collective-permute-start(bf16[2,256,1024]{2,1,0:T(8,128)(2,1)} %slice.508), channel_id=1, source_target_pairs={{0,16},{4,20},{8,24},{12,28},{16,0},{20,4},{24,8},{28,12},{1,17},{... | collective-permute-start | bytes 3145736 | tf_op jit(solution)/shard_map/ppermute | solution.py:1138
  522.4 64.7 %collective-permute-start.39 = (bf16[2,256,1024]{2,1,0:T(8,128)(2,1)}, bf16[2,256,1024]{2,1,0:T(8,128)(2,1)}, u32[]{:S(2)}, u32[]{:S(2)}) collective-permute-start(bf16[2,256,1024]{2,1,0:T(8,128)(2,1)} %slice.509), channel_id=1, source_target_pairs={{0,8},{4,12},{8,0},{12,4},{16,24},{20,28},{24,16},{28,20},{1,9},{5... | collective-permute-start | bytes 3145736 | tf_op jit(solution)/shard_map/ppermute | solution.py:1138
  675.2 70.4 %collective-permute-start.42 = (bf16[2,768,1024]{2,1,0:T(8,128)(2,1)}, bf16[2,768,1024]{2,1,0:T(8,128)(2,1)S(1)}, u32[]{:S(2)}, u32[]{:S(2)}) collective-permute-start(bf16[2,768,1024]{2,1,0:T(8,128)(2,1)} %shard_map.292), channel_id=1, source_target_pairs={{0,8},{4,12},{8,0},{12,4},{16,24},{20,28},{24,16},{28,20},{1,9},{5... | collective-permute-start | bytes 9437192 | tf_op jit(solution)/shard_map/ppermute | solution.py:1138
  676.0 70.2 %collective-permute-start.43 = (bf16[2,768,1024]{2,1,0:T(8,128)(2,1)}, bf16[2,768,1024]{2,1,0:T(8,128)(2,1)}, u32[]{:S(2)}, u32[]{:S(2)}) collective-permute-start(bf16[2,768,1024]{2,1,0:T(8,128)(2,1)} %shard_map.293), channel_id=1, source_target_pairs={{0,16},{4,20},{8,24},{12,28},{16,0},{20,4},{24,8},{28,12},{1,17},{... | collective-permute-start | bytes 9437192 | tf_op jit(solution)/shard_map/ppermute | solution.py:1138
  772.3 95.6 %collective-permute-start.50 = (bf16[1024,2048]{1,0:T(8,128)(2,1)}, bf16[1024,2048]{1,0:T(8,128)(2,1)S(1)}, u32[]{:S(2)}, u32[]{:S(2)}) collective-permute-start(bf16[1024,2048]{1,0:T(8,128)(2,1)} %shard_map.301), channel_id=1, source_target_pairs={{0,4},{4,0},{8,12},{12,8},{16,20},{20,16},{24,28},{28,24},{1,5},{5... | collective-permute-start | bytes 12582920 | tf_op jit(solution)/shard_map/ppermute | solution.py:1138
  772.4 105.4 %collective-permute-start.45 = (bf16[2,768,1024]{2,1,0:T(8,128)(2,1)}, bf16[2,768,1024]{2,1,0:T(8,128)(2,1)S(1)}, u32[]{:S(2)}, u32[]{:S(2)}) collective-permute-start(bf16[2,768,1024]{2,1,0:T(8,128)(2,1)} %shard_map.295), channel_id=1, source_target_pairs={{0,8},{4,12},{8,0},{12,4},{16,24},{20,28},{24,16},{28,20},{1,9},{5... | collective-permute-start | bytes 9437192 | tf_op jit(solution)/shard_map/ppermute | solution.py:1138
  773.7 104.1 %collective-permute-start.46 = (bf16[2,768,1024]{2,1,0:T(8,128)(2,1)}, bf16[2,768,1024]{2,1,0:T(8,128)(2,1)}, u32[]{:S(2)}, u32[]{:S(2)}) collective-permute-start(bf16[2,768,1024]{2,1,0:T(8,128)(2,1)} %shard_map.296), channel_id=1, source_target_pairs={{0,16},{4,20},{8,24},{12,28},{16,0},{20,4},{24,8},{28,12},{1,17},{... | collective-permute-start | bytes 9437192 | tf_op jit(solution)/shard_map/ppermute | solution.py:1138
  786.0 91.0 %collective-permute-start.47 = (bf16[768,1024]{1,0:T(8,128)(2,1)}, bf16[768,1024]{1,0:T(8,128)(2,1)}, u32[]{:S(2)}, u32[]{:S(2)}) collective-permute-start(bf16[768,1024]{1,0:T(8,128)(2,1)} %slice_bitcast_fusion.5), channel_id=1, source_target_pairs={{0,8},{4,12},{8,0},{12,4},{16,24},{20,28},{24,16},{28,20},{1,9},{5... | collective-permute-start | bytes 4718600 | tf_op jit(solution)/shard_map/ppermute | solution.py:1138
  797.9 79.9 %collective-permute-start.48 = (bf16[768,1024]{1,0:T(8,128)(2,1)}, bf16[768,1024]{1,0:T(8,128)(2,1)}, u32[]{:S(2)}, u32[]{:S(2)}) collective-permute-start(bf16[768,1024]{1,0:T(8,128)(2,1)} %slice_bitcast_fusion.4), channel_id=1, source_target_pairs={{0,16},{4,20},{8,24},{12,28},{16,0},{20,4},{24,8},{28,12},{1,17},{... | collective-permute-start | bytes 4718600 | tf_op jit(solution)/shard_map/ppermute | solution.py:1138
  895.6 103.2 %collective-permute-start.55 = (bf16[2,768,1024]{2,1,0:T(8,128)(2,1)S(1)}, bf16[2,768,1024]{2,1,0:T(8,128)(2,1)}, u32[]{:S(2)}, u32[]{:S(2)}) collective-permute-start(bf16[2,768,1024]{2,1,0:T(8,128)(2,1)S(1)} %pad_maximum_fusion.10), channel_id=1, source_target_pairs={{3,2},{0,1},{4,5},{7,6},{11,10},{8,9},{12,13},{15,14},{19,18},{16,... | collective-permute-start | bytes 9437192 | tf_op jit(solution)/shard_map/ppermute | solution.py:1154
  927.8 71.0 %collective-permute-start.51 = (bf16[768,1024]{1,0:T(8,128)(2,1)}, bf16[768,1024]{1,0:T(8,128)(2,1)}, u32[]{:S(2)}, u32[]{:S(2)}) collective-permute-start(bf16[768,1024]{1,0:T(8,128)(2,1)} %slice_bitcast_fusion.3), channel_id=1, source_target_pairs={{0,8},{4,12},{8,0},{12,4},{16,24},{20,28},{24,16},{28,20},{1,9},{5... | collective-permute-start | bytes 4718600 | tf_op jit(solution)/shard_map/ppermute | solution.py:1138
  1021.7 82.4 %collective-permute-start.60 = (bf16[1024,2048]{1,0:T(8,128)(2,1)}, bf16[1024,2048]{1,0:T(8,128)(2,1)}, u32[]{:S(2)}, u32[]{:S(2)}) collective-permute-start(bf16[1024,2048]{1,0:T(8,128)(2,1)} %shard_map.313), channel_id=1, source_target_pairs={{0,4},{4,0},{8,12},{12,8},{16,20},{20,16},{24,28},{28,24},{1,5},{5... | collective-permute-start | bytes 12582920 | tf_op jit(solution)/shard_map/ppermute | solution.py:1138
  1021.7 94.4 %collective-permute-start.59 = (bf16[1024,2048]{1,0:T(8,128)(2,1)}, bf16[1024,2048]{1,0:T(8,128)(2,1)}, u32[]{:S(2)}, u32[]{:S(2)}) collective-permute-start(bf16[1024,2048]{1,0:T(8,128)(2,1)} %shard_map.312), channel_id=1, source_target_pairs={{0,4},{4,0},{8,12},{12,8},{16,20},{20,16},{24,28},{28,24},{1,5},{5... | collective-permute-start | bytes 12582920 | tf_op jit(solution)/shard_map/ppermute | solution.py:1138
  1045.9 292.0 %reduce-scatter.5.cloned.1.call-start = ((), (), s32[]{:S(2)}) async-start(), calls=%async_computation.3 | async-start | bytes 2621440 | tf_op jit(solution)/shard_map/reduce_scatter | solution.py:1194
  1052.8 72.4 %collective-permute-start.67 = (bf16[2,768,1024]{2,1,0:T(8,128)(2,1)}, bf16[2,768,1024]{2,1,0:T(8,128)(2,1)}, u32[]{:S(2)}, u32[]{:S(2)}) collective-permute-start(bf16[2,768,1024]{2,1,0:T(8,128)(2,1)} %pad_maximum_fusion.11), channel_id=1, source_target_pairs={{3,2},{4,5},{11,10},{12,13},{19,18},{20,21},{27,26},{28,29}} | collective-permute-start | bytes 9437192 | tf_op jit(solution)/shard_map/ppermute | solution.py:1154
  1060.4 64.8 %collective-permute-start.66 = (bf16[2,768,1024]{2,1,0:T(8,128)(2,1)}, bf16[2,768,1024]{2,1,0:T(8,128)(2,1)}, u32[]{:S(2)}, u32[]{:S(2)}) collective-permute-start(bf16[2,768,1024]{2,1,0:T(8,128)(2,1)} %fusion), channel_id=1, source_target_pairs={{2,1},{5,6},{10,9},{13,14},{18,17},{21,22},{26,25},{29,30}} | collective-permute-start | bytes 9437192 | tf_op jit(solution)/shard_map/ppermute | solution.py:1154
  1187.1 102.1 %collective-permute-start.75 = (bf16[2,768,1024]{2,1,0:T(8,128)(2,1)S(1)}, bf16[2,768,1024]{2,1,0:T(8,128)(2,1)}, u32[]{:S(2)}, u32[]{:S(2)}) collective-permute-start(bf16[2,768,1024]{2,1,0:T(8,128)(2,1)S(1)} %add_convert_fusion.1), channel_id=1, source_target_pairs={{1,0},{6,7},{9,8},{14,15},{17,16},{22,23},{25,24},{30,31}} | collective-permute-start | bytes 9437192 | tf_op jit(solution)/shard_map/ppermute | solution.py:1154
  1193.4 95.8 %collective-permute-start.74 = (bf16[2,512,1024]{2,1,0:T(8,128)(2,1)}, bf16[2,512,1024]{2,1,0:T(8,128)(2,1)}, u32[]{:S(2)}, u32[]{:S(2)}) collective-permute-start(bf16[2,512,1024]{2,1,0:T(8,128)(2,1)} %add_convert_fusion.4), channel_id=1, source_target_pairs={{1,0},{2,1},{3,2},{5,4},{6,5},{7,6},{9,8},{10,9},{11,10},{13,12},{... | collective-permute-start | bytes 6291464 | tf_op jit(solution)/shard_map/ppermute | solution.py:24
  (130 other events, 2679.2 us)
Sparse Core Ops, SparseCore 0:
  70.1 55.3 all-gather.2
  1046.0 56.3 reduce-scatter.2
  1294.1 43.6 reduce-scatter.4

commit v8 on v7

--- a/solution.py
+++ b/solution.py
@@ -416,42 +416,55 @@
     return code % 2 * (blocks // 2) + code // 2
 
 
-def norm_kernel(rank, x_ref, gain_ref, o_ref, scale_ref, *, codes):
-    value = x_ref[...].astype(jnp.float32)
+def norm_kernel(rank, *refs, codes, tiles):
+    gain_ref, o_ref, scale_ref, x_ref = refs[-4:]
+    for k, ref in enumerate(refs[:-4]):
+
+        @pl.when(pl.program_id(0) // tiles == k)
+        def _(ref=ref):
+            x_ref[...] = ref[...].astype(jnp.float32)
+
+    value = x_ref[...]
     scale = lax.rsqrt(jnp.mean(value * value, axis=1, keepdims=True) + norm_eps)
     scale_ref[...] = scale
     half = len(codes) // 2
     block = x_ref.shape[1] // len(codes)
     for place, code in enumerate(codes):
-        start = pl.multiple_of((rank[0] ^ code) * block, block)
-        piece = x_ref[:, pl.ds(start, block)].astype(jnp.float32)
-        piece = piece * scale * gain_ref[:, pl.ds(start, block)]
+        columns = dynamic_block(rank[0] ^ code, block)
+        piece = x_ref[:, columns] * scale * gain_ref[:, columns]
         at = place % half * block
         o_ref[place // half, :, at : at + block] = piece.astype(jnp.bfloat16)
 
 
-def norm_rows(rank, value, gain, codes):
-    rows, width = value.shape
+def norm_rows(rank, parts, gain, codes):
+    rows, width = parts[0].shape
     tile = 256
+    tiles = rows // tile
+    rows = rows * len(parts)
+
+    def spec(k):
+        return pl.BlockSpec(
+            (tile, width), lambda i, rank: (jnp.clip(i - k * tiles, 0, tiles - 1), 0)
+        )
+
     return kernel_call(
-        functools.partial(norm_kernel, codes=codes),
+        functools.partial(norm_kernel, codes=codes, tiles=tiles),
         grid_spec=pltpu.PrefetchScalarGridSpec(
             num_scalar_prefetch=1,
             grid=(rows // tile,),
-            in_specs=[
-                pl.BlockSpec((tile, width), lambda i, rank: (i, 0)),
-                pl.BlockSpec((1, width), lambda i, rank: (0, 0)),
-            ],
+            in_specs=[spec(k) for k in range(len(parts))]
+            + [pl.BlockSpec((1, width), lambda i, rank: (0, 0))],
             out_specs=[
                 pl.BlockSpec((2, tile, width // 2), lambda i, rank: (0, i, 0)),
                 pl.BlockSpec((tile, 1), lambda i, rank: (i, 0)),
             ],
+            scratch_shapes=[pltpu.VMEM((tile, width), jnp.float32)],
         ),
         out_shape=[
             jax.ShapeDtypeStruct((2, rows, width // 2), jnp.bfloat16),
             jax.ShapeDtypeStruct((rows, 1), jnp.float32),
         ],
-    )(rank, value, gain[None])
+    )(rank, *parts, gain[None])
 
 
 def project_kernel(low_ref, high_ref, a_ref, b_ref, o_ref, s_ref):
@@ -1311,9 +1324,8 @@
     weight_router = small[4 : 4 + experts].T
     counts = small[4 + experts :, ::shard_rows].astype(f32)
     count = jnp.sum(counts[0]) * 16.0 + jnp.sum(counts[1])
-    tokens_all = jnp.concatenate([tokens_2, tokens_1, tokens], 0)
     key_segments = jnp.concatenate([segments_2, segments_1, segments], 0)
-    normed, scale_all = norm_rows(rank, tokens_all, gain_attn, order)
+    normed, scale_all = norm_rows(rank, (tokens_2, tokens_1, tokens), gain_attn, order)
     key_lin, key_squares = project(normed, *key_w, f32)
     value_all, _ = project(normed, *value_w, bf16)
     q_w, o_w, e_2, e_1, own, normed, key_lin, value_all = hold(
@@ -1371,7 +1383,7 @@
     mixed, lse_1 = attend(rank, operands, bias_small, HEADS // 2, (mixed,))
     branch, _ = project(mixed, *out_w, f32)
     residual = tokens.astype(f32) + branch
-    moe, scale_moe = norm_rows(quarter_rank, residual, gain_moe, (0, 1, 2, 3))
+    moe, scale_moe = norm_rows(quarter_rank, (residual,), gain_moe, (0, 1, 2, 3))
     moe_y = jnp.concatenate([moe, across(moe, 1)], 1)
     piece = half // 2
     moe_x = jnp.stack(

time: 1360 us -> 1350 us (level)
  no operation moved by 1% of the time
where the time goes in v8:
time: 1350 us; the launch traced here: 1340 us
  Pallas kernels  499 us (37%)
  waiting for transfers between devices  415 us (31%)
  other arithmetic  161 us (12%)
  starting transfers between devices  130 us (10%)
  local copies, waits for them, and re-layouts  111 us (8%)
  between operations  21.4 us (2%)
    ppermute x56, waiting for transfers between devices, across(): lax.ppermute(value, 'rep', [(place, place ^ bit) for place in range(count)])  251 us
    ppermute x6, waiting for transfers between devices, from_behind(): lax.ppermute(value, axis, [(source, source + steps) for source in range(l...  112 us
    pallas_call x8, Pallas kernels, chip_grad(): kernel_call(functools.partial(chip_grad_kernel, count=len(grads)), grid=(...  75 us
    pallas_call x8, Pallas kernels, experts_grad(): kernel_call(experts_grad_kernel, grid=(2,), in_specs=[pl.BlockSpec((1, ro...  63.4 us
    pallas_call x4, Pallas kernels, project(): kernel_call(project_kernel, grid=(rows // tile,), in_specs=[pl.BlockSpec(...  58.8 us
    pallas_call x2, Pallas kernels, attend_back(): kernel_call(functools.partial(attend_back_kernel, behind=all_rows - rows,...  57.7 us
    ppermute x56, starting transfers between devices, across(): lax.ppermute(value, 'rep', [(place, place ^ bit) for place in range(count)])  47.6 us
    pallas_call x1, Pallas kernels, project_back(): kernel_call(functools.partial(project_back_kernel, tile=512), grid=(2 * h...  41.2 us
  transfers between devices with their start and end apart: 83, of which 39 were waited for; matrix products, arithmetic and copies ran while one was open for 16% of the time, Pallas kernels for 29%

profile of v8, /device:TPU:0, one launch (start us, length us, event | category | flops | bytes accessed | tf_op | source)
XLA Modules:
  0.0 1342.7 jit_solution(15151648185840966682)
XLA Ops:
  40.0 18.7 %collective-permute-done.1 = bf16[2,64,2048]{2,1,0:T(8,128)(2,1)} collective-permute-done((bf16[2,64,2048]{2,1,0:T(8,128)(2,1)}, bf16[2,64,2048]{2,1,0:T(8,128)(2,1)}, u32[]{:S(2)}, u32[]{:S(2)}) %collective-permute-start.1) | collective-permute-done | bytes 524320 | tf_op jit(solution)/shard_map/ppermute | solution.py:1156
  125.5 19.8 %collective-permute-done.11 = bf16[2,256,2048]{2,1,0:T(8,128)(2,1)} collective-permute-done((bf16[2,256,2048]{2,1,0:T(8,128)(2,1)}, bf16[2,256,2048]{2,1,0:T(8,128)(2,1)}, u32[]{:S(2)}, u32[]{:S(2)}) %collective-permute-start.11) | collective-permute-done | bytes 2097184 | tf_op jit(solution)/shard_map/ppermute | solution.py:1151
  145.4 18.6 %collective-permute-done.12.refs_1_ = bf16[512,2048]{1,0:T(8,128)(2,1)} collective-permute-done((bf16[512,2048]{1,0:T(8,128)(2,1)}, bf16[512,2048]{1,0:T(8,128)(2,1)}, u32[]{:S(2)}, u32[]{:S(2)}) %collective-permute-start.12) | collective-permute-done | bytes 2097184 | tf_op jit(solution)/shard_map/ppermute | solution.py:24
  222.2 20.4 %collective-permute-done.17.refs_0_ = bf16[512,2048]{1,0:T(8,128)(2,1)} collective-permute-done((bf16[512,2048]{1,0:T(8,128)(2,1)}, bf16[512,2048]{1,0:T(8,128)(2,1)}, u32[]{:S(2)}, u32[]{:S(2)}) %collective-permute-start.17) | collective-permute-done | bytes 2097184 | tf_op jit(solution)/shard_map/ppermute | solution.py:24
  266.9 19.7 %shard_map.281 = (f32[1536,2048]{1,0:T(8,128)}, f32[1536,1]{1,0:T(8,128)}) custom-call(bf16[2,1536,1024]{2,1,0:T(8,128)(2,1)} %get-tuple-element.239.low_ref.high_ref.x_ref, bf16[2,1536,1024]{2,1,0:T(8,128)(2,1)} %get-tuple-element.239.low_ref.high_ref.x_ref, bf16[1040,2048]{1,0:T(8,128)(2,1)} %pad_dynamic-update-slice_fusion.a_ref.ka, ...), custom_call_target="tpu_custom_call" | custom-call | tf_op jit(solution)/shard_map/pallas_call | solution.py:483
  286.5 19.3 %shard_map.282 = (bf16[1536,2048]{1,0:T(8,128)(2,1)}, f32[1536,1]{1,0:T(8,128)}) custom-call(bf16[2,1536,1024]{2,1,0:T(8,128)(2,1)} %get-tuple-element.239.low_ref.high_ref.x_ref, bf16[2,1536,1024]{2,1,0:T(8,128)(2,1)} %get-tuple-element.239.low_ref.high_ref.x_ref, bf16[1024,2048]{1,0:T(8,128)(2,1)} %pad_maximum_fusion.a_ref.va, ...), custom_call_target="tpu_custom_call" | custom-call | tf_op jit(solution)/shard_map/pallas_call | solution.py:483
  345.3 19.6 %shard_map.284 = (bf16[2,512,1024]{2,1,0:T(8,128)(2,1)}, f32[8,1,512]{2,1,0:T(1,128)}) custom-call(s32[1]{0:T(128)} %bitcast.rank, f32[512,2048]{1,0:T(8,128)} %get-tuple-element.241.q_ref.lin_ref, f32[1536,2048]{1,0:T(8,128)} %get-tuple-element.242.k_ref.lin_ref, bf16[1536,2048]{1,0:T(8,128)(2,1)} %get-tuple-element.243.v_ref, ...), custom_call_target="tpu_custom_call" | custom-call | tf_op jit(solution)/shard_map/pallas_call | solution.py:658
  364.9 19.7 %shard_map.285 = (bf16[2,512,1024]{2,1,0:T(8,128)(2,1)}, f32[8,1,512]{2,1,0:T(1,128)}) custom-call(s32[1]{0:T(128)} %bitcast.rank, f32[512,2048]{1,0:T(8,128)} %get-tuple-element.241.q_ref.lin_ref, f32[1536,2048]{1,0:T(8,128)} %get-tuple-element.242.k_ref.lin_ref, bf16[1536,2048]{1,0:T(8,128)(2,1)} %get-tuple-element.243.v_ref, ...), custom_call_target="tpu_custom_call", output_to_operand_aliasing={{0}: (11, {})} | custom-call | tf_op jit(solution)/shard_map/pallas_call | solution.py:658
  430.1 27.7 %collective-permute-done.29.ub.refs_11_ = bf16[2,512,1024]{2,1,0:T(8,128)(2,1)} collective-permute-done((bf16[2,512,1024]{2,1,0:T(8,128)(2,1)}, bf16[2,512,1024]{2,1,0:T(8,128)(2,1)}, u32[]{:S(2)}, u32[]{:S(2)}) %collective-permute-start.29) | collective-permute-done | bytes 2097184 | tf_op jit(solution)/shard_map/ppermute | solution.py:1151
  466.8 15.2 %shard_map.288 = (f32[1024,1024]{1,0:T(8,128)}, f32[1024,1024]{1,0:T(8,128)}, bf16[2,1024,512]{2,1,0:T(8,128)(2,1)}, bf16[2,1024,512]{2,1,0:T(8,128)(2,1)}) custom-call(s32[1]{0:T(128)} %bitcast.56.rank, bf16[2,1024,1024]{2,1,0:T(8,128)(2,1)} %copy-done, bf16[2,1024,1024]{2,1,0:T(8,128)(2,1)} %pad_maximum_fusion.3.z_ref.x_ref, ...), custom_call_target="tpu_custom_call" | custom-call | tf_op jit(solution)/shard_map/pallas_call | solution.py:848
  482.0 17.6 %collective-permute-done.32 = bf16[768,1024]{1,0:T(8,128)(2,1)S(1)} collective-permute-done((bf16[768,1024]{1,0:T(8,128)(2,1)}, bf16[768,1024]{1,0:T(8,128)(2,1)S(1)}, u32[]{:S(2)}, u32[]{:S(2)}) %collective-permute-start.32) | collective-permute-done | bytes 1572896 | tf_op jit(solution)/shard_map/ppermute | solution.py:1151
  519.8 33.7 %collective-permute-done.35.ub.refs_5_ = bf16[2,512,1024]{2,1,0:T(8,128)(2,1)} collective-permute-done((bf16[2,512,1024]{2,1,0:T(8,128)(2,1)}, bf16[2,512,1024]{2,1,0:T(8,128)(2,1)}, u32[]{:S(2)}, u32[]{:S(2)}) %collective-permute-start.35) | collective-permute-done | bytes 2097184 | tf_op jit(solution)/shard_map/ppermute | solution.py:1151
  567.0 15.2 %shard_map.289 = (f32[1024,1024]{1,0:T(8,128)}, f32[1024,1024]{1,0:T(8,128)}, bf16[2,1024,512]{2,1,0:T(8,128)(2,1)}, bf16[2,1024,512]{2,1,0:T(8,128)(2,1)}) custom-call(s32[1]{0:T(128)} %bitcast.56.rank, bf16[2,1024,1024]{2,1,0:T(8,128)(2,1)} %copy-done, bf16[2,1024,1024]{2,1,0:T(8,128)(2,1)} %pad_maximum_fusion.3.z_ref.x_ref, ...), custom_call_target="tpu_custom_call" | custom-call | tf_op jit(solution)/shard_map/pallas_call | solution.py:848
  597.8 18.0 %shard_map.290 = (bf16[1024,2048]{1,0:T(8,128)(2,1)}, bf16[1024,2048]{1,0:T(8,128)(2,1)}, f32[512,2048]{1,0:T(8,128)}, f32[512,2048]{1,0:T(8,128)}) custom-call(f32[1024,1]{1,0:T(8,128)} %broadcast_select_fusion.2.refs_0_.gate_ref, f32[1024,1]{1,0:T(8,128)} %broadcast_select_fusion.1.refs_1_.gate_ref, ...), custom_call_target="tpu_custom_call" | custom-call | tf_op jit(solution)/shard_map/pallas_call | solution.py:897
  641.0 14.3 %shard_map.291 = (bf16[1024,2048]{1,0:T(8,128)(2,1)}, bf16[1024,1024]{1,0:T(8,128)(2,1)}, bf16[1024,1024]{1,0:T(8,128)(2,1)}, f32[1024,1]{1,0:T(8,128)}) custom-call(s32[1]{0:T(128)} %bitcast.56.rank, f32[512,2048]{1,0:T(8,128)} %copy-done.3, f32[512,2048]{1,0:T(8,128)} %copy-done.10, bf16[1024,2048]{1,0:T(8,128)(2,1)} %get-tuple-element.291.out_ref, ...), custom_call_target="tpu_custom_call" | custom-call | tf_op jit(solution)/shard_map/pallas_call | solution.py:948
  689.1 27.9 %shard_map.297 = (f32[4,512,512]{2,1,0:T(8,128)}, f32[4,512,512]{2,1,0:T(8,128)}) custom-call(bf16[1024,1024]{1,0:T(8,128)(2,1)} %get-tuple-element.301.d_ref.refs_0_, bf16[1024,1024]{1,0:T(8,128)(2,1)} %get-tuple-element.305.d_ref.refs_1_, bf16[2,768,1024]{2,1,0:T(8,128)(2,1)} %copy-done.2, bf16[2,512,1024]{2,1,0:T(8,128)(2,1)} %collective-permute-done.34.gb.refs_3_, ...), custom_call_target="tpu_custom_call" | custom-call | tf_op jit(solution)/shard_map/pallas_call | solution.py:999
  805.8 28.8 %shard_map.305 = (bf16[512,1024]{1,0:T(8,128)(2,1)}, bf16[1536,1024]{1,0:T(8,128)(2,1)}, bf16[1536,1024]{1,0:T(8,128)(2,1)}) custom-call(s32[1]{0:T(128)} %bitcast.rank, f32[512,2048]{1,0:T(8,128)} %get-tuple-element.241.q_ref.lin_ref, f32[1536,2048]{1,0:T(8,128)} %get-tuple-element.242.k_ref.lin_ref, bf16[1536,2048]{1,0:T(8,128)(2,1)} %get-tuple-element.243.v_ref, ...), custom_call_target="tpu_custom_call" | custom-call | tf_op jit(solution)/shard_map/pallas_call | solution.py:732
  834.7 28.9 %shard_map.304 = (bf16[512,1024]{1,0:T(8,128)(2,1)}, bf16[1536,1024]{1,0:T(8,128)(2,1)}, bf16[1536,1024]{1,0:T(8,128)(2,1)}) custom-call(s32[1]{0:T(128)} %bitcast.rank, f32[512,2048]{1,0:T(8,128)} %get-tuple-element.241.q_ref.lin_ref, f32[1536,2048]{1,0:T(8,128)} %get-tuple-element.242.k_ref.lin_ref, bf16[1536,2048]{1,0:T(8,128)(2,1)} %get-tuple-element.243.v_ref, ...), custom_call_target="tpu_custom_call" | custom-call | tf_op jit(solution)/shard_map/pallas_call | solution.py:732
  890.7 15.5 %collective-permute-start.55 = (bf16[2,768,1024]{2,1,0:T(8,128)(2,1)S(1)}, bf16[2,768,1024]{2,1,0:T(8,128)(2,1)}, u32[]{:S(2)}, u32[]{:S(2)}) collective-permute-start(bf16[2,768,1024]{2,1,0:T(8,128)(2,1)S(1)} %pad_maximum_fusion.9), channel_id=1, source_target_pairs={{3,2},{0,1},{4,5},{7,6},{11,10},{8,9},{12,13},{15,14},{19,18},{16,... | collective-permute-start | bytes 9437192 | tf_op jit(solution)/shard_map/ppermute | solution.py:1167
  1016.3 20.2 %collective-permute-done.64 = bf16[2,256,1024]{2,1,0:T(8,128)(2,1)S(1)} collective-permute-done((bf16[2,256,1024]{2,1,0:T(8,128)(2,1)S(1)}, bf16[2,256,1024]{2,1,0:T(8,128)(2,1)S(1)}, u32[]{:S(2)}, u32[]{:S(2)}) %collective-permute-start.64) | collective-permute-done | bytes 1048608 | tf_op jit(solution)/shard_map/ppermute | solution.py:1151
  1056.8 41.2 %shard_map.314.g_ref = f32[2,1536,1024]{2,1,0:T(8,128)} custom-call(bf16[1536,2048]{1,0:T(8,128)(2,1)} %get-tuple-element.345.refs_0_.k_ref, bf16[1536,1024]{1,0:T(8,128)(2,1)} %get-tuple-element.340.refs_0_.v_ref, bf16[1536,1024]{1,0:T(8,128)(2,1)} %get-tuple-element.341.refs_1_.w_ref, bf16[512,2048]{1,0:T(8,128)(2,1)} %get-tuple-element.346.refs_0_.q_ref, ...), custom_call_target="tpu_custom_call" | custom-call | tf_op jit(solution)/shard_map/pallas_call | solution.py:535
  1140.4 30.0 %collective-permute-done.68 = bf16[2,256,2048]{2,1,0:T(8,128)(2,1)S(1)} collective-permute-done((bf16[2,256,2048]{2,1,0:T(8,128)(2,1)S(1)}, bf16[2,256,2048]{2,1,0:T(8,128)(2,1)S(1)}, u32[]{:S(2)}, u32[]{:S(2)}) %collective-permute-start.68) | collective-permute-done | bytes 2097184 | tf_op jit(solution)/shard_map/ppermute | solution.py:1151
  1218.0 65.1 %collective-permute-done.74.c_ref = bf16[2,512,1024]{2,1,0:T(8,128)(2,1)} collective-permute-done((bf16[2,512,1024]{2,1,0:T(8,128)(2,1)}, bf16[2,512,1024]{2,1,0:T(8,128)(2,1)}, u32[]{:S(2)}, u32[]{:S(2)}) %collective-permute-start.74) | collective-permute-done | bytes 2097184 | tf_op jit(solution)/shard_map/ppermute | solution.py:24
  1313.5 18.4 %reduce-scatter.5.cloned.1.call-done = bf16[2,64,2048]{2,1,0:T(8,128)(2,1)} async-done(((bf16[2,256,2048]{2,1,0:T(8,128)(2,1)}), bf16[2,64,2048]{2,1,0:T(8,128)(2,1)}) %reduce-scatter.5.cloned.1.call-update) | async-done | bytes 524304 | tf_op jit(solution)/shard_map/reduce_scatter | solution.py:1207
  (559 shorter events, 747.8 us)
Async XLA Ops:
  7.2 118.4 %all-gather.3.cloned.1.call-start = ((), (), s32[]{:S(2)}) async-start(), calls=%async_computation.4 | async-start | bytes 2621440 | tf_op jit(solution)/shard_map/all_gather | solution.py:1284
  70.0 1047.1 %reduce-scatter.3.cloned.1.call-start = ((), (), s32[]{:S(2)}) async-start(), calls=%async_computation.2 | async-start | bytes 2621440 | tf_op jit(solution)/shard_map/reduce_scatter | solution.py:1207
  95.7 68.2 %collective-permute-start.10 = (bf16[2,272,2048]{2,1,0:T(8,128)(2,1)}, bf16[2,272,2048]{2,1,0:T(8,128)(2,1)}, u32[]{:S(2)}, u32[]{:S(2)}) collective-permute-start(bf16[2,272,2048]{2,1,0:T(8,128)(2,1)} %pad_maximum_fusion.13), channel_id=1, source_target_pairs={{0,16},{4,20},{8,24},{12,28},{16,0},{20,4},{24,8},{28,12},{1,17},{... | collective-permute-start | bytes 6684680 | tf_op jit(solution)/shard_map/ppermute | solution.py:1151
  114.5 88.8 %collective-permute-start.18 = (bf16[2,768,1024]{2,1,0:T(8,128)(2,1)S(1)}, bf16[2,768,1024]{2,1,0:T(8,128)(2,1)}, u32[]{:S(2)}, u32[]{:S(2)}) collective-permute-start(bf16[2,768,1024]{2,1,0:T(8,128)(2,1)S(1)} %pad_maximum_fusion.8), channel_id=1, source_target_pairs={{0,1},{1,2},{7,6},{6,5},{8,9},{9,10},{15,14},{14,13},{16,17},{17,1... | collective-permute-start | bytes 9437192 | tf_op jit(solution)/shard_map/ppermute | solution.py:1167
  178.9 63.7 %collective-permute-start.13 = (bf16[1040,2048]{1,0:T(8,128)(2,1)}, bf16[1040,2048]{1,0:T(8,128)(2,1)}, u32[]{:S(2)}, u32[]{:S(2)}) collective-permute-start(bf16[1040,2048]{1,0:T(8,128)(2,1)} %pad_dynamic-update-slice_fusion.a_ref.ka), channel_id=1, source_target_pairs={{0,4},{4,0},{8,12},{12,8},{16,20},{20,16},{24,28},{28,24},{1,5},{5... | collective-permute-start | bytes 12779528 | tf_op jit(solution)/shard_map/ppermute | solution.py:1151
  246.2 68.6 %collective-permute-start.21 = (bf16[2,768,1024]{2,1,0:T(8,128)(2,1)}, bf16[2,768,1024]{2,1,0:T(8,128)(2,1)}, u32[]{:S(2)}, u32[]{:S(2)}) collective-permute-start(bf16[2,768,1024]{2,1,0:T(8,128)(2,1)} %broadcast_select_fusion), channel_id=1, source_target_pairs={{1,0},{2,3},{6,7},{5,4},{9,8},{10,11},{14,15},{13,12},{17,16},{18,... | collective-permute-start | bytes 9437192 | tf_op jit(solution)/shard_map/ppermute | solution.py:1167
  516.5 65.7 %collective-permute-start.38 = (bf16[2,256,1024]{2,1,0:T(8,128)(2,1)}, bf16[2,256,1024]{2,1,0:T(8,128)(2,1)}, u32[]{:S(2)}, u32[]{:S(2)}) collective-permute-start(bf16[2,256,1024]{2,1,0:T(8,128)(2,1)} %slice.508), channel_id=1, source_target_pairs={{0,16},{4,20},{8,24},{12,28},{16,0},{20,4},{24,8},{28,12},{1,17},{... | collective-permute-start | bytes 3145736 | tf_op jit(solution)/shard_map/ppermute | solution.py:1151
  517.7 64.5 %collective-permute-start.39 = (bf16[2,256,1024]{2,1,0:T(8,128)(2,1)}, bf16[2,256,1024]{2,1,0:T(8,128)(2,1)}, u32[]{:S(2)}, u32[]{:S(2)}) collective-permute-start(bf16[2,256,1024]{2,1,0:T(8,128)(2,1)} %slice.509), channel_id=1, source_target_pairs={{0,8},{4,12},{8,0},{12,4},{16,24},{20,28},{24,16},{28,20},{1,9},{5... | collective-permute-start | bytes 3145736 | tf_op jit(solution)/shard_map/ppermute | solution.py:1151
  670.5 70.3 %collective-permute-start.42 = (bf16[2,768,1024]{2,1,0:T(8,128)(2,1)}, bf16[2,768,1024]{2,1,0:T(8,128)(2,1)S(1)}, u32[]{:S(2)}, u32[]{:S(2)}) collective-permute-start(bf16[2,768,1024]{2,1,0:T(8,128)(2,1)} %shard_map.292), channel_id=1, source_target_pairs={{0,8},{4,12},{8,0},{12,4},{16,24},{20,28},{24,16},{28,20},{1,9},{5... | collective-permute-start | bytes 9437192 | tf_op jit(solution)/shard_map/ppermute | solution.py:1151
  671.7 70.2 %collective-permute-start.43 = (bf16[2,768,1024]{2,1,0:T(8,128)(2,1)}, bf16[2,768,1024]{2,1,0:T(8,128)(2,1)}, u32[]{:S(2)}, u32[]{:S(2)}) collective-permute-start(bf16[2,768,1024]{2,1,0:T(8,128)(2,1)} %shard_map.293), channel_id=1, source_target_pairs={{0,16},{4,20},{8,24},{12,28},{16,0},{20,4},{24,8},{28,12},{1,17},{... | collective-permute-start | bytes 9437192 | tf_op jit(solution)/shard_map/ppermute | solution.py:1151
  768.0 95.6 %collective-permute-start.50 = (bf16[1024,2048]{1,0:T(8,128)(2,1)}, bf16[1024,2048]{1,0:T(8,128)(2,1)S(1)}, u32[]{:S(2)}, u32[]{:S(2)}) collective-permute-start(bf16[1024,2048]{1,0:T(8,128)(2,1)} %shard_map.301), channel_id=1, source_target_pairs={{0,4},{4,0},{8,12},{12,8},{16,20},{20,16},{24,28},{28,24},{1,5},{5... | collective-permute-start | bytes 12582920 | tf_op jit(solution)/shard_map/ppermute | solution.py:1151
  768.1 104.9 %collective-permute-start.45 = (bf16[2,768,1024]{2,1,0:T(8,128)(2,1)}, bf16[2,768,1024]{2,1,0:T(8,128)(2,1)S(1)}, u32[]{:S(2)}, u32[]{:S(2)}) collective-permute-start(bf16[2,768,1024]{2,1,0:T(8,128)(2,1)} %shard_map.295), channel_id=1, source_target_pairs={{0,8},{4,12},{8,0},{12,4},{16,24},{20,28},{24,16},{28,20},{1,9},{5... | collective-permute-start | bytes 9437192 | tf_op jit(solution)/shard_map/ppermute | solution.py:1151
  768.9 104.1 %collective-permute-start.46 = (bf16[2,768,1024]{2,1,0:T(8,128)(2,1)}, bf16[2,768,1024]{2,1,0:T(8,128)(2,1)}, u32[]{:S(2)}, u32[]{:S(2)}) collective-permute-start(bf16[2,768,1024]{2,1,0:T(8,128)(2,1)} %shard_map.296), channel_id=1, source_target_pairs={{0,16},{4,20},{8,24},{12,28},{16,0},{20,4},{24,8},{28,12},{1,17},{... | collective-permute-start | bytes 9437192 | tf_op jit(solution)/shard_map/ppermute | solution.py:1151
  780.4 92.3 %collective-permute-start.47 = (bf16[768,1024]{1,0:T(8,128)(2,1)}, bf16[768,1024]{1,0:T(8,128)(2,1)}, u32[]{:S(2)}, u32[]{:S(2)}) collective-permute-start(bf16[768,1024]{1,0:T(8,128)(2,1)} %slice_bitcast_fusion.5), channel_id=1, source_target_pairs={{0,8},{4,12},{8,0},{12,4},{16,24},{20,28},{24,16},{28,20},{1,9},{5... | collective-permute-start | bytes 4718600 | tf_op jit(solution)/shard_map/ppermute | solution.py:1151
  792.7 80.4 %collective-permute-start.48 = (bf16[768,1024]{1,0:T(8,128)(2,1)}, bf16[768,1024]{1,0:T(8,128)(2,1)}, u32[]{:S(2)}, u32[]{:S(2)}) collective-permute-start(bf16[768,1024]{1,0:T(8,128)(2,1)} %slice_bitcast_fusion.4), channel_id=1, source_target_pairs={{0,16},{4,20},{8,24},{12,28},{16,0},{20,4},{24,8},{28,12},{1,17},{... | collective-permute-start | bytes 4718600 | tf_op jit(solution)/shard_map/ppermute | solution.py:1151
  890.7 102.4 %collective-permute-start.55 = (bf16[2,768,1024]{2,1,0:T(8,128)(2,1)S(1)}, bf16[2,768,1024]{2,1,0:T(8,128)(2,1)}, u32[]{:S(2)}, u32[]{:S(2)}) collective-permute-start(bf16[2,768,1024]{2,1,0:T(8,128)(2,1)S(1)} %pad_maximum_fusion.9), channel_id=1, source_target_pairs={{3,2},{0,1},{4,5},{7,6},{11,10},{8,9},{12,13},{15,14},{19,18},{16,... | collective-permute-start | bytes 9437192 | tf_op jit(solution)/shard_map/ppermute | solution.py:1167
  921.8 71.2 %collective-permute-start.51 = (bf16[768,1024]{1,0:T(8,128)(2,1)}, bf16[768,1024]{1,0:T(8,128)(2,1)}, u32[]{:S(2)}, u32[]{:S(2)}) collective-permute-start(bf16[768,1024]{1,0:T(8,128)(2,1)} %slice_bitcast_fusion.3), channel_id=1, source_target_pairs={{0,8},{4,12},{8,0},{12,4},{16,24},{20,28},{24,16},{28,20},{1,9},{5... | collective-permute-start | bytes 4718600 | tf_op jit(solution)/shard_map/ppermute | solution.py:1151
  1015.7 82.3 %collective-permute-start.60 = (bf16[1024,2048]{1,0:T(8,128)(2,1)}, bf16[1024,2048]{1,0:T(8,128)(2,1)}, u32[]{:S(2)}, u32[]{:S(2)}) collective-permute-start(bf16[1024,2048]{1,0:T(8,128)(2,1)} %shard_map.313), channel_id=1, source_target_pairs={{0,4},{4,0},{8,12},{12,8},{16,20},{20,16},{24,28},{28,24},{1,5},{5... | collective-permute-start | bytes 12582920 | tf_op jit(solution)/shard_map/ppermute | solution.py:1151
  1015.8 94.3 %collective-permute-start.59 = (bf16[1024,2048]{1,0:T(8,128)(2,1)}, bf16[1024,2048]{1,0:T(8,128)(2,1)}, u32[]{:S(2)}, u32[]{:S(2)}) collective-permute-start(bf16[1024,2048]{1,0:T(8,128)(2,1)} %shard_map.312), channel_id=1, source_target_pairs={{0,4},{4,0},{8,12},{12,8},{16,20},{20,16},{24,28},{28,24},{1,5},{5... | collective-permute-start | bytes 12582920 | tf_op jit(solution)/shard_map/ppermute | solution.py:1151
  1039.9 292.0 %reduce-scatter.5.cloned.1.call-start = ((), (), s32[]{:S(2)}) async-start(), calls=%async_computation.3 | async-start | bytes 2621440 | tf_op jit(solution)/shard_map/reduce_scatter | solution.py:1207
  1046.9 72.3 %collective-permute-start.67 = (bf16[2,768,1024]{2,1,0:T(8,128)(2,1)}, bf16[2,768,1024]{2,1,0:T(8,128)(2,1)}, u32[]{:S(2)}, u32[]{:S(2)}) collective-permute-start(bf16[2,768,1024]{2,1,0:T(8,128)(2,1)} %pad_maximum_fusion.10), channel_id=1, source_target_pairs={{3,2},{4,5},{11,10},{12,13},{19,18},{20,21},{27,26},{28,29}} | collective-permute-start | bytes 9437192 | tf_op jit(solution)/shard_map/ppermute | solution.py:1167
  1054.4 64.8 %collective-permute-start.66 = (bf16[2,768,1024]{2,1,0:T(8,128)(2,1)}, bf16[2,768,1024]{2,1,0:T(8,128)(2,1)}, u32[]{:S(2)}, u32[]{:S(2)}) collective-permute-start(bf16[2,768,1024]{2,1,0:T(8,128)(2,1)} %fusion), channel_id=1, source_target_pairs={{2,1},{5,6},{10,9},{13,14},{18,17},{21,22},{26,25},{29,30}} | collective-permute-start | bytes 9437192 | tf_op jit(solution)/shard_map/ppermute | solution.py:1167
  1181.1 102.0 %collective-permute-start.75 = (bf16[2,768,1024]{2,1,0:T(8,128)(2,1)S(1)}, bf16[2,768,1024]{2,1,0:T(8,128)(2,1)}, u32[]{:S(2)}, u32[]{:S(2)}) collective-permute-start(bf16[2,768,1024]{2,1,0:T(8,128)(2,1)S(1)} %add_convert_fusion.1), channel_id=1, source_target_pairs={{1,0},{6,7},{9,8},{14,15},{17,16},{22,23},{25,24},{30,31}} | collective-permute-start | bytes 9437192 | tf_op jit(solution)/shard_map/ppermute | solution.py:1167
  1187.4 95.7 %collective-permute-start.74 = (bf16[2,512,1024]{2,1,0:T(8,128)(2,1)}, bf16[2,512,1024]{2,1,0:T(8,128)(2,1)}, u32[]{:S(2)}, u32[]{:S(2)}) collective-permute-start(bf16[2,512,1024]{2,1,0:T(8,128)(2,1)} %add_convert_fusion.4), channel_id=1, source_target_pairs={{1,0},{2,1},{3,2},{5,4},{6,5},{7,6},{9,8},{10,9},{11,10},{13,12},{... | collective-permute-start | bytes 6291464 | tf_op jit(solution)/shard_map/ppermute | solution.py:24
  (130 other events, 2668.0 us)
Sparse Core Ops, SparseCore 0:
  70.1 55.3 all-gather.2
  1040.0 56.4 reduce-scatter.2
  1288.1 43.7 reduce-scatter.4

commit v9 on v8

--- a/solution.py
+++ b/solution.py
@@ -1314,6 +1314,7 @@
     q_w = jnp.concatenate([q_w, q_y], 0)
     o_w = jnp.concatenate([o_w, o_x[0], o_y, o_x[1]], 0)
     e_2 = mirrored(jnp.where(m == 2, e_1, own), [(1, 0), (2, 3)])
+    e_3 = mirrored(e_1, [(1, 2)])
     small = jnp.stack([weight[4 * block : 4 * block + 8] for weight in key_w])
     small = small.reshape(2, 2, 2, -1)[..., : experts * columns * shard_rows]
     for axis, bit in enumerate((core, place[0], place[1])):
@@ -1328,14 +1329,14 @@
     normed, scale_all = norm_rows(rank, (tokens_2, tokens_1, tokens), gain_attn, order)
     key_lin, key_squares = project(normed, *key_w, f32)
     value_all, _ = project(normed, *value_w, bf16)
-    q_w, o_w, e_2, e_1, own, normed, key_lin, value_all = hold(
-        q_w, o_w, e_2, e_1, own, normed, key_lin, value_all
+    q_w, o_w, e_2, e_3, e_1, own, normed, key_lin, value_all = hold(
+        q_w, o_w, e_2, e_3, e_1, own, normed, key_lin, value_all
     )
 
     query_w, out_w = (q_w, across(q_w, 1)), (o_w, across(o_w, 1))
     e_b = jnp.where(m == 1, own, jnp.where(m == 2, e_1, e_2))
     b_x, b_y = both_ways(e_b)
-    e_3 = mirrored(e_1, [(1, 2)])
+    e_4 = mirrored(e_3, [(2, 3)])
     query_lin, query_squares = project(normed, *query_w, f32, behind)
     scale_key = lax.rsqrt(key_squares / width + norm_eps)
     scale_query = lax.rsqrt(query_squares / width + norm_eps)
@@ -1375,12 +1376,16 @@
     )
     bias_small = mask_of(local_rows // 4)
     mixed, lse_0 = attend(rank, operands, bias_small, 0)
-    mixed, out_w, e_b, b_x, b_y, e_3, e_1, own = hold(mixed, out_w, e_b, b_x, b_y, e_3, e_1, own)
+    mixed, out_w, e_b, b_x, b_y, e_4, e_3, e_1, own = hold(
+        mixed, out_w, e_b, b_x, b_y, e_4, e_3, e_1, own
+    )
 
     b_0, b_1 = jnp.stack([e_b[0], b_x]), jnp.stack([e_b[1], b_y])
     b_2, b_3 = other_ways(b_0[:, :quarter_rows], b_1[:, :quarter_rows])
-    e_4 = mirrored(e_3, [(2, 3)])
     mixed, lse_1 = attend(rank, operands, bias_small, HEADS // 2, (mixed,))
+    e_a = jnp.where(m == 0, own, jnp.where(m == 1, e_1, jnp.where(m == 2, e_3, e_4)))
+    mixed, b_2, b_3, e_a = hold(mixed, b_2, b_3, e_a)
+    a_x, a_y = both_ways(e_a)
     branch, _ = project(mixed, *out_w, f32)
     residual = tokens.astype(f32) + branch
     moe, scale_moe = norm_rows(quarter_rank, (residual,), gain_moe, (0, 1, 2, 3))
@@ -1404,20 +1409,14 @@
     gates_both = jnp.concatenate([gates, across(gates, 1)], 0)
     gates_a = jnp.where(core == 0, gates_both[:, :1], gates_both[:, -1:])
     gates_b = jnp.where(core == 0, gates_both[:, 1:2], gates_both[:, -2:-1])
-    b_0, b_1, b_2, b_3, e_4, e_3, e_1, own, moe_y, moe_x = hold(
-        b_0, b_1, b_2, b_3, e_4, e_3, e_1, own, moe_y, moe_x
-    )
-
-    e_a = jnp.where(m == 0, own, jnp.where(m == 1, e_1, jnp.where(m == 2, e_3, e_4)))
-    a_x, a_y = both_ways(e_a)
+    b_0, b_1, e_a, a_x, a_y, moe_y, moe_x = hold(b_0, b_1, e_a, a_x, a_y, moe_y, moe_x)
+
+    a_0, a_1 = jnp.stack([e_a[0], a_x]), jnp.stack([e_a[1], a_y])
+    a_2, a_3 = other_ways(a_0[:, :quarter_rows], a_1[:, :quarter_rows])
     b_4, b_5 = other_ways(b_0[:, quarter_rows:], b_1[:, quarter_rows:])
     up_weights_b, down_weights_b = (b_0, b_2, b_1, b_3), (b_0, b_4, b_1, b_5)
     gate_pre_b, up_pre_b, my_b, mx_b = experts_up(quarter_rank, moe_y, moe_x, up_weights_b)
-    e_a, a_x, a_y, my_b, mx_b, moe_y, moe_x = hold(e_a, a_x, a_y, my_b, mx_b, moe_y, moe_x)
-
-    a_0, a_1 = jnp.stack([e_a[0], a_x]), jnp.stack([e_a[1], a_y])
-    a_2, a_3 = other_ways(a_0[:, :quarter_rows], a_1[:, :quarter_rows])
-    a_0, a_1, a_2, a_3 = hold(a_0, a_1, a_2, a_3)
+    a_0, a_1, a_2, a_3, my_b, mx_b = hold(a_0, a_1, a_2, a_3, my_b, mx_b)
 
     a_4, a_5 = other_ways(a_0[:, quarter_rows:], a_1[:, quarter_rows:])
     up_weights_a, down_weights_a = (a_0, a_2, a_1, a_3), (a_0, a_4, a_1, a_5)

time: 1350 us -> 1330 us (0.985)
  waiting for transfers between devices: 415 us -> 392 us
    ppermute x56, waiting for transfers between devices: 251 us -> 229 us  [across(): lax.ppermute(value, 'rep', [(place, place ^ bit) for place in range(count)])]
  transfers between devices with their start and end apart: 83 -> 83, of which waited for: 39 -> 39; matrix products, arithmetic and copies ran while one was open for 16% -> 17% of each run, Pallas kernels for 29% -> 31%
where the time goes in v9:
time: 1330 us; the launch traced here: 1320 us
  Pallas kernels  500 us (38%)
  waiting for transfers between devices  392 us (29%)
  other arithmetic  164 us (12%)
  starting transfers between devices  127 us (10%)
  local copies, waits for them, and re-layouts  109 us (8%)
  between operations  21.7 us (2%)
    ppermute x56, waiting for transfers between devices, across(): lax.ppermute(value, 'rep', [(place, place ^ bit) for place in range(count)])  229 us
    ppermute x6, waiting for transfers between devices, from_behind(): lax.ppermute(value, axis, [(source, source + steps) for source in range(l...  112 us
    pallas_call x8, Pallas kernels, chip_grad(): kernel_call(functools.partial(chip_grad_kernel, count=len(grads)), grid=(...  75.2 us
    pallas_call x8, Pallas kernels, experts_grad(): kernel_call(experts_grad_kernel, grid=(2,), in_specs=[pl.BlockSpec((1, ro...  63.4 us
    pallas_call x4, Pallas kernels, project(): kernel_call(project_kernel, grid=(rows // tile,), in_specs=[pl.BlockSpec(...  58.8 us
    pallas_call x2, Pallas kernels, attend_back(): kernel_call(functools.partial(attend_back_kernel, behind=all_rows - rows,...  57.7 us
    ppermute x56, starting transfers between devices, across(): lax.ppermute(value, 'rep', [(place, place ^ bit) for place in range(count)])  47.9 us
    pallas_call x1, Pallas kernels, project_back(): kernel_call(functools.partial(project_back_kernel, tile=512), grid=(2 * h...  41.2 us
  transfers between devices with their start and end apart: 83, of which 39 were waited for; matrix products, arithmetic and copies ran while one was open for 17% of the time, Pallas kernels for 31%

profile of v9, /device:TPU:0, one launch (start us, length us, event | category | flops | bytes accessed | tf_op | source)
XLA Modules:
  0.0 1317.6 jit_solution(14420014645929906853)
XLA Ops:
  40.0 18.7 %collective-permute-done.1 = bf16[2,64,2048]{2,1,0:T(8,128)(2,1)} collective-permute-done((bf16[2,64,2048]{2,1,0:T(8,128)(2,1)}, bf16[2,64,2048]{2,1,0:T(8,128)(2,1)}, u32[]{:S(2)}, u32[]{:S(2)}) %collective-permute-start.1) | collective-permute-done | bytes 524320 | tf_op jit(solution)/shard_map/ppermute | solution.py:1156
  125.5 19.8 %collective-permute-done.11 = bf16[2,256,2048]{2,1,0:T(8,128)(2,1)} collective-permute-done((bf16[2,256,2048]{2,1,0:T(8,128)(2,1)}, bf16[2,256,2048]{2,1,0:T(8,128)(2,1)}, u32[]{:S(2)}, u32[]{:S(2)}) %collective-permute-start.11) | collective-permute-done | bytes 2097184 | tf_op jit(solution)/shard_map/ppermute | solution.py:1151
  145.4 18.6 %collective-permute-done.12.refs_1_ = bf16[512,2048]{1,0:T(8,128)(2,1)} collective-permute-done((bf16[512,2048]{1,0:T(8,128)(2,1)}, bf16[512,2048]{1,0:T(8,128)(2,1)}, u32[]{:S(2)}, u32[]{:S(2)}) %collective-permute-start.12) | collective-permute-done | bytes 2097184 | tf_op jit(solution)/shard_map/ppermute | solution.py:24
  222.6 20.0 %collective-permute-done.17.refs_0_ = bf16[512,2048]{1,0:T(8,128)(2,1)} collective-permute-done((bf16[512,2048]{1,0:T(8,128)(2,1)}, bf16[512,2048]{1,0:T(8,128)(2,1)}, u32[]{:S(2)}, u32[]{:S(2)}) %collective-permute-start.17) | collective-permute-done | bytes 2097184 | tf_op jit(solution)/shard_map/ppermute | solution.py:24
  269.1 19.7 %shard_map.281 = (f32[1536,2048]{1,0:T(8,128)}, f32[1536,1]{1,0:T(8,128)}) custom-call(bf16[2,1536,1024]{2,1,0:T(8,128)(2,1)} %get-tuple-element.237.low_ref.high_ref.x_ref, bf16[2,1536,1024]{2,1,0:T(8,128)(2,1)} %get-tuple-element.237.low_ref.high_ref.x_ref, bf16[1040,2048]{1,0:T(8,128)(2,1)} %pad_dynamic-update-slice_fusion.a_ref.ka, ...), custom_call_target="tpu_custom_call" | custom-call | tf_op jit(solution)/shard_map/pallas_call | solution.py:483
  288.8 19.3 %shard_map.282 = (bf16[1536,2048]{1,0:T(8,128)(2,1)}, f32[1536,1]{1,0:T(8,128)}) custom-call(bf16[2,1536,1024]{2,1,0:T(8,128)(2,1)} %get-tuple-element.237.low_ref.high_ref.x_ref, bf16[2,1536,1024]{2,1,0:T(8,128)(2,1)} %get-tuple-element.237.low_ref.high_ref.x_ref, bf16[1024,2048]{1,0:T(8,128)(2,1)} %pad_maximum_fusion.a_ref.va, ...), custom_call_target="tpu_custom_call" | custom-call | tf_op jit(solution)/shard_map/pallas_call | solution.py:483
  346.0 19.8 %shard_map.284 = (bf16[2,512,1024]{2,1,0:T(8,128)(2,1)}, f32[8,1,512]{2,1,0:T(1,128)}) custom-call(s32[1]{0:T(128)} %bitcast.rank, f32[512,2048]{1,0:T(8,128)} %get-tuple-element.239.q_ref.lin_ref, f32[1536,2048]{1,0:T(8,128)} %get-tuple-element.240.k_ref.lin_ref, bf16[1536,2048]{1,0:T(8,128)(2,1)} %get-tuple-element.241.v_ref, ...), custom_call_target="tpu_custom_call" | custom-call | tf_op jit(solution)/shard_map/pallas_call | solution.py:658
  375.2 19.6 %shard_map.285 = (bf16[2,512,1024]{2,1,0:T(8,128)(2,1)}, f32[8,1,512]{2,1,0:T(1,128)}) custom-call(s32[1]{0:T(128)} %bitcast.rank, f32[512,2048]{1,0:T(8,128)} %get-tuple-element.239.q_ref.lin_ref, f32[1536,2048]{1,0:T(8,128)} %get-tuple-element.240.k_ref.lin_ref, bf16[1536,2048]{1,0:T(8,128)(2,1)} %get-tuple-element.241.v_ref, ...), custom_call_target="tpu_custom_call", output_to_operand_aliasing={{0}: (11, {})} | custom-call | tf_op jit(solution)/shard_map/pallas_call | solution.py:658
  397.3 18.6 %collective-permute-done.29.ub.refs_11_ = bf16[2,512,1024]{2,1,0:T(8,128)(2,1)} collective-permute-done((bf16[2,512,1024]{2,1,0:T(8,128)(2,1)}, bf16[2,512,1024]{2,1,0:T(8,128)(2,1)}, u32[]{:S(2)}, u32[]{:S(2)}) %collective-permute-start.29) | collective-permute-done | bytes 2097184 | tf_op jit(solution)/shard_map/ppermute | solution.py:1151
  453.0 23.1 %collective-permute-done.31 = bf16[768,1024]{1,0:T(8,128)(2,1)S(1)} collective-permute-done((bf16[768,1024]{1,0:T(8,128)(2,1)S(1)}, bf16[768,1024]{1,0:T(8,128)(2,1)S(1)}, u32[]{:S(2)}, u32[]{:S(2)}) %collective-permute-start.31) | collective-permute-done | bytes 1572896 | tf_op jit(solution)/shard_map/ppermute | solution.py:1151
  493.1 15.2 %shard_map.288 = (f32[1024,1024]{1,0:T(8,128)}, f32[1024,1024]{1,0:T(8,128)}, bf16[2,1024,512]{2,1,0:T(8,128)(2,1)}, bf16[2,1024,512]{2,1,0:T(8,128)(2,1)}) custom-call(s32[1]{0:T(128)} %bitcast.58.rank, bf16[2,1024,1024]{2,1,0:T(8,128)(2,1)} %copy-done, bf16[2,1024,1024]{2,1,0:T(8,128)(2,1)} %pad_maximum_fusion.3.z_ref.x_ref, ...), custom_call_target="tpu_custom_call" | custom-call | tf_op jit(solution)/shard_map/pallas_call | solution.py:848
  510.5 18.3 %collective-permute-done.35.ub.refs_5_ = bf16[2,512,1024]{2,1,0:T(8,128)(2,1)} collective-permute-done((bf16[2,512,1024]{2,1,0:T(8,128)(2,1)}, bf16[2,512,1024]{2,1,0:T(8,128)(2,1)}, u32[]{:S(2)}, u32[]{:S(2)}) %collective-permute-start.35) | collective-permute-done | bytes 2097184 | tf_op jit(solution)/shard_map/ppermute | solution.py:1151
  548.2 15.2 %shard_map.289 = (f32[1024,1024]{1,0:T(8,128)}, f32[1024,1024]{1,0:T(8,128)}, bf16[2,1024,512]{2,1,0:T(8,128)(2,1)}, bf16[2,1024,512]{2,1,0:T(8,128)(2,1)}) custom-call(s32[1]{0:T(128)} %bitcast.58.rank, bf16[2,1024,1024]{2,1,0:T(8,128)(2,1)} %copy-done, bf16[2,1024,1024]{2,1,0:T(8,128)(2,1)} %pad_maximum_fusion.3.z_ref.x_ref, ...), custom_call_target="tpu_custom_call" | custom-call | tf_op jit(solution)/shard_map/pallas_call | solution.py:848
  575.6 18.2 %shard_map.290 = (bf16[1024,2048]{1,0:T(8,128)(2,1)}, bf16[1024,2048]{1,0:T(8,128)(2,1)}, f32[512,2048]{1,0:T(8,128)}, f32[512,2048]{1,0:T(8,128)}) custom-call(f32[1024,1]{1,0:T(8,128)} %broadcast_select_fusion.2.refs_0_.gate_ref, f32[1024,1]{1,0:T(8,128)} %broadcast_select_fusion.1.refs_1_.gate_ref, ...), custom_call_target="tpu_custom_call" | custom-call | tf_op jit(solution)/shard_map/pallas_call | solution.py:897
  650.8 14.3 %shard_map.294 = (bf16[1024,2048]{1,0:T(8,128)(2,1)}, bf16[1024,1024]{1,0:T(8,128)(2,1)}, bf16[1024,1024]{1,0:T(8,128)(2,1)}, f32[1024,1]{1,0:T(8,128)}) custom-call(s32[1]{0:T(128)} %bitcast.58.rank, f32[512,2048]{1,0:T(8,128)} %copy-done.4, f32[512,2048]{1,0:T(8,128)} %copy-done.11, bf16[1024,2048]{1,0:T(8,128)(2,1)} %get-tuple-element.294.out_ref, ...), custom_call_target="tpu_custom_call" | custom-call | tf_op jit(solution)/shard_map/pallas_call | solution.py:948
  667.6 27.7 %shard_map.297 = (f32[4,512,512]{2,1,0:T(8,128)}, f32[4,512,512]{2,1,0:T(8,128)}) custom-call(bf16[1024,1024]{1,0:T(8,128)(2,1)} %get-tuple-element.297.d_ref.refs_0_, bf16[1024,1024]{1,0:T(8,128)(2,1)} %get-tuple-element.301.d_ref.refs_1_, bf16[2,768,1024]{2,1,0:T(8,128)(2,1)} %copy-done.3, bf16[2,512,1024]{2,1,0:T(8,128)(2,1)} %collective-permute-done.34.gb.refs_3_, ...), custom_call_target="tpu_custom_call" | custom-call | tf_op jit(solution)/shard_map/pallas_call | solution.py:999
  783.7 28.8 %shard_map.305 = (bf16[512,1024]{1,0:T(8,128)(2,1)}, bf16[1536,1024]{1,0:T(8,128)(2,1)}, bf16[1536,1024]{1,0:T(8,128)(2,1)}) custom-call(s32[1]{0:T(128)} %bitcast.rank, f32[512,2048]{1,0:T(8,128)} %get-tuple-element.239.q_ref.lin_ref, f32[1536,2048]{1,0:T(8,128)} %get-tuple-element.240.k_ref.lin_ref, bf16[1536,2048]{1,0:T(8,128)(2,1)} %get-tuple-element.241.v_ref, ...), custom_call_target="tpu_custom_call" | custom-call | tf_op jit(solution)/shard_map/pallas_call | solution.py:732
  812.6 28.9 %shard_map.304 = (bf16[512,1024]{1,0:T(8,128)(2,1)}, bf16[1536,1024]{1,0:T(8,128)(2,1)}, bf16[1536,1024]{1,0:T(8,128)(2,1)}) custom-call(s32[1]{0:T(128)} %bitcast.rank, f32[512,2048]{1,0:T(8,128)} %get-tuple-element.239.q_ref.lin_ref, f32[1536,2048]{1,0:T(8,128)} %get-tuple-element.240.k_ref.lin_ref, bf16[1536,2048]{1,0:T(8,128)(2,1)} %get-tuple-element.241.v_ref, ...), custom_call_target="tpu_custom_call" | custom-call | tf_op jit(solution)/shard_map/pallas_call | solution.py:732
  991.3 20.4 %collective-permute-done.64 = bf16[2,256,1024]{2,1,0:T(8,128)(2,1)S(1)} collective-permute-done((bf16[2,256,1024]{2,1,0:T(8,128)(2,1)S(1)}, bf16[2,256,1024]{2,1,0:T(8,128)(2,1)S(1)}, u32[]{:S(2)}, u32[]{:S(2)}) %collective-permute-start.64) | collective-permute-done | bytes 1048608 | tf_op jit(solution)/shard_map/ppermute | solution.py:1151
  1032.0 41.2 %shard_map.314.g_ref = f32[2,1536,1024]{2,1,0:T(8,128)} custom-call(bf16[1536,2048]{1,0:T(8,128)(2,1)} %get-tuple-element.341.refs_0_.k_ref, bf16[1536,1024]{1,0:T(8,128)(2,1)} %get-tuple-element.336.refs_0_.v_ref, bf16[1536,1024]{1,0:T(8,128)(2,1)} %get-tuple-element.337.refs_1_.w_ref, bf16[512,2048]{1,0:T(8,128)(2,1)} %get-tuple-element.342.refs_0_.q_ref, ...), custom_call_target="tpu_custom_call" | custom-call | tf_op jit(solution)/shard_map/pallas_call | solution.py:535
  1115.5 30.3 %collective-permute-done.68 = bf16[2,256,2048]{2,1,0:T(8,128)(2,1)S(1)} collective-permute-done((bf16[2,256,2048]{2,1,0:T(8,128)(2,1)S(1)}, bf16[2,256,2048]{2,1,0:T(8,128)(2,1)S(1)}, u32[]{:S(2)}, u32[]{:S(2)}) %collective-permute-start.68) | collective-permute-done | bytes 2097184 | tf_op jit(solution)/shard_map/ppermute | solution.py:1151
  1174.7 14.6 %collective-permute-done.73 = bf16[256,2048]{1,0:T(8,128)(2,1)} collective-permute-done((bf16[256,2048]{1,0:T(8,128)(2,1)}, bf16[256,2048]{1,0:T(8,128)(2,1)}, u32[]{:S(2)}, u32[]{:S(2)}) %collective-permute-start.73) | collective-permute-done | bytes 1048608 | tf_op jit(solution)/shard_map/ppermute | solution.py:1151
  1192.5 65.8 %collective-permute-done.74.c_ref = bf16[2,512,1024]{2,1,0:T(8,128)(2,1)} collective-permute-done((bf16[2,512,1024]{2,1,0:T(8,128)(2,1)}, bf16[2,512,1024]{2,1,0:T(8,128)(2,1)}, u32[]{:S(2)}, u32[]{:S(2)}) %collective-permute-start.74) | collective-permute-done | bytes 2097184 | tf_op jit(solution)/shard_map/ppermute | solution.py:24
  1289.2 17.3 %reduce-scatter.5.cloned.1.call-done = bf16[2,64,2048]{2,1,0:T(8,128)(2,1)} async-done(((bf16[2,256,2048]{2,1,0:T(8,128)(2,1)}), bf16[2,64,2048]{2,1,0:T(8,128)(2,1)}) %reduce-scatter.5.cloned.1.call-update) | async-done | bytes 524304 | tf_op jit(solution)/shard_map/reduce_scatter | solution.py:1207
  (569 shorter events, 742.4 us)
Async XLA Ops:
  7.2 118.4 %all-gather.3.cloned.1.call-start = ((), (), s32[]{:S(2)}) async-start(), calls=%async_computation.4 | async-start | bytes 2621440 | tf_op jit(solution)/shard_map/all_gather | solution.py:1284
  70.0 1022.3 %reduce-scatter.3.cloned.1.call-start = ((), (), s32[]{:S(2)}) async-start(), calls=%async_computation.2 | async-start | bytes 2621440 | tf_op jit(solution)/shard_map/reduce_scatter | solution.py:1207
  95.7 68.2 %collective-permute-start.10 = (bf16[2,272,2048]{2,1,0:T(8,128)(2,1)}, bf16[2,272,2048]{2,1,0:T(8,128)(2,1)}, u32[]{:S(2)}, u32[]{:S(2)}) collective-permute-start(bf16[2,272,2048]{2,1,0:T(8,128)(2,1)} %pad_maximum_fusion.13), channel_id=1, source_target_pairs={{0,16},{4,20},{8,24},{12,28},{16,0},{20,4},{24,8},{28,12},{1,17},{... | collective-permute-start | bytes 6684680 | tf_op jit(solution)/shard_map/ppermute | solution.py:1151
  114.5 88.7 %collective-permute-start.18 = (bf16[2,768,1024]{2,1,0:T(8,128)(2,1)S(1)}, bf16[2,768,1024]{2,1,0:T(8,128)(2,1)}, u32[]{:S(2)}, u32[]{:S(2)}) collective-permute-start(bf16[2,768,1024]{2,1,0:T(8,128)(2,1)S(1)} %pad_maximum_fusion.8), channel_id=1, source_target_pairs={{0,1},{1,2},{7,6},{6,5},{8,9},{9,10},{15,14},{14,13},{16,17},{17,1... | collective-permute-start | bytes 9437192 | tf_op jit(solution)/shard_map/ppermute | solution.py:1167
  244.2 72.9 %collective-permute-start.22 = (bf16[2,768,1024]{2,1,0:T(8,128)(2,1)}, bf16[2,768,1024]{2,1,0:T(8,128)(2,1)}, u32[]{:S(2)}, u32[]{:S(2)}) collective-permute-start(bf16[2,768,1024]{2,1,0:T(8,128)(2,1)} %collective-permute-done.18), channel_id=1, source_target_pairs={{1,2},{6,5},{9,10},{14,13},{17,18},{22,21},{25,26},{30,29}} | collective-permute-start | bytes 9437192 | tf_op jit(solution)/shard_map/ppermute | solution.py:1167
  248.5 68.5 %collective-permute-start.21 = (bf16[2,768,1024]{2,1,0:T(8,128)(2,1)}, bf16[2,768,1024]{2,1,0:T(8,128)(2,1)}, u32[]{:S(2)}, u32[]{:S(2)}) collective-permute-start(bf16[2,768,1024]{2,1,0:T(8,128)(2,1)} %broadcast_select_fusion), channel_id=1, source_target_pairs={{1,0},{2,3},{6,7},{5,4},{9,8},{10,11},{14,15},{13,12},{17,16},{18,... | collective-permute-start | bytes 9437192 | tf_op jit(solution)/shard_map/ppermute | solution.py:1167
  490.2 73.3 %collective-permute-start.38 = (bf16[2,256,1024]{2,1,0:T(8,128)(2,1)}, bf16[2,256,1024]{2,1,0:T(8,128)(2,1)}, u32[]{:S(2)}, u32[]{:S(2)}) collective-permute-start(bf16[2,256,1024]{2,1,0:T(8,128)(2,1)} %slice.508), channel_id=1, source_target_pairs={{0,16},{4,20},{8,24},{12,28},{16,0},{20,4},{24,8},{28,12},{1,17},{... | collective-permute-start | bytes 3145736 | tf_op jit(solution)/shard_map/ppermute | solution.py:1151
  491.8 71.6 %collective-permute-start.39 = (bf16[2,256,1024]{2,1,0:T(8,128)(2,1)}, bf16[2,256,1024]{2,1,0:T(8,128)(2,1)S(1)}, u32[]{:S(2)}, u32[]{:S(2)}) collective-permute-start(bf16[2,256,1024]{2,1,0:T(8,128)(2,1)} %slice.509), channel_id=1, source_target_pairs={{0,8},{4,12},{8,0},{12,4},{16,24},{20,28},{24,16},{28,20},{1,9},{5... | collective-permute-start | bytes 3145736 | tf_op jit(solution)/shard_map/ppermute | solution.py:1151
  648.5 70.4 %collective-permute-start.42 = (bf16[2,768,1024]{2,1,0:T(8,128)(2,1)}, bf16[2,768,1024]{2,1,0:T(8,128)(2,1)S(1)}, u32[]{:S(2)}, u32[]{:S(2)}) collective-permute-start(bf16[2,768,1024]{2,1,0:T(8,128)(2,1)} %shard_map.292), channel_id=1, source_target_pairs={{0,8},{4,12},{8,0},{12,4},{16,24},{20,28},{24,16},{28,20},{1,9},{5... | collective-permute-start | bytes 9437192 | tf_op jit(solution)/shard_map/ppermute | solution.py:1151
  649.5 70.2 %collective-permute-start.43 = (bf16[2,768,1024]{2,1,0:T(8,128)(2,1)}, bf16[2,768,1024]{2,1,0:T(8,128)(2,1)}, u32[]{:S(2)}, u32[]{:S(2)}) collective-permute-start(bf16[2,768,1024]{2,1,0:T(8,128)(2,1)} %shard_map.293), channel_id=1, source_target_pairs={{0,16},{4,20},{8,24},{12,28},{16,0},{20,4},{24,8},{28,12},{1,17},{... | collective-permute-start | bytes 9437192 | tf_op jit(solution)/shard_map/ppermute | solution.py:1151
  745.8 95.7 %collective-permute-start.50 = (bf16[1024,2048]{1,0:T(8,128)(2,1)}, bf16[1024,2048]{1,0:T(8,128)(2,1)S(1)}, u32[]{:S(2)}, u32[]{:S(2)}) collective-permute-start(bf16[1024,2048]{1,0:T(8,128)(2,1)} %shard_map.301), channel_id=1, source_target_pairs={{0,4},{4,0},{8,12},{12,8},{16,20},{20,16},{24,28},{28,24},{1,5},{5... | collective-permute-start | bytes 12582920 | tf_op jit(solution)/shard_map/ppermute | solution.py:1151
  745.9 105.2 %collective-permute-start.45 = (bf16[2,768,1024]{2,1,0:T(8,128)(2,1)}, bf16[2,768,1024]{2,1,0:T(8,128)(2,1)S(1)}, u32[]{:S(2)}, u32[]{:S(2)}) collective-permute-start(bf16[2,768,1024]{2,1,0:T(8,128)(2,1)} %shard_map.295), channel_id=1, source_target_pairs={{0,8},{4,12},{8,0},{12,4},{16,24},{20,28},{24,16},{28,20},{1,9},{5... | collective-permute-start | bytes 9437192 | tf_op jit(solution)/shard_map/ppermute | solution.py:1151
  747.0 104.1 %collective-permute-start.46 = (bf16[2,768,1024]{2,1,0:T(8,128)(2,1)}, bf16[2,768,1024]{2,1,0:T(8,128)(2,1)}, u32[]{:S(2)}, u32[]{:S(2)}) collective-permute-start(bf16[2,768,1024]{2,1,0:T(8,128)(2,1)} %shard_map.296), channel_id=1, source_target_pairs={{0,16},{4,20},{8,24},{12,28},{16,0},{20,4},{24,8},{28,12},{1,17},{... | collective-permute-start | bytes 9437192 | tf_op jit(solution)/shard_map/ppermute | solution.py:1151
  759.1 91.5 %collective-permute-start.47 = (bf16[768,1024]{1,0:T(8,128)(2,1)}, bf16[768,1024]{1,0:T(8,128)(2,1)}, u32[]{:S(2)}, u32[]{:S(2)}) collective-permute-start(bf16[768,1024]{1,0:T(8,128)(2,1)} %slice_bitcast_fusion.5), channel_id=1, source_target_pairs={{0,8},{4,12},{8,0},{12,4},{16,24},{20,28},{24,16},{28,20},{1,9},{5... | collective-permute-start | bytes 4718600 | tf_op jit(solution)/shard_map/ppermute | solution.py:1151
  771.3 79.8 %collective-permute-start.48 = (bf16[768,1024]{1,0:T(8,128)(2,1)}, bf16[768,1024]{1,0:T(8,128)(2,1)}, u32[]{:S(2)}, u32[]{:S(2)}) collective-permute-start(bf16[768,1024]{1,0:T(8,128)(2,1)} %slice_bitcast_fusion.4), channel_id=1, source_target_pairs={{0,16},{4,20},{8,24},{12,28},{16,0},{20,4},{24,8},{28,12},{1,17},{... | collective-permute-start | bytes 4718600 | tf_op jit(solution)/shard_map/ppermute | solution.py:1151
  869.0 99.2 %collective-permute-start.55 = (bf16[2,768,1024]{2,1,0:T(8,128)(2,1)S(1)}, bf16[2,768,1024]{2,1,0:T(8,128)(2,1)}, u32[]{:S(2)}, u32[]{:S(2)}) collective-permute-start(bf16[2,768,1024]{2,1,0:T(8,128)(2,1)S(1)} %pad_maximum_fusion.9), channel_id=1, source_target_pairs={{3,2},{0,1},{4,5},{7,6},{11,10},{8,9},{12,13},{15,14},{19,18},{16,... | collective-permute-start | bytes 9437192 | tf_op jit(solution)/shard_map/ppermute | solution.py:1167
  897.2 71.0 %collective-permute-start.51 = (bf16[768,1024]{1,0:T(8,128)(2,1)}, bf16[768,1024]{1,0:T(8,128)(2,1)}, u32[]{:S(2)}, u32[]{:S(2)}) collective-permute-start(bf16[768,1024]{1,0:T(8,128)(2,1)} %slice_bitcast_fusion.3), channel_id=1, source_target_pairs={{0,8},{4,12},{8,0},{12,4},{16,24},{20,28},{24,16},{28,20},{1,9},{5... | collective-permute-start | bytes 4718600 | tf_op jit(solution)/shard_map/ppermute | solution.py:1151
  990.8 82.4 %collective-permute-start.60 = (bf16[1024,2048]{1,0:T(8,128)(2,1)}, bf16[1024,2048]{1,0:T(8,128)(2,1)}, u32[]{:S(2)}, u32[]{:S(2)}) collective-permute-start(bf16[1024,2048]{1,0:T(8,128)(2,1)} %shard_map.313), channel_id=1, source_target_pairs={{0,4},{4,0},{8,12},{12,8},{16,20},{20,16},{24,28},{28,24},{1,5},{5... | collective-permute-start | bytes 12582920 | tf_op jit(solution)/shard_map/ppermute | solution.py:1151
  990.8 94.4 %collective-permute-start.59 = (bf16[1024,2048]{1,0:T(8,128)(2,1)}, bf16[1024,2048]{1,0:T(8,128)(2,1)}, u32[]{:S(2)}, u32[]{:S(2)}) collective-permute-start(bf16[1024,2048]{1,0:T(8,128)(2,1)} %shard_map.312), channel_id=1, source_target_pairs={{0,4},{4,0},{8,12},{12,8},{16,20},{20,16},{24,28},{28,24},{1,5},{5... | collective-permute-start | bytes 12582920 | tf_op jit(solution)/shard_map/ppermute | solution.py:1151
  1015.2 291.3 %reduce-scatter.5.cloned.1.call-start = ((), (), s32[]{:S(2)}) async-start(), calls=%async_computation.3 | async-start | bytes 2621440 | tf_op jit(solution)/shard_map/reduce_scatter | solution.py:1207
  1022.2 72.2 %collective-permute-start.67 = (bf16[2,768,1024]{2,1,0:T(8,128)(2,1)}, bf16[2,768,1024]{2,1,0:T(8,128)(2,1)}, u32[]{:S(2)}, u32[]{:S(2)}) collective-permute-start(bf16[2,768,1024]{2,1,0:T(8,128)(2,1)} %pad_maximum_fusion.10), channel_id=1, source_target_pairs={{3,2},{4,5},{11,10},{12,13},{19,18},{20,21},{27,26},{28,29}} | collective-permute-start | bytes 9437192 | tf_op jit(solution)/shard_map/ppermute | solution.py:1167
  1029.6 64.9 %collective-permute-start.66 = (bf16[2,768,1024]{2,1,0:T(8,128)(2,1)}, bf16[2,768,1024]{2,1,0:T(8,128)(2,1)}, u32[]{:S(2)}, u32[]{:S(2)}) collective-permute-start(bf16[2,768,1024]{2,1,0:T(8,128)(2,1)} %fusion), channel_id=1, source_target_pairs={{2,1},{5,6},{10,9},{13,14},{18,17},{21,22},{26,25},{29,30}} | collective-permute-start | bytes 9437192 | tf_op jit(solution)/shard_map/ppermute | solution.py:1167
  1156.2 102.2 %collective-permute-start.75 = (bf16[2,768,1024]{2,1,0:T(8,128)(2,1)S(1)}, bf16[2,768,1024]{2,1,0:T(8,128)(2,1)}, u32[]{:S(2)}, u32[]{:S(2)}) collective-permute-start(bf16[2,768,1024]{2,1,0:T(8,128)(2,1)S(1)} %add_convert_fusion.1), channel_id=1, source_target_pairs={{1,0},{6,7},{9,8},{14,15},{17,16},{22,23},{25,24},{30,31}} | collective-permute-start | bytes 9437192 | tf_op jit(solution)/shard_map/ppermute | solution.py:1167
  1162.5 95.9 %collective-permute-start.74 = (bf16[2,512,1024]{2,1,0:T(8,128)(2,1)}, bf16[2,512,1024]{2,1,0:T(8,128)(2,1)}, u32[]{:S(2)}, u32[]{:S(2)}) collective-permute-start(bf16[2,512,1024]{2,1,0:T(8,128)(2,1)} %add_convert_fusion.4), channel_id=1, source_target_pairs={{1,0},{2,1},{3,2},{5,4},{6,5},{7,6},{9,8},{10,9},{11,10},{13,12},{... | collective-permute-start | bytes 6291464 | tf_op jit(solution)/shard_map/ppermute | solution.py:24
  (135 other events, 2688.3 us)
Sparse Core Ops, SparseCore 0:
  70.1 55.3 all-gather.2
  1015.3 54.9 reduce-scatter.2
  1263.3 43.1 reduce-scatter.4
